TPU v7x, 32 devices: a whole 2x2x4 slice. The times are simulated.
32 devices in a mesh: lat: 8 (over z, y), lev: 4 (over x, core).
Axes of the slice: x: 2, y: 2, z: 4, core: 2. Of those that a mesh axis runs over, the one named last changes fastest.
Arguments:
- grid: bfloat16 [16, 160, 3200], P('lev', 'lat'), may hold values from -6 to 6
- dep_row: int32 [160, 3200], P('lat'), may hold values from 0 to 158, as said below
- dep_col: int32 [160, 3200], P('lat'), may hold values from 0 to 3199, as said below
- lat_frac: bfloat16 [160, 3200], P('lat'), may hold values from 0 to 1
- lon_frac: bfloat16 [160, 3200], P('lat'), may hold values from 0 to 1
- pair_ids: int32 [8], replicated, may hold values from 1 to 639, as said below
- analysis: bfloat16 [8, 160, 1280], P('lat', None, 'lev'), may hold values from -0.0078125 to 0.0078125
Outputs:
- spectral: float32 [8, 16, 2, 1280], P('lat', None, None, 'lev')
Inputs may be any that keep to these rules, and one draw needn't show every extreme that they name: dep_row[j, i] lies from max(j - 2, 0) to min(j + 1, 158). dep_col[j, i] lies within 8 columns of i, modulo 3200. `pair_ids`: all distinct.
All inputs are finite; a program needn't handle non-finite values.
Results may differ from a plain program's by a relative error of at most 0.0046.
Values may be sent and summed in bfloat16 or wider, within the bound.
No kernel may reach another device: no remote copies, remote signals or barrier semaphores. Data moves between devices by JAX's collectives and lax.ppermute only.
A program may use at most 192 MiB of HBM per device.

v0:
```python
import math

import jax
import jax.numpy as jnp
from jax import lax
from jax.sharding import PartitionSpec as P

NMAX = 1279
REACH = 8


def padded_2(cells, sides, width):
    for axis, dim in sides:
        count = lax.axis_size(axis)
        ends = count - 1
        head = lax.slice_in_dim(cells, 0, width, axis=dim)
        tail = lax.slice_in_dim(cells, cells.shape[dim] - width, cells.shape[dim], axis=dim)
        cells = jnp.concatenate(
            [
                lax.ppermute(tail, axis, [(i, (i + 1) % count) for i in range(ends)]),
                cells,
                lax.ppermute(head, axis, [((i + 1) % count, i) for i in range(ends)]),
            ],
            axis=dim,
        )
    return cells


def fourier_basis(pair_ids, lon_count):
    longitude = jnp.arange(lon_count, dtype=jnp.int32)
    wavenumbers = jnp.stack([pair_ids, NMAX + 1 - pair_ids], axis=1)
    phase_turn = longitude[:, None, None] * wavenumbers[None, :, :] % lon_count
    angles = phase_turn.astype(jnp.float32) * (2.0 * math.pi / lon_count)
    basis_table = jnp.stack([jnp.cos(angles), -jnp.sin(angles)], axis=3)
    return basis_table.reshape(lon_count, -1).astype(jnp.bfloat16)


def shards(grid, dep_row, dep_col, lat_frac, lon_frac, pair_ids, analysis):
    rim_depth = 2
    slice_count, band_rows, lon_count = grid.shape
    padded = padded_2(grid, (("lat", 1),), rim_depth)
    latitude = lax.axis_index("lat") * band_rows + jnp.arange(band_rows, dtype=jnp.int32)[:, None]
    longitude = jnp.arange(lon_count, dtype=jnp.int32)[None, :]
    row_shift = dep_row - latitude
    col_shift = (dep_col - longitude + REACH) % lon_count - REACH
    lat_weight = lat_frac.astype(jnp.float32)
    lon_weight = lon_frac.astype(jnp.float32)
    offsets = list(range(-REACH, REACH + 2))
    col_weights = [
        (
            jnp.where(col_shift == offset, 1.0 - lon_weight, 0.0)
            + jnp.where(col_shift == offset - 1, lon_weight, 0.0)
        )[None, :, :]
        for offset in offsets
    ]
    departed_sum = jnp.zeros((slice_count, band_rows, lon_count), jnp.float32)
    for row_step in range(-rim_depth, rim_depth + 1):
        rows = padded[:, rim_depth + row_step : rim_depth + row_step + band_rows, :]
        zonal = jnp.zeros((slice_count, band_rows, lon_count), jnp.float32)
        for position, offset in enumerate(offsets):
            zonal = zonal + col_weights[position] * jnp.roll(rows, -offset, axis=2).astype(
                jnp.float32
            )
        row_weight = jnp.where(row_shift == row_step, 1.0 - lat_weight, 0.0) + jnp.where(
            row_shift == row_step - 1, lat_weight, 0.0
        )
        departed_sum = departed_sum + row_weight[None, :, :] * zonal
    departed = departed_sum.astype(jnp.bfloat16)
    basis = fourier_basis(pair_ids, lon_count)
    fourier = jnp.einsum("sji,iq->sjq", departed, basis, preferred_element_type=jnp.float32).astype(
        jnp.bfloat16
    )
    pair_dev = analysis.shape[0]
    col_count = analysis.shape[2]
    own_pairs = lax.dynamic_slice_in_dim(pair_ids, lax.axis_index("lat") * pair_dev, pair_dev)
    columns = lax.axis_index("lev") * col_count + jnp.arange(col_count, dtype=jnp.int32)
    first_wave = (columns[None, :] < (NMAX + 1 - own_pairs)[:, None])[:, None, None, :]
    arrived = lax.all_to_all(fourier, "lat", split_axis=2, concat_axis=1, tiled=True)
    coeffs = lax.all_gather(arrived, "lev", axis=0, tiled=True)
    piece_rows = coeffs.shape[0]
    shaped = coeffs.reshape(piece_rows, coeffs.shape[1], pair_dev, 4)
    products = jnp.einsum("sjdq,djc->dsqc", shaped, analysis, preferred_element_type=jnp.float32)
    return jnp.where(first_wave, products[:, :, 0:2, :], products[:, :, 2:4, :])


def solution(mesh):
    return jax.shard_map(
        shards,
        mesh=mesh,
        in_specs=(
            P("lev", "lat", None),
            P("lat", None),
            P("lat", None),
            P("lat", None),
            P("lat", None),
            P(),
            P("lat", None, "lev"),
        ),
        out_specs=P("lat", None, None, "lev"),
        check_vma=False,
    )
```

profile of v0, /device:TPU:0, one launch (start us, length us, event | category | flops | bytes accessed | tf_op | source)
XLA Modules:
  0.0 171.5 jit_solution(8048332191979455177)
XLA Ops:
  0.0 0.9 fusion.107
  0.9 4.9 %collective-permute-start = (bf16[4,2,3200]{2,0,1:T(4,128)(2,1)S(1)}, bf16[4,2,3200]{2,0,1:T(4,128)(2,1)S(1)}, u32[]{:S(2)}, u32[]{:S(2)}) collective-permute-start(bf16[4,2,3200]{2,0,1:T(4,128)(2,1)S(1)} %get-tuple-element.183), channel_id=1, source_target_pairs={{0,4},{4,8},{8,12},{12,16},{16,20},{20,24},{24,28},{1,5},{5,9},{9,... | collective-permute-start | bytes 153608 | tf_op jit(solution)/shard_map/ppermute | solution.py:20
  5.8 1.3 collective-permute-start.1
  7.1 2.6 %fusion.91 = (bf16[4,20,3192]{2,0,1:T(4,128)(2,1)}, bf16[4,20,3192]{2,0,1:T(4,128)(2,1)}) fusion(bf16[4,20,3200]{2,0,1:T(4,128)(2,1)} %param.7), kind=kLoop, calls=%fused_computation.156 | loop fusion | bytes 2042880 | tf_op jit(solution)/shard_map/jit(_roll_static)/slice | solution.py:61
  9.7 1.4 fusion.93
  11.1 1.4 fusion.95
  12.5 1.4 fusion.97
  13.9 1.4 fusion.99
  15.3 1.4 fusion.101
  16.7 1.5 fusion.103
  18.2 1.5 fusion.105
  23.9 3.2 %fusion.30 = (f32[20,3200]{1,0:T(8,128)}, f32[20,3200]{1,0:T(8,128)}, f32[20,3200]{1,0:T(8,128)}, pred[20,3200]{1,0:T(8,128)(4,1)S(1)}, f32[20,3200]{1,0:T(8,128...) fusion(bf16[20,3200]{1,0:T(8,128)(2,1)S(1)} %copy-done.3, ...), kind=kLoop, calls=%fused_computation.59 | loop fusion | flops 4416000 | bytes 4032000 | tf_op jit(solution)/shard_map/add | solution.py:51
  27.1 1.7 fusion.25
  29.1 1.0 fusion.36
  30.2 1.0 fusion.37
  31.2 0.9 cosine_convert_fusion
  33.4 0.8 reshape.90
  35.8 0.8 fusion.57
  36.6 1.6 fusion.59
  38.2 2.2 %fusion.61 = (bf16[4,20,3194]{2,0,1:T(4,128)(2,1)}, bf16[4,20,3194]{2,0,1:T(4,128)(2,1)}, bf16[4,20,3194]{2,0,1:T(4,128)(2,1)}, bf16[4,20,3194]{2,0,1:T(4,128)(2,1)}) fusion(bf16[4,22,3200]{2,0,1:T(4,128)(2,1)S(1)} %constant_dynamic-update-slice_fusion.2), kind=kLoop, calls=%fused_computation.126 | loop fusion | bytes 4088320 | tf_op jit(solution)/shard_map/jit(_roll_static)/slice | solution.py:61
  40.4 2.1 %fusion.63 = (bf16[4,20,3195]{2,0,1:T(4,128)(2,1)}, bf16[4,20,3195]{2,0,1:T(4,128)(2,1)}, bf16[4,20,3195]{2,0,1:T(4,128)(2,1)}, bf16[4,20,3195]{2,0,1:T(4,128)(2,1)}) fusion(bf16[4,22,3200]{2,0,1:T(4,128)(2,1)S(1)} %constant_dynamic-update-slice_fusion.2), kind=kLoop, calls=%fused_computation.128 | loop fusion | bytes 4089600 | tf_op jit(solution)/shard_map/jit(_roll_static)/slice | solution.py:61
  42.5 2.0 %fusion.65 = (bf16[4,20,3196]{2,0,1:T(4,128)(2,1)}, bf16[4,20,3196]{2,0,1:T(4,128)(2,1)}, bf16[4,20,3196]{2,0,1:T(4,128)(2,1)}, bf16[4,20,3196]{2,0,1:T(4,128)(2,1)}) fusion(bf16[4,22,3200]{2,0,1:T(4,128)(2,1)S(1)} %constant_dynamic-update-slice_fusion.2), kind=kLoop, calls=%fused_computation.130 | loop fusion | bytes 4090880 | tf_op jit(solution)/shard_map/jit(_roll_static)/slice | solution.py:61
  44.6 2.0 %fusion.67 = (bf16[4,20,3197]{2,0,1:T(4,128)(2,1)}, bf16[4,20,3197]{2,0,1:T(4,128)(2,1)}, bf16[4,20,3197]{2,0,1:T(4,128)(2,1)}, bf16[4,20,3197]{2,0,1:T(4,128)(2,1)}) fusion(bf16[4,22,3200]{2,0,1:T(4,128)(2,1)S(1)} %constant_dynamic-update-slice_fusion.2), kind=kLoop, calls=%fused_computation.132 | loop fusion | bytes 4092160 | tf_op jit(solution)/shard_map/jit(_roll_static)/slice | solution.py:61
  46.6 2.0 %fusion.69 = (bf16[4,20,3198]{2,0,1:T(4,128)(2,1)}, bf16[4,20,3198]{2,0,1:T(4,128)(2,1)}, bf16[4,20,3198]{2,0,1:T(4,128)(2,1)}, bf16[4,20,3198]{2,0,1:T(4,128)(2,1)}) fusion(bf16[4,22,3200]{2,0,1:T(4,128)(2,1)S(1)} %constant_dynamic-update-slice_fusion.2), kind=kLoop, calls=%fused_computation.134 | loop fusion | bytes 4093440 | tf_op jit(solution)/shard_map/jit(_roll_static)/slice | solution.py:61
  48.6 2.1 %fusion.71 = (bf16[4,20,3199]{2,0,1:T(4,128)(2,1)}, bf16[4,20,3199]{2,0,1:T(4,128)(2,1)}, bf16[4,20,3199]{2,0,1:T(4,128)(2,1)}, bf16[4,20,3199]{2,0,1:T(4,128)(2,1)}) fusion(bf16[4,22,3200]{2,0,1:T(4,128)(2,1)S(1)} %constant_dynamic-update-slice_fusion.2), kind=kLoop, calls=%fused_computation.136 | loop fusion | bytes 4094720 | tf_op jit(solution)/shard_map/jit(_roll_static)/slice | solution.py:61
  51.4 0.7 fusion.60
  52.1 0.7 fusion.62
  54.2 0.7 fusion.68
  54.9 0.7 fusion.70
  56.4 2.0 %fusion.79 = (bf16[4,20,3194]{2,0,1:T(4,128)(2,1)}, bf16[4,20,3194]{2,0,1:T(4,128)(2,1)}, bf16[4,20,3194]{2,0,1:T(4,128)(2,1)}, bf16[4,20,3194]{2,0,1:T(4,128)(2,1)}) fusion(bf16[4,22,3200]{2,0,1:T(4,128)(2,1)S(1)} %get-tuple-element.181), kind=kLoop, calls=%fused_computation.144 | loop fusion | bytes 4088320 | tf_op jit(solution)/shard_map/jit(_roll_static)/slice | solution.py:61
  58.4 2.0 %fusion.81 = (bf16[4,20,3195]{2,0,1:T(4,128)(2,1)}, bf16[4,20,3195]{2,0,1:T(4,128)(2,1)}, bf16[4,20,3195]{2,0,1:T(4,128)(2,1)}, bf16[4,20,3195]{2,0,1:T(4,128)(2,1)}) fusion(bf16[4,22,3200]{2,0,1:T(4,128)(2,1)S(1)} %get-tuple-element.181), kind=kLoop, calls=%fused_computation.146 | loop fusion | bytes 4089600 | tf_op jit(solution)/shard_map/jit(_roll_static)/slice | solution.py:61
  60.4 2.1 %fusion.83 = (bf16[4,20,3196]{2,0,1:T(4,128)(2,1)}, bf16[4,20,3196]{2,0,1:T(4,128)(2,1)}, bf16[4,20,3196]{2,0,1:T(4,128)(2,1)}, bf16[4,20,3196]{2,0,1:T(4,128)(2,1)}) fusion(bf16[4,22,3200]{2,0,1:T(4,128)(2,1)S(1)} %get-tuple-element.181), kind=kLoop, calls=%fused_computation.148 | loop fusion | bytes 4090880 | tf_op jit(solution)/shard_map/jit(_roll_static)/slice | solution.py:61
  62.5 2.0 %fusion.85 = (bf16[4,20,3197]{2,0,1:T(4,128)(2,1)}, bf16[4,20,3197]{2,0,1:T(4,128)(2,1)}, bf16[4,20,3197]{2,0,1:T(4,128)(2,1)}, bf16[4,20,3197]{2,0,1:T(4,128)(2,1)}) fusion(bf16[4,22,3200]{2,0,1:T(4,128)(2,1)S(1)} %get-tuple-element.181), kind=kLoop, calls=%fused_computation.150 | loop fusion | bytes 4092160 | tf_op jit(solution)/shard_map/jit(_roll_static)/slice | solution.py:61
  64.5 2.1 %fusion.87 = (bf16[4,20,3198]{2,0,1:T(4,128)(2,1)}, bf16[4,20,3198]{2,0,1:T(4,128)(2,1)}, bf16[4,20,3198]{2,0,1:T(4,128)(2,1)}, bf16[4,20,3198]{2,0,1:T(4,128)(2,1)}) fusion(bf16[4,22,3200]{2,0,1:T(4,128)(2,1)S(1)} %get-tuple-element.181), kind=kLoop, calls=%fused_computation.152 | loop fusion | bytes 4093440 | tf_op jit(solution)/shard_map/jit(_roll_static)/slice | solution.py:61
  66.6 2.0 %fusion.89 = (bf16[4,20,3199]{2,0,1:T(4,128)(2,1)}, bf16[4,20,3199]{2,0,1:T(4,128)(2,1)}, bf16[4,20,3199]{2,0,1:T(4,128)(2,1)}, bf16[4,20,3199]{2,0,1:T(4,128)(2,1)}) fusion(bf16[4,22,3200]{2,0,1:T(4,128)(2,1)S(1)} %get-tuple-element.181), kind=kLoop, calls=%fused_computation.154 | loop fusion | bytes 4094720 | tf_op jit(solution)/shard_map/jit(_roll_static)/slice | solution.py:61
  68.6 2.3 %fusion.75 = (bf16[4,20,3192]{2,0,1:T(4,128)(2,1)}, bf16[4,20,3192]{2,0,1:T(4,128)(2,1)}, bf16[4,20,3192]{2,0,1:T(4,128)(2,1)}, bf16[4,20,3192]{2,0,1:T(4,128)(2,1)}) fusion(bf16[4,22,3200]{2,0,1:T(4,128)(2,1)S(1)} %get-tuple-element.181), kind=kLoop, calls=%fused_computation.140 | loop fusion | bytes 4085760 | tf_op jit(solution)/shard_map/jit(_roll_static)/slice | solution.py:61
  70.9 2.0 %fusion.77 = (bf16[4,20,3193]{2,0,1:T(4,128)(2,1)}, bf16[4,20,3193]{2,0,1:T(4,128)(2,1)}, bf16[4,20,3193]{2,0,1:T(4,128)(2,1)}, bf16[4,20,3193]{2,0,1:T(4,128)(2,1)}) fusion(bf16[4,22,3200]{2,0,1:T(4,128)(2,1)S(1)} %get-tuple-element.181), kind=kLoop, calls=%fused_computation.142 | loop fusion | bytes 4087040 | tf_op jit(solution)/shard_map/jit(_roll_static)/slice | solution.py:61
  72.9 0.7 fusion.78
  74.3 0.7 fusion.82
  75.0 0.7 fusion.84
  77.2 0.7 fusion.90
  78.6 1.6 fusion.55
  80.8 1.6 fusion.73
  83.8 65.8 %add_convert_fusion = bf16[4,20,3200]{2,0,1:T(4,128)(2,1)} fusion(bf16[4,20,3200]{2,0,1:T(4,128)(2,1)S(1)} %copy-done.1, bf16[4,22,3200]{2,0,1:T(4,128)(2,1)S(1)} %constant_dynamic-update-slice_fusion.2, bf16[4,22,3200]{2,0,1:T(4,128)(2,1)S(1)} %get-tuple-element.181, bf16[4,20,3192]{2,0,1:T(4,128)(2,1)} %get-tuple-element.88, ...), kind=kLoop, calls=%fused_computation.39 | loop fusion | flops 135680000 | bytes 52480000 | tf_op jit(solution)/shard_map/convert_element_type | solution.py:68
  149.6 1.4 convolution_convert_fusion
  151.8 7.0 %all-to-all-start = ((bf16[8,2,160]{2,1,0:T(2,128)(2,1)}), bf16[8,2,160]{2,1,0:T(2,128)(2,1)S(1)}, u32[]{:S(2)}, u32[]{:S(2)}) async-start(bf16[8,2,160]{2,1,0:T(2,128)(2,1)} %reshape.93), calls=%async_computation | async-start | bytes 16384 | tf_op jit(solution)/shard_map/all_to_all | solution.py:78
  158.8 6.5 %all-to-all-done = bf16[8,2,160]{2,1,0:T(2,128)(2,1)S(1)} async-done(((bf16[8,2,160]{2,1,0:T(2,128)(2,1)}), bf16[8,2,160]{2,1,0:T(2,128)(2,1)S(1)}, u32[]{:S(2)}, u32[]{:S(2)}) %all-to-all-start) | async-done | bytes 5152 | tf_op jit(solution)/shard_map/all_to_all | solution.py:78
  165.5 5.2 %all_gather.3 = bf16[16,160,4]{1,2,0:T(4,128)(2,1)S(1)} all-gather(bf16[4,160,4]{1,2,0:T(4,128)(2,1)S(1)} %all_to_all.16), channel_id=1, replica_groups=mesh['lat'=8,'lev'=4] {'lev'}, dimensions={0}, use_global_device_ids=true | all-gather | bytes 25600 | tf_op jit(solution)/shard_map/all_gather | solution.py:79
  (75 shorter events, 16.3 us)
Async XLA Ops:
  0.0 170.7 %copy-start = (bf16[1,160,320]{2,1,0:T(8,128)(2,1)S(1)}, bf16[1,160,320]{2,1,0:T(8,128)(2,1)}, u32[]{:S(2)}) copy-start(bf16[1,160,320]{2,1,0:T(8,128)(2,1)} %param.13) | copy-start | bytes 307204
  0.9 34.5 %collective-permute-start = (bf16[4,2,3200]{2,0,1:T(4,128)(2,1)S(1)}, bf16[4,2,3200]{2,0,1:T(4,128)(2,1)S(1)}, u32[]{:S(2)}, u32[]{:S(2)}) collective-permute-start(bf16[4,2,3200]{2,0,1:T(4,128)(2,1)S(1)} %get-tuple-element.183), channel_id=1, source_target_pairs={{0,4},{4,8},{8,12},{12,16},{16,20},{20,24},{24,28},{1,5},{5,9},{9,... | collective-permute-start | bytes 153608 | tf_op jit(solution)/shard_map/ppermute | solution.py:20
  5.8 30.0 %collective-permute-start.1 = (bf16[4,2,3200]{2,0,1:T(4,128)(2,1)S(1)}, bf16[4,2,3200]{2,0,1:T(4,128)(2,1)S(1)}, u32[]{:S(2)}, u32[]{:S(2)}) collective-permute-start(bf16[4,2,3200]{2,0,1:T(4,128)(2,1)S(1)} %get-tuple-element.184), channel_id=1, source_target_pairs={{4,0},{8,4},{12,8},{16,12},{20,16},{24,20},{28,24},{5,1},{9,5},{13... | collective-permute-start | bytes 153608 | tf_op jit(solution)/shard_map/ppermute | solution.py:22
  7.1 2.6 %copy-start.1 = (bf16[4,20,3200]{2,0,1:T(4,128)(2,1)S(1)}, bf16[4,20,3200]{2,0,1:T(4,128)(2,1)}, u32[]{:S(2)}) copy-start(bf16[4,20,3200]{2,0,1:T(4,128)(2,1)} %param.7) | copy-start | bytes 1536004
  19.7 4.2 %copy-start.2 = (s32[20,3200]{1,0:T(8,128)S(1)}, s32[20,3200]{1,0:T(8,128)}, u32[]{:S(2)}) copy-start(s32[20,3200]{1,0:T(8,128)} %param.9) | copy-start | bytes 768004
  21.1 2.8 %copy-start.3 = (bf16[20,3200]{1,0:T(8,128)(2,1)S(1)}, bf16[20,3200]{1,0:T(8,128)(2,1)}, u32[]{:S(2)}) copy-start(bf16[20,3200]{1,0:T(8,128)(2,1)} %param.11) | copy-start | bytes 384004
  23.9 3.2 %copy-start.5 = (s32[20,3200]{1,0:T(8,128)S(1)}, s32[20,3200]{1,0:T(8,128)}, u32[]{:S(2)}) copy-start(s32[20,3200]{1,0:T(8,128)} %param.8) | copy-start | bytes 768004
  23.9 3.2 %copy-start.6 = (bf16[20,3200]{1,0:T(8,128)(2,1)S(1)}, bf16[20,3200]{1,0:T(8,128)(2,1)}, u32[]{:S(2)}) copy-start(bf16[20,3200]{1,0:T(8,128)(2,1)} %param.10) | copy-start | bytes 384004
  30.2 1.0 copy-start.15
  80.8 2.2 %copy-start.9 = (bf16[4,20,6]{2,0,1:T(4,128)(2,1)S(1)}, bf16[4,20,6]{2,0,1:T(4,128)(2,1)}, u32[]{:S(2)}) copy-start(bf16[4,20,6]{2,0,1:T(4,128)(2,1)} %get-tuple-element.159) | copy-start | bytes 2884
  80.8 2.2 %copy-start.10 = (bf16[4,20,6]{2,0,1:T(4,128)(2,1)S(1)}, bf16[4,20,6]{2,0,1:T(4,128)(2,1)}, u32[]{:S(2)}) copy-start(bf16[4,20,6]{2,0,1:T(4,128)(2,1)} %get-tuple-element.160) | copy-start | bytes 2884
  80.8 2.2 %copy-start.11 = (bf16[4,20,5]{2,0,1:T(4,128)(2,1)S(1)}, bf16[4,20,5]{2,0,1:T(4,128)(2,1)}, u32[]{:S(2)}) copy-start(bf16[4,20,5]{2,0,1:T(4,128)(2,1)} %get-tuple-element.163) | copy-start | bytes 2404
  80.8 2.3 %copy-start.12 = (bf16[4,20,5]{2,0,1:T(4,128)(2,1)S(1)}, bf16[4,20,5]{2,0,1:T(4,128)(2,1)}, u32[]{:S(2)}) copy-start(bf16[4,20,5]{2,0,1:T(4,128)(2,1)} %get-tuple-element.164) | copy-start | bytes 2404
  80.8 2.3 %copy-start.13 = (bf16[4,20,4]{2,0,1:T(4,128)(2,1)S(1)}, bf16[4,20,4]{2,0,1:T(4,128)(2,1)}, u32[]{:S(2)}) copy-start(bf16[4,20,4]{2,0,1:T(4,128)(2,1)} %get-tuple-element.167) | copy-start | bytes 1924
  80.8 2.3 %copy-start.14 = (bf16[4,20,4]{2,0,1:T(4,128)(2,1)S(1)}, bf16[4,20,4]{2,0,1:T(4,128)(2,1)}, u32[]{:S(2)}) copy-start(bf16[4,20,4]{2,0,1:T(4,128)(2,1)} %get-tuple-element.168) | copy-start | bytes 1924
  82.4 1.0 copy-start.4
  83.0 0.8 copy-start.8
  83.0 0.8 copy-start.7
  83.0 0.8 slice-start
  151.8 13.5 %all-to-all-start = ((bf16[8,2,160]{2,1,0:T(2,128)(2,1)}), bf16[8,2,160]{2,1,0:T(2,128)(2,1)S(1)}, u32[]{:S(2)}, u32[]{:S(2)}) async-start(bf16[8,2,160]{2,1,0:T(2,128)(2,1)} %reshape.93), calls=%async_computation | async-start | bytes 16384 | tf_op jit(solution)/shard_map/all_to_all | solution.py:78
where the time goes:
time: 172 us
  other arithmetic  74 us (43%)
  local copies, waits for them, and re-layouts  70.3 us (41%)
  starting transfers between devices  13.1 us (8%)
  waiting for transfers between devices  6.51 us (4%)
  blocking collectives  5.19 us (3%)
    convert_element_type x1, other arithmetic, shards(): departed = departed_sum.astype(jnp.bfloat16)  65.8 us
    slice x55, local copies, waits for them, and re-layouts, shards(): jnp.roll(rows, -offset, axis=2).astype(jnp.float32)  65 us
    all_to_all x1, starting transfers between devices, shards(): lax.all_to_all(fourier, 'lat', split_axis=2, concat_axis=1, tiled=True)  6.96 us
    all_to_all x1, waiting for transfers between devices, shards(): lax.all_to_all(fourier, 'lat', split_axis=2, concat_axis=1, tiled=True)  6.51 us
    add x4, other arithmetic, shards(): jnp.where(col_shift == offset, 1.0 - lon_weight, 0.0)  5.5 us
    all_gather x1, blocking collectives, shards(): coeffs = lax.all_gather(arrived, 'lev', axis=0, tiled=True)  5.19 us
    ppermute x1, starting transfers between devices, padded_2(): lax.ppermute(tail, axis, [(i, (i + 1) % count) for i in range(ends)])  4.87 us
  transfers between devices with their start and end apart: 3, of which 1 were waited for; matrix products, arithmetic and copies ran while one was open for 16% of the time, Pallas kernels for 0%

commit v1 on v0

v1 whole, which is shorter than its diff:
```python
import functools
import math

import jax
import jax.numpy as jnp
import numpy as np
from jax import lax
from jax.experimental import pallas as pl
from jax.experimental.pallas import tpu as pltpu
from jax.sharding import PartitionSpec as P

NMAX = 1279
LANES = 128
RIM = 2
EDGE = 2 * RIM


def lane_gather(values, indices):
    numbers = lax.GatherDimensionNumbers(
        offset_dims=(),
        collapsed_slice_dims=(1,),
        start_index_map=(1,),
        operand_batching_dims=(0,),
        start_indices_batching_dims=(0,),
    )
    return lax.gather(
        values,
        indices[..., None],
        numbers,
        (1, 1),
        mode=lax.GatherScatterMode.PROMISE_IN_BOUNDS,
    )


def tile_at(t):
    return pl.ds(pl.multiple_of(t * LANES, LANES), LANES)


def neighbours(t, tiles):
    return jnp.where(t == 0, tiles - 1, t - 1), jnp.where(t == tiles - 1, 0, t + 1)


def lane_plan(dep_col, t, lon_count):
    lane = lax.broadcasted_iota(jnp.int32, dep_col.shape, 1)
    shift = dep_col - (lane + t * LANES)
    shift = jnp.where(shift > lon_count // 2, shift - lon_count, shift)
    shift = jnp.where(shift < -(lon_count // 2), shift + lon_count, shift)
    west = lane + shift
    east = west + 1
    west_lane = west & (LANES - 1)
    east_lane = east & (LANES - 1)
    return west_lane, west == west_lane, east_lane, east == east_lane


def row_weights(row_shift, lat_weight):
    low, high = 1.0 - lat_weight, lat_weight
    return [
        jnp.where(row_shift == step, low, 0.0) + jnp.where(row_shift == step - 1, high, 0.0)
        for step in range(-RIM, RIM + 1)
    ]


def interpolate(load, plan, weights, lon_weight):
    west_lane, west_own, east_lane, east_own = plan
    west_sum = east_sum = None
    for position, weight in enumerate(weights):
        own, beside = load(position)
        west = jnp.where(west_own, lane_gather(own, west_lane), lane_gather(beside, west_lane))
        east = jnp.where(east_own, lane_gather(own, east_lane), lane_gather(beside, east_lane))
        west_sum = weight * west if position == 0 else west_sum + weight * west
        east_sum = weight * east if position == 0 else east_sum + weight * east
    return (1.0 - lon_weight) * west_sum + lon_weight * east_sum


def beside_of(west_tile, east_tile):
    lane = lax.broadcasted_iota(jnp.int32, west_tile.shape, 1)
    return jnp.where(lane < LANES // 2, east_tile, west_tile)


def inner_kernel(
    place, pair_ids, grid, dep_row, dep_col, lat_frac, lon_frac,
    inner_out, basis_out, own_tiles, beside_tiles, departed, waves,
):
    slices, band_rows, lon_count = grid.shape
    tiles = lon_count // LANES
    inner = band_rows - 2 * RIM
    orders = basis_out.shape[0]
    first_row = place[0]

    def wave_rows(group, carry):
        row = lax.broadcasted_iota(jnp.int32, (16, LANES), 0)
        pair = pair_ids[4 * group + 3]
        for at in (2, 1, 0):
            pair = jnp.where(row < 4 * (at + 1), pair_ids[4 * group + at], pair)
        wave = jnp.where((row & 2) == 0, pair, NMAX + 1 - pair)
        waves[pl.ds(pl.multiple_of(group * 16, 16), 16), :] = wave.astype(jnp.float32)
        return carry

    lax.fori_loop(0, orders // 16, wave_rows, 0)

    def fill(t, carry):
        before, after = neighbours(t, tiles)
        for f in range(slices):
            own_tiles[t, f, 0:band_rows, :] = grid[f, :, tile_at(t)].astype(jnp.float32)
            beside_tiles[t, f, 0:band_rows, :] = beside_of(
                grid[f, :, tile_at(before)].astype(jnp.float32),
                grid[f, :, tile_at(after)].astype(jnp.float32),
            )
        return carry

    lax.fori_loop(0, tiles, fill, 0)

    def basis_tile(t, group):
        rows = pl.ds(pl.multiple_of(group * 16, 16), 16)
        lane = lax.broadcasted_iota(jnp.int32, (16, LANES), 1)
        row = lax.broadcasted_iota(jnp.int32, (16, LANES), 0)
        longitude = (lane + t * LANES).astype(jnp.float32)
        quarter = jnp.where((row & 1) == 0, 0.0, float(lon_count // 4))
        steps = longitude * waves[rows, :] + quarter
        turns = jnp.floor(steps * (1.0 / lon_count) + 0.5)
        angle = (lon_count // 4 - jnp.abs(steps - turns * lon_count)) * (2.0 * math.pi / lon_count)
        square = angle * angle
        series = jnp.float32(-1.0 / 39916800.0)
        for term in (1.0 / 362880.0, -1.0 / 5040.0, 1.0 / 120.0, -1.0 / 6.0, 1.0):
            series = series * square + term
        basis_out[rows, tile_at(t)] = (angle * series).astype(jnp.bfloat16)

    def tile(t, carry):
        cols = tile_at(t)
        groups = []
        for start in range(RIM, RIM + inner, 8):
            rows = slice(start, start + 8)
            latitude = first_row + start + lax.broadcasted_iota(jnp.int32, (8, LANES), 0)
            plan = lane_plan(dep_col[rows, cols], t, lon_count)
            weights = row_weights(
                dep_row[rows, cols] - latitude, lat_frac[:, cols].astype(jnp.float32)[rows]
            )
            lon_weight = lon_frac[:, cols].astype(jnp.float32)[rows]
            groups.append((start - RIM, plan, weights, lon_weight))
        for f in range(slices):
            parts = [
                interpolate(
                    lambda position, base=base: (
                        own_tiles[t, f, base + position : base + position + 8, :],
                        beside_tiles[t, f, base + position : base + position + 8, :],
                    ),
                    plan,
                    weights,
                    lon_weight,
                )
                for base, plan, weights, lon_weight in groups
            ]
            departed[f * inner : (f + 1) * inner, cols] = jnp.concatenate(parts, axis=0).astype(
                jnp.bfloat16
            )
        if orders <= 64:
            for group in range(orders // 16):
                basis_tile(t, group)
        else:
            lax.fori_loop(0, orders // 16, lambda g, c: (basis_tile(t, g), c)[1], 0)
        return carry

    lax.fori_loop(0, tiles, tile, 0)
    inner_out[...] = lax.dot_general(
        basis_out[...],
        departed[...],
        (((1,), (1,)), ((), ())),
        preferred_element_type=jnp.float32,
    )


def rim_kernel(
    place, low_halo, high_halo, rim_rows, dep_row, dep_col, lat_frac, lon_frac, basis, inner_fourier,
    fourier_out, own_tiles, beside_tiles, departed,
):
    _, slices, lon_count = rim_rows.shape
    band_rows = dep_row.shape[0]
    tiles = lon_count // LANES
    first_row = place[0]

    def source(position, cols):
        if position < RIM:
            low = low_halo[position, :, cols]
        else:
            low = rim_rows[position - RIM, :, cols]
        if position < EDGE:
            high = rim_rows[EDGE + position, :, cols]
        else:
            high = high_halo[position - EDGE, :, cols]
        return jnp.concatenate([low.astype(jnp.float32), high.astype(jnp.float32)], axis=0)

    def fill(t, carry):
        for position in range(RIM + EDGE):
            own_tiles[t, position] = source(position, tile_at(t))
        return carry

    lax.fori_loop(0, tiles, fill, 0)

    def fill_beside(t, carry):
        before, after = neighbours(t, tiles)
        for position in range(RIM + EDGE):
            beside_tiles[t, position] = beside_of(
                own_tiles[before, position], own_tiles[after, position]
            )
        return carry

    lax.fori_loop(0, tiles, fill_beside, 0)

    def spread(values, out_row):
        high_row = band_rows - RIM + out_row
        return jnp.concatenate(
            [
                jnp.broadcast_to(values[row : row + 1], (slices, LANES))
                for row in (out_row, high_row)
            ],
            axis=0,
        )

    def tile(t, carry):
        cols = tile_at(t)
        side = jnp.where(
            lax.broadcasted_iota(jnp.int32, (2 * slices, LANES), 0) < slices, 0, band_rows - RIM
        )
        row_tile, col_tile = dep_row[:, cols], dep_col[:, cols]
        lat_tile = lat_frac[:, cols].astype(jnp.float32)
        lon_tile = lon_frac[:, cols].astype(jnp.float32)
        parts = []
        for out_row in range(RIM):
            plan = lane_plan(spread(col_tile, out_row), t, lon_count)
            weights = row_weights(
                spread(row_tile, out_row) - (first_row + out_row + side),
                spread(lat_tile, out_row),
            )
            parts.append(
                interpolate(
                    lambda position, out_row=out_row: (
                        own_tiles[t, out_row + position],
                        beside_tiles[t, out_row + position],
                    ),
                    plan,
                    weights,
                    spread(lon_tile, out_row),
                )
            )
        departed[:, cols] = jnp.concatenate(parts, axis=0).astype(jnp.bfloat16)
        return carry

    lax.fori_loop(0, tiles, tile, 0)
    rim_fourier = lax.dot_general(
        basis[...],
        departed[...],
        (((1,), (1,)), ((), ())),
        preferred_element_type=jnp.float32,
    )
    for pair in range(fourier_out.shape[0]):
        fourier_out[pair] = jnp.concatenate(
            [inner_fourier[4 * pair : 4 * pair + 4, :], rim_fourier[4 * pair : 4 * pair + 4, :]],
            axis=1,
        ).astype(jnp.bfloat16)


def legendre_kernel(place, pair_ids, coeffs, spread_analysis, out, *, bands, levs, slices):
    rows = spread_analysis.shape[1]
    col_count = spread_analysis.shape[2]
    inner = rows // slices - EDGE
    column = lax.broadcasted_iota(jnp.int32, (1, rows), 1)
    edge_slice = column - inner * slices
    slice_of = jnp.where(edge_slice < 0, column // inner, edge_slice % slices)

    def add(band, total):
        block = jnp.concatenate(
            [coeffs[band * levs + lev, 0].astype(jnp.float32) for lev in range(levs)], axis=0
        )
        masked = jnp.concatenate(
            [jnp.where(slice_of == f, block, 0.0) for f in range(slices)], axis=0
        ).astype(jnp.bfloat16)
        return total + jnp.dot(masked, spread_analysis[band], preferred_element_type=jnp.float32)

    total = jnp.zeros((slices * levs * 4, col_count), jnp.float32)
    if bands <= 16:
        for band in range(bands):
            total = add(band, total)
    else:
        total = lax.fori_loop(0, bands, add, total)
    pair_id = pair_ids[place[0]]
    columns = place[1] + lax.broadcasted_iota(jnp.int32, (2, col_count), 1)
    first_wave = columns < NMAX + 1 - pair_id
    for f in range(slices):
        for lev in range(levs):
            at = (f * levs + lev) * 4
            out[lev * slices + f] = jnp.where(first_wave, total[at : at + 2], total[at + 2 : at + 4])


def shards(grid, dep_row, dep_col, lat_frac, lon_frac, pair_ids, analysis):
    slices, band_rows, lon_count = grid.shape
    pairs = pair_ids.shape[0]
    col_count = analysis.shape[2]
    bands, levs = lax.axis_size("lat"), lax.axis_size("lev")
    inner = band_rows - 2 * RIM
    tiles = lon_count // LANES
    lat_at, lev_at = lax.axis_index("lat"), lax.axis_index("lev")
    band_start = jnp.reshape(lat_at * band_rows, (1,)).astype(jnp.int32)
    vmem = pl.BlockSpec(memory_space=pltpu.VMEM)
    smem = pl.BlockSpec(memory_space=pltpu.SMEM)
    params = pltpu.CompilerParams(vmem_limit_bytes=48 * 2**20)

    rim_rows = jnp.concatenate([grid[:, :EDGE], grid[:, band_rows - EDGE :]], axis=1)
    rim_rows = rim_rows.transpose(1, 0, 2)
    low_halo = lax.ppermute(rim_rows[2 * EDGE - RIM :], "lat", [(i, i + 1) for i in range(bands - 1)])
    high_halo = lax.ppermute(rim_rows[:RIM], "lat", [(i + 1, i) for i in range(bands - 1)])

    tile_shape = (tiles, slices, -(-band_rows // 8) * 8, LANES)
    inner_fourier, basis = pl.pallas_call(
        inner_kernel,
        out_shape=(
            jax.ShapeDtypeStruct((4 * pairs, slices * inner), jnp.float32),
            jax.ShapeDtypeStruct((4 * pairs, lon_count), jnp.bfloat16),
        ),
        in_specs=[smem, smem] + [vmem] * 5,
        out_specs=(vmem, vmem),
        scratch_shapes=[
            pltpu.VMEM(tile_shape, jnp.float32),
            pltpu.VMEM(tile_shape, jnp.float32),
            pltpu.VMEM((slices * inner, lon_count), jnp.bfloat16),
            pltpu.VMEM((4 * pairs, LANES), jnp.float32),
        ],
        compiler_params=params,
        cost_estimate=pl.CostEstimate(flops=100_000_000, bytes_accessed=2_000_000, transcendentals=0),
    )(band_start, pair_ids, grid, dep_row, dep_col, lat_frac, lon_frac)

    fourier = pl.pallas_call(
        rim_kernel,
        out_shape=jax.ShapeDtypeStruct((pairs, 4, slices * band_rows), jnp.bfloat16),
        in_specs=[smem] + [vmem] * 9,
        out_specs=vmem,
        scratch_shapes=[
            pltpu.VMEM((tiles, RIM + EDGE, 2 * slices, LANES), jnp.float32),
            pltpu.VMEM((tiles, RIM + EDGE, 2 * slices, LANES), jnp.float32),
            pltpu.VMEM((2 * RIM * slices, lon_count), jnp.bfloat16),
        ],
        compiler_params=params,
    )(band_start, low_halo, high_halo, rim_rows, dep_row, dep_col, lat_frac, lon_frac, basis, inner_fourier)

    values = analysis[0].reshape(bands, band_rows, col_count)
    spread_rows = [values[:, RIM : RIM + inner]] * slices
    for row in range(RIM):
        spread_rows += [values[:, row : row + 1]] * slices
        spread_rows += [values[:, band_rows - RIM + row : band_rows - RIM + row + 1]] * slices
    spread_analysis = jnp.concatenate(spread_rows, axis=1)

    if bands <= 16:
        coeffs = lax.all_gather(fourier, ("lat", "lev"), axis=0, tiled=False)
        own_block = pl.BlockSpec(
            (bands * levs, 1, 4, slices * band_rows), lambda place: (0, place[0], 0, 0)
        )
        picked = None
    else:
        arrived = lax.all_to_all(fourier, "lat", split_axis=0, concat_axis=0, tiled=True)
        coeffs = lax.all_gather(arrived, "lev", axis=1, tiled=False)
        coeffs = coeffs.reshape(bands * levs, 1, 4, slices * band_rows)
        own_block = pl.BlockSpec((bands * levs, 1, 4, slices * band_rows), lambda *_: (0, 0, 0, 0))
    place = jnp.stack([lat_at, lev_at * col_count]).astype(jnp.int32)
    if bands <= 16:
        coeffs = lax.dynamic_slice_in_dim(coeffs, lat_at, 1, axis=1)
    out = pl.pallas_call(
        functools.partial(legendre_kernel, bands=bands, levs=levs, slices=slices),
        out_shape=jax.ShapeDtypeStruct((levs * slices, 2, col_count), jnp.float32),
        in_specs=[smem, smem, vmem, vmem],
        out_specs=vmem,
        compiler_params=params,
    )(place, pair_ids, coeffs, spread_analysis)
    return out[None]


def solution(mesh):
    return jax.shard_map(
        shards,
        mesh=mesh,
        in_specs=(
            P("lev", "lat", None),
            P("lat", None),
            P("lat", None),
            P("lat", None),
            P("lat", None),
            P(),
            P("lat", None, "lev"),
        ),
        out_specs=P("lat", None, None, "lev"),
        check_vma=False,
    )
```

time: 172 us -> 71.4 us (0.42)
  other arithmetic: 74 us -> 0.21 us
  local copies, waits for them, and re-layouts: 70.3 us -> 2.47 us
  blocking collectives: 5.19 us -> 43.6 us
  Pallas kernels: 0 us -> 18.6 us
  starting transfers between devices: 13.1 us -> 6.17 us
  waiting for transfers between devices: 6.51 us -> 0.02 us
    convert_element_type x1 -> x0, other arithmetic: 65.8 us -> none  [shards(): departed = departed_sum.astype(jnp.bfloat16)]
    slice x56 -> x4, local copies, waits for them, and re-layouts: 65.9 us -> 1.16 us  [the longest x1 1.05 us: shards(): grid[:, :EDGE]]
    all_gather x1, blocking collectives: 5.19 us -> 43.6 us  [shards(): coeffs = lax.all_gather(fourier, ('lat', 'lev'), axis=0, tiled=False)]
    pallas_call x0 -> x3, Pallas kernels: none -> 18.6 us  [the longest x1 12.4 us: shards(): pl.pallas_call(inner_kernel, out_shape=(jax.ShapeDtypeStruct((4 * pairs,...]
    add x6 -> x0, other arithmetic: 7.22 us -> none  [the longest x4 5.5 us: shards(): jnp.where(col_shift == offset, 1.0 - lon_weight, 0.0)]
    all_to_all x1 -> x0, starting transfers between devices: 6.96 us -> none  [shards(): lax.all_to_all(fourier, 'lat', split_axis=2, concat_axis=1, tiled=True)]
    all_to_all x1 -> x0, waiting for transfers between devices: 6.51 us -> none  [shards(): lax.all_to_all(fourier, 'lat', split_axis=2, concat_axis=1, tiled=True)]
  transfers between devices with their start and end apart: 3 -> 2, of which waited for: 1 -> 0; matrix products, arithmetic and copies ran while one was open for 16% -> 1% of each run, Pallas kernels for 0% -> 17%
where the time goes in v1:
time: 71.4 us; the launch traced here: 71.2 us
  blocking collectives  43.6 us (61%)
  Pallas kernels  18.6 us (26%)
  starting transfers between devices  6.17 us (9%)
  local copies, waits for them, and re-layouts  2.47 us (3%)
    all_gather x1, blocking collectives, shards(): coeffs = lax.all_gather(fourier, ('lat', 'lev'), axis=0, tiled=False)  43.6 us
    pallas_call x1, Pallas kernels, shards(): pl.pallas_call(inner_kernel, out_shape=(jax.ShapeDtypeStruct((4 * pairs,...  12.4 us
    ppermute x1, starting transfers between devices, shards(): lax.ppermute(rim_rows[2 * EDGE - RIM:], 'lat', [(i, i + 1) for i in range...  4.87 us
    pallas_call x1, Pallas kernels, shards(): pl.pallas_call(rim_kernel, out_shape=jax.ShapeDtypeStruct((pairs, 4, slic...  4.74 us
  transfers between devices with their start and end apart: 2, of which 0 were waited for; matrix products, arithmetic and copies ran while one was open for 1% of the time, Pallas kernels for 17%

profile of v1, /device:TPU:0, one launch (start us, length us, event | category | flops | bytes accessed | tf_op | source)
XLA Modules:
  0.0 71.2 jit_solution(6094076590278080313)
XLA Ops:
  0.0 0.0 copy-start.6
  0.0 1.1 %fusion = (bf16[4,4,3200]{2,0,1:T(4,128)(2,1)S(1)}, bf16[4,4,3200]{2,0,1:T(4,128)(2,1)S(1)}) fusion(bf16[4,20,3200]{2,0,1:T(4,128)(2,1)} %param.7), kind=kLoop, calls=%fused_computation.3 | loop fusion | bytes 409600 | tf_op jit(solution)/shard_map/slice | solution.py:307
  1.1 0.0 copy-start.5
  1.1 0.1 maximum_bitcast_fusion.rim_rows
  1.3 4.9 %collective-permute-start = (bf16[2,4,3200]{2,1,0:T(4,128)(2,1)S(1)}, bf16[2,4,3200]{2,1,0:T(4,128)(2,1)S(1)}, u32[]{:S(2)}, u32[]{:S(2)}) collective-permute-start(bf16[2,4,3200]{2,1,0:T(4,128)(2,1)S(1)} %get-tuple-element.12), channel_id=1, source_target_pairs={{0,4},{4,8},{8,12},{12,16},{16,20},{20,24},{24,28},{1,5},{5,9},{9,... | collective-permute-start | bytes 153608 | tf_op jit(solution)/shard_map/ppermute | solution.py:309
  6.1 1.3 %collective-permute-start.1 = (bf16[2,4,3200]{2,1,0:T(4,128)(2,1)S(1)}, bf16[2,4,3200]{2,1,0:T(4,128)(2,1)S(1)}, u32[]{:S(2)}, u32[]{:S(2)}) collective-permute-start(bf16[2,4,3200]{2,1,0:T(4,128)(2,1)S(1)} %get-tuple-element.11), channel_id=1, source_target_pairs={{4,0},{8,4},{12,8},{16,12},{20,16},{24,20},{28,24},{5,1},{9,5},{13... | collective-permute-start | bytes 153608 | tf_op jit(solution)/shard_map/ppermute | solution.py:310
  7.4 0.0 copy-done.6
  7.6 0.1 pad_add_fusion.place
  7.6 0.0 copy-done.5
  7.6 0.1 copy.10.grid
  7.7 0.0 copy-start
  7.7 0.0 copy-start.1
  7.8 0.0 copy-start.2
  7.8 0.0 copy-start.3
  7.8 0.5 concatenate.7.spread_analysis
  8.2 0.0 copy-start.4
  8.2 0.5 copy-done
  8.7 0.1 copy-done.1
  8.8 0.0 copy-done.2
  8.8 0.0 copy-done.3
  8.9 0.1 copy-done.4
  9.0 12.4 %shard_map.73 = (f32[32,64]{1,0:T(8,128)S(1)}, bf16[32,3200]{1,0:T(8,128)(2,1)S(1)}) custom-call(s32[1]{0:T(128)} %bitcast.2.place, s32[8]{0:T(128)S(1)} %copy-done.4, bf16[4,20,3200]{2,1,0:T(8,128)(2,1)S(1)} %copy.10.grid, s32[20,3200]{1,0:T(8,128)S(1)} %copy-done, s32[20,3200]{1,0:T(8,128)S(1)} %copy-done.1, bf16[20,3200]{1,0:T(8,128)(2,1)S(1)} %copy-done.2, ...), custom_call_target="tpu_custom_call" | custom-call | flops 100000000 | bytes 2000000 | tf_op jit(solution)/shard_map/pallas_call | solution.py:313
  21.4 0.0 collective-permute-done.low_halo
  21.4 0.0 collective-permute-done.1.high_halo
  21.4 4.7 %shard_map.74 = bf16[8,4,80]{2,1,0:T(4,128)(2,1)S(1)} custom-call(s32[1]{0:T(128)} %bitcast.2.place, bf16[2,4,3200]{2,1,0:T(4,128)(2,1)S(1)} %collective-permute-done.low_halo, bf16[2,4,3200]{2,1,0:T(4,128)(2,1)S(1)} %collective-permute-done.1.high_halo, bf16[8,4,3200]{2,1,0:T(4,128)(2,1)S(1)} %maximum_bitcast_fusion.rim_rows, s32[20,3200]{1,0:T(8,128)S(1)} %copy-done, ...), custom_call_target="tpu_custom_call" | custom-call | tf_op jit(solution)/shard_map/pallas_call | solution.py:331
  26.2 43.6 %all-gather = bf16[256,4,80]{2,1,0:T(4,128)(2,1)S(1)} all-gather(bf16[8,4,80]{2,1,0:T(4,128)(2,1)S(1)} %shard_map.74), channel_id=2, replica_groups=mesh['lat'=8,'lev'=4] {'lat','lev'}, dimensions={0}, use_global_device_ids=true | all-gather | bytes 168960 | tf_op jit(solution)/shard_map/all_gather | solution.py:352
  69.8 1.4 %shard_map.75 = f32[16,2,320]{2,1,0:T(2,128)} custom-call(s32[2]{0:T(128)S(1)} %pad_add_fusion.place, s32[8]{0:T(128)S(1)} %copy-done.4, bf16[32,1,4,80]{3,2,1,0:T(4,128)(2,1)S(1)} %constant_dynamic-slice_fusion.coeffs, bf16[8,80,320]{2,1,0:T(8,128)(2,1)S(1)} %concatenate.7.spread_analysis), custom_call_target="tpu_custom_call" | custom-call | tf_op jit(solution)/shard_map/pallas_call | solution.py:365
  (5 shorter events, 0.2 us)
Async XLA Ops:
  0.0 7.4 %copy-start.6 = (bf16[1,160,320]{2,1,0:T(8,128)(2,1)S(1)}, bf16[1,160,320]{2,1,0:T(8,128)(2,1)}, u32[]{:S(2)}) copy-start(bf16[1,160,320]{2,1,0:T(8,128)(2,1)} %param.13) | copy-start | bytes 307204
  1.1 6.6 %copy-start.5 = (bf16[4,20,3200]{2,0,1:T(4,128)(2,1)S(1)}, bf16[4,20,3200]{2,0,1:T(4,128)(2,1)}, u32[]{:S(2)}) copy-start(bf16[4,20,3200]{2,0,1:T(4,128)(2,1)} %param.7) | copy-start | bytes 1536004
  1.3 20.2 %collective-permute-start = (bf16[2,4,3200]{2,1,0:T(4,128)(2,1)S(1)}, bf16[2,4,3200]{2,1,0:T(4,128)(2,1)S(1)}, u32[]{:S(2)}, u32[]{:S(2)}) collective-permute-start(bf16[2,4,3200]{2,1,0:T(4,128)(2,1)S(1)} %get-tuple-element.12), channel_id=1, source_target_pairs={{0,4},{4,8},{8,12},{12,16},{16,20},{20,24},{24,28},{1,5},{5,9},{9,... | collective-permute-start | bytes 153608 | tf_op jit(solution)/shard_map/ppermute | solution.py:309
  6.1 15.3 %collective-permute-start.1 = (bf16[2,4,3200]{2,1,0:T(4,128)(2,1)S(1)}, bf16[2,4,3200]{2,1,0:T(4,128)(2,1)S(1)}, u32[]{:S(2)}, u32[]{:S(2)}) collective-permute-start(bf16[2,4,3200]{2,1,0:T(4,128)(2,1)S(1)} %get-tuple-element.11), channel_id=1, source_target_pairs={{4,0},{8,4},{12,8},{16,12},{20,16},{24,20},{28,24},{5,1},{9,5},{13... | collective-permute-start | bytes 153608 | tf_op jit(solution)/shard_map/ppermute | solution.py:310
  7.7 1.0 %copy-start = (s32[20,3200]{1,0:T(8,128)S(1)}, s32[20,3200]{1,0:T(8,128)}, u32[]{:S(2)}) copy-start(s32[20,3200]{1,0:T(8,128)} %dep_row.3) | copy-start | bytes 768004
  7.7 1.1 %copy-start.1 = (s32[20,3200]{1,0:T(8,128)S(1)}, s32[20,3200]{1,0:T(8,128)}, u32[]{:S(2)}) copy-start(s32[20,3200]{1,0:T(8,128)} %dep_col.3) | copy-start | bytes 768004
  7.8 1.1 %copy-start.2 = (bf16[20,3200]{1,0:T(8,128)(2,1)S(1)}, bf16[20,3200]{1,0:T(8,128)(2,1)}, u32[]{:S(2)}) copy-start(bf16[20,3200]{1,0:T(8,128)(2,1)} %lat_frac.3) | copy-start | bytes 384004
  7.8 1.1 %copy-start.3 = (bf16[20,3200]{1,0:T(8,128)(2,1)S(1)}, bf16[20,3200]{1,0:T(8,128)(2,1)}, u32[]{:S(2)}) copy-start(bf16[20,3200]{1,0:T(8,128)(2,1)} %lon_frac.3) | copy-start | bytes 384004
  8.2 0.7 %copy-start.4 = (s32[8]{0:T(128)S(1)}, s32[8]{0:T(128)}, u32[]{:S(2)}) copy-start(s32[8]{0:T(128)} %pair_ids.3) | copy-start | bytes 100

commit v2 on v1

v2 whole, which is shorter than its diff:
```python
import functools
import math

import jax
import jax.numpy as jnp
from jax import lax
from jax.experimental import pallas as pl
from jax.experimental.pallas import tpu as pltpu
from jax.sharding import PartitionSpec as P

NMAX = 1279
LANES = 128
RIM = 2
EDGE = 2 * RIM
REACH = 8
SPAN = LANES - 2 * REACH - 1
CODE = 4096


def lane_gather(values, indices):
    numbers = lax.GatherDimensionNumbers(
        offset_dims=(),
        collapsed_slice_dims=(1,),
        start_index_map=(1,),
        operand_batching_dims=(0,),
        start_indices_batching_dims=(0,),
    )
    return lax.gather(
        values,
        indices[..., None],
        numbers,
        (1, 1),
        mode=lax.GatherScatterMode.PROMISE_IN_BOUNDS,
    )


def tile_at(t):
    return pl.ds(pl.multiple_of(t * LANES, LANES), LANES)


def cut_of(start, lon_count):
    tiles = lon_count // LANES
    start = start + lon_count
    first = start // LANES
    first = jnp.where(first >= tiles, first - tiles, first)
    second = jnp.where(first == tiles - 1, 0, first + 1)
    return tile_at(first), tile_at(second), start % LANES


def join(first, second, lane_at):
    lane = lax.broadcasted_iota(jnp.int32, first.shape, 1)
    return jnp.where(lane >= lane_at, first, second)


def turn(joined, lane_at):
    return pltpu.roll(joined, (LANES - lane_at) % LANES, 1)


def lane_plan(code, start, latitude, lon_count):
    west = (code & (CODE - 1)) - (start - REACH)
    west = jnp.where(west > lon_count // 2, west - lon_count, west)
    west = jnp.where(west < -(lon_count // 2), west + lon_count, west)
    west_lane = (west & (LANES - 1)).astype(jnp.int16)
    east_lane = ((west + 1) & (LANES - 1)).astype(jnp.int16)
    row_shift = (code // CODE - latitude).astype(jnp.float32).astype(jnp.bfloat16)
    return west_lane, east_lane, row_shift


def corner_weights(lat_weight, lon_weight):
    south, north = 1.0 - lat_weight, lat_weight
    west, east = 1.0 - lon_weight, lon_weight
    return south * west, south * east, north * west, north * east


def interpolate(sources, plan, weights):
    west_lane, east_lane, row_shift = plan
    masks = [row_shift == float(step) for step in range(-RIM, RIM - 1)]

    def pick(gathered):
        low, high = gathered[2 * RIM - 1], gathered[2 * RIM]
        for position in range(2 * RIM - 2, -1, -1):
            low = jnp.where(masks[position], gathered[position], low)
            high = jnp.where(masks[position], gathered[position + 1], high)
        return low.astype(jnp.float32), high.astype(jnp.float32)

    west_low, west_high = pick([lane_gather(source, west_lane) for source in sources])
    east_low, east_high = pick([lane_gather(source, east_lane) for source in sources])
    departed = (
        weights[0] * west_low
        + weights[1] * east_low
        + weights[2] * west_high
        + weights[3] * east_high
    )
    return departed.astype(jnp.bfloat16)


def inner_kernel(
    place, pair_ids, grid, dep_row, dep_col, lat_frac, lon_frac,
    inner_out, basis_out, windows, plans, departed, waves,
):
    slices, band_rows, lon_count = grid.shape
    inner = band_rows - 2 * RIM
    orders = basis_out.shape[0]
    first_row = place[0]

    def wave_rows(group, carry):
        row = lax.broadcasted_iota(jnp.int32, (16, LANES), 0)
        pair = jnp.full((16, LANES), pair_ids[4 * group + 3], jnp.int32)
        for at in (2, 1, 0):
            pair = jnp.where(row < 4 * (at + 1), pair_ids[4 * group + at], pair)
        wave = jnp.where((row & 2) == 0, pair, NMAX + 1 - pair)
        waves[pl.ds(pl.multiple_of(group * 16, 16), 16), :] = wave.astype(jnp.float32)
        return carry

    lax.fori_loop(0, orders // 16, wave_rows, 0)

    def basis_tile(t, group):
        rows = pl.ds(pl.multiple_of(group * 16, 16), 16)
        lane = lax.broadcasted_iota(jnp.int32, (16, LANES), 1)
        row = lax.broadcasted_iota(jnp.int32, (16, LANES), 0)
        longitude = lane + t * SPAN
        quarter = jnp.where((row & 1) == 0, 0.0, float(lon_count // 4))
        steps = longitude.astype(jnp.float32) * waves[rows, :] + quarter
        turns = jnp.floor(steps * (1.0 / lon_count) + 0.5)
        angle = (lon_count // 4 - jnp.abs(steps - turns * lon_count)) * (2.0 * math.pi / lon_count)
        square = angle * angle
        series = jnp.float32(-1.0 / 39916800.0)
        for term in (1.0 / 362880.0, -1.0 / 5040.0, 1.0 / 120.0, -1.0 / 6.0, 1.0):
            series = series * square + term
        held = (lane < SPAN) & (longitude < lon_count)
        basis_out[rows, tile_at(t)] = jnp.where(held, angle * series, 0.0).astype(jnp.bfloat16)

    def window(t, slot):
        start = t * SPAN
        first, second, lane_at = cut_of(start - REACH, lon_count)
        for f in range(slices):
            joined = join(
                grid[f, :, first].astype(jnp.float32),
                grid[f, :, second].astype(jnp.float32),
                lane_at,
            )
            windows[slot, f, 0:band_rows, :] = turn(joined, lane_at)
        first, second, lane_at = cut_of(start, lon_count)
        plans[slot, 0, 0:band_rows, :] = join(
            (dep_row[:, first] * CODE + dep_col[:, first]).astype(jnp.float32),
            (dep_row[:, second] * CODE + dep_col[:, second]).astype(jnp.float32),
            lane_at,
        )
        for at, frac in ((1, lat_frac), (2, lon_frac)):
            plans[slot, at, 0:band_rows, :] = join(
                frac[:, first].astype(jnp.float32), frac[:, second].astype(jnp.float32), lane_at
            )
        code, lat_weight, lon_weight = [
            turn(plans[slot, at, RIM : RIM + inner, :], lane_at) for at in range(3)
        ]
        latitude = first_row + RIM + lax.broadcasted_iota(jnp.int32, (inner, LANES), 0)
        plan = lane_plan(code.astype(jnp.int32), start, latitude, lon_count)
        weights = corner_weights(lat_weight, lon_weight)
        for f in range(slices):
            sources = [
                windows[slot, f, position : position + inner, :].astype(jnp.bfloat16)
                for position in range(2 * RIM + 1)
            ]
            departed[f * inner : (f + 1) * inner, tile_at(t)] = interpolate(sources, plan, weights)
        if orders <= 64:
            for group in range(orders // 16):
                basis_tile(t, group)
        else:
            lax.fori_loop(0, orders // 16, lambda g, c: (basis_tile(t, g), c)[1], 0)

    count = basis_out.shape[1] // LANES

    def pair_of_windows(step, carry):
        window(2 * step, 0)
        window(2 * step + 1, 1)
        return carry

    lax.fori_loop(0, count // 2, pair_of_windows, 0)
    if count % 2:
        window(count - 1, 0)
    inner_out[...] = lax.dot_general(
        basis_out[...],
        departed[...],
        (((1,), (1,)), ((), ())),
        preferred_element_type=jnp.float32,
    )


def rim_kernel(
    place, low_halo, high_halo, rim_rows, dep_row, dep_col, lat_frac, lon_frac, basis, inner_fourier,
    fourier_out, plans, departed,
):
    _, slices, lon_count = rim_rows.shape
    band_rows = dep_row.shape[0]
    first_row = place[0]
    last = band_rows // 8 * 8

    def source(position, cols):
        if position < RIM:
            low = low_halo[position, :, cols]
        else:
            low = rim_rows[position - RIM, :, cols]
        if position < EDGE:
            high = rim_rows[EDGE + position, :, cols]
        else:
            high = high_halo[position - EDGE, :, cols]
        return jnp.concatenate([low.astype(jnp.float32), high.astype(jnp.float32)], axis=0)

    def spread(slot, at):
        pieces = []
        for out_row in range(RIM):
            for row in (out_row, 8 + band_rows - RIM + out_row - last):
                pieces.append(
                    jnp.broadcast_to(plans[slot, at, row : row + 1, :], (slices, LANES))
                )
        return jnp.concatenate(pieces, axis=0)

    def window(t, slot):
        start = t * SPAN
        first, second, lane_at = cut_of(start - REACH, lon_count)
        tiles = [
            turn(join(source(position, first), source(position, second), lane_at), lane_at)
            for position in range(RIM + EDGE)
        ]
        first, second, lane_at = cut_of(start, lon_count)
        codes = [
            (dep_row[:, cols] * CODE + dep_col[:, cols]).astype(jnp.float32)
            for cols in (first, second)
        ]
        arrays = [codes] + [
            [frac[:, cols].astype(jnp.float32) for cols in (first, second)]
            for frac in (lat_frac, lon_frac)
        ]
        for at, (west_part, east_part) in enumerate(arrays):
            plans[slot, at, 0:8, :] = turn(join(west_part[:8], east_part[:8], lane_at), lane_at)
            plans[slot, at, 8 : 8 + band_rows - last, :] = turn(
                join(west_part[last:], east_part[last:], lane_at), lane_at
            )
        place_of = lax.broadcasted_iota(jnp.int32, (2 * RIM * slices, LANES), 0)
        latitude = (
            first_row
            + place_of // (2 * slices)
            + jnp.where(place_of % (2 * slices) < slices, 0, band_rows - RIM)
        )
        plan = lane_plan(spread(slot, 0).astype(jnp.int32), start, latitude, lon_count)
        weights = corner_weights(spread(slot, 1), spread(slot, 2))
        sources = [
            jnp.concatenate(tiles[position : position + RIM], axis=0).astype(jnp.bfloat16)
            for position in range(2 * RIM + 1)
        ]
        departed[:, tile_at(t)] = interpolate(sources, plan, weights)

    count = basis.shape[1] // LANES

    def pair_of_windows(step, carry):
        window(2 * step, 0)
        window(2 * step + 1, 1)
        return carry

    lax.fori_loop(0, count // 2, pair_of_windows, 0)
    if count % 2:
        window(count - 1, 0)
    rim_fourier = lax.dot_general(
        basis[...],
        departed[...],
        (((1,), (1,)), ((), ())),
        preferred_element_type=jnp.float32,
    )
    levs = fourier_out.shape[1]
    for pair in range(fourier_out.shape[0]):
        block = jnp.concatenate(
            [inner_fourier[4 * pair : 4 * pair + 4, :], rim_fourier[4 * pair : 4 * pair + 4, :]],
            axis=1,
        ).astype(jnp.bfloat16)
        for lev in range(levs):
            fourier_out[pair, lev] = block


def legendre_kernel(place, pair_ids, coeffs, spread_analysis, out, *, bands, levs, slices):
    rows = spread_analysis.shape[1]
    col_count = spread_analysis.shape[2]
    inner = rows // slices - EDGE
    column = lax.broadcasted_iota(jnp.int32, (1, rows), 1)
    edge_slice = column - inner * slices
    slice_of = jnp.where(edge_slice < 0, column // inner, edge_slice % slices)

    def add(band, total):
        block = jnp.concatenate(
            [coeffs[band * levs + lev].astype(jnp.float32) for lev in range(levs)], axis=0
        )
        masked = jnp.concatenate(
            [jnp.where(slice_of == f, block, 0.0) for f in range(slices)], axis=0
        ).astype(jnp.bfloat16)
        return total + jnp.dot(masked, spread_analysis[band], preferred_element_type=jnp.float32)

    total = jnp.zeros((slices * levs * 4, col_count), jnp.float32)
    if bands <= 16:
        for band in range(bands):
            total = add(band, total)
    else:
        total = lax.fori_loop(0, bands, add, total)
    pair_id = pair_ids[place[0]]
    columns = place[1] + lax.broadcasted_iota(jnp.int32, (2, col_count), 1)
    first_wave = columns < NMAX + 1 - pair_id
    for f in range(slices):
        for lev in range(levs):
            at = (f * levs + lev) * 4
            out[lev * slices + f] = jnp.where(first_wave, total[at : at + 2], total[at + 2 : at + 4])


def shards(grid, dep_row, dep_col, lat_frac, lon_frac, pair_ids, analysis):
    slices, band_rows, lon_count = grid.shape
    pairs = pair_ids.shape[0]
    col_count = analysis.shape[2]
    bands, levs = lax.axis_size("lat"), lax.axis_size("lev")
    inner = band_rows - 2 * RIM
    lat_at, lev_at = lax.axis_index("lat"), lax.axis_index("lev")
    band_start = jnp.reshape(lat_at * band_rows, (1,)).astype(jnp.int32)
    vmem = pl.BlockSpec(memory_space=pltpu.VMEM)
    smem = pl.BlockSpec(memory_space=pltpu.SMEM)
    params = pltpu.CompilerParams(vmem_limit_bytes=48 * 2**20)

    rim_rows = jnp.concatenate([grid[:, :EDGE], grid[:, band_rows - EDGE :]], axis=1)
    rim_rows = rim_rows.transpose(1, 0, 2)
    low_halo = lax.ppermute(rim_rows[2 * EDGE - RIM :], "lat", [(i, i + 1) for i in range(bands - 1)])
    high_halo = lax.ppermute(rim_rows[:RIM], "lat", [(i + 1, i) for i in range(bands - 1)])

    windows = -(-lon_count // SPAN)
    held_rows = -(-band_rows // 8) * 8
    inner_fourier, basis = pl.pallas_call(
        inner_kernel,
        out_shape=(
            jax.ShapeDtypeStruct((4 * pairs, slices * inner), jnp.float32),
            jax.ShapeDtypeStruct((4 * pairs, windows * LANES), jnp.bfloat16),
        ),
        in_specs=[smem, smem] + [vmem] * 5,
        out_specs=(vmem, vmem),
        scratch_shapes=[
            pltpu.VMEM((2, slices, held_rows, LANES), jnp.float32),
            pltpu.VMEM((2, 3, held_rows, LANES), jnp.float32),
            pltpu.VMEM((slices * inner, windows * LANES), jnp.bfloat16),
            pltpu.VMEM((4 * pairs, LANES), jnp.float32),
        ],
        compiler_params=params,
        cost_estimate=pl.CostEstimate(flops=100_000_000, bytes_accessed=2_000_000, transcendentals=0),
    )(band_start, pair_ids, grid, dep_row, dep_col, lat_frac, lon_frac)

    fourier = pl.pallas_call(
        rim_kernel,
        out_shape=jax.ShapeDtypeStruct((pairs, levs, 4, slices * band_rows), jnp.bfloat16),
        in_specs=[smem] + [vmem] * 9,
        out_specs=vmem,
        scratch_shapes=[
            pltpu.VMEM((2, 3, 16, LANES), jnp.float32),
            pltpu.VMEM((2 * RIM * slices, windows * LANES), jnp.bfloat16),
        ],
        compiler_params=params,
    )(band_start, low_halo, high_halo, rim_rows, dep_row, dep_col, lat_frac, lon_frac, basis, inner_fourier)

    values = analysis[0].reshape(bands, band_rows, col_count)
    spread_rows = [values[:, RIM : RIM + inner]] * slices
    for row in range(RIM):
        spread_rows += [values[:, row : row + 1]] * slices
        spread_rows += [values[:, band_rows - RIM + row : band_rows - RIM + row + 1]] * slices
    spread_analysis = jnp.concatenate(spread_rows, axis=1)

    coeffs = lax.all_to_all(
        fourier.reshape(pairs * levs, 4, slices * band_rows),
        ("lat", "lev"),
        split_axis=0,
        concat_axis=0,
        tiled=True,
    )
    place = jnp.stack([lat_at, lev_at * col_count]).astype(jnp.int32)
    out = pl.pallas_call(
        functools.partial(legendre_kernel, bands=bands, levs=levs, slices=slices),
        out_shape=jax.ShapeDtypeStruct((levs * slices, 2, col_count), jnp.float32),
        in_specs=[smem, smem, vmem, vmem],
        out_specs=vmem,
        compiler_params=params,
    )(place, pair_ids, coeffs, spread_analysis)
    return out[None]


def solution(mesh):
    return jax.shard_map(
        shards,
        mesh=mesh,
        in_specs=(
            P("lev", "lat", None),
            P("lat", None),
            P("lat", None),
            P("lat", None),
            P("lat", None),
            P(),
            P("lat", None, "lev"),
        ),
        out_specs=P("lat", None, None, "lev"),
        check_vma=False,
    )
```

time: 71.4 us -> 34.3 us (0.48)
  blocking collectives: 43.6 us -> 0 us
  Pallas kernels: 18.6 us -> 11.1 us
  starting transfers between devices: 6.17 us -> 13.1 us
  waiting for transfers between devices: 0.02 us -> 6.69 us
    all_gather x1 -> x0, blocking collectives: 43.6 us -> none  [shards(): coeffs = lax.all_gather(fourier, ('lat', 'lev'), axis=0, tiled=False)]
    all_to_all x0 -> x1, starting transfers between devices: none -> 6.97 us  [shards(): lax.all_to_all(fourier.reshape(pairs * levs, 4, slices * band_rows), ('la...]
    pallas_call x1, Pallas kernels: 12.4 us -> 5.48 us  [shards(): pl.pallas_call(inner_kernel, out_shape=(jax.ShapeDtypeStruct((4 * pairs,...]
    all_to_all x0 -> x1, waiting for transfers between devices: none -> 6.68 us  [shards(): lax.all_to_all(fourier.reshape(pairs * levs, 4, slices * band_rows), ('la...]
  transfers between devices with their start and end apart: 2 -> 3, of which waited for: 0 -> 1; matrix products, arithmetic and copies ran while one was open for 1% -> 2% of each run, Pallas kernels for 17% -> 16%
where the time goes in v2:
time: 34.3 us; the launch traced here: 34.1 us
  starting transfers between devices  13.1 us (38%)
  Pallas kernels  11.1 us (32%)
  waiting for transfers between devices  6.69 us (20%)
  local copies, waits for them, and re-layouts  2.76 us (8%)
    all_to_all x1, starting transfers between devices, shards(): lax.all_to_all(fourier.reshape(pairs * levs, 4, slices * band_rows), ('la...  6.97 us
    all_to_all x1, waiting for transfers between devices, shards(): lax.all_to_all(fourier.reshape(pairs * levs, 4, slices * band_rows), ('la...  6.68 us
    pallas_call x1, Pallas kernels, shards(): pl.pallas_call(inner_kernel, out_shape=(jax.ShapeDtypeStruct((4 * pairs,...  5.48 us
    ppermute x1, starting transfers between devices, shards(): lax.ppermute(rim_rows[2 * EDGE - RIM:], 'lat', [(i, i + 1) for i in range...  4.87 us
    pallas_call x1, Pallas kernels, shards(): pl.pallas_call(rim_kernel, out_shape=jax.ShapeDtypeStruct((pairs, levs, 4...  4.21 us
    pallas_call x1, Pallas kernels, shards(): pl.pallas_call(functools.partial(legendre_kernel, bands=bands, levs=levs,...  1.42 us
    ppermute x1, starting transfers between devices, shards(): lax.ppermute(rim_rows[:RIM], 'lat', [(i + 1, i) for i in range(bands - 1)])  1.29 us
    unnamed x15, local copies, waits for them, and re-layouts  1.11 us
  transfers between devices with their start and end apart: 3, of which 1 were waited for; matrix products, arithmetic and copies ran while one was open for 2% of the time, Pallas kernels for 16%

profile of v2, /device:TPU:0, one launch (start us, length us, event | category | flops | bytes accessed | tf_op | source)
XLA Modules:
  0.0 34.1 jit_solution(14107193071886563562)
XLA Ops:
  0.0 0.0 copy-start.6
  0.0 1.1 %fusion = (bf16[4,4,3200]{2,0,1:T(4,128)(2,1)S(1)}, bf16[4,4,3200]{2,0,1:T(4,128)(2,1)S(1)}) fusion(bf16[4,20,3200]{2,0,1:T(4,128)(2,1)} %param.7), kind=kLoop, calls=%fused_computation.2 | loop fusion | bytes 409600 | tf_op jit(solution)/shard_map/slice | solution.py:323
  1.1 0.0 copy-start.5
  1.1 0.1 maximum_bitcast_fusion.rim_rows
  1.3 4.9 %collective-permute-start = (bf16[2,4,3200]{2,1,0:T(4,128)(2,1)S(1)}, bf16[2,4,3200]{2,1,0:T(4,128)(2,1)S(1)}, u32[]{:S(2)}, u32[]{:S(2)}) collective-permute-start(bf16[2,4,3200]{2,1,0:T(4,128)(2,1)S(1)} %get-tuple-element.12), channel_id=1, source_target_pairs={{0,4},{4,8},{8,12},{12,16},{16,20},{20,24},{24,28},{1,5},{5,9},{9,... | collective-permute-start | bytes 153608 | tf_op jit(solution)/shard_map/ppermute | solution.py:325
  6.1 1.3 %collective-permute-start.1 = (bf16[2,4,3200]{2,1,0:T(4,128)(2,1)S(1)}, bf16[2,4,3200]{2,1,0:T(4,128)(2,1)S(1)}, u32[]{:S(2)}, u32[]{:S(2)}) collective-permute-start(bf16[2,4,3200]{2,1,0:T(4,128)(2,1)S(1)} %get-tuple-element.11), channel_id=1, source_target_pairs={{4,0},{8,4},{12,8},{16,12},{20,16},{24,20},{28,24},{5,1},{9,5},{13... | collective-permute-start | bytes 153608 | tf_op jit(solution)/shard_map/ppermute | solution.py:326
  7.4 0.0 copy-done.6
  7.5 0.0 copy-done.5
  7.6 0.0 copy-start
  7.6 0.0 copy-start.1
  7.6 0.0 copy-start.2
  7.6 0.0 copy-start.3
  7.6 0.1 copy.9.grid
  7.7 0.0 copy-start.4
  7.7 0.8 %copy-done = s32[20,3200]{1,0:T(8,128)S(1)} copy-done((s32[20,3200]{1,0:T(8,128)S(1)}, s32[20,3200]{1,0:T(8,128)}, u32[]{:S(2)}) %copy-start) | copy-done | bytes 256024
  8.5 0.1 copy-done.1
  8.6 0.0 copy-done.2
  8.7 0.0 copy-done.3
  8.7 0.0 copy-done.4
  8.7 5.5 %shard_map.73 = (f32[32,64]{1,0:T(8,128)S(1)}, bf16[32,3712]{1,0:T(8,128)(2,1)S(1)}) custom-call(s32[1]{0:T(128)} %bitcast.2.place, s32[8]{0:T(128)S(1)} %copy-done.4, bf16[4,20,3200]{2,1,0:T(8,128)(2,1)S(1)} %copy.9.grid, s32[20,3200]{1,0:T(8,128)S(1)} %copy-done, s32[20,3200]{1,0:T(8,128)S(1)} %copy-done.1, bf16[20,3200]{1,0:T(8,128)(2,1)S(1)} %copy-done.2, ...), custom_call_target="tpu_custom_call" | custom-call | flops 100000000 | bytes 2000000 | tf_op jit(solution)/shard_map/pallas_call | solution.py:330
  14.2 0.0 collective-permute-done.low_halo
  14.2 0.0 collective-permute-done.1.high_halo
  14.2 4.2 %shard_map.74 = bf16[8,4,4,80]{3,2,1,0:T(4,128)(2,1)} custom-call(s32[1]{0:T(128)} %bitcast.2.place, bf16[2,4,3200]{2,1,0:T(4,128)(2,1)S(1)} %collective-permute-done.low_halo, bf16[2,4,3200]{2,1,0:T(4,128)(2,1)S(1)} %collective-permute-done.1.high_halo, bf16[8,4,3200]{2,1,0:T(4,128)(2,1)S(1)} %maximum_bitcast_fusion.rim_rows, s32[20,3200]{1,0:T(8,128)S(1)} %copy-done, ...), custom_call_target="tpu_custom_call" | custom-call | tf_op jit(solution)/shard_map/pallas_call | solution.py:348
  18.4 7.0 %all-to-all-start = ((bf16[32,4,80]{2,1,0:T(4,128)(2,1)}), bf16[32,4,80]{2,1,0:T(4,128)(2,1)S(1)}, u32[]{:S(2)}, u32[]{:S(2)}) async-start(bf16[32,4,80]{2,1,0:T(4,128)(2,1)} %bitcast.4), calls=%async_computation | async-start | bytes 65536 | tf_op jit(solution)/shard_map/all_to_all | solution.py:367
  25.4 0.1 pad_add_fusion.place
  25.5 0.5 %concatenate.7.spread_analysis = bf16[8,80,320]{2,1,0:T(8,128)(2,1)S(1)} concatenate(bf16[8,16,320]{2,1,0:T(8,128)(2,1)S(1)} %slice.38, bf16[8,16,320]{2,1,0:T(8,128)(2,1)S(1)} %slice.38, bf16[8,16,320]{2,1,0:T(8,128)(2,1)S(1)} %slice.38, bf16[8,16,320]{2,1,0:T(8,128)(2,1)S(1)} %slice.38, bf16[8,1,320]{2,1,0:T(2,128)(2,1)S(1)} %get-tuple-element.16, ...), dimensions={1} | concatenate | bytes 819200 | tf_op jit(solution)/shard_map/concatenate | solution.py:365
  26.0 6.7 %all-to-all-done.coeffs = bf16[32,4,80]{2,1,0:T(4,128)(2,1)S(1)} async-done(((bf16[32,4,80]{2,1,0:T(4,128)(2,1)}), bf16[32,4,80]{2,1,0:T(4,128)(2,1)S(1)}, u32[]{:S(2)}, u32[]{:S(2)}) %all-to-all-start) | async-done | bytes 20512 | tf_op jit(solution)/shard_map/all_to_all | solution.py:367
  32.6 1.4 %shard_map.75 = f32[16,2,320]{2,1,0:T(2,128)} custom-call(s32[2]{0:T(128)S(1)} %pad_add_fusion.place, s32[8]{0:T(128)S(1)} %copy-done.4, bf16[32,4,80]{2,1,0:T(4,128)(2,1)S(1)} %all-to-all-done.coeffs, bf16[8,80,320]{2,1,0:T(8,128)(2,1)S(1)} %concatenate.7.spread_analysis), custom_call_target="tpu_custom_call" | custom-call | tf_op jit(solution)/shard_map/pallas_call | solution.py:375
  (4 shorter events, 0.1 us)
Async XLA Ops:
  0.0 7.4 %copy-start.6 = (bf16[1,160,320]{2,1,0:T(8,128)(2,1)S(1)}, bf16[1,160,320]{2,1,0:T(8,128)(2,1)}, u32[]{:S(2)}) copy-start(bf16[1,160,320]{2,1,0:T(8,128)(2,1)} %param.13) | copy-start | bytes 307204
  1.1 6.5 %copy-start.5 = (bf16[4,20,3200]{2,0,1:T(4,128)(2,1)S(1)}, bf16[4,20,3200]{2,0,1:T(4,128)(2,1)}, u32[]{:S(2)}) copy-start(bf16[4,20,3200]{2,0,1:T(4,128)(2,1)} %param.7) | copy-start | bytes 1536004
  1.3 12.9 %collective-permute-start = (bf16[2,4,3200]{2,1,0:T(4,128)(2,1)S(1)}, bf16[2,4,3200]{2,1,0:T(4,128)(2,1)S(1)}, u32[]{:S(2)}, u32[]{:S(2)}) collective-permute-start(bf16[2,4,3200]{2,1,0:T(4,128)(2,1)S(1)} %get-tuple-element.12), channel_id=1, source_target_pairs={{0,4},{4,8},{8,12},{12,16},{16,20},{20,24},{24,28},{1,5},{5,9},{9,... | collective-permute-start | bytes 153608 | tf_op jit(solution)/shard_map/ppermute | solution.py:325
  6.1 8.1 %collective-permute-start.1 = (bf16[2,4,3200]{2,1,0:T(4,128)(2,1)S(1)}, bf16[2,4,3200]{2,1,0:T(4,128)(2,1)S(1)}, u32[]{:S(2)}, u32[]{:S(2)}) collective-permute-start(bf16[2,4,3200]{2,1,0:T(4,128)(2,1)S(1)} %get-tuple-element.11), channel_id=1, source_target_pairs={{4,0},{8,4},{12,8},{16,12},{20,16},{24,20},{28,24},{5,1},{9,5},{13... | collective-permute-start | bytes 153608 | tf_op jit(solution)/shard_map/ppermute | solution.py:326
  7.6 1.0 %copy-start = (s32[20,3200]{1,0:T(8,128)S(1)}, s32[20,3200]{1,0:T(8,128)}, u32[]{:S(2)}) copy-start(s32[20,3200]{1,0:T(8,128)} %dep_row.3) | copy-start | bytes 768004
  7.6 1.1 %copy-start.1 = (s32[20,3200]{1,0:T(8,128)S(1)}, s32[20,3200]{1,0:T(8,128)}, u32[]{:S(2)}) copy-start(s32[20,3200]{1,0:T(8,128)} %dep_col.3) | copy-start | bytes 768004
  7.6 1.1 %copy-start.2 = (bf16[20,3200]{1,0:T(8,128)(2,1)S(1)}, bf16[20,3200]{1,0:T(8,128)(2,1)}, u32[]{:S(2)}) copy-start(bf16[20,3200]{1,0:T(8,128)(2,1)} %lat_frac.3) | copy-start | bytes 384004
  7.6 1.1 %copy-start.3 = (bf16[20,3200]{1,0:T(8,128)(2,1)S(1)}, bf16[20,3200]{1,0:T(8,128)(2,1)}, u32[]{:S(2)}) copy-start(bf16[20,3200]{1,0:T(8,128)(2,1)} %lon_frac.3) | copy-start | bytes 384004
  7.7 1.0 %copy-start.4 = (s32[8]{0:T(128)S(1)}, s32[8]{0:T(128)}, u32[]{:S(2)}) copy-start(s32[8]{0:T(128)} %pair_ids.3) | copy-start | bytes 100
  18.4 14.2 %all-to-all-start = ((bf16[32,4,80]{2,1,0:T(4,128)(2,1)}), bf16[32,4,80]{2,1,0:T(4,128)(2,1)S(1)}, u32[]{:S(2)}, u32[]{:S(2)}) async-start(bf16[32,4,80]{2,1,0:T(4,128)(2,1)} %bitcast.4), calls=%async_computation | async-start | bytes 65536 | tf_op jit(solution)/shard_map/all_to_all | solution.py:367

commit v3 on v2

v3 whole, which is shorter than its diff:
```python
import functools
import math

import jax
import jax.numpy as jnp
from jax import lax
from jax.experimental import pallas as pl
from jax.experimental.pallas import tpu as pltpu
from jax.sharding import PartitionSpec as P

NMAX = 1279
LANES = 128
RIM = 2
EDGE = 2 * RIM
REACH = 8
SPAN = LANES - 2 * REACH - 1
ROW_CODE = 32
AT_ONCE = 4


def lane_gather(values, indices):
    numbers = lax.GatherDimensionNumbers(
        offset_dims=(),
        collapsed_slice_dims=(1,),
        start_index_map=(1,),
        operand_batching_dims=(0,),
        start_indices_batching_dims=(0,),
    )
    return lax.gather(
        values,
        indices[..., None],
        numbers,
        (1, 1),
        mode=lax.GatherScatterMode.PROMISE_IN_BOUNDS,
    )


def tile_at(t):
    return pl.ds(pl.multiple_of(t * LANES, LANES), LANES)


def cut_of(start, lon_count):
    tiles = lon_count // LANES
    start = start + lon_count
    first = start // LANES
    first = jnp.where(first >= tiles, first - tiles, first)
    second = jnp.where(first == tiles - 1, 0, first + 1)
    return tile_at(first), tile_at(second), start % LANES


def cut(first, second, lane_at):
    lane = lax.broadcasted_iota(jnp.int32, first.shape, 1).astype(jnp.int16)
    joined = jnp.where(lane >= jnp.asarray(lane_at, jnp.int16), first, second)
    return pltpu.roll(joined, (LANES - lane_at) % LANES, 1)


def lane_plan(code):
    code = code.astype(jnp.int32)
    west = lax.broadcasted_iota(jnp.int32, code.shape, 1) + code % ROW_CODE
    west_lane = (west & (LANES - 1)).astype(jnp.int16)
    east_lane = ((west + 1) & (LANES - 1)).astype(jnp.int16)
    row_step = (code // ROW_CODE).astype(jnp.float32).astype(jnp.bfloat16)
    return west_lane, east_lane, row_step


def corner_weights(lat_weight, lon_weight):
    south, north = 1.0 - lat_weight, lat_weight
    west, east = 1.0 - lon_weight, lon_weight
    return south * west, south * east, north * west, north * east


def interpolate(sources, plan, weights):
    west_lane, east_lane, row_step = plan
    masks = [row_step == float(step) for step in range(2 * RIM - 1)]

    def pick(gathered):
        low, high = gathered[2 * RIM - 1], gathered[2 * RIM]
        for position in range(2 * RIM - 2, -1, -1):
            low = jnp.where(masks[position], gathered[position], low)
            high = jnp.where(masks[position], gathered[position + 1], high)
        return low.astype(jnp.float32), high.astype(jnp.float32)

    west_low, west_high = pick([lane_gather(source, west_lane) for source in sources])
    east_low, east_high = pick([lane_gather(source, east_lane) for source in sources])
    departed = (
        weights[0] * west_low
        + weights[1] * east_low
        + weights[2] * west_high
        + weights[3] * east_high
    )
    return departed.astype(jnp.bfloat16)


def in_steps(count, at_once, window):
    def several(step, carry):
        for slot in range(at_once):
            window(step * at_once + slot, slot)
        return carry

    lax.fori_loop(0, count // at_once, several, 0)
    for slot in range(count % at_once):
        window(count - count % at_once + slot, slot)


def pack_kernel(
    place, grid, dep_row, dep_col, lat_frac, lon_frac, own_out, sent_out, plan_out, held
):
    slices, band_rows, lon_count = grid.shape
    inner = band_rows - 2 * RIM
    first_row = place[0]
    fields = slices * EDGE

    def tile(t, slot):
        cols = tile_at(t)
        row = lax.broadcasted_iota(jnp.int32, (band_rows, LANES), 0)
        lane = lax.broadcasted_iota(jnp.int32, (band_rows, LANES), 1)
        shift = dep_col[:, cols] - (lane + t * LANES)
        shift = jnp.where(shift > lon_count // 2, shift - lon_count, shift)
        shift = jnp.where(shift < -(lon_count // 2), shift + lon_count, shift)
        row_step = dep_row[:, cols] - (first_row + row) + RIM
        held[slot, 0, 0:band_rows, :] = (row_step * ROW_CODE + shift + REACH).astype(jnp.float32)
        held[slot, 1, 0:band_rows, :] = lat_frac[:, cols].astype(jnp.float32)
        held[slot, 2, 0:band_rows, :] = lon_frac[:, cols].astype(jnp.float32)
        values = [grid[f, :, cols].astype(jnp.float32) for f in range(slices)]
        for out, start, plan_start in (
            (own_out, 0, 0),
            (sent_out, band_rows - EDGE, band_rows - RIM),
        ):
            block = [value[start : start + EDGE] for value in values]
            block += [held[slot, at, plan_start : plan_start + RIM, :] for at in range(3)]
            block.append(jnp.zeros((RIM, LANES), jnp.float32))
            out[:, cols] = jnp.concatenate(block, axis=0).astype(jnp.bfloat16)
        for at in range(3):
            plan_out[at * inner : (at + 1) * inner, cols] = held[
                slot, at, RIM : RIM + inner, :
            ].astype(jnp.bfloat16)

    in_steps(lon_count // LANES, 5, tile)


def inner_kernel(
    pair_ids, grid, plans, inner_out, basis_out, windows, departed, waves
):
    slices, band_rows, lon_count = grid.shape
    inner = band_rows - 2 * RIM
    orders = basis_out.shape[0]

    def wave_rows(group, carry):
        row = lax.broadcasted_iota(jnp.int32, (16, LANES), 0)
        pair = jnp.full((16, LANES), pair_ids[4 * group + 3], jnp.int32)
        for at in (2, 1, 0):
            pair = jnp.where(row < 4 * (at + 1), pair_ids[4 * group + at], pair)
        wave = jnp.where((row & 2) == 0, pair, NMAX + 1 - pair)
        waves[pl.ds(pl.multiple_of(group * 16, 16), 16), :] = wave.astype(jnp.float32)
        return carry

    lax.fori_loop(0, orders // 16, wave_rows, 0)

    def basis_tile(t, group):
        rows = pl.ds(pl.multiple_of(group * 16, 16), 16)
        lane = lax.broadcasted_iota(jnp.int32, (16, LANES), 1)
        row = lax.broadcasted_iota(jnp.int32, (16, LANES), 0)
        longitude = lane + t * SPAN
        quarter = jnp.where((row & 1) == 0, 0.0, float(lon_count // 4))
        steps = longitude.astype(jnp.float32) * waves[rows, :] + quarter
        turns = jnp.floor(steps * (1.0 / lon_count) + 0.5)
        angle = (lon_count // 4 - jnp.abs(steps - turns * lon_count)) * (2.0 * math.pi / lon_count)
        square = angle * angle
        series = jnp.float32(-1.0 / 39916800.0)
        for term in (1.0 / 362880.0, -1.0 / 5040.0, 1.0 / 120.0, -1.0 / 6.0, 1.0):
            series = series * square + term
        taken = (lane < SPAN) & (longitude < lon_count)
        basis_out[rows, tile_at(t)] = jnp.where(taken, angle * series, 0.0).astype(jnp.bfloat16)

    def window(t, slot):
        first, second, lane_at = cut_of(t * SPAN - REACH, lon_count)
        for f in range(slices):
            windows[slot, f, 0:band_rows, :] = cut(
                grid[f, :, first], grid[f, :, second], lane_at
            ).astype(jnp.float32)
        first, second, lane_at = cut_of(t * SPAN, lon_count)
        code, lat_weight, lon_weight = [
            cut(
                plans[at * inner : (at + 1) * inner, first],
                plans[at * inner : (at + 1) * inner, second],
                lane_at,
            ).astype(jnp.float32)
            for at in range(3)
        ]
        plan = lane_plan(code)
        weights = corner_weights(lat_weight, lon_weight)
        for f in range(slices):
            sources = [
                windows[slot, f, position : position + inner, :].astype(jnp.bfloat16)
                for position in range(2 * RIM + 1)
            ]
            departed[f * inner : (f + 1) * inner, tile_at(t)] = interpolate(sources, plan, weights)
        if orders <= 64:
            for group in range(orders // 16):
                basis_tile(t, group)
        else:
            lax.fori_loop(0, orders // 16, lambda g, c: (basis_tile(t, g), c)[1], 0)

    in_steps(basis_out.shape[1] // LANES, 2, window)
    inner_out[...] = lax.dot_general(
        basis_out[...],
        departed[...],
        (((1,), (1,)), ((), ())),
        preferred_element_type=jnp.float32,
    )


def rim_kernel(arrived, own, basis, inner_fourier, fourier_out, windows, plans, departed, *, slices):
    lon_count = arrived.shape[1]
    fields = slices * EDGE
    sublane = lax.broadcasted_iota(jnp.int32, (2 * EDGE, LANES), 0)

    def window(t, slot):
        first, second, lane_at = cut_of(t * SPAN - REACH, lon_count)
        for side, ref in enumerate((arrived, own)):
            block = cut(ref[0:fields, first], ref[0:fields, second], lane_at).astype(jnp.float32)
            for f in range(slices):
                at = 2 * EDGE * (f + 1) + EDGE * side
                windows[slot, at : at + EDGE, :] = block[f * EDGE : (f + 1) * EDGE]
        first, second, lane_at = cut_of(t * SPAN, lon_count)
        for side, ref in enumerate((arrived, own)):
            block = cut(ref[fields:, first], ref[fields:, second], lane_at).astype(jnp.float32)
            for at in range(3):
                for copy in range(2):
                    row = EDGE * copy + RIM * side
                    plans[slot, at, row : row + RIM, :] = block[RIM * at : RIM * (at + 1)]
        code, lat_weight, lon_weight = [
            jnp.concatenate([plans[slot, at]] * (slices // 2), axis=0) for at in range(3)
        ]
        plan = lane_plan(code)
        weights = corner_weights(lat_weight, lon_weight)

        def source(position):
            pieces = []
            for f in range(0, slices, 2):
                low = 2 * EDGE * (f + 1) + position
                high = 2 * EDGE * (f + 2) + position - EDGE
                pieces.append(
                    jnp.where(
                        sublane < EDGE,
                        windows[slot, low : low + 2 * EDGE, :],
                        windows[slot, high : high + 2 * EDGE, :],
                    )
                )
            return jnp.concatenate(pieces, axis=0).astype(jnp.bfloat16)

        sources = [source(position) for position in range(2 * RIM + 1)]
        departed[:, tile_at(t)] = interpolate(sources, plan, weights)

    in_steps(basis.shape[1] // LANES, AT_ONCE, window)
    rim_fourier = lax.dot_general(
        basis[...],
        departed[...],
        (((1,), (1,)), ((), ())),
        preferred_element_type=jnp.float32,
    )
    levs = fourier_out.shape[1]
    for pair in range(fourier_out.shape[0]):
        block = jnp.concatenate(
            [inner_fourier[4 * pair : 4 * pair + 4, :], rim_fourier[4 * pair : 4 * pair + 4, :]],
            axis=1,
        ).astype(jnp.bfloat16)
        for lev in range(levs):
            fourier_out[pair, lev] = block


def legendre_kernel(place, pair_ids, coeffs, spread_analysis, out, *, bands, levs, slices):
    rows = spread_analysis.shape[1]
    col_count = spread_analysis.shape[2]
    inner = rows // slices - EDGE
    column = lax.broadcasted_iota(jnp.int32, (1, rows), 1)
    rim_at = column - inner * slices
    slice_of = jnp.where(rim_at < 0, column // inner, rim_at // EDGE)

    def add(band, total):
        block = jnp.concatenate(
            [coeffs[band * levs + lev].astype(jnp.float32) for lev in range(levs)], axis=0
        )
        masked = jnp.concatenate(
            [jnp.where(slice_of == f, block, 0.0) for f in range(slices)], axis=0
        ).astype(jnp.bfloat16)
        return total + jnp.dot(masked, spread_analysis[band], preferred_element_type=jnp.float32)

    total = jnp.zeros((slices * levs * 4, col_count), jnp.float32)
    if bands <= 16:
        for band in range(bands):
            total = add(band, total)
    else:
        total = lax.fori_loop(0, bands, add, total)
    pair_id = pair_ids[place[0]]
    columns = place[1] + lax.broadcasted_iota(jnp.int32, (2, col_count), 1)
    first_wave = columns < NMAX + 1 - pair_id
    for f in range(slices):
        for lev in range(levs):
            at = (f * levs + lev) * 4
            out[lev * slices + f] = jnp.where(first_wave, total[at : at + 2], total[at + 2 : at + 4])


def shards(grid, dep_row, dep_col, lat_frac, lon_frac, pair_ids, analysis):
    slices, band_rows, lon_count = grid.shape
    pairs = pair_ids.shape[0]
    col_count = analysis.shape[2]
    bands, levs = lax.axis_size("lat"), lax.axis_size("lev")
    inner = band_rows - 2 * RIM
    windows = -(-lon_count // SPAN)
    held_rows = -(-band_rows // 8) * 8
    lat_at, lev_at = lax.axis_index("lat"), lax.axis_index("lev")
    band_start = jnp.reshape(lat_at * band_rows, (1,)).astype(jnp.int32)
    vmem = pl.BlockSpec(memory_space=pltpu.VMEM)
    smem = pl.BlockSpec(memory_space=pltpu.SMEM)
    params = pltpu.CompilerParams(vmem_limit_bytes=48 * 2**20)

    rim_shape = jax.ShapeDtypeStruct((slices * EDGE + 4 * RIM, lon_count), jnp.bfloat16)
    own_rim, sent_rim, plans = pl.pallas_call(
        pack_kernel,
        out_shape=(
            rim_shape,
            rim_shape,
            jax.ShapeDtypeStruct((3 * inner, lon_count), jnp.bfloat16),
        ),
        in_specs=[smem] + [vmem] * 5,
        out_specs=(vmem,) * 3,
        scratch_shapes=[pltpu.VMEM((5, 3, held_rows, LANES), jnp.float32)],
        compiler_params=params,
    )(band_start, grid, dep_row, dep_col, lat_frac, lon_frac)
    arrived_rim = lax.ppermute(sent_rim, "lat", [(i, (i + 1) % bands) for i in range(bands)])

    inner_fourier, basis = pl.pallas_call(
        inner_kernel,
        out_shape=(
            jax.ShapeDtypeStruct((4 * pairs, slices * inner), jnp.float32),
            jax.ShapeDtypeStruct((4 * pairs, windows * LANES), jnp.bfloat16),
        ),
        in_specs=[smem] + [vmem] * 2,
        out_specs=(vmem, vmem),
        scratch_shapes=[
            pltpu.VMEM((2, slices, held_rows, LANES), jnp.float32),
            pltpu.VMEM((slices * inner, windows * LANES), jnp.bfloat16),
            pltpu.VMEM((4 * pairs, LANES), jnp.float32),
        ],
        compiler_params=params,
        cost_estimate=pl.CostEstimate(flops=100_000_000, bytes_accessed=2_000_000, transcendentals=0),
    )(pair_ids, grid, plans)

    fourier = pl.pallas_call(
        functools.partial(rim_kernel, slices=slices),
        out_shape=jax.ShapeDtypeStruct((pairs, levs, 4, slices * band_rows), jnp.bfloat16),
        in_specs=[vmem] * 4,
        out_specs=vmem,
        scratch_shapes=[
            pltpu.VMEM((AT_ONCE, 2 * EDGE * (slices + 2), LANES), jnp.float32),
            pltpu.VMEM((AT_ONCE, 3, 2 * EDGE, LANES), jnp.float32),
            pltpu.VMEM((2 * RIM * slices, windows * LANES), jnp.bfloat16),
        ],
        compiler_params=params,
    )(arrived_rim, own_rim, basis, inner_fourier)

    values = analysis[0].reshape(bands, band_rows, col_count)
    before = jnp.roll(values[:, band_rows - RIM :], 1, axis=0)
    spread_analysis = jnp.concatenate(
        [values[:, RIM : RIM + inner]] * slices + [before, values[:, :RIM]] * slices, axis=1
    )
    coeffs = lax.all_to_all(
        fourier.reshape(pairs * levs, 4, slices * band_rows),
        ("lat", "lev"),
        split_axis=0,
        concat_axis=0,
        tiled=True,
    )
    place = jnp.stack([lat_at, lev_at * col_count]).astype(jnp.int32)
    out = pl.pallas_call(
        functools.partial(legendre_kernel, bands=bands, levs=levs, slices=slices),
        out_shape=jax.ShapeDtypeStruct((levs * slices, 2, col_count), jnp.float32),
        in_specs=[smem, smem, vmem, vmem],
        out_specs=vmem,
        compiler_params=params,
    )(place, pair_ids, coeffs, spread_analysis)
    return out[None]


def solution(mesh):
    return jax.shard_map(
        shards,
        mesh=mesh,
        in_specs=(
            P("lev", "lat", None),
            P("lat", None),
            P("lat", None),
            P("lat", None),
            P("lat", None),
            P(),
            P("lat", None, "lev"),
        ),
        out_specs=P("lat", None, None, "lev"),
        check_vma=False,
    )
```

time: 34.3 us -> 27.4 us (0.80)
  starting transfers between devices: 13.1 us -> 6.71 us
  waiting for transfers between devices: 6.69 us -> 8.06 us
  Pallas kernels: 11.1 us -> 9.99 us
  local copies, waits for them, and re-layouts: 2.76 us -> 2.32 us
    all_to_all x1, starting transfers between devices: 6.97 us -> 3.69 us  [shards(): lax.all_to_all(fourier.reshape(pairs * levs, 4, slices * band_rows), ('la...]
    ppermute x2 -> x1, starting transfers between devices: 6.17 us -> 3.02 us  [shards(): lax.ppermute(sent_rim, 'lat', [(i, (i + 1) % bands) for i in range(bands)])]
    ppermute x2 -> x1, waiting for transfers between devices: 0.01 us -> 1.23 us  [shards(): lax.ppermute(sent_rim, 'lat', [(i, (i + 1) % bands) for i in range(bands)])]
    slice x4, local copies, waits for them, and re-layouts: 1.16 us -> 0.06 us  [the longest x1 0.03 us: shards(): values[:, RIM:RIM + inner]]
    unnamed x15 -> x13, local copies, waits for them, and re-layouts: 1.11 us -> 1.93 us
    pallas_call x1 -> x2, Pallas kernels: 4.21 us -> 3.56 us  [the longest x1 3.15 us: shards(): pl.pallas_call(functools.partial(rim_kernel, slices=slices), out_shape=ja...]
    pallas_call x1, Pallas kernels: 5.48 us -> 5.01 us  [shards(): pl.pallas_call(inner_kernel, out_shape=(jax.ShapeDtypeStruct((4 * pairs,...]
  transfers between devices with their start and end apart: 3 -> 2, of which waited for: 1 -> 2; matrix products, arithmetic and copies ran while one was open for 2% -> 2% of each run, Pallas kernels for 16% -> 18%
where the time goes in v3:
time: 27.4 us; the launch traced here: 27.3 us
  Pallas kernels  9.99 us (36%)
  waiting for transfers between devices  8.06 us (29%)
  starting transfers between devices  6.71 us (24%)
  local copies, waits for them, and re-layouts  2.32 us (8%)
    all_to_all x1, waiting for transfers between devices, shards(): lax.all_to_all(fourier.reshape(pairs * levs, 4, slices * band_rows), ('la...  6.83 us
    pallas_call x1, Pallas kernels, shards(): pl.pallas_call(inner_kernel, out_shape=(jax.ShapeDtypeStruct((4 * pairs,...  5.01 us
    all_to_all x1, starting transfers between devices, shards(): lax.all_to_all(fourier.reshape(pairs * levs, 4, slices * band_rows), ('la...  3.69 us
    pallas_call x1, Pallas kernels, shards(): pl.pallas_call(functools.partial(rim_kernel, slices=slices), out_shape=ja...  3.15 us
    ppermute x1, starting transfers between devices, shards(): lax.ppermute(sent_rim, 'lat', [(i, (i + 1) % bands) for i in range(bands)])  3.02 us
    unnamed x13, local copies, waits for them, and re-layouts  1.93 us
    pallas_call x1, Pallas kernels, shards(): pl.pallas_call(functools.partial(legendre_kernel, bands=bands, levs=levs,...  1.42 us
    ppermute x1, waiting for transfers between devices, shards(): lax.ppermute(sent_rim, 'lat', [(i, (i + 1) % bands) for i in range(bands)])  1.23 us
  transfers between devices with their start and end apart: 2, of which 2 were waited for; matrix products, arithmetic and copies ran while one was open for 2% of the time, Pallas kernels for 18%

profile of v3, /device:TPU:0, one launch (start us, length us, event | category | flops | bytes accessed | tf_op | source)
XLA Modules:
  0.0 27.3 jit_solution(11914264525311710177)
XLA Ops:
  0.0 0.0 copy-start
  0.0 0.0 copy-start.1
  0.0 0.0 copy-start.2
  0.0 0.0 copy-start.3
  0.0 1.2 %copy.10.grid = bf16[4,20,3200]{2,1,0:T(8,128)(2,1)S(1)} copy(bf16[4,20,3200]{2,0,1:T(4,128)(2,1)} %param.7) | data formatting | bytes 1024000 | tf_op args[0]
  1.2 0.0 copy-done
  1.2 0.0 copy-done.1
  1.2 0.0 copy-done.2
  1.3 0.0 copy-done.3
  1.3 0.0 copy-start.5
  1.3 0.4 %shard_map.73 = (bf16[24,3200]{1,0:T(8,128)(2,1)S(1)}, bf16[24,3200]{1,0:T(8,128)(2,1)S(1)}, bf16[48,3200]{1,0:T(8,128)(2,1)S(1)}) custom-call(s32[1]{0:T(128)} %bitcast.2.place, bf16[4,20,3200]{2,1,0:T(8,128)(2,1)S(1)} %copy.10.grid, s32[20,3200]{1,0:T(8,128)S(1)} %copy-done, s32[20,3200]{1,0:T(8,128)S(1)} %copy-done.1, bf16[20,3200]{1,0:T(8,128)(2,1)S(1)} %copy-done.2, ...), custom_call_target="tpu_custom_call" | custom-call | tf_op jit(solution)/shard_map/pallas_call | solution.py:319
  1.7 3.0 %collective-permute-start = (bf16[24,3200]{1,0:T(8,128)(2,1)S(1)}, bf16[24,3200]{1,0:T(8,128)(2,1)S(1)}, u32[]{:S(2)}, u32[]{:S(2)}) collective-permute-start(bf16[24,3200]{1,0:T(8,128)(2,1)S(1)} %get-tuple-element.10), channel_id=1, source_target_pairs={{0,4},{4,8},{8,12},{12,16},{16,20},{20,24},{24,28},{28,0},{1,5},{5... | collective-permute-start | bytes 460808 | tf_op jit(solution)/shard_map/ppermute | solution.py:331
  4.7 0.0 copy-done.5
  4.8 0.0 copy-start.4
  4.8 0.6 %copy-done.4 = s32[8]{0:T(128)S(1)} copy-done((s32[8]{0:T(128)S(1)}, s32[8]{0:T(128)}, u32[]{:S(2)}) %copy-start.4) | copy-done | bytes 56
  5.5 5.0 %shard_map.74 = (f32[32,64]{1,0:T(8,128)S(1)}, bf16[32,3712]{1,0:T(8,128)(2,1)S(1)}) custom-call(s32[8]{0:T(128)S(1)} %copy-done.4, bf16[4,20,3200]{2,1,0:T(8,128)(2,1)S(1)} %copy.10.grid, bf16[48,3200]{1,0:T(8,128)(2,1)S(1)} %get-tuple-element.12.plans), custom_call_target="tpu_custom_call" | custom-call | flops 100000000 | bytes 2000000 | tf_op jit(solution)/shard_map/pallas_call | solution.py:333
  10.5 1.2 %collective-permute-done.arrived = bf16[24,3200]{1,0:T(8,128)(2,1)S(1)} collective-permute-done((bf16[24,3200]{1,0:T(8,128)(2,1)S(1)}, bf16[24,3200]{1,0:T(8,128)(2,1)S(1)}, u32[]{:S(2)}, u32[]{:S(2)}) %collective-permute-start) | collective-permute-done | bytes 153632 | tf_op jit(solution)/shard_map/ppermute | solution.py:331
  11.7 3.2 %shard_map.75 = bf16[8,4,4,80]{3,2,1,0:T(4,128)(2,1)} custom-call(bf16[24,3200]{1,0:T(8,128)(2,1)S(1)} %collective-permute-done.arrived, bf16[24,3200]{1,0:T(8,128)(2,1)S(1)} %get-tuple-element.11.own, bf16[32,3712]{1,0:T(8,128)(2,1)S(1)} %get-tuple-element.13.basis, f32[32,64]{1,0:T(8,128)S(1)} %get-tuple-element.14.inner_fourier), custom_call_target="tpu_custom_call" | custom-call | tf_op jit(solution)/shard_map/pallas_call | solution.py:350
  14.9 3.7 %all-to-all-start = ((bf16[32,4,80]{2,1,0:T(4,128)(2,1)}), bf16[32,4,80]{2,1,0:T(4,128)(2,1)S(1)}, u32[]{:S(2)}, u32[]{:S(2)}) async-start(bf16[32,4,80]{2,1,0:T(4,128)(2,1)} %bitcast.3), calls=%async_computation | async-start | bytes 65536 | tf_op jit(solution)/shard_map/all_to_all | solution.py:368
  18.6 0.1 pad_add_fusion.place
  18.7 0.3 %concatenate.8.spread_analysis = bf16[8,80,320]{2,1,0:T(8,128)(2,1)S(1)} concatenate(bf16[8,16,320]{2,1,0:T(8,128)(2,1)S(1)} %slice.21, bf16[8,16,320]{2,1,0:T(8,128)(2,1)S(1)} %slice.21, bf16[8,16,320]{2,1,0:T(8,128)(2,1)S(1)} %slice.21, bf16[8,16,320]{2,1,0:T(8,128)(2,1)S(1)} %slice.21, bf16[8,2,320]{2,1,0:T(2,128)(2,1)S(1)} %pad_maximum_fusion, bf16[8,2,320]{2,1,0:T(2,128)(2,1)S(1)} %slice.24, ...), dimensions={1} | concatenate | bytes 819200 | tf_op jit(solution)/shard_map/concatenate | solution.py:365
  19.0 6.8 %all-to-all-done.coeffs = bf16[32,4,80]{2,1,0:T(4,128)(2,1)S(1)} async-done(((bf16[32,4,80]{2,1,0:T(4,128)(2,1)}), bf16[32,4,80]{2,1,0:T(4,128)(2,1)S(1)}, u32[]{:S(2)}, u32[]{:S(2)}) %all-to-all-start) | async-done | bytes 20512 | tf_op jit(solution)/shard_map/all_to_all | solution.py:368
  25.9 1.4 %shard_map.76 = f32[16,2,320]{2,1,0:T(2,128)} custom-call(s32[2]{0:T(128)S(1)} %pad_add_fusion.place, s32[8]{0:T(128)S(1)} %copy-done.4, bf16[32,4,80]{2,1,0:T(4,128)(2,1)S(1)} %all-to-all-done.coeffs, bf16[8,80,320]{2,1,0:T(8,128)(2,1)S(1)} %concatenate.8.spread_analysis), custom_call_target="tpu_custom_call" | custom-call | tf_op jit(solution)/shard_map/pallas_call | solution.py:376
  (6 shorter events, 0.1 us)
Async XLA Ops:
  0.0 1.2 %copy-start = (s32[20,3200]{1,0:T(8,128)S(1)}, s32[20,3200]{1,0:T(8,128)}, u32[]{:S(2)}) copy-start(s32[20,3200]{1,0:T(8,128)} %dep_row.1) | copy-start | bytes 768004
  0.0 1.2 %copy-start.1 = (s32[20,3200]{1,0:T(8,128)S(1)}, s32[20,3200]{1,0:T(8,128)}, u32[]{:S(2)}) copy-start(s32[20,3200]{1,0:T(8,128)} %dep_col.1) | copy-start | bytes 768004
  0.0 1.2 %copy-start.2 = (bf16[20,3200]{1,0:T(8,128)(2,1)S(1)}, bf16[20,3200]{1,0:T(8,128)(2,1)}, u32[]{:S(2)}) copy-start(bf16[20,3200]{1,0:T(8,128)(2,1)} %lat_frac.1) | copy-start | bytes 384004
  0.0 1.3 %copy-start.3 = (bf16[20,3200]{1,0:T(8,128)(2,1)S(1)}, bf16[20,3200]{1,0:T(8,128)(2,1)}, u32[]{:S(2)}) copy-start(bf16[20,3200]{1,0:T(8,128)(2,1)} %lon_frac.1) | copy-start | bytes 384004
  1.3 3.4 %copy-start.5 = (bf16[1,160,320]{2,1,0:T(8,128)(2,1)S(1)}, bf16[1,160,320]{2,1,0:T(8,128)(2,1)}, u32[]{:S(2)}) copy-start(bf16[1,160,320]{2,1,0:T(8,128)(2,1)} %param.13) | copy-start | bytes 307204
  1.7 10.0 %collective-permute-start = (bf16[24,3200]{1,0:T(8,128)(2,1)S(1)}, bf16[24,3200]{1,0:T(8,128)(2,1)S(1)}, u32[]{:S(2)}, u32[]{:S(2)}) collective-permute-start(bf16[24,3200]{1,0:T(8,128)(2,1)S(1)} %get-tuple-element.10), channel_id=1, source_target_pairs={{0,4},{4,8},{8,12},{12,16},{16,20},{20,24},{24,28},{28,0},{1,5},{5... | collective-permute-start | bytes 460808 | tf_op jit(solution)/shard_map/ppermute | solution.py:331
  4.8 0.7 %copy-start.4 = (s32[8]{0:T(128)S(1)}, s32[8]{0:T(128)}, u32[]{:S(2)}) copy-start(s32[8]{0:T(128)} %pair_ids.3) | copy-start | bytes 100
  14.9 10.9 %all-to-all-start = ((bf16[32,4,80]{2,1,0:T(4,128)(2,1)}), bf16[32,4,80]{2,1,0:T(4,128)(2,1)S(1)}, u32[]{:S(2)}, u32[]{:S(2)}) async-start(bf16[32,4,80]{2,1,0:T(4,128)(2,1)} %bitcast.3), calls=%async_computation | async-start | bytes 65536 | tf_op jit(solution)/shard_map/all_to_all | solution.py:368

commit v4 on v3

v4 whole, which is shorter than its diff:
```python
import functools
import math

import jax
import jax.numpy as jnp
from jax import lax
from jax.experimental import pallas as pl
from jax.experimental.pallas import tpu as pltpu
from jax.sharding import PartitionSpec as P

NMAX = 1279
LANES = 128
RIM = 2
EDGE = 2 * RIM
REACH = 8
SPAN = LANES - 2 * REACH - 1
ROW_BITS = 5
AT_ONCE = 4


def lane_gather(values, indices):
    numbers = lax.GatherDimensionNumbers(
        offset_dims=(),
        collapsed_slice_dims=(1,),
        start_index_map=(1,),
        operand_batching_dims=(0,),
        start_indices_batching_dims=(0,),
    )
    return lax.gather(
        values,
        indices[..., None],
        numbers,
        (1, 1),
        mode=lax.GatherScatterMode.PROMISE_IN_BOUNDS,
    )


def tile_at(t):
    return pl.ds(pl.multiple_of(t * LANES, LANES), LANES)


def cut_of(start, lon_count):
    tiles = lon_count // LANES
    start = jnp.asarray(start, jnp.int32) + lon_count
    first = start >> LANES.bit_length() - 1
    first = jnp.where(first >= tiles, first - tiles, first)
    second = jnp.where(first == tiles - 1, 0, first + 1)
    return tile_at(first), tile_at(second), start & LANES - 1


def cut(first, second, lane_at):
    lane = lax.broadcasted_iota(jnp.int32, first.shape, 1).astype(jnp.int16)
    joined = jnp.where(lane >= lane_at.astype(jnp.int16), first, second)
    return pltpu.roll(joined, (LANES - lane_at) & LANES - 1, 1)


def lane_plan(code):
    code = code.astype(jnp.int32)
    west = lax.broadcasted_iota(jnp.int32, code.shape, 1) + (code & (1 << ROW_BITS) - 1)
    west_lane = (west & (LANES - 1)).astype(jnp.int16)
    east_lane = ((west + 1) & (LANES - 1)).astype(jnp.int16)
    row_step = (code >> ROW_BITS).astype(jnp.float32).astype(jnp.bfloat16)
    return west_lane, east_lane, row_step


def corner_weights(lat_weight, lon_weight):
    south, north = 1.0 - lat_weight, lat_weight
    west, east = 1.0 - lon_weight, lon_weight
    return south * west, south * east, north * west, north * east


def interpolate(sources, plan, weights):
    west_lane, east_lane, row_step = plan
    masks = [row_step == float(step) for step in range(2 * RIM - 1)]

    def pick(gathered):
        low, high = gathered[2 * RIM - 1], gathered[2 * RIM]
        for position in range(2 * RIM - 2, -1, -1):
            low = jnp.where(masks[position], gathered[position], low)
            high = jnp.where(masks[position], gathered[position + 1], high)
        return low.astype(jnp.float32), high.astype(jnp.float32)

    west_low, west_high = pick([lane_gather(source, west_lane) for source in sources])
    east_low, east_high = pick([lane_gather(source, east_lane) for source in sources])
    departed = (
        weights[0] * west_low
        + weights[1] * east_low
        + weights[2] * west_high
        + weights[3] * east_high
    )
    return departed.astype(jnp.bfloat16)


def in_steps(count, at_once, window):
    def several(step, carry):
        for slot in range(at_once):
            window(step * at_once + slot, slot)
        return carry

    lax.fori_loop(0, count // at_once, several, 0)
    for slot in range(count % at_once):
        window(count - count % at_once + slot, slot)


def pack_kernel(
    band_start, col_start, pair_ids, grid, dep_row, dep_col, lat_frac, lon_frac,
    own_out, sent_out, grid_out, plan_out, waves_out, limit_out, held, rows,
):
    band_rows, slices, lon_count = grid.shape
    inner = band_rows - 2 * RIM
    fields = slices * EDGE
    first_row = band_start[0]

    def tile(t, slot):
        cols = tile_at(t)
        for row in range(band_rows):
            rows[slot, row * slices : (row + 1) * slices, :] = grid[row, :, cols].astype(
                jnp.float32
            )
        row = lax.broadcasted_iota(jnp.int32, (band_rows, LANES), 0)
        lane = lax.broadcasted_iota(jnp.int32, (band_rows, LANES), 1)
        shift = dep_col[:, cols] - (lane + t * LANES)
        shift = jnp.where(shift > lon_count // 2, shift - lon_count, shift)
        shift = jnp.where(shift < -(lon_count // 2), shift + lon_count, shift)
        row_step = dep_row[:, cols] - (first_row + row) + RIM
        held[slot, 0, 0:band_rows, :] = ((row_step << ROW_BITS) + shift + REACH).astype(
            jnp.float32
        )
        held[slot, 1, 0:band_rows, :] = lat_frac[:, cols].astype(jnp.float32)
        held[slot, 2, 0:band_rows, :] = lon_frac[:, cols].astype(jnp.float32)
        grid_out[:, cols] = rows[slot].astype(jnp.bfloat16)
        for out, start, plan_start in (
            (own_out, 0, 0),
            (sent_out, slices * band_rows - fields, band_rows - RIM),
        ):
            block = [rows[slot, start : start + fields, :]]
            block += [held[slot, at, plan_start : plan_start + RIM, :] for at in range(3)]
            block.append(jnp.zeros((RIM, LANES), jnp.float32))
            out[:, cols] = jnp.concatenate(block, axis=0).astype(jnp.bfloat16)
        for at in range(3):
            plan_out[at * inner : (at + 1) * inner, cols] = held[
                slot, at, RIM : RIM + inner, :
            ].astype(jnp.bfloat16)

    in_steps(lon_count // LANES, 5, tile)

    def wave_rows(group, carry):
        row = lax.broadcasted_iota(jnp.int32, (16, LANES), 0)
        pair = jnp.full((16, LANES), pair_ids[4 * group + 3], jnp.int32)
        for at in (2, 1, 0):
            pair = jnp.where(row < 4 * (at + 1), pair_ids[4 * group + at], pair)
        wave = jnp.where((row & 2) == 0, pair, NMAX + 1 - pair)
        waves_out[pl.ds(pl.multiple_of(group * 16, 16), 16), :] = wave.astype(jnp.float32)
        return carry

    lax.fori_loop(0, waves_out.shape[0] // 16, wave_rows, 0)
    limit = NMAX + 1 - pair_ids[first_row // band_rows] - col_start[0]
    limit_out[...] = jnp.full(limit_out.shape, limit, jnp.int32)


def inner_kernel(grid, plans, waves, inner_out, basis_out, windows, departed, *, slices):
    lon_count = grid.shape[1]
    inner = plans.shape[0] // 3
    orders = basis_out.shape[0]

    def basis_tile(t, group):
        rows = pl.ds(pl.multiple_of(group * 16, 16), 16)
        lane = lax.broadcasted_iota(jnp.int32, (16, LANES), 1)
        row = lax.broadcasted_iota(jnp.int32, (16, LANES), 0)
        longitude = lane + t * SPAN
        quarter = jnp.where((row & 1) == 0, 0.0, float(lon_count // 4))
        steps = longitude.astype(jnp.float32) * waves[rows, :] + quarter
        turns = jnp.floor(steps * (1.0 / lon_count) + 0.5)
        angle = (lon_count // 4 - jnp.abs(steps - turns * lon_count)) * (2.0 * math.pi / lon_count)
        square = angle * angle
        series = jnp.float32(-1.0 / 39916800.0)
        for term in (1.0 / 362880.0, -1.0 / 5040.0, 1.0 / 120.0, -1.0 / 6.0, 1.0):
            series = series * square + term
        taken = (lane < SPAN) & (longitude < lon_count)
        basis_out[rows, tile_at(t)] = jnp.where(taken, angle * series, 0.0).astype(jnp.bfloat16)

    def window(t, slot):
        first, second, lane_at = cut_of(t * SPAN - REACH, lon_count)
        windows[slot] = cut(grid[:, first], grid[:, second], lane_at).astype(jnp.float32)
        first, second, lane_at = cut_of(t * SPAN, lon_count)
        code, lat_weight, lon_weight = [
            cut(
                plans[at * inner : (at + 1) * inner, first],
                plans[at * inner : (at + 1) * inner, second],
                lane_at,
            ).astype(jnp.float32)
            for at in range(3)
        ]
        plan = lane_plan(code)
        weights = corner_weights(lat_weight, lon_weight)
        for f in range(slices):
            sources = [
                windows[slot, pl.ds(slices * position + f, inner, stride=slices), :].astype(
                    jnp.bfloat16
                )
                for position in range(2 * RIM + 1)
            ]
            departed[f * inner : (f + 1) * inner, tile_at(t)] = interpolate(sources, plan, weights)
        if orders <= 64:
            for group in range(orders // 16):
                basis_tile(t, group)
        else:
            lax.fori_loop(0, orders // 16, lambda g, c: (basis_tile(t, g), c)[1], 0)

    in_steps(basis_out.shape[1] // LANES, 2, window)
    inner_out[...] = lax.dot_general(
        basis_out[...],
        departed[...],
        (((1,), (1,)), ((), ())),
        preferred_element_type=jnp.float32,
    )


def rim_kernel(arrived, own, basis, inner_fourier, fourier_out, windows, plans, departed, *, slices):
    lon_count = arrived.shape[1]
    fields = slices * EDGE
    sublane = lax.broadcasted_iota(jnp.int32, (2 * slices, LANES), 0)

    def window(t, slot):
        first, second, lane_at = cut_of(t * SPAN - REACH, lon_count)
        for side, ref in enumerate((arrived, own)):
            windows[slot, fields * side : fields * (side + 1), :] = cut(
                ref[0:fields, first], ref[0:fields, second], lane_at
            ).astype(jnp.float32)
        first, second, lane_at = cut_of(t * SPAN, lon_count)
        for side, ref in enumerate((arrived, own)):
            plans[slot, 8 * side : 8 * (side + 1), :] = cut(
                ref[fields:, first], ref[fields:, second], lane_at
            ).astype(jnp.float32)

        def spread(at):
            pieces = []
            for side in range(2):
                two = [
                    jnp.broadcast_to(plans[slot, row : row + 1, :], (2 * slices, LANES))
                    for row in range(8 * side + RIM * at, 8 * side + RIM * (at + 1))
                ]
                pieces.append(jnp.where(sublane < slices, two[0], two[1]))
            return jnp.concatenate(pieces, axis=0)

        plan = lane_plan(spread(0))
        weights = corner_weights(spread(1), spread(2))
        sources = [
            windows[slot, slices * position : slices * position + fields, :].astype(jnp.bfloat16)
            for position in range(2 * RIM + 1)
        ]
        departed[:, tile_at(t)] = interpolate(sources, plan, weights)

    in_steps(basis.shape[1] // LANES, AT_ONCE, window)
    rim_fourier = lax.dot_general(
        basis[...],
        departed[...],
        (((1,), (1,)), ((), ())),
        preferred_element_type=jnp.float32,
    )
    levs = fourier_out.shape[1]
    for pair in range(fourier_out.shape[0]):
        block = jnp.concatenate(
            [inner_fourier[4 * pair : 4 * pair + 4, :], rim_fourier[4 * pair : 4 * pair + 4, :]],
            axis=1,
        ).astype(jnp.bfloat16)
        for lev in range(levs):
            fourier_out[pair, lev] = block


def legendre_kernel(limit, coeffs, spread_analysis, out, spread_coeffs, *, levs, slices):
    members, _, rows = coeffs.shape
    bands = members // levs
    col_count = spread_analysis.shape[1]
    inner = rows // slices - EDGE
    column = lax.broadcasted_iota(jnp.int32, (1, LANES), 1)
    rim_at = column - inner * slices
    slice_of = jnp.where(rim_at < 0, column // inner, rim_at % slices)
    slice_of = jnp.where(column < rows, slice_of, -1)

    def spread(band):
        block = jnp.concatenate(
            [coeffs[band * levs + lev].astype(jnp.float32) for lev in range(levs)], axis=0
        )
        block = jnp.concatenate(
            [block, jnp.zeros((block.shape[0], LANES - rows), jnp.float32)], axis=1
        )
        spread_coeffs[:, tile_at(band)] = jnp.concatenate(
            [jnp.where(slice_of == f, block, 0.0) for f in range(slices)], axis=0
        ).astype(jnp.bfloat16)

    if bands <= 16:
        for band in range(bands):
            spread(band)
    else:
        lax.fori_loop(0, bands, lambda band, carry: (spread(band), carry)[1], 0)
    total = jnp.dot(
        spread_coeffs[...], spread_analysis[...], preferred_element_type=jnp.float32
    )
    first_wave = lax.broadcasted_iota(jnp.int32, (2, col_count), 1) < limit[0:1, 0:1]
    for f in range(slices):
        for lev in range(levs):
            at = (f * levs + lev) * 4
            out[lev * slices + f] = jnp.where(first_wave, total[at : at + 2], total[at + 2 : at + 4])


def shards(grid, dep_row, dep_col, lat_frac, lon_frac, pair_ids, analysis):
    slices, band_rows, lon_count = grid.shape
    pairs = pair_ids.shape[0]
    col_count = analysis.shape[2]
    bands, levs = lax.axis_size("lat"), lax.axis_size("lev")
    inner = band_rows - 2 * RIM
    windows = -(-lon_count // SPAN)
    held_rows = -(-band_rows // 8) * 8
    fields = slices * EDGE
    band_start = jnp.reshape(lax.axis_index("lat") * band_rows, (1,)).astype(jnp.int32)
    col_start = jnp.reshape(lax.axis_index("lev") * col_count, (1,)).astype(jnp.int32)
    vmem = pl.BlockSpec(memory_space=pltpu.VMEM)
    smem = pl.BlockSpec(memory_space=pltpu.SMEM)
    params = pltpu.CompilerParams(vmem_limit_bytes=48 * 2**20)

    rim_shape = jax.ShapeDtypeStruct((fields + 4 * RIM, lon_count), jnp.bfloat16)
    own_rim, sent_rim, rows, plans, waves, limit = pl.pallas_call(
        pack_kernel,
        out_shape=(
            rim_shape,
            rim_shape,
            jax.ShapeDtypeStruct((band_rows * slices, lon_count), jnp.bfloat16),
            jax.ShapeDtypeStruct((3 * inner, lon_count), jnp.bfloat16),
            jax.ShapeDtypeStruct((4 * pairs, LANES), jnp.float32),
            jax.ShapeDtypeStruct((8, LANES), jnp.int32),
        ),
        in_specs=[smem] * 3 + [vmem] * 5,
        out_specs=(vmem,) * 6,
        scratch_shapes=[
            pltpu.VMEM((5, 3, held_rows, LANES), jnp.float32),
            pltpu.VMEM((5, band_rows * slices, LANES), jnp.float32),
        ],
        compiler_params=params,
    )(
        band_start, col_start, pair_ids, grid.transpose(1, 0, 2), dep_row, dep_col, lat_frac, lon_frac
    )
    arrived_rim = lax.ppermute(sent_rim, "lat", [(i, (i + 1) % bands) for i in range(bands)])

    inner_fourier, basis = pl.pallas_call(
        functools.partial(inner_kernel, slices=slices),
        out_shape=(
            jax.ShapeDtypeStruct((4 * pairs, slices * inner), jnp.float32),
            jax.ShapeDtypeStruct((4 * pairs, windows * LANES), jnp.bfloat16),
        ),
        in_specs=[vmem] * 3,
        out_specs=(vmem, vmem),
        scratch_shapes=[
            pltpu.VMEM((2, band_rows * slices, LANES), jnp.float32),
            pltpu.VMEM((slices * inner, windows * LANES), jnp.bfloat16),
        ],
        compiler_params=params,
        cost_estimate=pl.CostEstimate(flops=100_000_000, bytes_accessed=2_000_000, transcendentals=0),
    )(rows, plans, waves)

    fourier = pl.pallas_call(
        functools.partial(rim_kernel, slices=slices),
        out_shape=jax.ShapeDtypeStruct((pairs, levs, 4, slices * band_rows), jnp.bfloat16),
        in_specs=[vmem] * 4,
        out_specs=vmem,
        scratch_shapes=[
            pltpu.VMEM((AT_ONCE, 2 * fields, LANES), jnp.float32),
            pltpu.VMEM((AT_ONCE, 16, LANES), jnp.float32),
            pltpu.VMEM((fields, windows * LANES), jnp.bfloat16),
        ],
        compiler_params=params,
    )(arrived_rim, own_rim, basis, inner_fourier)

    values = analysis[0].reshape(bands, band_rows, col_count)
    before = jnp.roll(values[:, band_rows - RIM :], 1, axis=0)
    spread_rows = [values[:, RIM : RIM + inner]] * slices
    for rim in (before, values[:, :RIM]):
        for row in range(RIM):
            spread_rows += [rim[:, row : row + 1]] * slices
    spread_rows.append(jnp.zeros((bands, LANES - slices * band_rows, col_count), jnp.bfloat16))
    spread_analysis = jnp.concatenate(spread_rows, axis=1).reshape(bands * LANES, col_count)

    coeffs = lax.all_to_all(
        fourier.reshape(pairs * levs, 4, slices * band_rows),
        ("lat", "lev"),
        split_axis=0,
        concat_axis=0,
        tiled=True,
    )
    out = pl.pallas_call(
        functools.partial(legendre_kernel, levs=levs, slices=slices),
        out_shape=jax.ShapeDtypeStruct((levs * slices, 2, col_count), jnp.float32),
        in_specs=[vmem] * 3,
        out_specs=vmem,
        scratch_shapes=[pltpu.VMEM((4 * levs * slices, bands * LANES), jnp.bfloat16)],
        compiler_params=params,
    )(limit, coeffs, spread_analysis)
    return out[None]


def solution(mesh):
    return jax.shard_map(
        shards,
        mesh=mesh,
        in_specs=(
            P("lev", "lat", None),
            P("lat", None),
            P("lat", None),
            P("lat", None),
            P("lat", None),
            P(),
            P("lat", None, "lev"),
        ),
        out_specs=P("lat", None, None, "lev"),
        check_vma=False,
    )
```

time: 27.4 us -> 30.9 us (1.13)
  local copies, waits for them, and re-layouts: 2.32 us -> 6.18 us
  waiting for transfers between devices: 8.06 us -> 9.01 us
  Pallas kernels: 9.99 us -> 9.13 us
  starting transfers between devices: 6.71 us -> 6.05 us
    unnamed x13 -> x14, local copies, waits for them, and re-layouts: 1.93 us -> 5.45 us
    ppermute x1, waiting for transfers between devices: 1.23 us -> 2.49 us  [shards(): lax.ppermute(sent_rim, 'lat', [(i, (i + 1) % bands) for i in range(bands)])]
    pallas_call x2, Pallas kernels: 6.43 us -> 5.26 us  [the longest x1 4.37 us: shards(): pl.pallas_call(functools.partial(inner_kernel, slices=slices), out_shape=...]
    pallas_call x1, Pallas kernels: 0.41 us -> 1.09 us  [shards(): pl.pallas_call(pack_kernel, out_shape=(rim_shape, rim_shape, jax.ShapeDty...]
    all_to_all x1, starting transfers between devices: 3.69 us -> 3.03 us  [shards(): lax.all_to_all(fourier.reshape(pairs * levs, 4, slices * band_rows), ('la...]
    pallas_call x1, Pallas kernels: 3.15 us -> 2.78 us  [shards(): pl.pallas_call(functools.partial(rim_kernel, slices=slices), out_shape=ja...]
    all_to_all x1, waiting for transfers between devices: 6.83 us -> 6.51 us  [shards(): lax.all_to_all(fourier.reshape(pairs * levs, 4, slices * band_rows), ('la...]
    concatenate x1, local copies, waits for them, and re-layouts: 0.29 us -> 0.61 us  [shards(): jnp.concatenate(spread_rows, axis=1).reshape(bands * LANES, col_count)]
  transfers between devices with their start and end apart: 2 -> 2, of which waited for: 2 -> 2; matrix products, arithmetic and copies ran while one was open for 2% -> 3% of each run, Pallas kernels for 18% -> 14%
where the time goes in v4:
time: 30.9 us; the launch traced here: 30.6 us
  Pallas kernels  9.13 us (30%)
  waiting for transfers between devices  9.01 us (29%)
  local copies, waits for them, and re-layouts  6.18 us (20%)
  starting transfers between devices  6.05 us (20%)
    all_to_all x1, waiting for transfers between devices, shards(): lax.all_to_all(fourier.reshape(pairs * levs, 4, slices * band_rows), ('la...  6.51 us
    unnamed x14, local copies, waits for them, and re-layouts  5.45 us
    pallas_call x1, Pallas kernels, shards(): pl.pallas_call(functools.partial(inner_kernel, slices=slices), out_shape=...  4.37 us
    all_to_all x1, starting transfers between devices, shards(): lax.all_to_all(fourier.reshape(pairs * levs, 4, slices * band_rows), ('la...  3.03 us
    ppermute x1, starting transfers between devices, shards(): lax.ppermute(sent_rim, 'lat', [(i, (i + 1) % bands) for i in range(bands)])  3.02 us
    pallas_call x1, Pallas kernels, shards(): pl.pallas_call(functools.partial(rim_kernel, slices=slices), out_shape=ja...  2.78 us
    ppermute x1, waiting for transfers between devices, shards(): lax.ppermute(sent_rim, 'lat', [(i, (i + 1) % bands) for i in range(bands)])  2.49 us
    pallas_call x1, Pallas kernels, shards(): pl.pallas_call(pack_kernel, out_shape=(rim_shape, rim_shape, jax.ShapeDty...  1.09 us
  transfers between devices with their start and end apart: 2, of which 2 were waited for; matrix products, arithmetic and copies ran while one was open for 3% of the time, Pallas kernels for 14%

profile of v4, /device:TPU:0, one launch (start us, length us, event | category | flops | bytes accessed | tf_op | source)
XLA Modules:
  0.0 30.6 jit_solution(984288525052702110)
XLA Ops:
  0.0 0.0 copy-start.5
  0.0 0.7 %copy-done.5 = s32[8]{0:T(128)S(1)} copy-done((s32[8]{0:T(128)S(1)}, s32[8]{0:T(128)}, u32[]{:S(2)}) %copy-start.5) | copy-done | bytes 56
  0.7 0.0 copy-start
  0.7 1.0 %copy-done = bf16[4,20,3200]{2,0,1:T(4,128)(2,1)S(1)} copy-done((bf16[4,20,3200]{2,0,1:T(4,128)(2,1)S(1)}, bf16[4,20,3200]{2,0,1:T(4,128)(2,1)}, u32[]{:S(2)}) %copy-start) | copy-done | bytes 512024
  1.7 0.0 copy-start.1
  1.7 1.0 %copy-done.1 = s32[20,3200]{1,0:T(8,128)S(1)} copy-done((s32[20,3200]{1,0:T(8,128)S(1)}, s32[20,3200]{1,0:T(8,128)}, u32[]{:S(2)}) %copy-start.1) | copy-done | bytes 256024
  2.7 0.0 copy-start.2
  2.7 1.0 %copy-done.2 = s32[20,3200]{1,0:T(8,128)S(1)} copy-done((s32[20,3200]{1,0:T(8,128)S(1)}, s32[20,3200]{1,0:T(8,128)}, u32[]{:S(2)}) %copy-start.2) | copy-done | bytes 256024
  3.6 0.0 copy-start.3
  3.6 0.9 %copy-done.3 = bf16[20,3200]{1,0:T(8,128)(2,1)S(1)} copy-done((bf16[20,3200]{1,0:T(8,128)(2,1)S(1)}, bf16[20,3200]{1,0:T(8,128)(2,1)}, u32[]{:S(2)}) %copy-start.3) | copy-done | bytes 128024
  4.5 0.0 copy-start.4
  4.5 0.9 %copy-done.4 = bf16[20,3200]{1,0:T(8,128)(2,1)S(1)} copy-done((bf16[20,3200]{1,0:T(8,128)(2,1)S(1)}, bf16[20,3200]{1,0:T(8,128)(2,1)}, u32[]{:S(2)}) %copy-start.4) | copy-done | bytes 128024
  5.5 0.0 copy-start.6
  5.5 1.1 %shard_map.73 = (bf16[24,3200]{1,0:T(8,128)(2,1)S(1)}, bf16[24,3200]{1,0:T(8,128)(2,1)S(1)}, bf16[80,3200]{1,0:T(8,128)(2,1)S(1)}, bf16[48,3200]{1,0:T(8,128)(2,...) custom-call(s32[1]{0:T(128)} %bitcast.band_start, s32[1]{0:T(128)} %bitcast.1.col_start, s32[8]{0:T(128)S(1)} %copy-done.5, ...), custom_call_target="tpu_custom_call" | custom-call | tf_op jit(solution)/shard_map/pallas_call | solution.py:323
  6.6 3.0 %collective-permute-start = (bf16[24,3200]{1,0:T(8,128)(2,1)S(1)}, bf16[24,3200]{1,0:T(8,128)(2,1)S(1)}, u32[]{:S(2)}, u32[]{:S(2)}) collective-permute-start(bf16[24,3200]{1,0:T(8,128)(2,1)S(1)} %get-tuple-element.14), channel_id=1, source_target_pairs={{0,4},{4,8},{8,12},{12,16},{16,20},{20,24},{24,28},{28,0},{1,5},{5... | collective-permute-start | bytes 460808 | tf_op jit(solution)/shard_map/ppermute | solution.py:343
  9.6 0.0 copy-done.6
  9.6 4.4 %shard_map.74 = (f32[32,64]{1,0:T(8,128)S(1)}, bf16[32,3712]{1,0:T(8,128)(2,1)S(1)}) custom-call(bf16[80,3200]{1,0:T(8,128)(2,1)S(1)} %get-tuple-element.16.grid, bf16[48,3200]{1,0:T(8,128)(2,1)S(1)} %get-tuple-element.17.plans, f32[32,128]{1,0:T(8,128)S(1)} %get-tuple-element.18.waves), custom_call_target="tpu_custom_call" | custom-call | flops 100000000 | bytes 2000000 | tf_op jit(solution)/shard_map/pallas_call | solution.py:345
  14.0 0.1 slice_maximum_fusion
  14.1 2.5 %collective-permute-done.arrived = bf16[24,3200]{1,0:T(8,128)(2,1)S(1)} collective-permute-done((bf16[24,3200]{1,0:T(8,128)(2,1)S(1)}, bf16[24,3200]{1,0:T(8,128)(2,1)S(1)}, u32[]{:S(2)}, u32[]{:S(2)}) %collective-permute-start) | collective-permute-done | bytes 153632 | tf_op jit(solution)/shard_map/ppermute | solution.py:343
  16.6 2.8 %shard_map.75 = bf16[8,4,4,80]{3,2,1,0:T(4,128)(2,1)} custom-call(bf16[24,3200]{1,0:T(8,128)(2,1)S(1)} %collective-permute-done.arrived, bf16[24,3200]{1,0:T(8,128)(2,1)S(1)} %get-tuple-element.15.own, bf16[32,3712]{1,0:T(8,128)(2,1)S(1)} %get-tuple-element.19.basis, f32[32,64]{1,0:T(8,128)S(1)} %get-tuple-element.20.inner_fourier), custom_call_target="tpu_custom_call" | custom-call | tf_op jit(solution)/shard_map/pallas_call | solution.py:361
  19.4 3.0 %all-to-all-start = ((bf16[32,4,80]{2,1,0:T(4,128)(2,1)}), bf16[32,4,80]{2,1,0:T(4,128)(2,1)S(1)}, u32[]{:S(2)}, u32[]{:S(2)}) async-start(bf16[32,4,80]{2,1,0:T(4,128)(2,1)} %bitcast.3), calls=%async_computation | async-start | bytes 65536 | tf_op jit(solution)/shard_map/all_to_all | solution.py:383
  22.5 0.6 %concatenate.9 = bf16[8,128,320]{2,1,0:T(8,128)(2,1)S(1)} concatenate(bf16[8,16,320]{2,1,0:T(8,128)(2,1)S(1)} %slice.41, bf16[8,16,320]{2,1,0:T(8,128)(2,1)S(1)} %slice.41, bf16[8,16,320]{2,1,0:T(8,128)(2,1)S(1)} %slice.41, bf16[8,16,320]{2,1,0:T(8,128)(2,1)S(1)} %slice.41, bf16[8,1,320]{2,1,0:T(2,128)(2,1)S(1)} %get-tuple-element.24, bf16[8,1,320]{2,1,0:T(2,128)(2,1)S(1)} %get-tuple-element.24, ...), dimensions={1} | concatenate | bytes 1310720 | tf_op jit(solution)/shard_map/concatenate | solution.py:381
  23.2 6.5 %all-to-all-done.coeffs = bf16[32,4,80]{2,1,0:T(4,128)(2,1)S(1)} async-done(((bf16[32,4,80]{2,1,0:T(4,128)(2,1)}), bf16[32,4,80]{2,1,0:T(4,128)(2,1)S(1)}, u32[]{:S(2)}, u32[]{:S(2)}) %all-to-all-start) | async-done | bytes 20512 | tf_op jit(solution)/shard_map/all_to_all | solution.py:383
  29.7 0.9 %shard_map.76 = f32[16,2,320]{2,1,0:T(2,128)} custom-call(s32[8,128]{1,0:T(8,128)S(1)} %get-tuple-element.13.limit, bf16[32,4,80]{2,1,0:T(4,128)(2,1)S(1)} %all-to-all-done.coeffs, bf16[1024,320]{1,0:T(8,128)(2,1)S(1)} %bitcast.6), custom_call_target="tpu_custom_call" | custom-call | tf_op jit(solution)/shard_map/pallas_call | solution.py:390
  (7 shorter events, 0.2 us)
Async XLA Ops:
  0.0 0.7 %copy-start.5 = (s32[8]{0:T(128)S(1)}, s32[8]{0:T(128)}, u32[]{:S(2)}) copy-start(s32[8]{0:T(128)} %pair_ids.1) | copy-start | bytes 100
  0.7 1.0 %copy-start = (bf16[4,20,3200]{2,0,1:T(4,128)(2,1)S(1)}, bf16[4,20,3200]{2,0,1:T(4,128)(2,1)}, u32[]{:S(2)}) copy-start(bf16[4,20,3200]{2,0,1:T(4,128)(2,1)} %param.7) | copy-start | bytes 1536004
  1.7 1.0 %copy-start.1 = (s32[20,3200]{1,0:T(8,128)S(1)}, s32[20,3200]{1,0:T(8,128)}, u32[]{:S(2)}) copy-start(s32[20,3200]{1,0:T(8,128)} %dep_row.1) | copy-start | bytes 768004
  2.7 1.0 %copy-start.2 = (s32[20,3200]{1,0:T(8,128)S(1)}, s32[20,3200]{1,0:T(8,128)}, u32[]{:S(2)}) copy-start(s32[20,3200]{1,0:T(8,128)} %dep_col.1) | copy-start | bytes 768004
  3.6 0.9 %copy-start.3 = (bf16[20,3200]{1,0:T(8,128)(2,1)S(1)}, bf16[20,3200]{1,0:T(8,128)(2,1)}, u32[]{:S(2)}) copy-start(bf16[20,3200]{1,0:T(8,128)(2,1)} %lat_frac.1) | copy-start | bytes 384004
  4.5 0.9 %copy-start.4 = (bf16[20,3200]{1,0:T(8,128)(2,1)S(1)}, bf16[20,3200]{1,0:T(8,128)(2,1)}, u32[]{:S(2)}) copy-start(bf16[20,3200]{1,0:T(8,128)(2,1)} %lon_frac.1) | copy-start | bytes 384004
  5.5 4.1 %copy-start.6 = (bf16[1,160,320]{2,1,0:T(8,128)(2,1)S(1)}, bf16[1,160,320]{2,1,0:T(8,128)(2,1)}, u32[]{:S(2)}) copy-start(bf16[1,160,320]{2,1,0:T(8,128)(2,1)} %param.13) | copy-start | bytes 307204
  6.6 10.0 %collective-permute-start = (bf16[24,3200]{1,0:T(8,128)(2,1)S(1)}, bf16[24,3200]{1,0:T(8,128)(2,1)S(1)}, u32[]{:S(2)}, u32[]{:S(2)}) collective-permute-start(bf16[24,3200]{1,0:T(8,128)(2,1)S(1)} %get-tuple-element.14), channel_id=1, source_target_pairs={{0,4},{4,8},{8,12},{12,16},{16,20},{20,24},{24,28},{28,0},{1,5},{5... | collective-permute-start | bytes 460808 | tf_op jit(solution)/shard_map/ppermute | solution.py:343
  19.4 10.3 %all-to-all-start = ((bf16[32,4,80]{2,1,0:T(4,128)(2,1)}), bf16[32,4,80]{2,1,0:T(4,128)(2,1)S(1)}, u32[]{:S(2)}, u32[]{:S(2)}) async-start(bf16[32,4,80]{2,1,0:T(4,128)(2,1)} %bitcast.3), calls=%async_computation | async-start | bytes 65536 | tf_op jit(solution)/shard_map/all_to_all | solution.py:383

commit v5 on v4

--- a/solution.py
+++ b/solution.py
@@ -15,7 +15,8 @@
 REACH = 8
 SPAN = LANES - 2 * REACH - 1
 ROW_BITS = 5
-AT_ONCE = 4
+INNER_AT_ONCE = 2
+RIM_AT_ONCE = 4
 
 
 def lane_gather(values, indices):
@@ -91,21 +92,38 @@
     return departed.astype(jnp.bfloat16)
 
 
-def in_steps(count, at_once, window):
-    def several(step, carry):
-        for slot in range(at_once):
-            window(step * at_once + slot, slot)
+def in_groups(count, at_once, group):
+    def step(at, carry):
+        group([at * at_once + slot for slot in range(at_once)])
         return carry
 
-    lax.fori_loop(0, count // at_once, several, 0)
-    for slot in range(count % at_once):
-        window(count - count % at_once + slot, slot)
+    lax.fori_loop(0, count // at_once, step, 0)
+    if count % at_once:
+        group(list(range(count - count % at_once, count)))
 
 
 def pack_kernel(
-    band_start, col_start, pair_ids, grid, dep_row, dep_col, lat_frac, lon_frac,
-    own_out, sent_out, grid_out, plan_out, waves_out, limit_out, held, rows,
+    band_start, col_start, pair_ids_at, grid_at, dep_row_at, dep_col_at, lat_frac_at, lon_frac_at,
+    own_out, sent_out, grid_out, plan_out, waves_out, limit_out,
+    pair_ids, grid, dep_row, dep_col, lat_frac, lon_frac, held, rows, arrivals,
 ):
+    copies = [
+        pltpu.make_async_copy(source, target, arrivals.at[at])
+        for at, (source, target) in enumerate(
+            (
+                (grid_at, grid),
+                (dep_row_at, dep_row),
+                (dep_col_at, dep_col),
+                (lat_frac_at, lat_frac),
+                (lon_frac_at, lon_frac),
+                (pair_ids_at, pair_ids),
+            )
+        )
+    ]
+    for copy in copies:
+        copy.start()
+    for copy in copies:
+        copy.wait()
     band_rows, slices, lon_count = grid.shape
     inner = band_rows - 2 * RIM
     fields = slices * EDGE
@@ -130,8 +148,8 @@
         held[slot, 2, 0:band_rows, :] = lon_frac[:, cols].astype(jnp.float32)
         grid_out[:, cols] = rows[slot].astype(jnp.bfloat16)
         for out, start, plan_start in (
-            (own_out, 0, 0),
-            (sent_out, slices * band_rows - fields, band_rows - RIM),
+            (own_out, slices * band_rows - fields, band_rows - RIM),
+            (sent_out, 0, 0),
         ):
             block = [rows[slot, start : start + fields, :]]
             block += [held[slot, at, plan_start : plan_start + RIM, :] for at in range(3)]
@@ -142,7 +160,8 @@
                 slot, at, RIM : RIM + inner, :
             ].astype(jnp.bfloat16)
 
-    in_steps(lon_count // LANES, 5, tile)
+    for t in range(lon_count // LANES):
+        tile(t, t % 5)
 
     def wave_rows(group, carry):
         row = lax.broadcasted_iota(jnp.int32, (16, LANES), 0)
@@ -164,12 +183,12 @@
     orders = basis_out.shape[0]
 
     def basis_tile(t, group):
-        rows = pl.ds(pl.multiple_of(group * 16, 16), 16)
         lane = lax.broadcasted_iota(jnp.int32, (16, LANES), 1)
         row = lax.broadcasted_iota(jnp.int32, (16, LANES), 0)
         longitude = lane + t * SPAN
         quarter = jnp.where((row & 1) == 0, 0.0, float(lon_count // 4))
-        steps = longitude.astype(jnp.float32) * waves[rows, :] + quarter
+        wave = waves[pl.ds(pl.multiple_of(group * 16, 16), 16), :]
+        steps = longitude.astype(jnp.float32) * wave + quarter
         turns = jnp.floor(steps * (1.0 / lon_count) + 0.5)
         angle = (lon_count // 4 - jnp.abs(steps - turns * lon_count)) * (2.0 * math.pi / lon_count)
         square = angle * angle
@@ -177,37 +196,64 @@
         for term in (1.0 / 362880.0, -1.0 / 5040.0, 1.0 / 120.0, -1.0 / 6.0, 1.0):
             series = series * square + term
         taken = (lane < SPAN) & (longitude < lon_count)
-        basis_out[rows, tile_at(t)] = jnp.where(taken, angle * series, 0.0).astype(jnp.bfloat16)
-
-    def window(t, slot):
-        first, second, lane_at = cut_of(t * SPAN - REACH, lon_count)
-        windows[slot] = cut(grid[:, first], grid[:, second], lane_at).astype(jnp.float32)
-        first, second, lane_at = cut_of(t * SPAN, lon_count)
-        code, lat_weight, lon_weight = [
-            cut(
-                plans[at * inner : (at + 1) * inner, first],
-                plans[at * inner : (at + 1) * inner, second],
-                lane_at,
-            ).astype(jnp.float32)
-            for at in range(3)
+        return jnp.where(taken, angle * series, 0.0).astype(jnp.bfloat16)
+
+    inline = orders <= 64
+
+    def group_of(ts):
+        blocks, plan_blocks = [], []
+        for t in ts:
+            first, second, lane_at = cut_of(t * SPAN - REACH, lon_count)
+            blocks.append(cut(grid[:, first], grid[:, second], lane_at).astype(jnp.float32))
+            first, second, lane_at = cut_of(t * SPAN, lon_count)
+            plan_blocks.append(
+                [
+                    cut(
+                        plans[at * inner : (at + 1) * inner, first],
+                        plans[at * inner : (at + 1) * inner, second],
+                        lane_at,
+                    ).astype(jnp.float32)
+                    for at in range(3)
+                ]
+            )
+        for slot, block in enumerate(blocks):
+            windows[slot] = block
+        results = []
+        for slot, (code, lat_weight, lon_weight) in enumerate(plan_blocks):
+            plan = lane_plan(code)
+            weights = corner_weights(lat_weight, lon_weight)
+            for f in range(slices):
+                sources = [
+                    windows[slot, pl.ds(slices * position + f, inner, stride=slices), :].astype(
+                        jnp.bfloat16
+                    )
+                    for position in range(2 * RIM + 1)
+                ]
+                results.append((ts[slot], f, interpolate(sources, plan, weights)))
+        waves_here = [
+            (t, group, basis_tile(t, group))
+            for t in ts
+            for group in range(orders // 16 if inline else 0)
         ]
-        plan = lane_plan(code)
-        weights = corner_weights(lat_weight, lon_weight)
-        for f in range(slices):
-            sources = [
-                windows[slot, pl.ds(slices * position + f, inner, stride=slices), :].astype(
-                    jnp.bfloat16
-                )
-                for position in range(2 * RIM + 1)
-            ]
-            departed[f * inner : (f + 1) * inner, tile_at(t)] = interpolate(sources, plan, weights)
-        if orders <= 64:
-            for group in range(orders // 16):
-                basis_tile(t, group)
-        else:
-            lax.fori_loop(0, orders // 16, lambda g, c: (basis_tile(t, g), c)[1], 0)
-
-    in_steps(basis_out.shape[1] // LANES, 2, window)
+        for t, f, result in results:
+            departed[f * inner : (f + 1) * inner, tile_at(t)] = result
+        for t, group, result in waves_here:
+            basis_out[group * 16 : (group + 1) * 16, tile_at(t)] = result
+
+    count = basis_out.shape[1] // LANES
+    in_groups(count, INNER_AT_ONCE, group_of)
+    if not inline:
+
+        def basis_rows(group, carry):
+            rows = pl.ds(pl.multiple_of(group * 16, 16), 16)
+
+            def one(t, inner_carry):
+                basis_out[rows, tile_at(t)] = basis_tile(t, group)
+                return inner_carry
+
+            return lax.fori_loop(0, count, one, carry)
+
+        lax.fori_loop(0, orders // 16, basis_rows, 0)
     inner_out[...] = lax.dot_general(
         basis_out[...],
         departed[...],
@@ -216,53 +262,82 @@
     )
 
 
-def rim_kernel(arrived, own, basis, inner_fourier, fourier_out, windows, plans, departed, *, slices):
+def rim_kernel(
+    band_start, own, arrived, sent, basis, inner_fourier, fourier_out, windows, plans, departed, top,
+    *, slices,
+):
     lon_count = arrived.shape[1]
     fields = slices * EDGE
     sublane = lax.broadcasted_iota(jnp.int32, (2 * slices, LANES), 0)
 
-    def window(t, slot):
-        first, second, lane_at = cut_of(t * SPAN - REACH, lon_count)
-        for side, ref in enumerate((arrived, own)):
-            windows[slot, fields * side : fields * (side + 1), :] = cut(
-                ref[0:fields, first], ref[0:fields, second], lane_at
-            ).astype(jnp.float32)
-        first, second, lane_at = cut_of(t * SPAN, lon_count)
-        for side, ref in enumerate((arrived, own)):
-            plans[slot, 8 * side : 8 * (side + 1), :] = cut(
-                ref[fields:, first], ref[fields:, second], lane_at
-            ).astype(jnp.float32)
-
-        def spread(at):
-            pieces = []
-            for side in range(2):
-                two = [
-                    jnp.broadcast_to(plans[slot, row : row + 1, :], (2 * slices, LANES))
-                    for row in range(8 * side + RIM * at, 8 * side + RIM * (at + 1))
+    def spread(slot, at):
+        pieces = []
+        for side in range(2):
+            two = [
+                jnp.broadcast_to(plans[slot, row : row + 1, :], (2 * slices, LANES))
+                for row in range(8 * side + RIM * at, 8 * side + RIM * (at + 1))
+            ]
+            pieces.append(jnp.where(sublane < slices, two[0], two[1]))
+        return jnp.concatenate(pieces, axis=0)
+
+    def rim_sums(sides):
+        def group_of(ts):
+            blocks, plan_blocks = [], []
+            for t in ts:
+                first, second, lane_at = cut_of(t * SPAN - REACH, lon_count)
+                blocks.append(
+                    [
+                        cut(ref[0:fields, first], ref[0:fields, second], lane_at)
+                        for ref in sides
+                    ]
+                )
+                first, second, lane_at = cut_of(t * SPAN, lon_count)
+                plan_blocks.append(
+                    [cut(ref[fields:, first], ref[fields:, second], lane_at) for ref in sides]
+                )
+            for slot in range(len(ts)):
+                for side in range(2):
+                    windows[slot, fields * side : fields * (side + 1), :] = blocks[slot][
+                        side
+                    ].astype(jnp.float32)
+                    plans[slot, 8 * side : 8 * (side + 1), :] = plan_blocks[slot][side].astype(
+                        jnp.float32
+                    )
+            results = []
+            for slot in range(len(ts)):
+                plan = lane_plan(spread(slot, 0))
+                weights = corner_weights(spread(slot, 1), spread(slot, 2))
+                sources = [
+                    windows[slot, slices * position : slices * position + fields, :].astype(
+                        jnp.bfloat16
+                    )
+                    for position in range(2 * RIM + 1)
                 ]
-                pieces.append(jnp.where(sublane < slices, two[0], two[1]))
-            return jnp.concatenate(pieces, axis=0)
-
-        plan = lane_plan(spread(0))
-        weights = corner_weights(spread(1), spread(2))
-        sources = [
-            windows[slot, slices * position : slices * position + fields, :].astype(jnp.bfloat16)
-            for position in range(2 * RIM + 1)
-        ]
-        departed[:, tile_at(t)] = interpolate(sources, plan, weights)
-
-    in_steps(basis.shape[1] // LANES, AT_ONCE, window)
-    rim_fourier = lax.dot_general(
-        basis[...],
-        departed[...],
-        (((1,), (1,)), ((), ())),
-        preferred_element_type=jnp.float32,
-    )
+                results.append(interpolate(sources, plan, weights))
+            for t, result in zip(ts, results):
+                departed[:, tile_at(t)] = result
+
+        in_groups(basis.shape[1] // LANES, RIM_AT_ONCE, group_of)
+        return lax.dot_general(
+            basis[...],
+            departed[...],
+            (((1,), (1,)), ((), ())),
+            preferred_element_type=jnp.float32,
+        )
+
+    top[...] = jnp.zeros(top.shape, jnp.float32)
+
+    @pl.when(band_start[0] == 0)
+    def _():
+        top[...] = rim_sums((sent, sent))
+
+    rim_fourier = rim_sums((own, arrived))
+    top_fourier = top[:, RIM * slices :]
     levs = fourier_out.shape[1]
     for pair in range(fourier_out.shape[0]):
+        rows = slice(4 * pair, 4 * pair + 4)
         block = jnp.concatenate(
-            [inner_fourier[4 * pair : 4 * pair + 4, :], rim_fourier[4 * pair : 4 * pair + 4, :]],
-            axis=1,
+            [inner_fourier[rows, :], rim_fourier[rows, :], top_fourier[rows, :]], axis=1
         ).astype(jnp.bfloat16)
         for lev in range(levs):
             fourier_out[pair, lev] = block
@@ -272,7 +347,7 @@
     members, _, rows = coeffs.shape
     bands = members // levs
     col_count = spread_analysis.shape[1]
-    inner = rows // slices - EDGE
+    inner = rows // slices - EDGE - RIM
     column = lax.broadcasted_iota(jnp.int32, (1, LANES), 1)
     rim_at = column - inner * slices
     slice_of = jnp.where(rim_at < 0, column // inner, rim_at % slices)
@@ -330,17 +405,24 @@
             jax.ShapeDtypeStruct((4 * pairs, LANES), jnp.float32),
             jax.ShapeDtypeStruct((8, LANES), jnp.int32),
         ),
-        in_specs=[smem] * 3 + [vmem] * 5,
+        in_specs=[smem] * 2 + [pl.BlockSpec(memory_space=pltpu.HBM)] * 6,
         out_specs=(vmem,) * 6,
         scratch_shapes=[
+            pltpu.SMEM(pair_ids.shape, jnp.int32),
+            pltpu.VMEM((band_rows, slices, lon_count), jnp.bfloat16),
+            pltpu.VMEM((band_rows, lon_count), jnp.int32),
+            pltpu.VMEM((band_rows, lon_count), jnp.int32),
+            pltpu.VMEM((band_rows, lon_count), jnp.bfloat16),
+            pltpu.VMEM((band_rows, lon_count), jnp.bfloat16),
             pltpu.VMEM((5, 3, held_rows, LANES), jnp.float32),
             pltpu.VMEM((5, band_rows * slices, LANES), jnp.float32),
+            pltpu.SemaphoreType.DMA((6,)),
         ],
         compiler_params=params,
     )(
         band_start, col_start, pair_ids, grid.transpose(1, 0, 2), dep_row, dep_col, lat_frac, lon_frac
     )
-    arrived_rim = lax.ppermute(sent_rim, "lat", [(i, (i + 1) % bands) for i in range(bands)])
+    arrived_rim = lax.ppermute(sent_rim, "lat", [(i + 1, i) for i in range(bands - 1)])
 
     inner_fourier, basis = pl.pallas_call(
         functools.partial(inner_kernel, slices=slices),
@@ -351,37 +433,39 @@
         in_specs=[vmem] * 3,
         out_specs=(vmem, vmem),
         scratch_shapes=[
-            pltpu.VMEM((2, band_rows * slices, LANES), jnp.float32),
+            pltpu.VMEM((INNER_AT_ONCE, band_rows * slices, LANES), jnp.float32),
             pltpu.VMEM((slices * inner, windows * LANES), jnp.bfloat16),
         ],
         compiler_params=params,
         cost_estimate=pl.CostEstimate(flops=100_000_000, bytes_accessed=2_000_000, transcendentals=0),
     )(rows, plans, waves)
 
+    held_coeffs = slices * (band_rows + RIM)
     fourier = pl.pallas_call(
         functools.partial(rim_kernel, slices=slices),
-        out_shape=jax.ShapeDtypeStruct((pairs, levs, 4, slices * band_rows), jnp.bfloat16),
-        in_specs=[vmem] * 4,
+        out_shape=jax.ShapeDtypeStruct((pairs, levs, 4, held_coeffs), jnp.bfloat16),
+        in_specs=[smem] + [vmem] * 5,
         out_specs=vmem,
         scratch_shapes=[
-            pltpu.VMEM((AT_ONCE, 2 * fields, LANES), jnp.float32),
-            pltpu.VMEM((AT_ONCE, 16, LANES), jnp.float32),
+            pltpu.VMEM((RIM_AT_ONCE, 2 * fields, LANES), jnp.float32),
+            pltpu.VMEM((RIM_AT_ONCE, 16, LANES), jnp.float32),
             pltpu.VMEM((fields, windows * LANES), jnp.bfloat16),
+            pltpu.VMEM((4 * pairs, fields), jnp.float32),
         ],
         compiler_params=params,
-    )(arrived_rim, own_rim, basis, inner_fourier)
+    )(band_start, own_rim, arrived_rim, sent_rim, basis, inner_fourier)
 
     values = analysis[0].reshape(bands, band_rows, col_count)
-    before = jnp.roll(values[:, band_rows - RIM :], 1, axis=0)
+    after = jnp.concatenate([values[1:, :RIM], jnp.zeros_like(values[:1, :RIM])], axis=0)
     spread_rows = [values[:, RIM : RIM + inner]] * slices
-    for rim in (before, values[:, :RIM]):
+    for rim in (values[:, band_rows - RIM :], after, values[:, :RIM]):
         for row in range(RIM):
             spread_rows += [rim[:, row : row + 1]] * slices
-    spread_rows.append(jnp.zeros((bands, LANES - slices * band_rows, col_count), jnp.bfloat16))
+    spread_rows.append(jnp.zeros((bands, LANES - held_coeffs, col_count), jnp.bfloat16))
     spread_analysis = jnp.concatenate(spread_rows, axis=1).reshape(bands * LANES, col_count)
 
     coeffs = lax.all_to_all(
-        fourier.reshape(pairs * levs, 4, slices * band_rows),
+        fourier.reshape(pairs * levs, 4, held_coeffs),
         ("lat", "lev"),
         split_axis=0,
         concat_axis=0,

time: 30.9 us -> 33.4 us (1.081)
  Pallas kernels: 9.13 us -> 12 us
  starting transfers between devices: 6.05 us -> 5.19 us
  waiting for transfers between devices: 9.01 us -> 9.36 us
    pallas_call x1, Pallas kernels: 2.78 us -> 4.83 us  [shards(): pl.pallas_call(functools.partial(rim_kernel, slices=slices), out_shape=ja...]
    ppermute x1, starting transfers between devices: 3.02 us -> 1.29 us  [shards(): lax.ppermute(sent_rim, 'lat', [(i + 1, i) for i in range(bands - 1)])]
    all_to_all x1, starting transfers between devices: 3.03 us -> 3.9 us  [shards(): lax.all_to_all(fourier.reshape(pairs * levs, 4, held_coeffs), ('lat', 'le...]
    pallas_call x1, Pallas kernels: 1.09 us -> 1.93 us  [shards(): pl.pallas_call(pack_kernel, out_shape=(rim_shape, rim_shape, jax.ShapeDty...]
    ppermute x1, waiting for transfers between devices: 2.49 us -> 3.03 us  [shards(): lax.ppermute(sent_rim, 'lat', [(i + 1, i) for i in range(bands - 1)])]
  transfers between devices with their start and end apart: 2 -> 2, of which waited for: 2 -> 2; matrix products, arithmetic and copies ran while one was open for 3% -> 3% of each run, Pallas kernels for 14% -> 13%
where the time goes in v5:
time: 33.4 us; the launch traced here: 33.1 us
  Pallas kernels  12 us (36%)
  waiting for transfers between devices  9.36 us (28%)
  local copies, waits for them, and re-layouts  6.44 us (19%)
  starting transfers between devices  5.19 us (16%)
    all_to_all x1, waiting for transfers between devices, shards(): lax.all_to_all(fourier.reshape(pairs * levs, 4, held_coeffs), ('lat', 'le...  6.33 us
    unnamed x14, local copies, waits for them, and re-layouts  5.45 us
    pallas_call x1, Pallas kernels, shards(): pl.pallas_call(functools.partial(rim_kernel, slices=slices), out_shape=ja...  4.83 us
    pallas_call x1, Pallas kernels, shards(): pl.pallas_call(functools.partial(inner_kernel, slices=slices), out_shape=...  4.37 us
    all_to_all x1, starting transfers between devices, shards(): lax.all_to_all(fourier.reshape(pairs * levs, 4, held_coeffs), ('lat', 'le...  3.9 us
    ppermute x1, waiting for transfers between devices, shards(): lax.ppermute(sent_rim, 'lat', [(i + 1, i) for i in range(bands - 1)])  3.03 us
    pallas_call x1, Pallas kernels, shards(): pl.pallas_call(pack_kernel, out_shape=(rim_shape, rim_shape, jax.ShapeDty...  1.93 us
    ppermute x1, starting transfers between devices, shards(): lax.ppermute(sent_rim, 'lat', [(i + 1, i) for i in range(bands - 1)])  1.29 us
  transfers between devices with their start and end apart: 2, of which 2 were waited for; matrix products, arithmetic and copies ran while one was open for 3% of the time, Pallas kernels for 13%

profile of v5, /device:TPU:0, one launch (start us, length us, event | category | flops | bytes accessed | tf_op | source)
XLA Modules:
  0.0 33.1 jit_solution(8335169477791280544)
XLA Ops:
  0.0 0.0 copy-start.5
  0.0 0.7 %copy-done.5 = s32[8]{0:T(128)S(1)} copy-done((s32[8]{0:T(128)S(1)}, s32[8]{0:T(128)}, u32[]{:S(2)}) %copy-start.5) | copy-done | bytes 56
  0.7 0.0 copy-start
  0.7 1.0 %copy-done = bf16[4,20,3200]{2,0,1:T(4,128)(2,1)S(1)} copy-done((bf16[4,20,3200]{2,0,1:T(4,128)(2,1)S(1)}, bf16[4,20,3200]{2,0,1:T(4,128)(2,1)}, u32[]{:S(2)}) %copy-start) | copy-done | bytes 512024
  1.7 0.0 copy-start.1
  1.7 1.0 %copy-done.1 = s32[20,3200]{1,0:T(8,128)S(1)} copy-done((s32[20,3200]{1,0:T(8,128)S(1)}, s32[20,3200]{1,0:T(8,128)}, u32[]{:S(2)}) %copy-start.1) | copy-done | bytes 256024
  2.7 0.0 copy-start.2
  2.7 1.0 %copy-done.2 = s32[20,3200]{1,0:T(8,128)S(1)} copy-done((s32[20,3200]{1,0:T(8,128)S(1)}, s32[20,3200]{1,0:T(8,128)}, u32[]{:S(2)}) %copy-start.2) | copy-done | bytes 256024
  3.6 0.0 copy-start.3
  3.6 0.9 %copy-done.3 = bf16[20,3200]{1,0:T(8,128)(2,1)S(1)} copy-done((bf16[20,3200]{1,0:T(8,128)(2,1)S(1)}, bf16[20,3200]{1,0:T(8,128)(2,1)}, u32[]{:S(2)}) %copy-start.3) | copy-done | bytes 128024
  4.5 0.0 copy-start.4
  4.5 0.9 %copy-done.4 = bf16[20,3200]{1,0:T(8,128)(2,1)S(1)} copy-done((bf16[20,3200]{1,0:T(8,128)(2,1)S(1)}, bf16[20,3200]{1,0:T(8,128)(2,1)}, u32[]{:S(2)}) %copy-start.4) | copy-done | bytes 128024
  5.5 0.0 copy-start.6
  5.5 1.9 %shard_map.73 = (bf16[24,3200]{1,0:T(8,128)(2,1)S(1)}, bf16[24,3200]{1,0:T(8,128)(2,1)S(1)}, bf16[80,3200]{1,0:T(8,128)(2,1)S(1)}, bf16[48,3200]{1,0:T(8,128)(2,...) custom-call(s32[1]{0:T(128)} %bitcast.band_start, s32[1]{0:T(128)} %bitcast.1.col_start, s32[8]{0:T(128)S(1)} %copy-done.5, ...), custom_call_target="tpu_custom_call" | custom-call | tf_op jit(solution)/shard_map/pallas_call | solution.py:398
  7.4 1.3 %collective-permute-start = (bf16[24,3200]{1,0:T(8,128)(2,1)S(1)}, bf16[24,3200]{1,0:T(8,128)(2,1)S(1)}, u32[]{:S(2)}, u32[]{:S(2)}) collective-permute-start(bf16[24,3200]{1,0:T(8,128)(2,1)S(1)} %get-tuple-element.15.sent), channel_id=1, source_target_pairs={{4,0},{8,4},{12,8},{16,12},{20,16},{24,20},{28,24},{5,1},{9,5},{13... | collective-permute-start | bytes 460808 | tf_op jit(solution)/shard_map/ppermute | solution.py:425
  8.7 0.0 copy-done.6
  8.8 4.4 %shard_map.74 = (f32[32,64]{1,0:T(8,128)S(1)}, bf16[32,3712]{1,0:T(8,128)(2,1)S(1)}) custom-call(bf16[80,3200]{1,0:T(8,128)(2,1)S(1)} %get-tuple-element.16.grid, bf16[48,3200]{1,0:T(8,128)(2,1)S(1)} %get-tuple-element.17.plans, f32[32,128]{1,0:T(8,128)S(1)} %get-tuple-element.18.waves), custom_call_target="tpu_custom_call" | custom-call | flops 100000000 | bytes 2000000 | tf_op jit(solution)/shard_map/pallas_call | solution.py:427
  13.1 0.1 pad_slice_fusion
  13.2 3.0 %collective-permute-done.arrived = bf16[24,3200]{1,0:T(8,128)(2,1)S(1)} collective-permute-done((bf16[24,3200]{1,0:T(8,128)(2,1)S(1)}, bf16[24,3200]{1,0:T(8,128)(2,1)S(1)}, u32[]{:S(2)}, u32[]{:S(2)}) %collective-permute-start) | collective-permute-done | bytes 153632 | tf_op jit(solution)/shard_map/ppermute | solution.py:425
  16.2 4.8 %shard_map.75 = bf16[8,4,4,88]{3,2,1,0:T(4,128)(2,1)} custom-call(s32[1]{0:T(128)} %bitcast.band_start, bf16[24,3200]{1,0:T(8,128)(2,1)S(1)} %get-tuple-element.14.own, bf16[24,3200]{1,0:T(8,128)(2,1)S(1)} %collective-permute-done.arrived, bf16[24,3200]{1,0:T(8,128)(2,1)S(1)} %get-tuple-element.15.sent, bf16[32,3712]{1,0:T(8,128)(2,1)S(1)} %get-tuple-element.19.basis, ...), custom_call_target="tpu_custom_call" | custom-call | tf_op jit(solution)/shard_map/pallas_call | solution.py:444
  21.1 3.9 %all-to-all-start = ((bf16[32,4,88]{2,1,0:T(4,128)(2,1)}), bf16[32,4,88]{2,1,0:T(4,128)(2,1)S(1)}, u32[]{:S(2)}, u32[]{:S(2)}) async-start(bf16[32,4,88]{2,1,0:T(4,128)(2,1)} %bitcast.3), calls=%async_computation | async-start | bytes 65536 | tf_op jit(solution)/shard_map/all_to_all | solution.py:467
  25.1 0.7 %concatenate.8 = bf16[8,128,320]{2,1,0:T(8,128)(2,1)S(1)} concatenate(bf16[8,16,320]{2,1,0:T(8,128)(2,1)S(1)} %slice.51, bf16[8,16,320]{2,1,0:T(8,128)(2,1)S(1)} %slice.51, bf16[8,16,320]{2,1,0:T(8,128)(2,1)S(1)} %slice.51, bf16[8,17,320]{2,1,0:T(8,128)(2,1)S(1)} %slice.52, bf16[8,1,320]{2,1,0:T(2,128)(2,1)S(1)} %get-tuple-element.29, bf16[8,1,320]{2,1,0:T(2,128)(2,1)S(1)} %get-tuple-element.29, ...), dimensions={1} | concatenate | bytes 1310720 | tf_op jit(solution)/shard_map/concatenate | solution.py:465
  25.9 6.3 %all-to-all-done.coeffs = bf16[32,4,88]{2,1,0:T(4,128)(2,1)S(1)} async-done(((bf16[32,4,88]{2,1,0:T(4,128)(2,1)}), bf16[32,4,88]{2,1,0:T(4,128)(2,1)S(1)}, u32[]{:S(2)}, u32[]{:S(2)}) %all-to-all-start) | async-done | bytes 22560 | tf_op jit(solution)/shard_map/all_to_all | solution.py:467
  32.2 0.9 %shard_map.76 = f32[16,2,320]{2,1,0:T(2,128)} custom-call(s32[8,128]{1,0:T(8,128)S(1)} %get-tuple-element.13.limit, bf16[32,4,88]{2,1,0:T(4,128)(2,1)S(1)} %all-to-all-done.coeffs, bf16[1024,320]{1,0:T(8,128)(2,1)S(1)} %bitcast.6), custom_call_target="tpu_custom_call" | custom-call | tf_op jit(solution)/shard_map/pallas_call | solution.py:474
  (7 shorter events, 0.2 us)
Async XLA Ops:
  0.0 0.7 %copy-start.5 = (s32[8]{0:T(128)S(1)}, s32[8]{0:T(128)}, u32[]{:S(2)}) copy-start(s32[8]{0:T(128)} %pair_ids_at.1) | copy-start | bytes 100
  0.7 1.0 %copy-start = (bf16[4,20,3200]{2,0,1:T(4,128)(2,1)S(1)}, bf16[4,20,3200]{2,0,1:T(4,128)(2,1)}, u32[]{:S(2)}) copy-start(bf16[4,20,3200]{2,0,1:T(4,128)(2,1)} %param.7) | copy-start | bytes 1536004
  1.7 1.0 %copy-start.1 = (s32[20,3200]{1,0:T(8,128)S(1)}, s32[20,3200]{1,0:T(8,128)}, u32[]{:S(2)}) copy-start(s32[20,3200]{1,0:T(8,128)} %dep_row_at.1) | copy-start | bytes 768004
  2.7 1.0 %copy-start.2 = (s32[20,3200]{1,0:T(8,128)S(1)}, s32[20,3200]{1,0:T(8,128)}, u32[]{:S(2)}) copy-start(s32[20,3200]{1,0:T(8,128)} %dep_col_at.1) | copy-start | bytes 768004
  3.6 0.9 %copy-start.3 = (bf16[20,3200]{1,0:T(8,128)(2,1)S(1)}, bf16[20,3200]{1,0:T(8,128)(2,1)}, u32[]{:S(2)}) copy-start(bf16[20,3200]{1,0:T(8,128)(2,1)} %lat_frac_at.1) | copy-start | bytes 384004
  4.5 0.9 %copy-start.4 = (bf16[20,3200]{1,0:T(8,128)(2,1)S(1)}, bf16[20,3200]{1,0:T(8,128)(2,1)}, u32[]{:S(2)}) copy-start(bf16[20,3200]{1,0:T(8,128)(2,1)} %lon_frac_at.1) | copy-start | bytes 384004
  5.5 3.2 %copy-start.6 = (bf16[1,160,320]{2,1,0:T(8,128)(2,1)S(1)}, bf16[1,160,320]{2,1,0:T(8,128)(2,1)}, u32[]{:S(2)}) copy-start(bf16[1,160,320]{2,1,0:T(8,128)(2,1)} %param.13) | copy-start | bytes 307204
  7.4 8.8 %collective-permute-start = (bf16[24,3200]{1,0:T(8,128)(2,1)S(1)}, bf16[24,3200]{1,0:T(8,128)(2,1)S(1)}, u32[]{:S(2)}, u32[]{:S(2)}) collective-permute-start(bf16[24,3200]{1,0:T(8,128)(2,1)S(1)} %get-tuple-element.15.sent), channel_id=1, source_target_pairs={{4,0},{8,4},{12,8},{16,12},{20,16},{24,20},{28,24},{5,1},{9,5},{13... | collective-permute-start | bytes 460808 | tf_op jit(solution)/shard_map/ppermute | solution.py:425
  21.1 11.2 %all-to-all-start = ((bf16[32,4,88]{2,1,0:T(4,128)(2,1)}), bf16[32,4,88]{2,1,0:T(4,128)(2,1)S(1)}, u32[]{:S(2)}, u32[]{:S(2)}) async-start(bf16[32,4,88]{2,1,0:T(4,128)(2,1)} %bitcast.3), calls=%async_computation | async-start | bytes 65536 | tf_op jit(solution)/shard_map/all_to_all | solution.py:467

commit v6 on v4

v6 whole, which is shorter than its diff:
```python
import functools
import math

import jax
import jax.numpy as jnp
from jax import lax
from jax.experimental import pallas as pl
from jax.experimental.pallas import tpu as pltpu
from jax.sharding import PartitionSpec as P

NMAX = 1279
LANES = 128
RIM = 2
EDGE = 2 * RIM
REACH = 8
SPAN = LANES - 2 * REACH - 1
ROW_BITS = 5
INNER_AT_ONCE = 2
RIM_AT_ONCE = 4


def lane_gather(values, indices):
    numbers = lax.GatherDimensionNumbers(
        offset_dims=(),
        collapsed_slice_dims=(1,),
        start_index_map=(1,),
        operand_batching_dims=(0,),
        start_indices_batching_dims=(0,),
    )
    return lax.gather(
        values,
        indices[..., None],
        numbers,
        (1, 1),
        mode=lax.GatherScatterMode.PROMISE_IN_BOUNDS,
    )


def tile_at(t):
    return pl.ds(pl.multiple_of(t * LANES, LANES), LANES)


def cut_of(start, lon_count):
    tiles = lon_count // LANES
    start = jnp.asarray(start, jnp.int32) + lon_count
    first = start >> LANES.bit_length() - 1
    first = jnp.where(first >= tiles, first - tiles, first)
    second = jnp.where(first == tiles - 1, 0, first + 1)
    return tile_at(first), tile_at(second), start & LANES - 1


def cut(first, second, lane_at):
    lane = lax.broadcasted_iota(jnp.int32, first.shape, 1).astype(jnp.int16)
    joined = jnp.where(lane >= lane_at.astype(jnp.int16), first, second)
    return pltpu.roll(joined, (LANES - lane_at) & LANES - 1, 1)


def lane_plan(code):
    code = code.astype(jnp.int32)
    west = lax.broadcasted_iota(jnp.int32, code.shape, 1) + (code & (1 << ROW_BITS) - 1)
    west_lane = (west & (LANES - 1)).astype(jnp.int16)
    east_lane = ((west + 1) & (LANES - 1)).astype(jnp.int16)
    row_step = (code >> ROW_BITS).astype(jnp.float32).astype(jnp.bfloat16)
    return west_lane, east_lane, row_step


def corner_weights(lat_weight, lon_weight):
    south, north = 1.0 - lat_weight, lat_weight
    west, east = 1.0 - lon_weight, lon_weight
    return south * west, south * east, north * west, north * east


def interpolate(sources, plan, weights):
    west_lane, east_lane, row_step = plan
    masks = [row_step == float(step) for step in range(2 * RIM - 1)]

    def pick(gathered):
        low, high = gathered[2 * RIM - 1], gathered[2 * RIM]
        for position in range(2 * RIM - 2, -1, -1):
            low = jnp.where(masks[position], gathered[position], low)
            high = jnp.where(masks[position], gathered[position + 1], high)
        return low.astype(jnp.float32), high.astype(jnp.float32)

    west_low, west_high = pick([lane_gather(source, west_lane) for source in sources])
    east_low, east_high = pick([lane_gather(source, east_lane) for source in sources])
    departed = (
        weights[0] * west_low
        + weights[1] * east_low
        + weights[2] * west_high
        + weights[3] * east_high
    )
    return departed.astype(jnp.bfloat16)


def in_groups(count, at_once, group):
    def step(at, carry):
        group([at * at_once + slot for slot in range(at_once)])
        return carry

    lax.fori_loop(0, count // at_once, step, 0)
    if count % at_once:
        group(list(range(count - count % at_once, count)))


def pack_kernel(
    band_start, rows, dep_row, dep_col, lat_frac, lon_frac, own_out, sent_out, plan_out, held
):
    band_rows, lon_count = dep_row.shape
    inner = band_rows - 2 * RIM
    fields = rows.shape[0] // band_rows * EDGE
    first_row = band_start[0]

    for t in range(lon_count // LANES):
        cols, slot = tile_at(t), t % 5
        row = lax.broadcasted_iota(jnp.int32, (band_rows, LANES), 0)
        lane = lax.broadcasted_iota(jnp.int32, (band_rows, LANES), 1)
        shift = dep_col[:, cols] - (lane + t * LANES)
        shift = jnp.where(shift > lon_count // 2, shift - lon_count, shift)
        shift = jnp.where(shift < -(lon_count // 2), shift + lon_count, shift)
        row_step = dep_row[:, cols] - (first_row + row) + RIM
        held[slot, 0, 0:band_rows, :] = row_step.astype(jnp.float32)
        held[slot, 1, 0:band_rows, :] = (shift + REACH).astype(jnp.float32)
        held[slot, 2, 0:band_rows, :] = lat_frac[:, cols].astype(jnp.float32)
        held[slot, 3, 0:band_rows, :] = lon_frac[:, cols].astype(jnp.float32)
        for out, start, plan_start in (
            (own_out, 0, 0),
            (sent_out, rows.shape[0] - fields, band_rows - RIM),
        ):
            out[0:fields, cols] = rows[start : start + fields, cols]
            out[fields:, cols] = jnp.concatenate(
                [held[slot, at, plan_start : plan_start + RIM, :] for at in range(4)], axis=0
            ).astype(jnp.bfloat16)
        middle = [held[slot, at, RIM : RIM + inner, :] for at in range(4)]
        middle = [middle[0] * (1 << ROW_BITS) + middle[1], middle[2], middle[3]]
        for at in range(3):
            plan_out[at * inner : (at + 1) * inner, cols] = middle[at].astype(jnp.bfloat16)


def basis_kernel(place, pair_ids, basis_out, limit_out, waves, *, lon_count):
    orders = basis_out.shape[0]

    def wave_rows(group, carry):
        row = lax.broadcasted_iota(jnp.int32, (16, LANES), 0)
        pair = jnp.full((16, LANES), pair_ids[4 * group + 3], jnp.int32)
        for at in (2, 1, 0):
            pair = jnp.where(row < 4 * (at + 1), pair_ids[4 * group + at], pair)
        wave = jnp.where((row & 2) == 0, pair, NMAX + 1 - pair)
        waves[pl.ds(pl.multiple_of(group * 16, 16), 16), :] = wave.astype(jnp.float32)
        return carry

    lax.fori_loop(0, orders // 16, wave_rows, 0)

    def tile(t):
        def rows_of(group, carry):
            rows = pl.ds(pl.multiple_of(group * 16, 16), 16)
            lane = lax.broadcasted_iota(jnp.int32, (16, LANES), 1)
            row = lax.broadcasted_iota(jnp.int32, (16, LANES), 0)
            longitude = lane + t * SPAN
            quarter = jnp.where((row & 1) == 0, 0.0, float(lon_count // 4))
            steps = longitude.astype(jnp.float32) * waves[rows, :] + quarter
            turns = jnp.floor(steps * (1.0 / lon_count) + 0.5)
            angle = lon_count // 4 - jnp.abs(steps - turns * lon_count)
            angle = angle * (2.0 * math.pi / lon_count)
            square = angle * angle
            series = jnp.float32(-1.0 / 39916800.0)
            for term in (1.0 / 362880.0, -1.0 / 5040.0, 1.0 / 120.0, -1.0 / 6.0, 1.0):
                series = series * square + term
            taken = (lane < SPAN) & (longitude < lon_count)
            basis_out[rows, tile_at(t)] = jnp.where(taken, angle * series, 0.0).astype(
                jnp.bfloat16
            )
            return carry

        lax.fori_loop(0, orders // 16, rows_of, 0, unroll=orders <= 64)

    for t in range(basis_out.shape[1] // LANES):
        tile(t)
    limit = NMAX + 1 - pair_ids[place[0]] - place[1]
    limit_out[...] = jnp.full(limit_out.shape, limit, jnp.int32)


def inner_kernel(grid, plans, departed, windows, *, slices):
    lon_count = grid.shape[1]
    inner = plans.shape[0] // 3

    def group_of(ts):
        blocks, plan_blocks = [], []
        for t in ts:
            first, second, lane_at = cut_of(t * SPAN - REACH, lon_count)
            blocks.append(cut(grid[:, first], grid[:, second], lane_at).astype(jnp.float32))
            first, second, lane_at = cut_of(t * SPAN, lon_count)
            plan_blocks.append(
                [
                    cut(
                        plans[at * inner : (at + 1) * inner, first],
                        plans[at * inner : (at + 1) * inner, second],
                        lane_at,
                    ).astype(jnp.float32)
                    for at in range(3)
                ]
            )
        for slot, block in enumerate(blocks):
            windows[slot] = block
        results = []
        for slot, (code, lat_weight, lon_weight) in enumerate(plan_blocks):
            plan = lane_plan(code)
            weights = corner_weights(lat_weight, lon_weight)
            for f in range(slices):
                sources = [
                    windows[slot, pl.ds(slices * position + f, inner, stride=slices), :].astype(
                        jnp.bfloat16
                    )
                    for position in range(2 * RIM + 1)
                ]
                results.append((ts[slot], f, interpolate(sources, plan, weights)))
        for t, f, result in results:
            departed[f * inner : (f + 1) * inner, tile_at(t)] = result

    in_groups(departed.shape[1] // LANES, INNER_AT_ONCE, group_of)


def rim_kernel(
    arrived, own, basis, inner_departed, fourier_out, windows, departed, *, slices
):
    lon_count = arrived.shape[1]
    fields = slices * EDGE
    sides = (arrived, own)
    wanted = lax.broadcasted_iota(jnp.int32, (3 * fields, 16), 0)
    held = lax.broadcasted_iota(jnp.int32, (3 * fields, 16), 1)
    kind, rim_row = wanted // fields, wanted % fields // slices
    base = rim_row // RIM * 8 + rim_row % RIM
    spread = jnp.where((kind == 0) & (held == base), float(1 << ROW_BITS), 0.0)
    spread += jnp.where(held == base + RIM * (kind + 1), 1.0, 0.0)
    spread = spread.astype(jnp.bfloat16)

    def group_of(ts):
        blocks, plan_blocks = [], []
        for t in ts:
            first, second, lane_at = cut_of(t * SPAN - REACH, lon_count)
            blocks.append(
                [cut(ref[0:fields, first], ref[0:fields, second], lane_at) for ref in sides]
            )
            first, second, lane_at = cut_of(t * SPAN, lon_count)
            plan_block = jnp.concatenate(
                [cut(ref[fields:, first], ref[fields:, second], lane_at) for ref in sides], axis=0
            )
            plan_blocks.append(jnp.dot(spread, plan_block, preferred_element_type=jnp.float32))
        for slot in range(len(ts)):
            for side in range(2):
                windows[slot, fields * side : fields * (side + 1), :] = blocks[slot][side].astype(
                    jnp.float32
                )
        results = []
        for slot in range(len(ts)):
            code, lat_weight, lon_weight = [
                plan_blocks[slot][fields * at : fields * (at + 1)] for at in range(3)
            ]
            sources = [
                windows[slot, slices * position : slices * position + fields, :].astype(
                    jnp.bfloat16
                )
                for position in range(2 * RIM + 1)
            ]
            results.append(
                interpolate(sources, lane_plan(code), corner_weights(lat_weight, lon_weight))
            )
        for t, result in zip(ts, results):
            departed[:, tile_at(t)] = result

    in_groups(basis.shape[1] // LANES, RIM_AT_ONCE, group_of)
    fourier = jnp.concatenate(
        [
            lax.dot_general(
                basis[...],
                values[...],
                (((1,), (1,)), ((), ())),
                preferred_element_type=jnp.float32,
            )
            for values in (inner_departed, departed)
        ],
        axis=1,
    )
    levs = fourier_out.shape[1]
    for pair in range(fourier_out.shape[0]):
        block = fourier[4 * pair : 4 * pair + 4].astype(jnp.bfloat16)
        for lev in range(levs):
            fourier_out[pair, lev] = block


def legendre_kernel(limit, coeffs, spread_analysis, out, spread_coeffs, *, levs, slices):
    members, _, rows = coeffs.shape
    bands = members // levs
    col_count = spread_analysis.shape[1]
    inner = rows // slices - EDGE
    column = lax.broadcasted_iota(jnp.int32, (1, LANES), 1)
    rim_at = column - inner * slices
    slice_of = jnp.where(rim_at < 0, column // inner, rim_at % slices)
    slice_of = jnp.where(column < rows, slice_of, -1)

    def spread(band):
        block = jnp.concatenate(
            [coeffs[band * levs + lev].astype(jnp.float32) for lev in range(levs)], axis=0
        )
        block = jnp.concatenate(
            [block, jnp.zeros((block.shape[0], LANES - rows), jnp.float32)], axis=1
        )
        spread_coeffs[:, tile_at(band)] = jnp.concatenate(
            [jnp.where(slice_of == f, block, 0.0) for f in range(slices)], axis=0
        ).astype(jnp.bfloat16)

    if bands <= 16:
        for band in range(bands):
            spread(band)
    else:
        lax.fori_loop(0, bands, lambda band, carry: (spread(band), carry)[1], 0)
    total = jnp.dot(
        spread_coeffs[...], spread_analysis[...], preferred_element_type=jnp.float32
    )
    first_wave = lax.broadcasted_iota(jnp.int32, (2, col_count), 1) < limit[0:1, 0:1]
    for f in range(slices):
        for lev in range(levs):
            at = (f * levs + lev) * 4
            out[lev * slices + f] = jnp.where(first_wave, total[at : at + 2], total[at + 2 : at + 4])


def shards(grid, dep_row, dep_col, lat_frac, lon_frac, pair_ids, analysis):
    slices, band_rows, lon_count = grid.shape
    pairs = pair_ids.shape[0]
    col_count = analysis.shape[2]
    bands, levs = lax.axis_size("lat"), lax.axis_size("lev")
    inner = band_rows - 2 * RIM
    windows = -(-lon_count // SPAN)
    held_rows = -(-band_rows // 8) * 8
    fields = slices * EDGE
    band_start = jnp.reshape(lax.axis_index("lat") * band_rows, (1,)).astype(jnp.int32)
    place = jnp.stack([lax.axis_index("lat"), lax.axis_index("lev") * col_count])
    vmem = pl.BlockSpec(memory_space=pltpu.VMEM)
    smem = pl.BlockSpec(memory_space=pltpu.SMEM)
    params = pltpu.CompilerParams(vmem_limit_bytes=48 * 2**20)

    rows = grid.transpose(1, 0, 2).reshape(band_rows * slices, lon_count)
    rim_shape = jax.ShapeDtypeStruct((fields + 4 * RIM, lon_count), jnp.bfloat16)
    own_rim, sent_rim, plans = pl.pallas_call(
        pack_kernel,
        out_shape=(
            rim_shape,
            rim_shape,
            jax.ShapeDtypeStruct((3 * inner, lon_count), jnp.bfloat16),
        ),
        in_specs=[smem] + [vmem] * 5,
        out_specs=(vmem,) * 3,
        scratch_shapes=[pltpu.VMEM((5, 4, held_rows, LANES), jnp.float32)],
        compiler_params=params,
    )(band_start, rows, dep_row, dep_col, lat_frac, lon_frac)
    arrived_rim = lax.ppermute(sent_rim, "lat", [(i, (i + 1) % bands) for i in range(bands)])

    inner_departed = pl.pallas_call(
        functools.partial(inner_kernel, slices=slices),
        out_shape=jax.ShapeDtypeStruct((slices * inner, windows * LANES), jnp.bfloat16),
        in_specs=[vmem] * 2,
        out_specs=vmem,
        scratch_shapes=[pltpu.VMEM((INNER_AT_ONCE, band_rows * slices, LANES), jnp.float32)],
        compiler_params=params,
        cost_estimate=pl.CostEstimate(flops=100_000_000, bytes_accessed=2_000_000, transcendentals=0),
    )(rows, plans)

    basis, limit = pl.pallas_call(
        functools.partial(basis_kernel, lon_count=lon_count),
        out_shape=(
            jax.ShapeDtypeStruct((4 * pairs, windows * LANES), jnp.bfloat16),
            jax.ShapeDtypeStruct((8, LANES), jnp.int32),
        ),
        in_specs=[smem] * 2,
        out_specs=(vmem,) * 2,
        scratch_shapes=[pltpu.VMEM((4 * pairs, LANES), jnp.float32)],
        compiler_params=params,
    )(place, pair_ids)

    held_coeffs = slices * band_rows
    fourier = pl.pallas_call(
        functools.partial(rim_kernel, slices=slices),
        out_shape=jax.ShapeDtypeStruct((pairs, levs, 4, held_coeffs), jnp.bfloat16),
        in_specs=[vmem] * 4,
        out_specs=vmem,
        scratch_shapes=[
            pltpu.VMEM((RIM_AT_ONCE, 2 * fields, LANES), jnp.float32),
            pltpu.VMEM((fields, windows * LANES), jnp.bfloat16),
        ],
        compiler_params=params,
    )(arrived_rim, own_rim, basis, inner_departed)

    values = analysis[0].reshape(bands, band_rows, col_count)
    before = jnp.roll(values[:, band_rows - RIM :], 1, axis=0)
    spread_rows = [values[:, RIM : RIM + inner]] * slices
    for rim in (before, values[:, :RIM]):
        for row in range(RIM):
            spread_rows += [rim[:, row : row + 1]] * slices
    spread_rows.append(jnp.zeros((bands, LANES - held_coeffs, col_count), jnp.bfloat16))
    spread_analysis = jnp.concatenate(spread_rows, axis=1).reshape(bands * LANES, col_count)

    coeffs = lax.all_to_all(
        fourier.reshape(pairs * levs, 4, held_coeffs),
        ("lat", "lev"),
        split_axis=0,
        concat_axis=0,
        tiled=True,
    )
    out = pl.pallas_call(
        functools.partial(legendre_kernel, levs=levs, slices=slices),
        out_shape=jax.ShapeDtypeStruct((levs * slices, 2, col_count), jnp.float32),
        in_specs=[vmem] * 3,
        out_specs=vmem,
        scratch_shapes=[pltpu.VMEM((4 * levs * slices, bands * LANES), jnp.bfloat16)],
        compiler_params=params,
    )(limit, coeffs, spread_analysis)
    return out[None]


def solution(mesh):
    return jax.shard_map(
        shards,
        mesh=mesh,
        in_specs=(
            P("lev", "lat", None),
            P("lat", None),
            P("lat", None),
            P("lat", None),
            P("lat", None),
            P(),
            P("lat", None, "lev"),
        ),
        out_specs=P("lat", None, None, "lev"),
        check_vma=False,
    )
```

time: 30.9 us -> 27.4 us (0.89)
  local copies, waits for them, and re-layouts: 6.18 us -> 2.58 us
  waiting for transfers between devices: 9.01 us -> 7.57 us
  starting transfers between devices: 6.05 us -> 6.88 us
  Pallas kernels: 9.13 us -> 9.9 us
    unnamed x14 -> x12, local copies, waits for them, and re-layouts: 5.45 us -> 0.61 us
    ppermute x1, waiting for transfers between devices: 2.49 us -> 1.06 us  [shards(): lax.ppermute(sent_rim, 'lat', [(i, (i + 1) % bands) for i in range(bands)])]
    reshape x0 -> x1, local copies, waits for them, and re-layouts: none -> 1.23 us  [shards(): rows = grid.transpose(1, 0, 2).reshape(band_rows * slices, lon_count)]
    pallas_call x0 -> x1, Pallas kernels: none -> 0.96 us  [shards(): pl.pallas_call(functools.partial(basis_kernel, lon_count=lon_count), out_...]
    all_to_all x1, starting transfers between devices: 3.03 us -> 3.85 us  [shards(): lax.all_to_all(fourier.reshape(pairs * levs, 4, held_coeffs), ('lat', 'le...]
    pallas_call x1, Pallas kernels: 2.78 us -> 3.55 us  [shards(): pl.pallas_call(functools.partial(rim_kernel, slices=slices), out_shape=ja...]
    pallas_call x1, Pallas kernels: 1.09 us -> 0.32 us  [shards(): pl.pallas_call(pack_kernel, out_shape=(rim_shape, rim_shape, jax.ShapeDty...]
  transfers between devices with their start and end apart: 2 -> 2, of which waited for: 2 -> 2; matrix products, arithmetic and copies ran while one was open for 3% -> 3% of each run, Pallas kernels for 14% -> 19%
where the time goes in v6:
time: 27.4 us; the launch traced here: 27.2 us
  Pallas kernels  9.9 us (36%)
  waiting for transfers between devices  7.57 us (28%)
  starting transfers between devices  6.88 us (25%)
  local copies, waits for them, and re-layouts  2.58 us (9%)
    all_to_all x1, waiting for transfers between devices, shards(): lax.all_to_all(fourier.reshape(pairs * levs, 4, held_coeffs), ('lat', 'le...  6.51 us
    pallas_call x1, Pallas kernels, shards(): pl.pallas_call(functools.partial(inner_kernel, slices=slices), out_shape=...  4.18 us
    all_to_all x1, starting transfers between devices, shards(): lax.all_to_all(fourier.reshape(pairs * levs, 4, held_coeffs), ('lat', 'le...  3.85 us
    pallas_call x1, Pallas kernels, shards(): pl.pallas_call(functools.partial(rim_kernel, slices=slices), out_shape=ja...  3.55 us
    ppermute x1, starting transfers between devices, shards(): lax.ppermute(sent_rim, 'lat', [(i, (i + 1) % bands) for i in range(bands)])  3.03 us
    reshape x1, local copies, waits for them, and re-layouts, shards(): rows = grid.transpose(1, 0, 2).reshape(band_rows * slices, lon_count)  1.23 us
    ppermute x1, waiting for transfers between devices, shards(): lax.ppermute(sent_rim, 'lat', [(i, (i + 1) % bands) for i in range(bands)])  1.06 us
    pallas_call x1, Pallas kernels, shards(): pl.pallas_call(functools.partial(basis_kernel, lon_count=lon_count), out_...  0.96 us
  transfers between devices with their start and end apart: 2, of which 2 were waited for; matrix products, arithmetic and copies ran while one was open for 3% of the time, Pallas kernels for 19%

profile of v6, /device:TPU:0, one launch (start us, length us, event | category | flops | bytes accessed | tf_op | source)
XLA Modules:
  0.0 27.2 jit_solution(8072922616030184488)
XLA Ops:
  0.0 0.0 copy-start
  0.0 0.0 copy-start.1
  0.0 0.0 copy-start.2
  0.0 0.0 copy-start.3
  0.0 1.2 %reshape.13.rows.grid = bf16[80,3200]{1,0:T(8,128)(2,1)S(1)} reshape(bf16[20,4,3200]{2,1,0:T(4,128)(2,1)} %bitcast.8) | data formatting | bytes 1024000 | tf_op jit(solution)/shard_map/reshape | solution.py:341
  1.2 0.0 copy-done
  1.3 0.0 copy-done.1
  1.3 0.0 copy-done.2
  1.3 0.0 copy-done.3
  1.3 0.0 copy-start.5
  1.3 0.3 %shard_map.74 = (bf16[24,3200]{1,0:T(8,128)(2,1)S(1)}, bf16[24,3200]{1,0:T(8,128)(2,1)S(1)}, bf16[48,3200]{1,0:T(8,128)(2,1)S(1)}) custom-call(s32[1]{0:T(128)} %bitcast.2.band_start, bf16[80,3200]{1,0:T(8,128)(2,1)S(1)} %reshape.13.rows.grid, s32[20,3200]{1,0:T(8,128)S(1)} %copy-done, s32[20,3200]{1,0:T(8,128)S(1)} %copy-done.1, ...), custom_call_target="tpu_custom_call" | custom-call | tf_op jit(solution)/shard_map/pallas_call | solution.py:343
  1.6 3.0 %collective-permute-start = (bf16[24,3200]{1,0:T(8,128)(2,1)S(1)}, bf16[24,3200]{1,0:T(8,128)(2,1)S(1)}, u32[]{:S(2)}, u32[]{:S(2)}) collective-permute-start(bf16[24,3200]{1,0:T(8,128)(2,1)S(1)} %get-tuple-element.11), channel_id=1, source_target_pairs={{0,4},{4,8},{8,12},{12,16},{16,20},{20,24},{24,28},{28,0},{1,5},{5... | collective-permute-start | bytes 460808 | tf_op jit(solution)/shard_map/ppermute | solution.py:355
  4.7 0.0 copy-done.5
  4.7 4.2 %shard_map.75.inner_departed = bf16[64,3712]{1,0:T(8,128)(2,1)S(1)} custom-call(bf16[80,3200]{1,0:T(8,128)(2,1)S(1)} %reshape.13.rows.grid, bf16[48,3200]{1,0:T(8,128)(2,1)S(1)} %get-tuple-element.14.plans), custom_call_target="tpu_custom_call" | custom-call | flops 100000000 | bytes 2000000 | tf_op jit(solution)/shard_map/pallas_call | solution.py:357
  8.9 0.0 copy-start.4
  8.9 0.1 pad_add_fusion.place
  9.0 0.6 %copy-done.4 = s32[8]{0:T(128)S(1)} copy-done((s32[8]{0:T(128)S(1)}, s32[8]{0:T(128)}, u32[]{:S(2)}) %copy-start.4) | copy-done | bytes 56
  9.6 1.0 %shard_map.73 = (bf16[32,3712]{1,0:T(8,128)(2,1)S(1)}, s32[8,128]{1,0:T(8,128)S(1)}) custom-call(s32[2]{0:T(128)S(1)} %pad_add_fusion.place, s32[8]{0:T(128)S(1)} %copy-done.4), custom_call_target="tpu_custom_call" | custom-call | tf_op jit(solution)/shard_map/pallas_call | solution.py:367
  10.5 0.1 slice_maximum_fusion
  10.6 1.1 %collective-permute-done.arrived = bf16[24,3200]{1,0:T(8,128)(2,1)S(1)} collective-permute-done((bf16[24,3200]{1,0:T(8,128)(2,1)S(1)}, bf16[24,3200]{1,0:T(8,128)(2,1)S(1)}, u32[]{:S(2)}, u32[]{:S(2)}) %collective-permute-start) | collective-permute-done | bytes 153632 | tf_op jit(solution)/shard_map/ppermute | solution.py:355
  11.7 3.5 %shard_map.76 = bf16[8,4,4,80]{3,2,1,0:T(4,128)(2,1)} custom-call(bf16[24,3200]{1,0:T(8,128)(2,1)S(1)} %collective-permute-done.arrived, bf16[24,3200]{1,0:T(8,128)(2,1)S(1)} %get-tuple-element.12.own, bf16[32,3712]{1,0:T(8,128)(2,1)S(1)} %get-tuple-element.13.basis, bf16[64,3712]{1,0:T(8,128)(2,1)S(1)} %shard_map.75.inner_departed), custom_call_target="tpu_custom_call" | custom-call | tf_op jit(solution)/shard_map/pallas_call | solution.py:380
  15.2 3.9 %all-to-all-start = ((bf16[32,4,80]{2,1,0:T(4,128)(2,1)}), bf16[32,4,80]{2,1,0:T(4,128)(2,1)S(1)}, u32[]{:S(2)}, u32[]{:S(2)}) async-start(bf16[32,4,80]{2,1,0:T(4,128)(2,1)} %bitcast.4), calls=%async_computation | async-start | bytes 65536 | tf_op jit(solution)/shard_map/all_to_all | solution.py:401
  19.2 0.6 %concatenate.9 = bf16[8,128,320]{2,1,0:T(8,128)(2,1)S(1)} concatenate(bf16[8,16,320]{2,1,0:T(8,128)(2,1)S(1)} %slice.41, bf16[8,16,320]{2,1,0:T(8,128)(2,1)S(1)} %slice.41, bf16[8,16,320]{2,1,0:T(8,128)(2,1)S(1)} %slice.41, bf16[8,16,320]{2,1,0:T(8,128)(2,1)S(1)} %slice.41, bf16[8,1,320]{2,1,0:T(2,128)(2,1)S(1)} %get-tuple-element.18, bf16[8,1,320]{2,1,0:T(2,128)(2,1)S(1)} %get-tuple-element.18, ...), dimensions={1} | concatenate | bytes 1310720 | tf_op jit(solution)/shard_map/concatenate | solution.py:399
  19.8 6.5 %all-to-all-done.coeffs = bf16[32,4,80]{2,1,0:T(4,128)(2,1)S(1)} async-done(((bf16[32,4,80]{2,1,0:T(4,128)(2,1)}), bf16[32,4,80]{2,1,0:T(4,128)(2,1)S(1)}, u32[]{:S(2)}, u32[]{:S(2)}) %all-to-all-start) | async-done | bytes 20512 | tf_op jit(solution)/shard_map/all_to_all | solution.py:401
  26.3 0.9 %shard_map.77 = f32[16,2,320]{2,1,0:T(2,128)} custom-call(s32[8,128]{1,0:T(8,128)S(1)} %get-tuple-element.10.limit, bf16[32,4,80]{2,1,0:T(4,128)(2,1)S(1)} %all-to-all-done.coeffs, bf16[1024,320]{1,0:T(8,128)(2,1)S(1)} %bitcast.7), custom_call_target="tpu_custom_call" | custom-call | tf_op jit(solution)/shard_map/pallas_call | solution.py:408
  (7 shorter events, 0.2 us)
Async XLA Ops:
  0.0 1.3 %copy-start = (s32[20,3200]{1,0:T(8,128)S(1)}, s32[20,3200]{1,0:T(8,128)}, u32[]{:S(2)}) copy-start(s32[20,3200]{1,0:T(8,128)} %dep_row.1) | copy-start | bytes 768004
  0.0 1.3 %copy-start.1 = (s32[20,3200]{1,0:T(8,128)S(1)}, s32[20,3200]{1,0:T(8,128)}, u32[]{:S(2)}) copy-start(s32[20,3200]{1,0:T(8,128)} %dep_col.1) | copy-start | bytes 768004
  0.0 1.3 %copy-start.2 = (bf16[20,3200]{1,0:T(8,128)(2,1)S(1)}, bf16[20,3200]{1,0:T(8,128)(2,1)}, u32[]{:S(2)}) copy-start(bf16[20,3200]{1,0:T(8,128)(2,1)} %lat_frac.1) | copy-start | bytes 384004
  0.0 1.3 %copy-start.3 = (bf16[20,3200]{1,0:T(8,128)(2,1)S(1)}, bf16[20,3200]{1,0:T(8,128)(2,1)}, u32[]{:S(2)}) copy-start(bf16[20,3200]{1,0:T(8,128)(2,1)} %lon_frac.1) | copy-start | bytes 384004
  1.3 3.4 %copy-start.5 = (bf16[1,160,320]{2,1,0:T(8,128)(2,1)S(1)}, bf16[1,160,320]{2,1,0:T(8,128)(2,1)}, u32[]{:S(2)}) copy-start(bf16[1,160,320]{2,1,0:T(8,128)(2,1)} %param.13) | copy-start | bytes 307204
  1.6 10.0 %collective-permute-start = (bf16[24,3200]{1,0:T(8,128)(2,1)S(1)}, bf16[24,3200]{1,0:T(8,128)(2,1)S(1)}, u32[]{:S(2)}, u32[]{:S(2)}) collective-permute-start(bf16[24,3200]{1,0:T(8,128)(2,1)S(1)} %get-tuple-element.11), channel_id=1, source_target_pairs={{0,4},{4,8},{8,12},{12,16},{16,20},{20,24},{24,28},{28,0},{1,5},{5... | collective-permute-start | bytes 460808 | tf_op jit(solution)/shard_map/ppermute | solution.py:355
  8.9 0.7 %copy-start.4 = (s32[8]{0:T(128)S(1)}, s32[8]{0:T(128)}, u32[]{:S(2)}) copy-start(s32[8]{0:T(128)} %pair_ids.1) | copy-start | bytes 100
  15.2 11.1 %all-to-all-start = ((bf16[32,4,80]{2,1,0:T(4,128)(2,1)}), bf16[32,4,80]{2,1,0:T(4,128)(2,1)S(1)}, u32[]{:S(2)}, u32[]{:S(2)}) async-start(bf16[32,4,80]{2,1,0:T(4,128)(2,1)} %bitcast.4), calls=%async_computation | async-start | bytes 65536 | tf_op jit(solution)/shard_map/all_to_all | solution.py:401

commit v7 on v6

--- a/solution.py
+++ b/solution.py
@@ -37,22 +37,21 @@
 
 
 def tile_at(t):
-    return pl.ds(pl.multiple_of(t * LANES, LANES), LANES)
+    return slice(t * LANES, (t + 1) * LANES)
 
 
 def cut_of(start, lon_count):
     tiles = lon_count // LANES
-    start = jnp.asarray(start, jnp.int32) + lon_count
-    first = start >> LANES.bit_length() - 1
-    first = jnp.where(first >= tiles, first - tiles, first)
-    second = jnp.where(first == tiles - 1, 0, first + 1)
-    return tile_at(first), tile_at(second), start & LANES - 1
+    first, lane_at = divmod(start % lon_count, LANES)
+    return tile_at(first), tile_at((first + 1) % tiles), lane_at
 
 
 def cut(first, second, lane_at):
+    if lane_at == 0:
+        return first
     lane = lax.broadcasted_iota(jnp.int32, first.shape, 1).astype(jnp.int16)
-    joined = jnp.where(lane >= lane_at.astype(jnp.int16), first, second)
-    return pltpu.roll(joined, (LANES - lane_at) & LANES - 1, 1)
+    joined = jnp.where(lane >= jnp.int16(lane_at), first, second)
+    return pltpu.roll(joined, LANES - lane_at, 1)
 
 
 def lane_plan(code):
@@ -93,13 +92,8 @@
 
 
 def in_groups(count, at_once, group):
-    def step(at, carry):
-        group([at * at_once + slot for slot in range(at_once)])
-        return carry
-
-    lax.fori_loop(0, count // at_once, step, 0)
-    if count % at_once:
-        group(list(range(count - count % at_once, count)))
+    for at in range(0, count, at_once):
+        group(list(range(at, min(at + at_once, count))))
 
 
 def pack_kernel(
@@ -136,10 +130,8 @@
             plan_out[at * inner : (at + 1) * inner, cols] = middle[at].astype(jnp.bfloat16)
 
 
-def basis_kernel(place, pair_ids, basis_out, limit_out, waves, *, lon_count):
-    orders = basis_out.shape[0]
-
-    def wave_rows(group, carry):
+def fill_waves(pair_ids, waves):
+    def rows_of(group, carry):
         row = lax.broadcasted_iota(jnp.int32, (16, LANES), 0)
         pair = jnp.full((16, LANES), pair_ids[4 * group + 3], jnp.int32)
         for at in (2, 1, 0):
@@ -148,35 +140,24 @@
         waves[pl.ds(pl.multiple_of(group * 16, 16), 16), :] = wave.astype(jnp.float32)
         return carry
 
-    lax.fori_loop(0, orders // 16, wave_rows, 0)
-
-    def tile(t):
-        def rows_of(group, carry):
-            rows = pl.ds(pl.multiple_of(group * 16, 16), 16)
-            lane = lax.broadcasted_iota(jnp.int32, (16, LANES), 1)
-            row = lax.broadcasted_iota(jnp.int32, (16, LANES), 0)
-            longitude = lane + t * SPAN
-            quarter = jnp.where((row & 1) == 0, 0.0, float(lon_count // 4))
-            steps = longitude.astype(jnp.float32) * waves[rows, :] + quarter
-            turns = jnp.floor(steps * (1.0 / lon_count) + 0.5)
-            angle = lon_count // 4 - jnp.abs(steps - turns * lon_count)
-            angle = angle * (2.0 * math.pi / lon_count)
-            square = angle * angle
-            series = jnp.float32(-1.0 / 39916800.0)
-            for term in (1.0 / 362880.0, -1.0 / 5040.0, 1.0 / 120.0, -1.0 / 6.0, 1.0):
-                series = series * square + term
-            taken = (lane < SPAN) & (longitude < lon_count)
-            basis_out[rows, tile_at(t)] = jnp.where(taken, angle * series, 0.0).astype(
-                jnp.bfloat16
-            )
-            return carry
-
-        lax.fori_loop(0, orders // 16, rows_of, 0, unroll=orders <= 64)
-
-    for t in range(basis_out.shape[1] // LANES):
-        tile(t)
-    limit = NMAX + 1 - pair_ids[place[0]] - place[1]
-    limit_out[...] = jnp.full(limit_out.shape, limit, jnp.int32)
+    lax.fori_loop(0, waves.shape[0] // 16, rows_of, 0)
+
+
+def basis_tile(t, wave, lon_count):
+    lane = lax.broadcasted_iota(jnp.int32, (16, LANES), 1)
+    row = lax.broadcasted_iota(jnp.int32, (16, LANES), 0)
+    longitude = lane + t * SPAN
+    quarter = jnp.where((row & 1) == 0, 0.0, float(lon_count // 4))
+    steps = longitude.astype(jnp.float32) * wave + quarter
+    turns = jnp.floor(steps * (1.0 / lon_count) + 0.5)
+    angle = lon_count // 4 - jnp.abs(steps - turns * lon_count)
+    angle = angle * (2.0 * math.pi / lon_count)
+    square = angle * angle
+    series = jnp.float32(-1.0 / 39916800.0)
+    for term in (1.0 / 362880.0, -1.0 / 5040.0, 1.0 / 120.0, -1.0 / 6.0, 1.0):
+        series = series * square + term
+    taken = (lane < SPAN) & (longitude < lon_count)
+    return jnp.where(taken, angle * series, 0.0).astype(jnp.bfloat16)
 
 
 def inner_kernel(grid, plans, departed, windows, *, slices):
@@ -220,7 +201,7 @@
 
 
 def rim_kernel(
-    arrived, own, basis, inner_departed, fourier_out, windows, departed, *, slices
+    pair_ids, arrived, own, inner_departed, fourier_out, windows, departed, basis, waves, *, slices
 ):
     lon_count = arrived.shape[1]
     fields = slices * EDGE
@@ -266,7 +247,20 @@
             )
         for t, result in zip(ts, results):
             departed[:, tile_at(t)] = result
-
+            for at in range(0, waves.shape[0] if few else 0, 16):
+                basis[at : at + 16, tile_at(t)] = basis_tile(t, waves[at : at + 16, :], lon_count)
+
+    fill_waves(pair_ids, waves)
+    few = waves.shape[0] <= 64
+    if not few:
+
+        def rows_of(group, carry):
+            rows = pl.ds(pl.multiple_of(group * 16, 16), 16)
+            for t in range(basis.shape[1] // LANES):
+                basis[rows, tile_at(t)] = basis_tile(t, waves[rows, :], lon_count)
+            return carry
+
+        lax.fori_loop(0, waves.shape[0] // 16, rows_of, 0)
     in_groups(basis.shape[1] // LANES, RIM_AT_ONCE, group_of)
     fourier = jnp.concatenate(
         [
@@ -287,7 +281,7 @@
             fourier_out[pair, lev] = block
 
 
-def legendre_kernel(limit, coeffs, spread_analysis, out, spread_coeffs, *, levs, slices):
+def legendre_kernel(place, pair_ids, coeffs, spread_analysis, out, spread_coeffs, *, levs, slices):
     members, _, rows = coeffs.shape
     bands = members // levs
     col_count = spread_analysis.shape[1]
@@ -308,15 +302,13 @@
             [jnp.where(slice_of == f, block, 0.0) for f in range(slices)], axis=0
         ).astype(jnp.bfloat16)
 
-    if bands <= 16:
-        for band in range(bands):
-            spread(band)
-    else:
-        lax.fori_loop(0, bands, lambda band, carry: (spread(band), carry)[1], 0)
+    for band in range(bands):
+        spread(band)
     total = jnp.dot(
         spread_coeffs[...], spread_analysis[...], preferred_element_type=jnp.float32
     )
-    first_wave = lax.broadcasted_iota(jnp.int32, (2, col_count), 1) < limit[0:1, 0:1]
+    columns = place[1] + lax.broadcasted_iota(jnp.int32, (2, col_count), 1)
+    first_wave = columns < NMAX + 1 - pair_ids[place[0]]
     for f in range(slices):
         for lev in range(levs):
             at = (f * levs + lev) * 4
@@ -364,30 +356,21 @@
         cost_estimate=pl.CostEstimate(flops=100_000_000, bytes_accessed=2_000_000, transcendentals=0),
     )(rows, plans)
 
-    basis, limit = pl.pallas_call(
-        functools.partial(basis_kernel, lon_count=lon_count),
-        out_shape=(
-            jax.ShapeDtypeStruct((4 * pairs, windows * LANES), jnp.bfloat16),
-            jax.ShapeDtypeStruct((8, LANES), jnp.int32),
-        ),
-        in_specs=[smem] * 2,
-        out_specs=(vmem,) * 2,
-        scratch_shapes=[pltpu.VMEM((4 * pairs, LANES), jnp.float32)],
-        compiler_params=params,
-    )(place, pair_ids)
-
     held_coeffs = slices * band_rows
     fourier = pl.pallas_call(
         functools.partial(rim_kernel, slices=slices),
         out_shape=jax.ShapeDtypeStruct((pairs, levs, 4, held_coeffs), jnp.bfloat16),
-        in_specs=[vmem] * 4,
+        in_specs=[smem] + [vmem] * 3,
         out_specs=vmem,
         scratch_shapes=[
             pltpu.VMEM((RIM_AT_ONCE, 2 * fields, LANES), jnp.float32),
             pltpu.VMEM((fields, windows * LANES), jnp.bfloat16),
+            pltpu.VMEM((4 * pairs, windows * LANES), jnp.bfloat16),
+            pltpu.VMEM((4 * pairs, LANES), jnp.float32),
         ],
         compiler_params=params,
-    )(arrived_rim, own_rim, basis, inner_departed)
+    )(pair_ids, arrived_rim, own_rim, inner_departed)
+    fourier, analysis = lax.optimization_barrier((fourier, analysis))
 
     values = analysis[0].reshape(bands, band_rows, col_count)
     before = jnp.roll(values[:, band_rows - RIM :], 1, axis=0)
@@ -408,11 +391,11 @@
     out = pl.pallas_call(
         functools.partial(legendre_kernel, levs=levs, slices=slices),
         out_shape=jax.ShapeDtypeStruct((levs * slices, 2, col_count), jnp.float32),
-        in_specs=[vmem] * 3,
+        in_specs=[smem] * 2 + [vmem] * 2,
         out_specs=vmem,
         scratch_shapes=[pltpu.VMEM((4 * levs * slices, bands * LANES), jnp.bfloat16)],
         compiler_params=params,
-    )(limit, coeffs, spread_analysis)
+    )(place, pair_ids, coeffs, spread_analysis)
     return out[None]
 
 

time: 27.4 us -> 26.1 us (0.953)
  waiting for transfers between devices: 7.57 us -> 10.2 us
  Pallas kernels: 9.9 us -> 7.43 us
  starting transfers between devices: 6.88 us -> 6.06 us
  local copies, waits for them, and re-layouts: 2.58 us -> 2 us
    ppermute x1, waiting for transfers between devices: 1.06 us -> 3.71 us  [shards(): lax.ppermute(sent_rim, 'lat', [(i, (i + 1) % bands) for i in range(bands)])]
    pallas_call x1, Pallas kernels: 3.55 us -> 2.46 us  [shards(): pl.pallas_call(functools.partial(rim_kernel, slices=slices), out_shape=ja...]
    pallas_call x1, Pallas kernels: 4.18 us -> 3.22 us  [shards(): pl.pallas_call(functools.partial(inner_kernel, slices=slices), out_shape=...]
    pallas_call x1 -> x0, Pallas kernels: 0.96 us -> none  [shards(): pl.pallas_call(functools.partial(basis_kernel, lon_count=lon_count), out_...]
    all_to_all x1, starting transfers between devices: 3.85 us -> 3.04 us  [shards(): lax.all_to_all(fourier.reshape(pairs * levs, 4, held_coeffs), ('lat', 'le...]
    unnamed x12, local copies, waits for them, and re-layouts: 0.61 us -> 0.04 us
    pallas_call x1, Pallas kernels: 0.89 us -> 1.43 us  [shards(): pl.pallas_call(functools.partial(legendre_kernel, levs=levs, slices=slice...]
  transfers between devices with their start and end apart: 2 -> 2, of which waited for: 2 -> 2; matrix products, arithmetic and copies ran while one was open for 3% -> 3% of each run, Pallas kernels for 19% -> 12%
where the time goes in v7:
time: 26.1 us; the launch traced here: 25.9 us
  waiting for transfers between devices  10.2 us (39%)
  Pallas kernels  7.43 us (28%)
  starting transfers between devices  6.06 us (23%)
  local copies, waits for them, and re-layouts  2 us (8%)
    all_to_all x1, waiting for transfers between devices, shards(): lax.all_to_all(fourier.reshape(pairs * levs, 4, held_coeffs), ('lat', 'le...  6.44 us
    ppermute x1, waiting for transfers between devices, shards(): lax.ppermute(sent_rim, 'lat', [(i, (i + 1) % bands) for i in range(bands)])  3.71 us
    pallas_call x1, Pallas kernels, shards(): pl.pallas_call(functools.partial(inner_kernel, slices=slices), out_shape=...  3.22 us
    all_to_all x1, starting transfers between devices, shards(): lax.all_to_all(fourier.reshape(pairs * levs, 4, held_coeffs), ('lat', 'le...  3.04 us
    ppermute x1, starting transfers between devices, shards(): lax.ppermute(sent_rim, 'lat', [(i, (i + 1) % bands) for i in range(bands)])  3.02 us
    pallas_call x1, Pallas kernels, shards(): pl.pallas_call(functools.partial(rim_kernel, slices=slices), out_shape=ja...  2.46 us
    pallas_call x1, Pallas kernels, shards(): pl.pallas_call(functools.partial(legendre_kernel, levs=levs, slices=slice...  1.43 us
    reshape x1, local copies, waits for them, and re-layouts, shards(): rows = grid.transpose(1, 0, 2).reshape(band_rows * slices, lon_count)  1.23 us
  transfers between devices with their start and end apart: 2, of which 2 were waited for; matrix products, arithmetic and copies ran while one was open for 3% of the time, Pallas kernels for 12%

profile of v7, /device:TPU:0, one launch (start us, length us, event | category | flops | bytes accessed | tf_op | source)
XLA Modules:
  0.0 25.9 jit_solution(53163281234383884)
XLA Ops:
  0.0 0.0 copy-start
  0.0 0.0 copy-start.1
  0.0 0.0 copy-start.2
  0.0 0.0 copy-start.3
  0.0 1.2 %reshape.13.rows.grid = bf16[80,3200]{1,0:T(8,128)(2,1)S(1)} reshape(bf16[20,4,3200]{2,1,0:T(4,128)(2,1)} %bitcast.8) | data formatting | bytes 1024000 | tf_op jit(solution)/shard_map/reshape | solution.py:333
  1.2 0.0 copy-done
  1.3 0.0 copy-done.1
  1.3 0.0 copy-done.2
  1.3 0.0 copy-done.3
  1.3 0.3 %shard_map.73 = (bf16[24,3200]{1,0:T(8,128)(2,1)S(1)}, bf16[24,3200]{1,0:T(8,128)(2,1)S(1)}, bf16[48,3200]{1,0:T(8,128)(2,1)S(1)}) custom-call(s32[1]{0:T(128)} %bitcast.2.band_start, bf16[80,3200]{1,0:T(8,128)(2,1)S(1)} %reshape.13.rows.grid, s32[20,3200]{1,0:T(8,128)S(1)} %copy-done, s32[20,3200]{1,0:T(8,128)S(1)} %copy-done.1, ...), custom_call_target="tpu_custom_call" | custom-call | tf_op jit(solution)/shard_map/pallas_call | solution.py:335
  1.6 3.0 %collective-permute-start = (bf16[24,3200]{1,0:T(8,128)(2,1)S(1)}, bf16[24,3200]{1,0:T(8,128)(2,1)S(1)}, u32[]{:S(2)}, u32[]{:S(2)}) collective-permute-start(bf16[24,3200]{1,0:T(8,128)(2,1)S(1)} %get-tuple-element.10), channel_id=1, source_target_pairs={{0,4},{4,8},{8,12},{12,16},{16,20},{20,24},{24,28},{28,0},{1,5},{5... | collective-permute-start | bytes 460808 | tf_op jit(solution)/shard_map/ppermute | solution.py:347
  4.6 3.2 %shard_map.74.inner_departed = bf16[64,3712]{1,0:T(8,128)(2,1)S(1)} custom-call(bf16[80,3200]{1,0:T(8,128)(2,1)S(1)} %reshape.13.rows.grid, bf16[48,3200]{1,0:T(8,128)(2,1)S(1)} %get-tuple-element.12.plans), custom_call_target="tpu_custom_call" | custom-call | flops 100000000 | bytes 2000000 | tf_op jit(solution)/shard_map/pallas_call | solution.py:349
  7.9 0.1 pad_add_fusion.place
  7.9 0.0 copy-start.4
  7.9 3.7 %collective-permute-done.arrived = bf16[24,3200]{1,0:T(8,128)(2,1)S(1)} collective-permute-done((bf16[24,3200]{1,0:T(8,128)(2,1)S(1)}, bf16[24,3200]{1,0:T(8,128)(2,1)S(1)}, u32[]{:S(2)}, u32[]{:S(2)}) %collective-permute-start) | collective-permute-done | bytes 153632 | tf_op jit(solution)/shard_map/ppermute | solution.py:347
  11.7 0.0 copy-done.4
  11.7 0.0 copy-start.5
  11.7 2.5 %shard_map.75 = bf16[8,4,4,80]{3,2,1,0:T(4,128)(2,1)} custom-call(s32[8]{0:T(128)S(1)} %copy-done.4, bf16[24,3200]{1,0:T(8,128)(2,1)S(1)} %collective-permute-done.arrived, bf16[24,3200]{1,0:T(8,128)(2,1)S(1)} %get-tuple-element.11.own, bf16[64,3712]{1,0:T(8,128)(2,1)S(1)} %shard_map.74.inner_departed), custom_call_target="tpu_custom_call" | custom-call | tf_op jit(solution)/shard_map/pallas_call | solution.py:360
  14.1 0.0 copy-done.5
  14.2 3.0 %all-to-all-start = ((bf16[32,4,80]{2,1,0:T(4,128)(2,1)}), bf16[32,4,80]{2,1,0:T(4,128)(2,1)S(1)}, u32[]{:S(2)}, u32[]{:S(2)}) async-start(bf16[32,4,80]{2,1,0:T(4,128)(2,1)} %bitcast.4), calls=%async_computation | async-start | bytes 65536 | tf_op jit(solution)/shard_map/all_to_all | solution.py:384
  17.3 0.1 slice_maximum_fusion
  17.4 0.6 %concatenate.9 = bf16[8,128,320]{2,1,0:T(8,128)(2,1)S(1)} concatenate(bf16[8,16,320]{2,1,0:T(8,128)(2,1)S(1)} %slice.41, bf16[8,16,320]{2,1,0:T(8,128)(2,1)S(1)} %slice.41, bf16[8,16,320]{2,1,0:T(8,128)(2,1)S(1)} %slice.41, bf16[8,16,320]{2,1,0:T(8,128)(2,1)S(1)} %slice.41, bf16[8,1,320]{2,1,0:T(2,128)(2,1)S(1)} %get-tuple-element.18, bf16[8,1,320]{2,1,0:T(2,128)(2,1)S(1)} %get-tuple-element.18, ...), dimensions={1} | concatenate | bytes 1310720 | tf_op jit(solution)/shard_map/concatenate | solution.py:382
  18.1 6.4 %all-to-all-done.coeffs = bf16[32,4,80]{2,1,0:T(4,128)(2,1)S(1)} async-done(((bf16[32,4,80]{2,1,0:T(4,128)(2,1)}), bf16[32,4,80]{2,1,0:T(4,128)(2,1)S(1)}, u32[]{:S(2)}, u32[]{:S(2)}) %all-to-all-start) | async-done | bytes 20512 | tf_op jit(solution)/shard_map/all_to_all | solution.py:384
  24.5 1.4 %shard_map.76 = f32[16,2,320]{2,1,0:T(2,128)} custom-call(s32[2]{0:T(128)S(1)} %pad_add_fusion.place, s32[8]{0:T(128)S(1)} %copy-done.4, bf16[32,4,80]{2,1,0:T(4,128)(2,1)S(1)} %all-to-all-done.coeffs, bf16[1024,320]{1,0:T(8,128)(2,1)S(1)} %bitcast.7), custom_call_target="tpu_custom_call" | custom-call | tf_op jit(solution)/shard_map/pallas_call | solution.py:391
  (7 shorter events, 0.2 us)
Async XLA Ops:
  0.0 1.3 %copy-start = (s32[20,3200]{1,0:T(8,128)S(1)}, s32[20,3200]{1,0:T(8,128)}, u32[]{:S(2)}) copy-start(s32[20,3200]{1,0:T(8,128)} %dep_row.1) | copy-start | bytes 768004
  0.0 1.3 %copy-start.1 = (s32[20,3200]{1,0:T(8,128)S(1)}, s32[20,3200]{1,0:T(8,128)}, u32[]{:S(2)}) copy-start(s32[20,3200]{1,0:T(8,128)} %dep_col.1) | copy-start | bytes 768004
  0.0 1.3 %copy-start.2 = (bf16[20,3200]{1,0:T(8,128)(2,1)S(1)}, bf16[20,3200]{1,0:T(8,128)(2,1)}, u32[]{:S(2)}) copy-start(bf16[20,3200]{1,0:T(8,128)(2,1)} %lat_frac.1) | copy-start | bytes 384004
  0.0 1.3 %copy-start.3 = (bf16[20,3200]{1,0:T(8,128)(2,1)S(1)}, bf16[20,3200]{1,0:T(8,128)(2,1)}, u32[]{:S(2)}) copy-start(bf16[20,3200]{1,0:T(8,128)(2,1)} %lon_frac.1) | copy-start | bytes 384004
  1.6 10.0 %collective-permute-start = (bf16[24,3200]{1,0:T(8,128)(2,1)S(1)}, bf16[24,3200]{1,0:T(8,128)(2,1)S(1)}, u32[]{:S(2)}, u32[]{:S(2)}) collective-permute-start(bf16[24,3200]{1,0:T(8,128)(2,1)S(1)} %get-tuple-element.10), channel_id=1, source_target_pairs={{0,4},{4,8},{8,12},{12,16},{16,20},{20,24},{24,28},{28,0},{1,5},{5... | collective-permute-start | bytes 460808 | tf_op jit(solution)/shard_map/ppermute | solution.py:347
  7.9 3.7 %copy-start.4 = (s32[8]{0:T(128)S(1)}, s32[8]{0:T(128)}, u32[]{:S(2)}) copy-start(s32[8]{0:T(128)} %pair_ids.3) | copy-start | bytes 100
  11.7 2.5 %copy-start.5 = (bf16[1,160,320]{2,1,0:T(8,128)(2,1)S(1)}, bf16[1,160,320]{2,1,0:T(8,128)(2,1)}, u32[]{:S(2)}) copy-start(bf16[1,160,320]{2,1,0:T(8,128)(2,1)} %param.13) | copy-start | bytes 307204
  14.2 10.3 %all-to-all-start = ((bf16[32,4,80]{2,1,0:T(4,128)(2,1)}), bf16[32,4,80]{2,1,0:T(4,128)(2,1)S(1)}, u32[]{:S(2)}, u32[]{:S(2)}) async-start(bf16[32,4,80]{2,1,0:T(4,128)(2,1)} %bitcast.4), calls=%async_computation | async-start | bytes 65536 | tf_op jit(solution)/shard_map/all_to_all | solution.py:384

commit v8 on v7

--- a/solution.py
+++ b/solution.py
@@ -130,17 +130,12 @@
             plan_out[at * inner : (at + 1) * inner, cols] = middle[at].astype(jnp.bfloat16)
 
 
-def fill_waves(pair_ids, waves):
-    def rows_of(group, carry):
-        row = lax.broadcasted_iota(jnp.int32, (16, LANES), 0)
-        pair = jnp.full((16, LANES), pair_ids[4 * group + 3], jnp.int32)
-        for at in (2, 1, 0):
-            pair = jnp.where(row < 4 * (at + 1), pair_ids[4 * group + at], pair)
-        wave = jnp.where((row & 2) == 0, pair, NMAX + 1 - pair)
-        waves[pl.ds(pl.multiple_of(group * 16, 16), 16), :] = wave.astype(jnp.float32)
-        return carry
-
-    lax.fori_loop(0, waves.shape[0] // 16, rows_of, 0)
+def waves_of(ids, group):
+    pair = jnp.concatenate(
+        [jnp.broadcast_to(ids[pl.ds(4 * group + at, 1), :], (4, LANES)) for at in range(4)], axis=0
+    )
+    row = lax.broadcasted_iota(jnp.int32, (16, LANES), 0)
+    return jnp.where((row & 2) == 0, pair, NMAX + 1 - pair)
 
 
 def basis_tile(t, wave, lon_count):
@@ -160,9 +155,18 @@
     return jnp.where(taken, angle * series, 0.0).astype(jnp.bfloat16)
 
 
-def inner_kernel(grid, plans, departed, windows, *, slices):
+def add_up(basis, values):
+    return lax.dot_general(
+        basis, values, (((1,), (1,)), ((), ())), preferred_element_type=jnp.float32
+    )
+
+
+def inner_kernel(grid, plans, ids, fourier_out, basis, windows, departed, *, slices):
     lon_count = grid.shape[1]
     inner = plans.shape[0] // 3
+    groups = ids.shape[0] // 4
+    few = groups <= 4
+    waves = [waves_of(ids, at) for at in range(groups if few else 0)]
 
     def group_of(ts):
         blocks, plan_blocks = [], []
@@ -196,12 +200,25 @@
                 results.append((ts[slot], f, interpolate(sources, plan, weights)))
         for t, f, result in results:
             departed[f * inner : (f + 1) * inner, tile_at(t)] = result
-
+        for t in ts if few else ():
+            for at, wave in enumerate(waves):
+                basis[16 * at : 16 * at + 16, tile_at(t)] = basis_tile(t, wave, lon_count)
+
+    if not few:
+
+        def rows_of(group, carry):
+            rows = pl.ds(pl.multiple_of(group * 16, 16), 16)
+            for t in range(basis.shape[1] // LANES):
+                basis[rows, tile_at(t)] = basis_tile(t, waves_of(ids, group), lon_count)
+            return carry
+
+        lax.fori_loop(0, groups, rows_of, 0)
     in_groups(departed.shape[1] // LANES, INNER_AT_ONCE, group_of)
+    fourier_out[...] = add_up(basis[...], departed[...])
 
 
 def rim_kernel(
-    pair_ids, arrived, own, inner_departed, fourier_out, windows, departed, basis, waves, *, slices
+    arrived, own, basis, inner_fourier, fourier_out, windows, departed, *, slices, owners
 ):
     lon_count = arrived.shape[1]
     fields = slices * EDGE
@@ -247,41 +264,14 @@
             )
         for t, result in zip(ts, results):
             departed[:, tile_at(t)] = result
-            for at in range(0, waves.shape[0] if few else 0, 16):
-                basis[at : at + 16, tile_at(t)] = basis_tile(t, waves[at : at + 16, :], lon_count)
-
-    fill_waves(pair_ids, waves)
-    few = waves.shape[0] <= 64
-    if not few:
-
-        def rows_of(group, carry):
-            rows = pl.ds(pl.multiple_of(group * 16, 16), 16)
-            for t in range(basis.shape[1] // LANES):
-                basis[rows, tile_at(t)] = basis_tile(t, waves[rows, :], lon_count)
-            return carry
-
-        lax.fori_loop(0, waves.shape[0] // 16, rows_of, 0)
+
     in_groups(basis.shape[1] // LANES, RIM_AT_ONCE, group_of)
-    fourier = jnp.concatenate(
-        [
-            lax.dot_general(
-                basis[...],
-                values[...],
-                (((1,), (1,)), ((), ())),
-                preferred_element_type=jnp.float32,
-            )
-            for values in (inner_departed, departed)
-        ],
-        axis=1,
-    )
-    levs = fourier_out.shape[1]
-    for pair in range(fourier_out.shape[0]):
-        block = fourier[4 * pair : 4 * pair + 4].astype(jnp.bfloat16)
-        for lev in range(levs):
-            fourier_out[pair, lev] = block
-
-
-def legendre_kernel(place, pair_ids, coeffs, spread_analysis, out, spread_coeffs, *, levs, slices):
+    fourier = jnp.concatenate([inner_fourier[...], add_up(basis[...], departed[...])], axis=1)
+    for at, pair in enumerate(owners):
+        fourier_out[at] = fourier[4 * pair : 4 * pair + 4].astype(jnp.bfloat16)
+
+
+def legendre_kernel(first_wave, coeffs, spread_analysis, out, spread_coeffs, *, levs, slices, order):
     members, _, rows = coeffs.shape
     bands = members // levs
     col_count = spread_analysis.shape[1]
@@ -293,7 +283,8 @@
 
     def spread(band):
         block = jnp.concatenate(
-            [coeffs[band * levs + lev].astype(jnp.float32) for lev in range(levs)], axis=0
+            [coeffs[order.index(band * levs + lev)].astype(jnp.float32) for lev in range(levs)],
+            axis=0,
         )
         block = jnp.concatenate(
             [block, jnp.zeros((block.shape[0], LANES - rows), jnp.float32)], axis=1
@@ -307,12 +298,11 @@
     total = jnp.dot(
         spread_coeffs[...], spread_analysis[...], preferred_element_type=jnp.float32
     )
-    columns = place[1] + lax.broadcasted_iota(jnp.int32, (2, col_count), 1)
-    first_wave = columns < NMAX + 1 - pair_ids[place[0]]
+    first = first_wave[0:2, :] > 0.0
     for f in range(slices):
         for lev in range(levs):
             at = (f * levs + lev) * 4
-            out[lev * slices + f] = jnp.where(first_wave, total[at : at + 2], total[at + 2 : at + 4])
+            out[lev * slices + f] = jnp.where(first, total[at : at + 2], total[at + 2 : at + 4])
 
 
 def shards(grid, dep_row, dep_col, lat_frac, lon_frac, pair_ids, analysis):
@@ -325,7 +315,6 @@
     held_rows = -(-band_rows // 8) * 8
     fields = slices * EDGE
     band_start = jnp.reshape(lax.axis_index("lat") * band_rows, (1,)).astype(jnp.int32)
-    place = jnp.stack([lax.axis_index("lat"), lax.axis_index("lev") * col_count])
     vmem = pl.BlockSpec(memory_space=pltpu.VMEM)
     smem = pl.BlockSpec(memory_space=pltpu.SMEM)
     params = pltpu.CompilerParams(vmem_limit_bytes=48 * 2**20)
@@ -346,31 +335,41 @@
     )(band_start, rows, dep_row, dep_col, lat_frac, lon_frac)
     arrived_rim = lax.ppermute(sent_rim, "lat", [(i, (i + 1) % bands) for i in range(bands)])
 
-    inner_departed = pl.pallas_call(
+    plans, ids = lax.optimization_barrier((plans, pair_ids))
+    ids = jnp.broadcast_to(ids.astype(jnp.float32)[:, None], (pairs, LANES))
+    inner_fourier, basis = pl.pallas_call(
         functools.partial(inner_kernel, slices=slices),
-        out_shape=jax.ShapeDtypeStruct((slices * inner, windows * LANES), jnp.bfloat16),
-        in_specs=[vmem] * 2,
-        out_specs=vmem,
-        scratch_shapes=[pltpu.VMEM((INNER_AT_ONCE, band_rows * slices, LANES), jnp.float32)],
+        out_shape=(
+            jax.ShapeDtypeStruct((4 * pairs, slices * inner), jnp.float32),
+            jax.ShapeDtypeStruct((4 * pairs, windows * LANES), jnp.bfloat16),
+        ),
+        in_specs=[vmem] * 3,
+        out_specs=(vmem,) * 2,
+        scratch_shapes=[
+            pltpu.VMEM((INNER_AT_ONCE, band_rows * slices, LANES), jnp.float32),
+            pltpu.VMEM((slices * inner, windows * LANES), jnp.bfloat16),
+        ],
         compiler_params=params,
         cost_estimate=pl.CostEstimate(flops=100_000_000, bytes_accessed=2_000_000, transcendentals=0),
-    )(rows, plans)
+    )(rows, plans, ids)
 
     held_coeffs = slices * band_rows
+    members = bands * levs
+    order = [(at + members // 2) % members for at in range(members)]
     fourier = pl.pallas_call(
-        functools.partial(rim_kernel, slices=slices),
-        out_shape=jax.ShapeDtypeStruct((pairs, levs, 4, held_coeffs), jnp.bfloat16),
-        in_specs=[smem] + [vmem] * 3,
+        functools.partial(
+            rim_kernel, slices=slices, owners=[member // levs for member in order]
+        ),
+        out_shape=jax.ShapeDtypeStruct((members, 4, held_coeffs), jnp.bfloat16),
+        in_specs=[vmem] * 4,
         out_specs=vmem,
         scratch_shapes=[
             pltpu.VMEM((RIM_AT_ONCE, 2 * fields, LANES), jnp.float32),
             pltpu.VMEM((fields, windows * LANES), jnp.bfloat16),
-            pltpu.VMEM((4 * pairs, windows * LANES), jnp.bfloat16),
-            pltpu.VMEM((4 * pairs, LANES), jnp.float32),
         ],
         compiler_params=params,
-    )(pair_ids, arrived_rim, own_rim, inner_departed)
-    fourier, analysis = lax.optimization_barrier((fourier, analysis))
+    )(arrived_rim, own_rim, basis, inner_fourier)
+    fourier, analysis, late_ids = lax.optimization_barrier((fourier, analysis, pair_ids))
 
     values = analysis[0].reshape(bands, band_rows, col_count)
     before = jnp.roll(values[:, band_rows - RIM :], 1, axis=0)
@@ -381,21 +380,22 @@
     spread_rows.append(jnp.zeros((bands, LANES - held_coeffs, col_count), jnp.bfloat16))
     spread_analysis = jnp.concatenate(spread_rows, axis=1).reshape(bands * LANES, col_count)
 
+    own_id = lax.dynamic_slice_in_dim(late_ids, lax.axis_index("lat"), 1)
+    columns = lax.axis_index("lev") * col_count + jnp.arange(col_count, dtype=jnp.int32)
+    first_wave = jnp.where(columns < NMAX + 1 - own_id, 1.0, 0.0)
+    first_wave = jnp.broadcast_to(first_wave[None, :], (8, col_count))
+
     coeffs = lax.all_to_all(
-        fourier.reshape(pairs * levs, 4, held_coeffs),
-        ("lat", "lev"),
-        split_axis=0,
-        concat_axis=0,
-        tiled=True,
+        fourier, ("lat", "lev"), split_axis=0, concat_axis=0, axis_index_groups=[order], tiled=True
     )
     out = pl.pallas_call(
-        functools.partial(legendre_kernel, levs=levs, slices=slices),
+        functools.partial(legendre_kernel, levs=levs, slices=slices, order=order),
         out_shape=jax.ShapeDtypeStruct((levs * slices, 2, col_count), jnp.float32),
-        in_specs=[smem] * 2 + [vmem] * 2,
+        in_specs=[vmem] * 3,
         out_specs=vmem,
         scratch_shapes=[pltpu.VMEM((4 * levs * slices, bands * LANES), jnp.bfloat16)],
         compiler_params=params,
-    )(place, pair_ids, coeffs, spread_analysis)
+    )(first_wave, coeffs, spread_analysis)
     return out[None]
 
 

time: 26.1 us -> 24.9 us (0.954)
  waiting for transfers between devices: 10.2 us -> 8.73 us
  Pallas kernels: 7.43 us -> 6.39 us
  local copies, waits for them, and re-layouts: 2 us -> 2.73 us
  between operations: 0.11 us -> 0.75 us
    all_to_all x1, waiting for transfers between devices: 6.44 us -> 5.25 us  [shards(): lax.all_to_all(fourier, ('lat', 'lev'), split_axis=0, concat_axis=0, axis...]
    pallas_call x1, Pallas kernels: 2.46 us -> 1.72 us  [shards(): pl.pallas_call(functools.partial(rim_kernel, slices=slices, owners=[membe...]
    dynamic_slice x0 -> x1, local copies, waits for them, and re-layouts: none -> 0.65 us  [shards(): own_id = lax.dynamic_slice_in_dim(late_ids, lax.axis_index('lat'), 1)]
    pallas_call x1, Pallas kernels: 1.43 us -> 0.89 us  [shards(): pl.pallas_call(functools.partial(legendre_kernel, levs=levs, slices=slice...]
  transfers between devices with their start and end apart: 2 -> 2, of which waited for: 2 -> 2; matrix products, arithmetic and copies ran while one was open for 3% -> 6% of each run, Pallas kernels for 12% -> 14%
where the time goes in v8:
time: 24.9 us; the launch traced here: 24.8 us
  waiting for transfers between devices  8.73 us (35%)
  Pallas kernels  6.39 us (26%)
  starting transfers between devices  6.06 us (24%)
  local copies, waits for them, and re-layouts  2.73 us (11%)
  between operations  0.75 us (3%)
    all_to_all x1, waiting for transfers between devices, shards(): lax.all_to_all(fourier, ('lat', 'lev'), split_axis=0, concat_axis=0, axis...  5.25 us
    ppermute x1, waiting for transfers between devices, shards(): lax.ppermute(sent_rim, 'lat', [(i, (i + 1) % bands) for i in range(bands)])  3.48 us
    pallas_call x1, Pallas kernels, shards(): pl.pallas_call(functools.partial(inner_kernel, slices=slices), out_shape=...  3.46 us
    all_to_all x1, starting transfers between devices, shards(): lax.all_to_all(fourier, ('lat', 'lev'), split_axis=0, concat_axis=0, axis...  3.04 us
    ppermute x1, starting transfers between devices, shards(): lax.ppermute(sent_rim, 'lat', [(i, (i + 1) % bands) for i in range(bands)])  3.02 us
    pallas_call x1, Pallas kernels, shards(): pl.pallas_call(functools.partial(rim_kernel, slices=slices, owners=[membe...  1.72 us
    reshape x1, local copies, waits for them, and re-layouts, shards(): rows = grid.transpose(1, 0, 2).reshape(band_rows * slices, lon_count)  1.23 us
    pallas_call x1, Pallas kernels, shards(): pl.pallas_call(functools.partial(legendre_kernel, levs=levs, slices=slice...  0.89 us
  transfers between devices with their start and end apart: 2, of which 2 were waited for; matrix products, arithmetic and copies ran while one was open for 6% of the time, Pallas kernels for 14%

profile of v8, /device:TPU:0, one launch (start us, length us, event | category | flops | bytes accessed | tf_op | source)
XLA Modules:
  0.0 24.8 jit_solution(863412228168349369)
XLA Ops:
  0.0 0.0 copy-start
  0.0 0.0 copy-start.1
  0.0 0.0 copy-start.2
  0.0 0.0 copy-start.3
  0.0 1.2 %reshape.17.rows.grid = bf16[80,3200]{1,0:T(8,128)(2,1)S(1)} reshape(bf16[20,4,3200]{2,1,0:T(4,128)(2,1)} %bitcast.6) | data formatting | bytes 1024000 | tf_op jit(solution)/shard_map/reshape | solution.py:322
  1.2 0.0 copy-done
  1.3 0.0 copy-done.1
  1.3 0.0 copy-done.2
  1.3 0.0 copy-done.3
  1.3 0.3 %shard_map.73 = (bf16[24,3200]{1,0:T(8,128)(2,1)S(1)}, bf16[24,3200]{1,0:T(8,128)(2,1)S(1)}, bf16[48,3200]{1,0:T(8,128)(2,1)S(1)}) custom-call(s32[1]{0:T(128)} %bitcast.band_start, bf16[80,3200]{1,0:T(8,128)(2,1)S(1)} %reshape.17.rows.grid, s32[20,3200]{1,0:T(8,128)S(1)} %copy-done, s32[20,3200]{1,0:T(8,128)S(1)} %copy-done.1, ...), custom_call_target="tpu_custom_call" | custom-call | tf_op jit(solution)/shard_map/pallas_call | solution.py:324
  1.6 0.0 copy-start.5
  1.6 3.0 %collective-permute-start = (bf16[24,3200]{1,0:T(8,128)(2,1)S(1)}, bf16[24,3200]{1,0:T(8,128)(2,1)S(1)}, u32[]{:S(2)}, u32[]{:S(2)}) collective-permute-start(bf16[24,3200]{1,0:T(8,128)(2,1)S(1)} %get-tuple-element.15), channel_id=1, source_target_pairs={{0,4},{4,8},{8,12},{12,16},{16,20},{20,24},{24,28},{28,0},{1,5},{5... | collective-permute-start | bytes 460808 | tf_op jit(solution)/shard_map/ppermute | solution.py:336
  4.7 0.0 copy-done.5
  4.7 0.1 broadcast_in_dim.26.ids
  4.7 3.5 %shard_map.74 = (f32[32,64]{1,0:T(8,128)S(1)}, bf16[32,3712]{1,0:T(8,128)(2,1)S(1)}) custom-call(bf16[80,3200]{1,0:T(8,128)(2,1)S(1)} %reshape.17.rows.grid, bf16[48,3200]{1,0:T(8,128)(2,1)S(1)} %get-tuple-element.18.plans, f32[8,128]{1,0:T(8,128)S(1)} %broadcast_in_dim.26.ids), custom_call_target="tpu_custom_call" | custom-call | flops 100000000 | bytes 2000000 | tf_op jit(solution)/shard_map/pallas_call | solution.py:340
  8.2 3.5 %collective-permute-done.arrived = bf16[24,3200]{1,0:T(8,128)(2,1)S(1)} collective-permute-done((bf16[24,3200]{1,0:T(8,128)(2,1)S(1)}, bf16[24,3200]{1,0:T(8,128)(2,1)S(1)}, u32[]{:S(2)}, u32[]{:S(2)}) %collective-permute-start) | collective-permute-done | bytes 153632 | tf_op jit(solution)/shard_map/ppermute | solution.py:336
  11.7 0.0 copy-start.4
  11.7 1.7 %shard_map.75 = bf16[32,4,80]{2,1,0:T(4,128)(2,1)} custom-call(bf16[24,3200]{1,0:T(8,128)(2,1)S(1)} %collective-permute-done.arrived, bf16[24,3200]{1,0:T(8,128)(2,1)S(1)} %get-tuple-element.16.own, bf16[32,3712]{1,0:T(8,128)(2,1)S(1)} %get-tuple-element.20.basis, f32[32,64]{1,0:T(8,128)S(1)} %get-tuple-element.21.inner_fourier), custom_call_target="tpu_custom_call" | custom-call | tf_op jit(solution)/shard_map/pallas_call | solution.py:359
  13.4 0.0 copy-done.4
  13.5 0.1 slice_maximum_fusion
  13.6 3.0 %all-to-all-start = ((bf16[32,4,80]{2,1,0:T(4,128)(2,1)}), bf16[32,4,80]{2,1,0:T(4,128)(2,1)S(1)}, u32[]{:S(2)}, u32[]{:S(2)}) async-start(bf16[32,4,80]{2,1,0:T(4,128)(2,1)} %shard_map.75), calls=%async_computation | async-start | bytes 65536 | tf_op jit(solution)/shard_map/all_to_all | solution.py:388
  16.6 0.7 %dynamic_slice.3 = s32[1]{0:T(128)} dynamic-slice(s32[8]{0:T(128)S(1)} %copy-done.5, s32[]{:T(128)S(6)} %select_n.11), dynamic_slice_sizes={1} | dynamic-slice | bytes 12 | tf_op jit(solution)/shard_map/dynamic_slice | solution.py:383
  18.0 0.6 %concatenate.9 = bf16[8,128,320]{2,1,0:T(8,128)(2,1)S(1)} concatenate(bf16[8,16,320]{2,1,0:T(8,128)(2,1)S(1)} %slice.41, bf16[8,16,320]{2,1,0:T(8,128)(2,1)S(1)} %slice.41, bf16[8,16,320]{2,1,0:T(8,128)(2,1)S(1)} %slice.41, bf16[8,16,320]{2,1,0:T(8,128)(2,1)S(1)} %slice.41, bf16[8,1,320]{2,1,0:T(2,128)(2,1)S(1)} %get-tuple-element.28, bf16[8,1,320]{2,1,0:T(2,128)(2,1)S(1)} %get-tuple-element.28, ...), dimensions={1} | concatenate | bytes 1310720 | tf_op jit(solution)/shard_map/concatenate | solution.py:381
  18.6 5.2 %all-to-all-done.coeffs = bf16[32,4,80]{2,1,0:T(4,128)(2,1)S(1)} async-done(((bf16[32,4,80]{2,1,0:T(4,128)(2,1)}), bf16[32,4,80]{2,1,0:T(4,128)(2,1)S(1)}, u32[]{:S(2)}, u32[]{:S(2)}) %all-to-all-start) | async-done | bytes 20512 | tf_op jit(solution)/shard_map/all_to_all | solution.py:388
  23.9 0.9 %shard_map.76 = f32[16,2,320]{2,1,0:T(2,128)} custom-call(f32[8,320]{1,0:T(8,128)S(1)} %broadcast_in_dim.29.first_wave, bf16[32,4,80]{2,1,0:T(4,128)(2,1)S(1)} %all-to-all-done.coeffs, bf16[1024,320]{1,0:T(8,128)(2,1)S(1)} %bitcast.5), custom_call_target="tpu_custom_call" | custom-call | tf_op jit(solution)/shard_map/pallas_call | solution.py:391
  (10 shorter events, 0.2 us)
Async XLA Ops:
  0.0 1.3 %copy-start = (s32[20,3200]{1,0:T(8,128)S(1)}, s32[20,3200]{1,0:T(8,128)}, u32[]{:S(2)}) copy-start(s32[20,3200]{1,0:T(8,128)} %dep_row.1) | copy-start | bytes 768004
  0.0 1.3 %copy-start.1 = (s32[20,3200]{1,0:T(8,128)S(1)}, s32[20,3200]{1,0:T(8,128)}, u32[]{:S(2)}) copy-start(s32[20,3200]{1,0:T(8,128)} %dep_col.1) | copy-start | bytes 768004
  0.0 1.3 %copy-start.2 = (bf16[20,3200]{1,0:T(8,128)(2,1)S(1)}, bf16[20,3200]{1,0:T(8,128)(2,1)}, u32[]{:S(2)}) copy-start(bf16[20,3200]{1,0:T(8,128)(2,1)} %lat_frac.1) | copy-start | bytes 384004
  0.0 1.3 %copy-start.3 = (bf16[20,3200]{1,0:T(8,128)(2,1)S(1)}, bf16[20,3200]{1,0:T(8,128)(2,1)}, u32[]{:S(2)}) copy-start(bf16[20,3200]{1,0:T(8,128)(2,1)} %lon_frac.1) | copy-start | bytes 384004
  1.6 3.0 %copy-start.5 = (s32[8]{0:T(128)S(1)}, s32[8]{0:T(128)}, u32[]{:S(2)}) copy-start(s32[8]{0:T(128)} %param.12) | copy-start | bytes 100
  1.6 10.0 %collective-permute-start = (bf16[24,3200]{1,0:T(8,128)(2,1)S(1)}, bf16[24,3200]{1,0:T(8,128)(2,1)S(1)}, u32[]{:S(2)}, u32[]{:S(2)}) collective-permute-start(bf16[24,3200]{1,0:T(8,128)(2,1)S(1)} %get-tuple-element.15), channel_id=1, source_target_pairs={{0,4},{4,8},{8,12},{12,16},{16,20},{20,24},{24,28},{28,0},{1,5},{5... | collective-permute-start | bytes 460808 | tf_op jit(solution)/shard_map/ppermute | solution.py:336
  11.7 1.7 %copy-start.4 = (bf16[1,160,320]{2,1,0:T(8,128)(2,1)S(1)}, bf16[1,160,320]{2,1,0:T(8,128)(2,1)}, u32[]{:S(2)}) copy-start(bf16[1,160,320]{2,1,0:T(8,128)(2,1)} %param.13) | copy-start | bytes 307204
  13.6 10.3 %all-to-all-start = ((bf16[32,4,80]{2,1,0:T(4,128)(2,1)}), bf16[32,4,80]{2,1,0:T(4,128)(2,1)S(1)}, u32[]{:S(2)}, u32[]{:S(2)}) async-start(bf16[32,4,80]{2,1,0:T(4,128)(2,1)} %shard_map.75), calls=%async_computation | async-start | bytes 65536 | tf_op jit(solution)/shard_map/all_to_all | solution.py:388

commit v9 on v8

--- a/solution.py
+++ b/solution.py
@@ -17,6 +17,7 @@
 ROW_BITS = 5
 INNER_AT_ONCE = 2
 RIM_AT_ONCE = 4
+SUM_AT_ONCE = 8
 
 
 def lane_gather(values, indices):
@@ -97,11 +98,30 @@
 
 
 def pack_kernel(
-    band_start, rows, dep_row, dep_col, lat_frac, lon_frac, own_out, sent_out, plan_out, held
+    band_start, grid_at, dep_row_at, dep_col_at, lat_frac_at, lon_frac_at,
+    own_out, sent_out, plan_out,
+    last_rows, dep_row, dep_col, lat_frac, lon_frac, held, joined, arrivals,
 ):
     band_rows, lon_count = dep_row.shape
+    copies = [
+        pltpu.make_async_copy(source, target, arrivals.at[at])
+        for at, (source, target) in enumerate(
+            (
+                (dep_row_at, dep_row),
+                (dep_col_at, dep_col),
+                (lat_frac_at, lat_frac),
+                (lon_frac_at, lon_frac),
+                (grid_at.at[band_rows - EDGE : band_rows], last_rows),
+            )
+        )
+    ]
+    for copy in copies:
+        copy.start()
+    for copy in copies:
+        copy.wait()
     inner = band_rows - 2 * RIM
-    fields = rows.shape[0] // band_rows * EDGE
+    slices = last_rows.shape[1]
+    fields = slices * EDGE
     first_row = band_start[0]
 
     for t in range(lon_count // LANES):
@@ -116,13 +136,14 @@
         held[slot, 1, 0:band_rows, :] = (shift + REACH).astype(jnp.float32)
         held[slot, 2, 0:band_rows, :] = lat_frac[:, cols].astype(jnp.float32)
         held[slot, 3, 0:band_rows, :] = lon_frac[:, cols].astype(jnp.float32)
-        for out, start, plan_start in (
-            (own_out, 0, 0),
-            (sent_out, rows.shape[0] - fields, band_rows - RIM),
-        ):
-            out[0:fields, cols] = rows[start : start + fields, cols]
-            out[fields:, cols] = jnp.concatenate(
-                [held[slot, at, plan_start : plan_start + RIM, :] for at in range(4)], axis=0
+        for at in range(EDGE):
+            joined[slot, at * slices : (at + 1) * slices, :] = last_rows[at, :, cols].astype(
+                jnp.float32
+            )
+        sent_out[0:fields, cols] = joined[slot].astype(jnp.bfloat16)
+        for out, to, start in ((own_out, 0, 0), (sent_out, fields, band_rows - RIM)):
+            out[to : to + 4 * RIM, cols] = jnp.concatenate(
+                [held[slot, at, start : start + RIM, :] for at in range(4)], axis=0
             ).astype(jnp.bfloat16)
         middle = [held[slot, at, RIM : RIM + inner, :] for at in range(4)]
         middle = [middle[0] * (1 << ROW_BITS) + middle[1], middle[2], middle[3]]
@@ -156,9 +177,17 @@
 
 
 def add_up(basis, values):
-    return lax.dot_general(
-        basis, values, (((1,), (1,)), ((), ())), preferred_element_type=jnp.float32
-    )
+    total = None
+    for at in range(0, basis.shape[1], SUM_AT_ONCE * LANES):
+        cols = slice(at, min(at + SUM_AT_ONCE * LANES, basis.shape[1]))
+        part = lax.dot_general(
+            basis[:, cols],
+            values[:, cols],
+            (((1,), (1,)), ((), ())),
+            preferred_element_type=jnp.float32,
+        )
+        total = part if total is None else total + part
+    return total
 
 
 def inner_kernel(grid, plans, ids, fourier_out, basis, windows, departed, *, slices):
@@ -214,15 +243,14 @@
 
         lax.fori_loop(0, groups, rows_of, 0)
     in_groups(departed.shape[1] // LANES, INNER_AT_ONCE, group_of)
-    fourier_out[...] = add_up(basis[...], departed[...])
+    fourier_out[...] = add_up(basis, departed)
 
 
 def rim_kernel(
-    arrived, own, basis, inner_fourier, fourier_out, windows, departed, *, slices, owners
+    arrived, rows, own, basis, inner_fourier, fourier_out, windows, departed, *, slices, owners
 ):
     lon_count = arrived.shape[1]
     fields = slices * EDGE
-    sides = (arrived, own)
     wanted = lax.broadcasted_iota(jnp.int32, (3 * fields, 16), 0)
     held = lax.broadcasted_iota(jnp.int32, (3 * fields, 16), 1)
     kind, rim_row = wanted // fields, wanted % fields // slices
@@ -236,11 +264,18 @@
         for t in ts:
             first, second, lane_at = cut_of(t * SPAN - REACH, lon_count)
             blocks.append(
-                [cut(ref[0:fields, first], ref[0:fields, second], lane_at) for ref in sides]
+                [
+                    cut(ref[0:fields, first], ref[0:fields, second], lane_at)
+                    for ref in (arrived, rows)
+                ]
             )
             first, second, lane_at = cut_of(t * SPAN, lon_count)
             plan_block = jnp.concatenate(
-                [cut(ref[fields:, first], ref[fields:, second], lane_at) for ref in sides], axis=0
+                [
+                    cut(arrived[fields:, first], arrived[fields:, second], lane_at),
+                    cut(own[:, first], own[:, second], lane_at),
+                ],
+                axis=0,
             )
             plan_blocks.append(jnp.dot(spread, plan_block, preferred_element_type=jnp.float32))
         for slot in range(len(ts)):
@@ -266,12 +301,12 @@
             departed[:, tile_at(t)] = result
 
     in_groups(basis.shape[1] // LANES, RIM_AT_ONCE, group_of)
-    fourier = jnp.concatenate([inner_fourier[...], add_up(basis[...], departed[...])], axis=1)
+    fourier = jnp.concatenate([inner_fourier[...], add_up(basis, departed)], axis=1)
     for at, pair in enumerate(owners):
         fourier_out[at] = fourier[4 * pair : 4 * pair + 4].astype(jnp.bfloat16)
 
 
-def legendre_kernel(first_wave, coeffs, spread_analysis, out, spread_coeffs, *, levs, slices, order):
+def legendre_kernel(first_wave, coeffs, spread_analysis, out, spread_coeffs, *, levs, slices):
     members, _, rows = coeffs.shape
     bands = members // levs
     col_count = spread_analysis.shape[1]
@@ -283,7 +318,7 @@
 
     def spread(band):
         block = jnp.concatenate(
-            [coeffs[order.index(band * levs + lev)].astype(jnp.float32) for lev in range(levs)],
+            [coeffs[band * levs + lev].astype(jnp.float32) for lev in range(levs)],
             axis=0,
         )
         block = jnp.concatenate(
@@ -319,23 +354,32 @@
     smem = pl.BlockSpec(memory_space=pltpu.SMEM)
     params = pltpu.CompilerParams(vmem_limit_bytes=48 * 2**20)
 
-    rows = grid.transpose(1, 0, 2).reshape(band_rows * slices, lon_count)
-    rim_shape = jax.ShapeDtypeStruct((fields + 4 * RIM, lon_count), jnp.bfloat16)
+    by_row = grid.transpose(1, 0, 2)
     own_rim, sent_rim, plans = pl.pallas_call(
         pack_kernel,
         out_shape=(
-            rim_shape,
-            rim_shape,
+            jax.ShapeDtypeStruct((4 * RIM, lon_count), jnp.bfloat16),
+            jax.ShapeDtypeStruct((fields + 4 * RIM, lon_count), jnp.bfloat16),
             jax.ShapeDtypeStruct((3 * inner, lon_count), jnp.bfloat16),
         ),
-        in_specs=[smem] + [vmem] * 5,
+        in_specs=[smem] + [pl.BlockSpec(memory_space=pl.ANY)] * 5,
         out_specs=(vmem,) * 3,
-        scratch_shapes=[pltpu.VMEM((5, 4, held_rows, LANES), jnp.float32)],
-        compiler_params=params,
-    )(band_start, rows, dep_row, dep_col, lat_frac, lon_frac)
+        scratch_shapes=[
+            pltpu.VMEM((EDGE, slices, lon_count), jnp.bfloat16),
+            pltpu.VMEM((band_rows, lon_count), jnp.int32),
+            pltpu.VMEM((band_rows, lon_count), jnp.int32),
+            pltpu.VMEM((band_rows, lon_count), jnp.bfloat16),
+            pltpu.VMEM((band_rows, lon_count), jnp.bfloat16),
+            pltpu.VMEM((5, 4, held_rows, LANES), jnp.float32),
+            pltpu.VMEM((5, fields, LANES), jnp.float32),
+            pltpu.SemaphoreType.DMA((5,)),
+        ],
+        compiler_params=pltpu.CompilerParams(vmem_limit_bytes=127 * 2**19),
+    )(band_start, by_row, dep_row, dep_col, lat_frac, lon_frac)
     arrived_rim = lax.ppermute(sent_rim, "lat", [(i, (i + 1) % bands) for i in range(bands)])
 
-    plans, ids = lax.optimization_barrier((plans, pair_ids))
+    plans, ids, by_row = lax.optimization_barrier((plans, pair_ids, by_row))
+    rows = by_row.reshape(band_rows * slices, lon_count)
     ids = jnp.broadcast_to(ids.astype(jnp.float32)[:, None], (pairs, LANES))
     inner_fourier, basis = pl.pallas_call(
         functools.partial(inner_kernel, slices=slices),
@@ -355,20 +399,19 @@
 
     held_coeffs = slices * band_rows
     members = bands * levs
-    order = [(at + members // 2) % members for at in range(members)]
     fourier = pl.pallas_call(
         functools.partial(
-            rim_kernel, slices=slices, owners=[member // levs for member in order]
+            rim_kernel, slices=slices, owners=[member // levs for member in range(members)]
         ),
         out_shape=jax.ShapeDtypeStruct((members, 4, held_coeffs), jnp.bfloat16),
-        in_specs=[vmem] * 4,
+        in_specs=[vmem] * 5,
         out_specs=vmem,
         scratch_shapes=[
             pltpu.VMEM((RIM_AT_ONCE, 2 * fields, LANES), jnp.float32),
             pltpu.VMEM((fields, windows * LANES), jnp.bfloat16),
         ],
         compiler_params=params,
-    )(arrived_rim, own_rim, basis, inner_fourier)
+    )(arrived_rim, rows, own_rim, basis, inner_fourier)
     fourier, analysis, late_ids = lax.optimization_barrier((fourier, analysis, pair_ids))
 
     values = analysis[0].reshape(bands, band_rows, col_count)
@@ -386,10 +429,10 @@
     first_wave = jnp.broadcast_to(first_wave[None, :], (8, col_count))
 
     coeffs = lax.all_to_all(
-        fourier, ("lat", "lev"), split_axis=0, concat_axis=0, axis_index_groups=[order], tiled=True
+        fourier, ("lat", "lev"), split_axis=0, concat_axis=0, tiled=True
     )
     out = pl.pallas_call(
-        functools.partial(legendre_kernel, levs=levs, slices=slices, order=order),
+        functools.partial(legendre_kernel, levs=levs, slices=slices),
         out_shape=jax.ShapeDtypeStruct((levs * slices, 2, col_count), jnp.float32),
         in_specs=[vmem] * 3,
         out_specs=vmem,

time: 24.9 us -> 25.9 us (1.040)
  Pallas kernels: 6.39 us -> 8.35 us
  waiting for transfers between devices: 8.73 us -> 7.75 us
    pallas_call x1, Pallas kernels: 0.32 us -> 2.32 us  [shards(): pl.pallas_call(pack_kernel, out_shape=(jax.ShapeDtypeStruct((4 * RIM, lon...]
    ppermute x1, waiting for transfers between devices: 3.48 us -> 2.49 us  [shards(): lax.ppermute(sent_rim, 'lat', [(i, (i + 1) % bands) for i in range(bands)])]
  transfers between devices with their start and end apart: 2 -> 2, of which waited for: 2 -> 2; matrix products, arithmetic and copies ran while one was open for 6% -> 10% of each run, Pallas kernels for 14% -> 13%
where the time goes in v9:
time: 25.9 us; the launch traced here: 25.7 us
  Pallas kernels  8.35 us (32%)
  waiting for transfers between devices  7.75 us (30%)
  starting transfers between devices  6.06 us (23%)
  local copies, waits for them, and re-layouts  2.66 us (10%)
  between operations  0.75 us (3%)
    all_to_all x1, waiting for transfers between devices, shards(): lax.all_to_all(fourier, ('lat', 'lev'), split_axis=0, concat_axis=0, tile...  5.26 us
    pallas_call x1, Pallas kernels, shards(): pl.pallas_call(functools.partial(inner_kernel, slices=slices), out_shape=...  3.43 us
    all_to_all x1, starting transfers between devices, shards(): lax.all_to_all(fourier, ('lat', 'lev'), split_axis=0, concat_axis=0, tile...  3.04 us
    ppermute x1, starting transfers between devices, shards(): lax.ppermute(sent_rim, 'lat', [(i, (i + 1) % bands) for i in range(bands)])  3.02 us
    ppermute x1, waiting for transfers between devices, shards(): lax.ppermute(sent_rim, 'lat', [(i, (i + 1) % bands) for i in range(bands)])  2.49 us
    pallas_call x1, Pallas kernels, shards(): pl.pallas_call(pack_kernel, out_shape=(jax.ShapeDtypeStruct((4 * RIM, lon...  2.32 us
    pallas_call x1, Pallas kernels, shards(): pl.pallas_call(functools.partial(rim_kernel, slices=slices, owners=[membe...  1.72 us
    reshape x1, local copies, waits for them, and re-layouts, shards(): rows = by_row.reshape(band_rows * slices, lon_count)  1.2 us
  transfers between devices with their start and end apart: 2, of which 2 were waited for; matrix products, arithmetic and copies ran while one was open for 10% of the time, Pallas kernels for 13%

profile of v9, /device:TPU:0, one launch (start us, length us, event | category | flops | bytes accessed | tf_op | source)
XLA Modules:
  0.0 25.7 jit_solution(9301720883456042232)
XLA Ops:
  0.0 2.3 %shard_map.73 = (bf16[8,3200]{1,0:T(8,128)(2,1)}, bf16[24,3200]{1,0:T(8,128)(2,1)}, bf16[48,3200]{1,0:T(8,128)(2,1)}) custom-call(s32[1]{0:T(128)} %bitcast.band_start, bf16[20,4,3200]{2,1,0:T(4,128)(2,1)} %bitcast.6, s32[20,3200]{1,0:T(8,128)} %dep_row_at.1, s32[20,3200]{1,0:T(8,128)} %dep_col_at.1, bf16[20,3200]{1,0:T(8,128)(2,1)} %lat_frac_at.1, ...), custom_call_target="tpu_custom_call" | custom-call | tf_op jit(solution)/shard_map/pallas_call | solution.py:358
  2.3 3.0 %collective-permute-start = (bf16[24,3200]{1,0:T(8,128)(2,1)}, bf16[24,3200]{1,0:T(8,128)(2,1)S(1)}, u32[]{:S(2)}, u32[]{:S(2)}) collective-permute-start(bf16[24,3200]{1,0:T(8,128)(2,1)} %get-tuple-element.16), channel_id=1, source_target_pairs={{0,4},{4,8},{8,12},{12,16},{16,20},{20,24},{24,28},{28,0},{1,5},{5... | collective-permute-start | bytes 460808 | tf_op jit(solution)/shard_map/ppermute | solution.py:379
  5.3 0.0 copy-start.3
  5.3 0.0 copy-start
  5.3 1.2 %reshape.17.grid.rows = bf16[80,3200]{1,0:T(8,128)(2,1)S(1)} reshape(bf16[20,4,3200]{2,1,0:T(4,128)(2,1)} %bitcast.7) | data formatting | bytes 1024000 | tf_op jit(solution)/shard_map/reshape | solution.py:382
  6.6 0.0 copy-done.3
  6.6 0.1 broadcast_in_dim.26.ids
  6.6 0.0 copy-done
  6.7 0.0 copy-start.1
  6.7 3.4 %shard_map.74 = (f32[32,64]{1,0:T(8,128)S(1)}, bf16[32,3712]{1,0:T(8,128)(2,1)S(1)}) custom-call(bf16[80,3200]{1,0:T(8,128)(2,1)S(1)} %reshape.17.grid.rows, bf16[48,3200]{1,0:T(8,128)(2,1)S(1)} %copy-done, f32[8,128]{1,0:T(8,128)S(1)} %broadcast_in_dim.26.ids), custom_call_target="tpu_custom_call" | custom-call | flops 100000000 | bytes 2000000 | tf_op jit(solution)/shard_map/pallas_call | solution.py:384
  10.1 2.5 %collective-permute-done.arrived = bf16[24,3200]{1,0:T(8,128)(2,1)S(1)} collective-permute-done((bf16[24,3200]{1,0:T(8,128)(2,1)}, bf16[24,3200]{1,0:T(8,128)(2,1)S(1)}, u32[]{:S(2)}, u32[]{:S(2)}) %collective-permute-start) | collective-permute-done | bytes 153632 | tf_op jit(solution)/shard_map/ppermute | solution.py:379
  12.6 0.0 copy-done.1
  12.6 0.0 copy-start.2
  12.6 1.7 %shard_map.75 = bf16[32,4,80]{2,1,0:T(4,128)(2,1)} custom-call(bf16[24,3200]{1,0:T(8,128)(2,1)S(1)} %collective-permute-done.arrived, bf16[80,3200]{1,0:T(8,128)(2,1)S(1)} %reshape.17.grid.rows, bf16[8,3200]{1,0:T(8,128)(2,1)S(1)} %copy-done.1, bf16[32,3712]{1,0:T(8,128)(2,1)S(1)} %get-tuple-element.22.basis, f32[32,64]{1,0:T(8,128)S(1)} %get-tuple-element.23.inner_fourier), custom_call_target="tpu_custom_call" | custom-call | tf_op jit(solution)/shard_map/pallas_call | solution.py:402
  14.3 0.0 copy-done.2
  14.4 0.1 slice_maximum_fusion
  14.5 3.0 %all-to-all-start = ((bf16[32,4,80]{2,1,0:T(4,128)(2,1)}), bf16[32,4,80]{2,1,0:T(4,128)(2,1)S(1)}, u32[]{:S(2)}, u32[]{:S(2)}) async-start(bf16[32,4,80]{2,1,0:T(4,128)(2,1)} %shard_map.75), calls=%async_computation | async-start | bytes 65536 | tf_op jit(solution)/shard_map/all_to_all | solution.py:431
  17.5 0.6 %dynamic_slice.3 = s32[1]{0:T(128)} dynamic-slice(s32[8]{0:T(128)S(1)} %copy-done.3, s32[]{:T(128)S(6)} %select_n.11), dynamic_slice_sizes={1} | dynamic-slice | bytes 12 | tf_op jit(solution)/shard_map/dynamic_slice | solution.py:426
  18.9 0.6 %concatenate.9 = bf16[8,128,320]{2,1,0:T(8,128)(2,1)S(1)} concatenate(bf16[8,16,320]{2,1,0:T(8,128)(2,1)S(1)} %slice.41, bf16[8,16,320]{2,1,0:T(8,128)(2,1)S(1)} %slice.41, bf16[8,16,320]{2,1,0:T(8,128)(2,1)S(1)} %slice.41, bf16[8,16,320]{2,1,0:T(8,128)(2,1)S(1)} %slice.41, bf16[8,1,320]{2,1,0:T(2,128)(2,1)S(1)} %get-tuple-element.30, bf16[8,1,320]{2,1,0:T(2,128)(2,1)S(1)} %get-tuple-element.30, ...), dimensions={1} | concatenate | bytes 1310720 | tf_op jit(solution)/shard_map/concatenate | solution.py:424
  19.5 5.3 %all-to-all-done.coeffs = bf16[32,4,80]{2,1,0:T(4,128)(2,1)S(1)} async-done(((bf16[32,4,80]{2,1,0:T(4,128)(2,1)}), bf16[32,4,80]{2,1,0:T(4,128)(2,1)S(1)}, u32[]{:S(2)}, u32[]{:S(2)}) %all-to-all-start) | async-done | bytes 20512 | tf_op jit(solution)/shard_map/all_to_all | solution.py:431
  24.8 0.9 %shard_map.76 = f32[16,2,320]{2,1,0:T(2,128)} custom-call(f32[8,320]{1,0:T(8,128)S(1)} %broadcast_in_dim.29.first_wave, bf16[32,4,80]{2,1,0:T(4,128)(2,1)S(1)} %all-to-all-done.coeffs, bf16[1024,320]{1,0:T(8,128)(2,1)S(1)} %bitcast.5), custom_call_target="tpu_custom_call" | custom-call | tf_op jit(solution)/shard_map/pallas_call | solution.py:434
  (10 shorter events, 0.2 us)
Async XLA Ops:
  2.3 10.2 %collective-permute-start = (bf16[24,3200]{1,0:T(8,128)(2,1)}, bf16[24,3200]{1,0:T(8,128)(2,1)S(1)}, u32[]{:S(2)}, u32[]{:S(2)}) collective-permute-start(bf16[24,3200]{1,0:T(8,128)(2,1)} %get-tuple-element.16), channel_id=1, source_target_pairs={{0,4},{4,8},{8,12},{12,16},{16,20},{20,24},{24,28},{28,0},{1,5},{5... | collective-permute-start | bytes 460808 | tf_op jit(solution)/shard_map/ppermute | solution.py:379
  5.3 1.2 %copy-start.3 = (s32[8]{0:T(128)S(1)}, s32[8]{0:T(128)}, u32[]{:S(2)}) copy-start(s32[8]{0:T(128)} %param.12) | copy-start | bytes 100
  5.3 1.3 %copy-start = (bf16[48,3200]{1,0:T(8,128)(2,1)S(1)}, bf16[48,3200]{1,0:T(8,128)(2,1)}, u32[]{:S(2)}) copy-start(bf16[48,3200]{1,0:T(8,128)(2,1)} %get-tuple-element.20.plans) | copy-start | bytes 921604
  6.7 5.9 %copy-start.1 = (bf16[8,3200]{1,0:T(8,128)(2,1)S(1)}, bf16[8,3200]{1,0:T(8,128)(2,1)}, u32[]{:S(2)}) copy-start(bf16[8,3200]{1,0:T(8,128)(2,1)} %get-tuple-element.19.own) | copy-start | bytes 153604
  12.6 1.7 %copy-start.2 = (bf16[1,160,320]{2,1,0:T(8,128)(2,1)S(1)}, bf16[1,160,320]{2,1,0:T(8,128)(2,1)}, u32[]{:S(2)}) copy-start(bf16[1,160,320]{2,1,0:T(8,128)(2,1)} %param.13) | copy-start | bytes 307204
  14.5 10.3 %all-to-all-start = ((bf16[32,4,80]{2,1,0:T(4,128)(2,1)}), bf16[32,4,80]{2,1,0:T(4,128)(2,1)S(1)}, u32[]{:S(2)}, u32[]{:S(2)}) async-start(bf16[32,4,80]{2,1,0:T(4,128)(2,1)} %shard_map.75), calls=%async_computation | async-start | bytes 65536 | tf_op jit(solution)/shard_map/all_to_all | solution.py:431

commit v10 on v8

--- a/solution.py
+++ b/solution.py
@@ -88,7 +88,7 @@
         + weights[2] * west_high
         + weights[3] * east_high
     )
-    return departed.astype(jnp.bfloat16)
+    return departed
 
 
 def in_groups(count, at_once, group):
@@ -101,7 +101,8 @@
 ):
     band_rows, lon_count = dep_row.shape
     inner = band_rows - 2 * RIM
-    fields = rows.shape[0] // band_rows * EDGE
+    slices = rows.shape[0] // band_rows
+    rim = RIM * slices
     first_row = band_start[0]
 
     for t in range(lon_count // LANES):
@@ -116,13 +117,12 @@
         held[slot, 1, 0:band_rows, :] = (shift + REACH).astype(jnp.float32)
         held[slot, 2, 0:band_rows, :] = lat_frac[:, cols].astype(jnp.float32)
         held[slot, 3, 0:band_rows, :] = lon_frac[:, cols].astype(jnp.float32)
-        for out, start, plan_start in (
-            (own_out, 0, 0),
-            (sent_out, rows.shape[0] - fields, band_rows - RIM),
+        for out, first_of, start in (
+            (own_out, jnp.zeros((rim, LANES), jnp.float32), 0),
+            (sent_out, rows[rows.shape[0] - 2 * rim :, cols].astype(jnp.float32)[rim:], band_rows - RIM),
         ):
-            out[0:fields, cols] = rows[start : start + fields, cols]
-            out[fields:, cols] = jnp.concatenate(
-                [held[slot, at, plan_start : plan_start + RIM, :] for at in range(4)], axis=0
+            out[:, cols] = jnp.concatenate(
+                [first_of] + [held[slot, at, start : start + RIM, :] for at in range(4)], axis=0
             ).astype(jnp.bfloat16)
         middle = [held[slot, at, RIM : RIM + inner, :] for at in range(4)]
         middle = [middle[0] * (1 << ROW_BITS) + middle[1], middle[2], middle[3]]
@@ -155,25 +155,51 @@
     return jnp.where(taken, angle * series, 0.0).astype(jnp.bfloat16)
 
 
+def rim_spread(slices):
+    fields = EDGE * slices
+    shape = (3 * fields, 2 * RIM * (slices + 4))
+    wanted = lax.broadcasted_iota(jnp.int32, shape, 0)
+    held = lax.broadcasted_iota(jnp.int32, shape, 1)
+    kind, rim_row = wanted // fields, wanted % fields // slices
+    base = rim_row // RIM * RIM * (slices + 4) + RIM * slices + rim_row % RIM
+    spread = jnp.where((kind == 0) & (held == base), float(1 << ROW_BITS), 0.0)
+    spread += jnp.where(held == base + RIM * (kind + 1), 1.0, 0.0)
+    return spread.astype(jnp.bfloat16)
+
+
+def rim_plan(spread, packed):
+    plan = jnp.dot(spread, jnp.concatenate(packed, axis=0), preferred_element_type=jnp.float32)
+    fields = spread.shape[0] // 3
+    code, lat_weight, lon_weight = [plan[fields * at : fields * (at + 1)] for at in range(3)]
+    return lane_plan(code), corner_weights(lat_weight, lon_weight)
+
+
 def add_up(basis, values):
     return lax.dot_general(
         basis, values, (((1,), (1,)), ((), ())), preferred_element_type=jnp.float32
     )
 
 
-def inner_kernel(grid, plans, ids, fourier_out, basis, windows, departed, *, slices):
+def inner_kernel(
+    grid, plans, sent, ids, fourier_out, basis, windows, departed, last_departed, *, slices
+):
     lon_count = grid.shape[1]
     inner = plans.shape[0] // 3
+    rim = RIM * slices
+    spread = rim_spread(slices)
+    for slot in range(INNER_AT_ONCE):
+        windows[slot, grid.shape[0] :, :] = jnp.zeros((rim, LANES), jnp.float32)
     groups = ids.shape[0] // 4
     few = groups <= 4
     waves = [waves_of(ids, at) for at in range(groups if few else 0)]
 
     def group_of(ts):
-        blocks, plan_blocks = [], []
+        blocks, plan_blocks, last_plans = [], [], []
         for t in ts:
             first, second, lane_at = cut_of(t * SPAN - REACH, lon_count)
             blocks.append(cut(grid[:, first], grid[:, second], lane_at).astype(jnp.float32))
             first, second, lane_at = cut_of(t * SPAN, lon_count)
+            last_plans.append(cut(sent[:, first], sent[:, second], lane_at))
             plan_blocks.append(
                 [
                     cut(
@@ -185,7 +211,7 @@
                 ]
             )
         for slot, block in enumerate(blocks):
-            windows[slot] = block
+            windows[slot, 0 : grid.shape[0], :] = block
         results = []
         for slot, (code, lat_weight, lon_weight) in enumerate(plan_blocks):
             plan = lane_plan(code)
@@ -198,8 +224,25 @@
                     for position in range(2 * RIM + 1)
                 ]
                 results.append((ts[slot], f, interpolate(sources, plan, weights)))
+        two = [0, len(ts) - 1]
+        last_rows = grid.shape[0] - slices * EDGE
+        sources = [
+            jnp.concatenate(
+                [
+                    windows[slot, last_rows + slices * position : last_rows + slices * position + rim]
+                    for slot in two
+                ],
+                axis=0,
+            ).astype(jnp.bfloat16)
+            for position in range(2 * RIM + 1)
+        ]
+        last = interpolate(sources, *rim_plan(spread, [last_plans[slot] for slot in two]))
         for t, f, result in results:
-            departed[f * inner : (f + 1) * inner, tile_at(t)] = result
+            departed[f * inner : (f + 1) * inner, tile_at(t)] = result.astype(jnp.bfloat16)
+        for slot, t in enumerate(ts):
+            last_departed[:, tile_at(t)] = jnp.concatenate(
+                [last[rim * slot : rim * (slot + 1)], jnp.zeros((rim, LANES), jnp.float32)], axis=0
+            ).astype(jnp.bfloat16)
         for t in ts if few else ():
             for at, wave in enumerate(waves):
                 basis[16 * at : 16 * at + 16, tile_at(t)] = basis_tile(t, wave, lon_count)
@@ -214,68 +257,69 @@
 
         lax.fori_loop(0, groups, rows_of, 0)
     in_groups(departed.shape[1] // LANES, INNER_AT_ONCE, group_of)
-    fourier_out[...] = add_up(basis[...], departed[...])
+    fourier_out[...] = jnp.concatenate(
+        [add_up(basis[...], departed[...]), add_up(basis[...], last_departed[...])[:, :rim]], axis=1
+    )
 
 
 def rim_kernel(
-    arrived, own, basis, inner_fourier, fourier_out, windows, departed, *, slices, owners
+    arrived, rows, own, basis, inner_fourier, fourier_out, windows, departed, *, slices, levs
 ):
     lon_count = arrived.shape[1]
-    fields = slices * EDGE
-    sides = (arrived, own)
-    wanted = lax.broadcasted_iota(jnp.int32, (3 * fields, 16), 0)
-    held = lax.broadcasted_iota(jnp.int32, (3 * fields, 16), 1)
-    kind, rim_row = wanted // fields, wanted % fields // slices
-    base = rim_row // RIM * 8 + rim_row % RIM
-    spread = jnp.where((kind == 0) & (held == base), float(1 << ROW_BITS), 0.0)
-    spread += jnp.where(held == base + RIM * (kind + 1), 1.0, 0.0)
-    spread = spread.astype(jnp.bfloat16)
+    rim, fields = RIM * slices, EDGE * slices
+    spread = rim_spread(slices)
+    sublane = lax.broadcasted_iota(jnp.int32, (rim, LANES), 0)
+
+    def source(slot, position):
+        start = slices * position
+        before = jnp.zeros((rim, LANES), jnp.float32)
+        if position == 2 * RIM - 1:
+            before = jnp.where(sublane < slices, before, windows[slot, slices : slices + rim, :])
+        elif position == 2 * RIM:
+            before = windows[slot, rim : 2 * rim, :]
+        return jnp.concatenate([before, windows[slot, start : start + rim, :]], axis=0).astype(
+            jnp.bfloat16
+        )
 
     def group_of(ts):
         blocks, plan_blocks = [], []
         for t in ts:
             first, second, lane_at = cut_of(t * SPAN - REACH, lon_count)
             blocks.append(
-                [cut(ref[0:fields, first], ref[0:fields, second], lane_at) for ref in sides]
+                [
+                    cut(arrived[:, first], arrived[:, second], lane_at).astype(jnp.float32)[:rim],
+                    cut(rows[0:fields, first], rows[0:fields, second], lane_at).astype(jnp.float32),
+                ]
             )
             first, second, lane_at = cut_of(t * SPAN, lon_count)
-            plan_block = jnp.concatenate(
-                [cut(ref[fields:, first], ref[fields:, second], lane_at) for ref in sides], axis=0
+            plan_blocks.append(
+                [cut(ref[:, first], ref[:, second], lane_at) for ref in (arrived, own)]
             )
-            plan_blocks.append(jnp.dot(spread, plan_block, preferred_element_type=jnp.float32))
-        for slot in range(len(ts)):
-            for side in range(2):
-                windows[slot, fields * side : fields * (side + 1), :] = blocks[slot][side].astype(
-                    jnp.float32
-                )
-        results = []
-        for slot in range(len(ts)):
-            code, lat_weight, lon_weight = [
-                plan_blocks[slot][fields * at : fields * (at + 1)] for at in range(3)
-            ]
-            sources = [
-                windows[slot, slices * position : slices * position + fields, :].astype(
-                    jnp.bfloat16
-                )
-                for position in range(2 * RIM + 1)
-            ]
-            results.append(
-                interpolate(sources, lane_plan(code), corner_weights(lat_weight, lon_weight))
+        for slot, (before, first_rows) in enumerate(blocks):
+            windows[slot, 0:rim, :] = before
+            windows[slot, rim : rim + fields, :] = first_rows
+        results = [
+            interpolate(
+                [source(slot, position) for position in range(2 * RIM + 1)],
+                *rim_plan(spread, plan_blocks[slot]),
             )
+            for slot in range(len(ts))
+        ]
         for t, result in zip(ts, results):
-            departed[:, tile_at(t)] = result
+            departed[:, tile_at(t)] = result.astype(jnp.bfloat16)
 
     in_groups(basis.shape[1] // LANES, RIM_AT_ONCE, group_of)
     fourier = jnp.concatenate([inner_fourier[...], add_up(basis[...], departed[...])], axis=1)
-    for at, pair in enumerate(owners):
+    for at in range(fourier_out.shape[0]):
+        pair = at // levs
         fourier_out[at] = fourier[4 * pair : 4 * pair + 4].astype(jnp.bfloat16)
 
 
-def legendre_kernel(first_wave, coeffs, spread_analysis, out, spread_coeffs, *, levs, slices, order):
+def legendre_kernel(first_wave, coeffs, spread_analysis, out, spread_coeffs, *, levs, slices):
     members, _, rows = coeffs.shape
     bands = members // levs
     col_count = spread_analysis.shape[1]
-    inner = rows // slices - EDGE
+    inner = rows // slices - EDGE - RIM
     column = lax.broadcasted_iota(jnp.int32, (1, LANES), 1)
     rim_at = column - inner * slices
     slice_of = jnp.where(rim_at < 0, column // inner, rim_at % slices)
@@ -283,7 +327,7 @@
 
     def spread(band):
         block = jnp.concatenate(
-            [coeffs[order.index(band * levs + lev)].astype(jnp.float32) for lev in range(levs)],
+            [coeffs[band * levs + lev].astype(jnp.float32) for lev in range(levs)],
             axis=0,
         )
         block = jnp.concatenate(
@@ -320,7 +364,7 @@
     params = pltpu.CompilerParams(vmem_limit_bytes=48 * 2**20)
 
     rows = grid.transpose(1, 0, 2).reshape(band_rows * slices, lon_count)
-    rim_shape = jax.ShapeDtypeStruct((fields + 4 * RIM, lon_count), jnp.bfloat16)
+    rim_shape = jax.ShapeDtypeStruct((RIM * (slices + 4), lon_count), jnp.bfloat16)
     own_rim, sent_rim, plans = pl.pallas_call(
         pack_kernel,
         out_shape=(
@@ -340,41 +384,38 @@
     inner_fourier, basis = pl.pallas_call(
         functools.partial(inner_kernel, slices=slices),
         out_shape=(
-            jax.ShapeDtypeStruct((4 * pairs, slices * inner), jnp.float32),
+            jax.ShapeDtypeStruct((4 * pairs, slices * (inner + RIM)), jnp.float32),
             jax.ShapeDtypeStruct((4 * pairs, windows * LANES), jnp.bfloat16),
         ),
-        in_specs=[vmem] * 3,
+        in_specs=[vmem] * 4,
         out_specs=(vmem,) * 2,
         scratch_shapes=[
-            pltpu.VMEM((INNER_AT_ONCE, band_rows * slices, LANES), jnp.float32),
+            pltpu.VMEM((INNER_AT_ONCE, (band_rows + RIM) * slices, LANES), jnp.float32),
             pltpu.VMEM((slices * inner, windows * LANES), jnp.bfloat16),
+            pltpu.VMEM((2 * RIM * slices, windows * LANES), jnp.bfloat16),
         ],
         compiler_params=params,
         cost_estimate=pl.CostEstimate(flops=100_000_000, bytes_accessed=2_000_000, transcendentals=0),
-    )(rows, plans, ids)
-
-    held_coeffs = slices * band_rows
-    members = bands * levs
-    order = [(at + members // 2) % members for at in range(members)]
+    )(rows, plans, sent_rim, ids)
+
+    held_coeffs = slices * (band_rows + RIM)
     fourier = pl.pallas_call(
-        functools.partial(
-            rim_kernel, slices=slices, owners=[member // levs for member in order]
-        ),
-        out_shape=jax.ShapeDtypeStruct((members, 4, held_coeffs), jnp.bfloat16),
-        in_specs=[vmem] * 4,
+        functools.partial(rim_kernel, slices=slices, levs=levs),
+        out_shape=jax.ShapeDtypeStruct((bands * levs, 4, held_coeffs), jnp.bfloat16),
+        in_specs=[vmem] * 5,
         out_specs=vmem,
         scratch_shapes=[
-            pltpu.VMEM((RIM_AT_ONCE, 2 * fields, LANES), jnp.float32),
+            pltpu.VMEM((RIM_AT_ONCE, (RIM + EDGE) * slices, LANES), jnp.float32),
             pltpu.VMEM((fields, windows * LANES), jnp.bfloat16),
         ],
         compiler_params=params,
-    )(arrived_rim, own_rim, basis, inner_fourier)
+    )(arrived_rim, rows, own_rim, basis, inner_fourier)
     fourier, analysis, late_ids = lax.optimization_barrier((fourier, analysis, pair_ids))
 
     values = analysis[0].reshape(bands, band_rows, col_count)
     before = jnp.roll(values[:, band_rows - RIM :], 1, axis=0)
     spread_rows = [values[:, RIM : RIM + inner]] * slices
-    for rim in (before, values[:, :RIM]):
+    for rim in (values[:, band_rows - RIM :], before, values[:, :RIM]):
         for row in range(RIM):
             spread_rows += [rim[:, row : row + 1]] * slices
     spread_rows.append(jnp.zeros((bands, LANES - held_coeffs, col_count), jnp.bfloat16))
@@ -386,10 +427,10 @@
     first_wave = jnp.broadcast_to(first_wave[None, :], (8, col_count))
 
     coeffs = lax.all_to_all(
-        fourier, ("lat", "lev"), split_axis=0, concat_axis=0, axis_index_groups=[order], tiled=True
+        fourier, ("lat", "lev"), split_axis=0, concat_axis=0, tiled=True
     )
     out = pl.pallas_call(
-        functools.partial(legendre_kernel, levs=levs, slices=slices, order=order),
+        functools.partial(legendre_kernel, levs=levs, slices=slices),
         out_shape=jax.ShapeDtypeStruct((levs * slices, 2, col_count), jnp.float32),
         in_specs=[vmem] * 3,
         out_specs=vmem,

time: 24.9 us -> 23.9 us (0.960)
  waiting for transfers between devices: 8.73 us -> 7.08 us
  Pallas kernels: 6.39 us -> 6.82 us
    ppermute x1, waiting for transfers between devices: 3.48 us -> 1.96 us  [shards(): lax.ppermute(sent_rim, 'lat', [(i, (i + 1) % bands) for i in range(bands)])]
    pallas_call x1, Pallas kernels: 3.46 us -> 3.88 us  [shards(): pl.pallas_call(functools.partial(inner_kernel, slices=slices), out_shape=...]
  transfers between devices with their start and end apart: 2 -> 2, of which waited for: 2 -> 2; matrix products, arithmetic and copies ran while one was open for 6% -> 6% of each run, Pallas kernels for 14% -> 16%
where the time goes in v10:
time: 23.9 us; the launch traced here: 23.8 us
  waiting for transfers between devices  7.08 us (30%)
  Pallas kernels  6.82 us (29%)
  starting transfers between devices  6.1 us (26%)
  local copies, waits for them, and re-layouts  2.85 us (12%)
  between operations  0.77 us (3%)
    all_to_all x1, waiting for transfers between devices, shards(): lax.all_to_all(fourier, ('lat', 'lev'), split_axis=0, concat_axis=0, tile...  5.12 us
    pallas_call x1, Pallas kernels, shards(): pl.pallas_call(functools.partial(inner_kernel, slices=slices), out_shape=...  3.88 us
    all_to_all x1, starting transfers between devices, shards(): lax.all_to_all(fourier, ('lat', 'lev'), split_axis=0, concat_axis=0, tile...  3.08 us
    ppermute x1, starting transfers between devices, shards(): lax.ppermute(sent_rim, 'lat', [(i, (i + 1) % bands) for i in range(bands)])  3.02 us
    ppermute x1, waiting for transfers between devices, shards(): lax.ppermute(sent_rim, 'lat', [(i, (i + 1) % bands) for i in range(bands)])  1.96 us
    pallas_call x1, Pallas kernels, shards(): pl.pallas_call(functools.partial(rim_kernel, slices=slices, levs=levs), o...  1.72 us
    reshape x1, local copies, waits for them, and re-layouts, shards(): rows = grid.transpose(1, 0, 2).reshape(band_rows * slices, lon_count)  1.23 us
    pallas_call x1, Pallas kernels, shards(): pl.pallas_call(functools.partial(legendre_kernel, levs=levs, slices=slice...  0.89 us
  transfers between devices with their start and end apart: 2, of which 2 were waited for; matrix products, arithmetic and copies ran while one was open for 6% of the time, Pallas kernels for 16%

profile of v10, /device:TPU:0, one launch (start us, length us, event | category | flops | bytes accessed | tf_op | source)
XLA Modules:
  0.0 23.8 jit_solution(6827744105148311702)
XLA Ops:
  0.0 0.0 copy-start
  0.0 0.0 copy-start.1
  0.0 0.0 copy-start.2
  0.0 0.0 copy-start.3
  0.0 1.2 %reshape.17.rows.grid = bf16[80,3200]{1,0:T(8,128)(2,1)S(1)} reshape(bf16[20,4,3200]{2,1,0:T(4,128)(2,1)} %bitcast.6) | data formatting | bytes 1024000 | tf_op jit(solution)/shard_map/reshape | solution.py:366
  1.2 0.0 copy-done
  1.3 0.0 copy-done.1
  1.3 0.0 copy-done.2
  1.3 0.0 copy-done.3
  1.3 0.3 %shard_map.73 = (bf16[16,3200]{1,0:T(8,128)(2,1)S(1)}, bf16[16,3200]{1,0:T(8,128)(2,1)S(1)}, bf16[48,3200]{1,0:T(8,128)(2,1)S(1)}) custom-call(s32[1]{0:T(128)} %bitcast.band_start, bf16[80,3200]{1,0:T(8,128)(2,1)S(1)} %reshape.17.rows.grid, s32[20,3200]{1,0:T(8,128)S(1)} %copy-done, s32[20,3200]{1,0:T(8,128)S(1)} %copy-done.1, ...), custom_call_target="tpu_custom_call" | custom-call | tf_op jit(solution)/shard_map/pallas_call | solution.py:368
  1.6 0.0 copy-start.5
  1.6 3.0 %collective-permute-start = (bf16[16,3200]{1,0:T(8,128)(2,1)S(1)}, bf16[16,3200]{1,0:T(8,128)(2,1)S(1)}, u32[]{:S(2)}, u32[]{:S(2)}) collective-permute-start(bf16[16,3200]{1,0:T(8,128)(2,1)S(1)} %get-tuple-element.15.sent), channel_id=1, source_target_pairs={{0,4},{4,8},{8,12},{12,16},{16,20},{20,24},{24,28},{28,0},{1,5},{5... | collective-permute-start | bytes 307208 | tf_op jit(solution)/shard_map/ppermute | solution.py:380
  4.7 0.0 copy-done.5
  4.7 0.1 broadcast_in_dim.26.ids
  4.7 3.9 %shard_map.74 = (f32[32,72]{1,0:T(8,128)S(1)}, bf16[32,3712]{1,0:T(8,128)(2,1)S(1)}) custom-call(bf16[80,3200]{1,0:T(8,128)(2,1)S(1)} %reshape.17.rows.grid, bf16[48,3200]{1,0:T(8,128)(2,1)S(1)} %get-tuple-element.18.plans, bf16[16,3200]{1,0:T(8,128)(2,1)S(1)} %get-tuple-element.15.sent, f32[8,128]{1,0:T(8,128)S(1)} %broadcast_in_dim.26.ids), custom_call_target="tpu_custom_call" | custom-call | flops 100000000 | bytes 2000000 | tf_op jit(solution)/shard_map/pallas_call | solution.py:384
  8.6 2.0 %collective-permute-done.arrived = bf16[16,3200]{1,0:T(8,128)(2,1)S(1)} collective-permute-done((bf16[16,3200]{1,0:T(8,128)(2,1)S(1)}, bf16[16,3200]{1,0:T(8,128)(2,1)S(1)}, u32[]{:S(2)}, u32[]{:S(2)}) %collective-permute-start) | collective-permute-done | bytes 102432 | tf_op jit(solution)/shard_map/ppermute | solution.py:380
  10.6 0.0 copy-start.4
  10.6 1.7 %shard_map.75 = bf16[32,4,88]{2,1,0:T(4,128)(2,1)} custom-call(bf16[16,3200]{1,0:T(8,128)(2,1)S(1)} %collective-permute-done.arrived, bf16[80,3200]{1,0:T(8,128)(2,1)S(1)} %reshape.17.rows.grid, bf16[16,3200]{1,0:T(8,128)(2,1)S(1)} %get-tuple-element.16.own, bf16[32,3712]{1,0:T(8,128)(2,1)S(1)} %get-tuple-element.20.basis, ...), custom_call_target="tpu_custom_call" | custom-call | tf_op jit(solution)/shard_map/pallas_call | solution.py:402
  12.3 0.0 copy-done.4
  12.4 0.1 slice_maximum_fusion
  12.5 3.1 %all-to-all-start = ((bf16[32,4,88]{2,1,0:T(4,128)(2,1)}), bf16[32,4,88]{2,1,0:T(4,128)(2,1)S(1)}, u32[]{:S(2)}, u32[]{:S(2)}) async-start(bf16[32,4,88]{2,1,0:T(4,128)(2,1)} %shard_map.75), calls=%async_computation | async-start | bytes 65536 | tf_op jit(solution)/shard_map/all_to_all | solution.py:429
  15.6 0.6 %dynamic_slice.3 = s32[1]{0:T(128)} dynamic-slice(s32[8]{0:T(128)S(1)} %copy-done.5, s32[]{:T(128)S(6)} %select_n.11), dynamic_slice_sizes={1} | dynamic-slice | bytes 12 | tf_op jit(solution)/shard_map/dynamic_slice | solution.py:424
  17.0 0.7 %concatenate.9 = bf16[8,128,320]{2,1,0:T(8,128)(2,1)S(1)} concatenate(bf16[8,16,320]{2,1,0:T(8,128)(2,1)S(1)} %slice.60, bf16[8,16,320]{2,1,0:T(8,128)(2,1)S(1)} %slice.60, bf16[8,16,320]{2,1,0:T(8,128)(2,1)S(1)} %slice.60, bf16[8,17,320]{2,1,0:T(8,128)(2,1)S(1)} %slice.61, bf16[8,1,320]{2,1,0:T(2,128)(2,1)S(1)} %get-tuple-element.33, bf16[8,1,320]{2,1,0:T(2,128)(2,1)S(1)} %get-tuple-element.33, ...), dimensions={1} | concatenate | bytes 1310720 | tf_op jit(solution)/shard_map/concatenate | solution.py:422
  17.7 5.1 %all-to-all-done.coeffs = bf16[32,4,88]{2,1,0:T(4,128)(2,1)S(1)} async-done(((bf16[32,4,88]{2,1,0:T(4,128)(2,1)}), bf16[32,4,88]{2,1,0:T(4,128)(2,1)S(1)}, u32[]{:S(2)}, u32[]{:S(2)}) %all-to-all-start) | async-done | bytes 22560 | tf_op jit(solution)/shard_map/all_to_all | solution.py:429
  22.9 0.9 %shard_map.76 = f32[16,2,320]{2,1,0:T(2,128)} custom-call(f32[8,320]{1,0:T(8,128)S(1)} %broadcast_in_dim.29.first_wave, bf16[32,4,88]{2,1,0:T(4,128)(2,1)S(1)} %all-to-all-done.coeffs, bf16[1024,320]{1,0:T(8,128)(2,1)S(1)} %bitcast.5), custom_call_target="tpu_custom_call" | custom-call | tf_op jit(solution)/shard_map/pallas_call | solution.py:432
  (10 shorter events, 0.2 us)
Async XLA Ops:
  0.0 1.3 %copy-start = (s32[20,3200]{1,0:T(8,128)S(1)}, s32[20,3200]{1,0:T(8,128)}, u32[]{:S(2)}) copy-start(s32[20,3200]{1,0:T(8,128)} %dep_row.1) | copy-start | bytes 768004
  0.0 1.3 %copy-start.1 = (s32[20,3200]{1,0:T(8,128)S(1)}, s32[20,3200]{1,0:T(8,128)}, u32[]{:S(2)}) copy-start(s32[20,3200]{1,0:T(8,128)} %dep_col.1) | copy-start | bytes 768004
  0.0 1.3 %copy-start.2 = (bf16[20,3200]{1,0:T(8,128)(2,1)S(1)}, bf16[20,3200]{1,0:T(8,128)(2,1)}, u32[]{:S(2)}) copy-start(bf16[20,3200]{1,0:T(8,128)(2,1)} %lat_frac.1) | copy-start | bytes 384004
  0.0 1.3 %copy-start.3 = (bf16[20,3200]{1,0:T(8,128)(2,1)S(1)}, bf16[20,3200]{1,0:T(8,128)(2,1)}, u32[]{:S(2)}) copy-start(bf16[20,3200]{1,0:T(8,128)(2,1)} %lon_frac.1) | copy-start | bytes 384004
  1.6 3.0 %copy-start.5 = (s32[8]{0:T(128)S(1)}, s32[8]{0:T(128)}, u32[]{:S(2)}) copy-start(s32[8]{0:T(128)} %param.12) | copy-start | bytes 100
  1.6 8.9 %collective-permute-start = (bf16[16,3200]{1,0:T(8,128)(2,1)S(1)}, bf16[16,3200]{1,0:T(8,128)(2,1)S(1)}, u32[]{:S(2)}, u32[]{:S(2)}) collective-permute-start(bf16[16,3200]{1,0:T(8,128)(2,1)S(1)} %get-tuple-element.15.sent), channel_id=1, source_target_pairs={{0,4},{4,8},{8,12},{12,16},{16,20},{20,24},{24,28},{28,0},{1,5},{5... | collective-permute-start | bytes 307208 | tf_op jit(solution)/shard_map/ppermute | solution.py:380
  10.6 1.7 %copy-start.4 = (bf16[1,160,320]{2,1,0:T(8,128)(2,1)S(1)}, bf16[1,160,320]{2,1,0:T(8,128)(2,1)}, u32[]{:S(2)}) copy-start(bf16[1,160,320]{2,1,0:T(8,128)(2,1)} %param.13) | copy-start | bytes 307204
  12.5 10.3 %all-to-all-start = ((bf16[32,4,88]{2,1,0:T(4,128)(2,1)}), bf16[32,4,88]{2,1,0:T(4,128)(2,1)S(1)}, u32[]{:S(2)}, u32[]{:S(2)}) async-start(bf16[32,4,88]{2,1,0:T(4,128)(2,1)} %shard_map.75), calls=%async_computation | async-start | bytes 65536 | tf_op jit(solution)/shard_map/all_to_all | solution.py:429

commit v11 on v10

--- a/solution.py
+++ b/solution.py
@@ -40,23 +40,31 @@
     return slice(t * LANES, (t + 1) * LANES)
 
 
-def cut_of(start, lon_count):
+def cut(arrays, t, lon_count, steps):
     tiles = lon_count // LANES
-    first, lane_at = divmod(start % lon_count, LANES)
-    return tile_at(first), tile_at((first + 1) % tiles), lane_at
-
-
-def cut(first, second, lane_at):
-    if lane_at == 0:
-        return first
-    lane = lax.broadcasted_iota(jnp.int32, first.shape, 1).astype(jnp.int16)
-    joined = jnp.where(lane >= jnp.int16(lane_at), first, second)
-    return pltpu.roll(joined, LANES - lane_at, 1)
+    first, lane_at = divmod((t * SPAN - REACH) % lon_count, LANES)
+    second = (first + 1) % tiles
+    chosen = jnp.where(steps[...] == jnp.int16(lane_at), jnp.bfloat16(1), jnp.bfloat16(0))
+    columns = jnp.concatenate(
+        [
+            jnp.concatenate([array[:, tile_at(tile)] for array in arrays], axis=0)
+            for tile in (first, second)
+        ],
+        axis=1,
+    )
+    return jnp.dot(columns, chosen, preferred_element_type=jnp.float32)
+
+
+def fill_steps(steps):
+    shape = steps.shape
+    step = lax.broadcasted_iota(jnp.int32, shape, 0) - lax.broadcasted_iota(jnp.int32, shape, 1)
+    steps[...] = step.astype(jnp.int16)
 
 
 def lane_plan(code):
     code = code.astype(jnp.int32)
-    west = lax.broadcasted_iota(jnp.int32, code.shape, 1) + (code & (1 << ROW_BITS) - 1)
+    lane = lax.broadcasted_iota(jnp.int32, code.shape, 1)
+    west = lane - REACH + (code & (1 << ROW_BITS) - 1)
     west_lane = (west & (LANES - 1)).astype(jnp.int16)
     east_lane = ((west + 1) & (LANES - 1)).astype(jnp.int16)
     row_step = (code >> ROW_BITS).astype(jnp.float32).astype(jnp.bfloat16)
@@ -117,12 +125,14 @@
         held[slot, 1, 0:band_rows, :] = (shift + REACH).astype(jnp.float32)
         held[slot, 2, 0:band_rows, :] = lat_frac[:, cols].astype(jnp.float32)
         held[slot, 3, 0:band_rows, :] = lon_frac[:, cols].astype(jnp.float32)
-        for out, first_of, start in (
-            (own_out, jnp.zeros((rim, LANES), jnp.float32), 0),
-            (sent_out, rows[rows.shape[0] - 2 * rim :, cols].astype(jnp.float32)[rim:], band_rows - RIM),
+        edges = rows[0 : 2 * rim, cols], rows[rows.shape[0] - 2 * rim :, cols]
+        first_rows, last_rows = [edge.astype(jnp.float32) for edge in edges]
+        for out, grid_rows, start in (
+            (own_out, first_rows[:rim], 0),
+            (sent_out, last_rows[rim:], band_rows - RIM),
         ):
             out[:, cols] = jnp.concatenate(
-                [first_of] + [held[slot, at, start : start + RIM, :] for at in range(4)], axis=0
+                [grid_rows] + [held[slot, at, start : start + RIM, :] for at in range(4)], axis=0
             ).astype(jnp.bfloat16)
         middle = [held[slot, at, RIM : RIM + inner, :] for at in range(4)]
         middle = [middle[0] * (1 << ROW_BITS) + middle[1], middle[2], middle[3]]
@@ -141,7 +151,7 @@
 def basis_tile(t, wave, lon_count):
     lane = lax.broadcasted_iota(jnp.int32, (16, LANES), 1)
     row = lax.broadcasted_iota(jnp.int32, (16, LANES), 0)
-    longitude = lane + t * SPAN
+    longitude = lane + (t * SPAN - REACH)
     quarter = jnp.where((row & 1) == 0, 0.0, float(lon_count // 4))
     steps = longitude.astype(jnp.float32) * wave + quarter
     turns = jnp.floor(steps * (1.0 / lon_count) + 0.5)
@@ -151,7 +161,7 @@
     series = jnp.float32(-1.0 / 39916800.0)
     for term in (1.0 / 362880.0, -1.0 / 5040.0, 1.0 / 120.0, -1.0 / 6.0, 1.0):
         series = series * square + term
-    taken = (lane < SPAN) & (longitude < lon_count)
+    taken = (lane >= REACH) & (lane < REACH + SPAN) & (longitude < lon_count)
     return jnp.where(taken, angle * series, 0.0).astype(jnp.bfloat16)
 
 
@@ -168,7 +178,7 @@
 
 
 def rim_plan(spread, packed):
-    plan = jnp.dot(spread, jnp.concatenate(packed, axis=0), preferred_element_type=jnp.float32)
+    plan = jnp.dot(spread, packed.astype(jnp.bfloat16), preferred_element_type=jnp.float32)
     fields = spread.shape[0] // 3
     code, lat_weight, lon_weight = [plan[fields * at : fields * (at + 1)] for at in range(3)]
     return lane_plan(code), corner_weights(lat_weight, lon_weight)
@@ -181,68 +191,56 @@
 
 
 def inner_kernel(
-    grid, plans, sent, ids, fourier_out, basis, windows, departed, last_departed, *, slices
+    grid, plans, own, sent, ids,
+    fourier_out, basis, windows, departed, rim_departed, steps, *, slices,
 ):
     lon_count = grid.shape[1]
     inner = plans.shape[0] // 3
-    rim = RIM * slices
+    rim, fields, held = RIM * slices, EDGE * slices, grid.shape[0]
+    plan_end = held + 3 * inner
     spread = rim_spread(slices)
+    fill_steps(steps)
     for slot in range(INNER_AT_ONCE):
-        windows[slot, grid.shape[0] :, :] = jnp.zeros((rim, LANES), jnp.float32)
+        windows[slot, 0:rim, :] = jnp.zeros((rim, LANES), jnp.float32)
+        windows[slot, rim + held :, :] = jnp.zeros((rim, LANES), jnp.float32)
     groups = ids.shape[0] // 4
     few = groups <= 4
     waves = [waves_of(ids, at) for at in range(groups if few else 0)]
 
     def group_of(ts):
-        blocks, plan_blocks, last_plans = [], [], []
-        for t in ts:
-            first, second, lane_at = cut_of(t * SPAN - REACH, lon_count)
-            blocks.append(cut(grid[:, first], grid[:, second], lane_at).astype(jnp.float32))
-            first, second, lane_at = cut_of(t * SPAN, lon_count)
-            last_plans.append(cut(sent[:, first], sent[:, second], lane_at))
-            plan_blocks.append(
-                [
-                    cut(
-                        plans[at * inner : (at + 1) * inner, first],
-                        plans[at * inner : (at + 1) * inner, second],
-                        lane_at,
-                    ).astype(jnp.float32)
-                    for at in range(3)
-                ]
-            )
+        blocks = [cut((grid, plans, own, sent), t, lon_count, steps) for t in ts]
         for slot, block in enumerate(blocks):
-            windows[slot, 0 : grid.shape[0], :] = block
-        results = []
-        for slot, (code, lat_weight, lon_weight) in enumerate(plan_blocks):
+            windows[slot, rim : rim + held, :] = block[:held]
+        results, rim_results = [], []
+        for slot, t in enumerate(ts):
+            code, lat_weight, lon_weight = [
+                blocks[slot][held + at * inner : held + (at + 1) * inner] for at in range(3)
+            ]
             plan = lane_plan(code)
             weights = corner_weights(lat_weight, lon_weight)
             for f in range(slices):
                 sources = [
-                    windows[slot, pl.ds(slices * position + f, inner, stride=slices), :].astype(
-                        jnp.bfloat16
-                    )
+                    windows[
+                        slot, pl.ds(rim + slices * position + f, inner, stride=slices), :
+                    ].astype(jnp.bfloat16)
                     for position in range(2 * RIM + 1)
                 ]
-                results.append((ts[slot], f, interpolate(sources, plan, weights)))
-        two = [0, len(ts) - 1]
-        last_rows = grid.shape[0] - slices * EDGE
-        sources = [
-            jnp.concatenate(
-                [
-                    windows[slot, last_rows + slices * position : last_rows + slices * position + rim]
-                    for slot in two
-                ],
-                axis=0,
-            ).astype(jnp.bfloat16)
-            for position in range(2 * RIM + 1)
-        ]
-        last = interpolate(sources, *rim_plan(spread, [last_plans[slot] for slot in two]))
+                results.append((t, f, interpolate(sources, plan, weights)))
+            sources = [
+                jnp.concatenate(
+                    [
+                        windows[slot, start + slices * position : start + slices * position + rim, :]
+                        for start in (0, held - rim)
+                    ],
+                    axis=0,
+                ).astype(jnp.bfloat16)
+                for position in range(2 * RIM + 1)
+            ]
+            rim_results.append(interpolate(sources, *rim_plan(spread, blocks[slot][plan_end:])))
         for t, f, result in results:
             departed[f * inner : (f + 1) * inner, tile_at(t)] = result.astype(jnp.bfloat16)
-        for slot, t in enumerate(ts):
-            last_departed[:, tile_at(t)] = jnp.concatenate(
-                [last[rim * slot : rim * (slot + 1)], jnp.zeros((rim, LANES), jnp.float32)], axis=0
-            ).astype(jnp.bfloat16)
+        for t, result in zip(ts, rim_results):
+            rim_departed[:, tile_at(t)] = result.astype(jnp.bfloat16)
         for t in ts if few else ():
             for at, wave in enumerate(waves):
                 basis[16 * at : 16 * at + 16, tile_at(t)] = basis_tile(t, wave, lon_count)
@@ -258,54 +256,43 @@
         lax.fori_loop(0, groups, rows_of, 0)
     in_groups(departed.shape[1] // LANES, INNER_AT_ONCE, group_of)
     fourier_out[...] = jnp.concatenate(
-        [add_up(basis[...], departed[...]), add_up(basis[...], last_departed[...])[:, :rim]], axis=1
+        [add_up(basis[...], departed[...]), add_up(basis[...], rim_departed[...])], axis=1
     )
 
 
 def rim_kernel(
-    arrived, rows, own, basis, inner_fourier, fourier_out, windows, departed, *, slices, levs
+    arrived, own, basis, inner_fourier, fourier_out, windows, departed, steps, *, slices, levs
 ):
     lon_count = arrived.shape[1]
     rim, fields = RIM * slices, EDGE * slices
     spread = rim_spread(slices)
-    sublane = lax.broadcasted_iota(jnp.int32, (rim, LANES), 0)
-
-    def source(slot, position):
-        start = slices * position
-        before = jnp.zeros((rim, LANES), jnp.float32)
-        if position == 2 * RIM - 1:
-            before = jnp.where(sublane < slices, before, windows[slot, slices : slices + rim, :])
-        elif position == 2 * RIM:
-            before = windows[slot, rim : 2 * rim, :]
-        return jnp.concatenate([before, windows[slot, start : start + rim, :]], axis=0).astype(
-            jnp.bfloat16
-        )
+    fill_steps(steps)
+    out_row = lax.broadcasted_iota(jnp.int32, (fields, LANES), 0) // slices
+    far_step = jnp.where(out_row < RIM, 2 * RIM, 0)
+    near_step = jnp.where(out_row == RIM - 1, 2 * RIM - 1, jnp.where(out_row == RIM, 1, -2))
+
+    def part(source, plan, weights, step):
+        west_lane, east_lane, row_step = plan
+        source = source.astype(jnp.bfloat16)
+        low, high = row_step == step, row_step == step - 1
+        west = jnp.where(low, weights[0], jnp.where(high, weights[2], 0.0))
+        east = jnp.where(low, weights[1], jnp.where(high, weights[3], 0.0))
+        return west * lane_gather(source, west_lane).astype(
+            jnp.float32
+        ) + east * lane_gather(source, east_lane).astype(jnp.float32)
 
     def group_of(ts):
-        blocks, plan_blocks = [], []
-        for t in ts:
-            first, second, lane_at = cut_of(t * SPAN - REACH, lon_count)
-            blocks.append(
-                [
-                    cut(arrived[:, first], arrived[:, second], lane_at).astype(jnp.float32)[:rim],
-                    cut(rows[0:fields, first], rows[0:fields, second], lane_at).astype(jnp.float32),
-                ]
-            )
-            first, second, lane_at = cut_of(t * SPAN, lon_count)
-            plan_blocks.append(
-                [cut(ref[:, first], ref[:, second], lane_at) for ref in (arrived, own)]
-            )
-        for slot, (before, first_rows) in enumerate(blocks):
-            windows[slot, 0:rim, :] = before
-            windows[slot, rim : rim + fields, :] = first_rows
-        results = [
-            interpolate(
-                [source(slot, position) for position in range(2 * RIM + 1)],
-                *rim_plan(spread, plan_blocks[slot]),
-            )
-            for slot in range(len(ts))
-        ]
-        for t, result in zip(ts, results):
+        blocks = [cut((arrived, own), t, lon_count, steps) for t in ts]
+        for slot, block in enumerate(blocks):
+            windows[slot, 0:rim, :] = block[:rim]
+            windows[slot, rim:, :] = block[fields : fields + rim]
+        for slot, t in enumerate(ts):
+            block = blocks[slot]
+            (west_lane, east_lane, row_step), weights = rim_plan(spread, block)
+            plan = west_lane, east_lane, row_step.astype(jnp.float32).astype(jnp.int32)
+            far = jnp.concatenate([block[fields : fields + rim], block[:rim]], axis=0)
+            near = jnp.concatenate([windows[slot, slices : slices + rim, :]] * 2, axis=0)
+            result = part(far, plan, weights, far_step) + part(near, plan, weights, near_step)
             departed[:, tile_at(t)] = result.astype(jnp.bfloat16)
 
     in_groups(basis.shape[1] // LANES, RIM_AT_ONCE, group_of)
@@ -319,7 +306,7 @@
     members, _, rows = coeffs.shape
     bands = members // levs
     col_count = spread_analysis.shape[1]
-    inner = rows // slices - EDGE - RIM
+    inner = rows // slices - 2 * EDGE
     column = lax.broadcasted_iota(jnp.int32, (1, LANES), 1)
     rim_at = column - inner * slices
     slice_of = jnp.where(rim_at < 0, column // inner, rim_at % slices)
@@ -339,9 +326,13 @@
 
     for band in range(bands):
         spread(band)
-    total = jnp.dot(
-        spread_coeffs[...], spread_analysis[...], preferred_element_type=jnp.float32
-    )
+    total = None
+    for at in range(0, bands * LANES, 2 * LANES):
+        part = slice(at, min(at + 2 * LANES, bands * LANES))
+        product = jnp.dot(
+            spread_coeffs[:, part], spread_analysis[part, :], preferred_element_type=jnp.float32
+        )
+        total = product if total is None else total + product
     first = first_wave[0:2, :] > 0.0
     for f in range(slices):
         for lev in range(levs):
@@ -384,44 +375,47 @@
     inner_fourier, basis = pl.pallas_call(
         functools.partial(inner_kernel, slices=slices),
         out_shape=(
-            jax.ShapeDtypeStruct((4 * pairs, slices * (inner + RIM)), jnp.float32),
+            jax.ShapeDtypeStruct((4 * pairs, slices * band_rows), jnp.float32),
             jax.ShapeDtypeStruct((4 * pairs, windows * LANES), jnp.bfloat16),
         ),
-        in_specs=[vmem] * 4,
+        in_specs=[vmem] * 5,
         out_specs=(vmem,) * 2,
         scratch_shapes=[
-            pltpu.VMEM((INNER_AT_ONCE, (band_rows + RIM) * slices, LANES), jnp.float32),
+            pltpu.VMEM((INNER_AT_ONCE, (band_rows + 2 * RIM) * slices, LANES), jnp.float32),
             pltpu.VMEM((slices * inner, windows * LANES), jnp.bfloat16),
-            pltpu.VMEM((2 * RIM * slices, windows * LANES), jnp.bfloat16),
+            pltpu.VMEM((fields, windows * LANES), jnp.bfloat16),
+            pltpu.VMEM((2 * LANES, LANES), jnp.int16),
         ],
         compiler_params=params,
         cost_estimate=pl.CostEstimate(flops=100_000_000, bytes_accessed=2_000_000, transcendentals=0),
-    )(rows, plans, sent_rim, ids)
-
-    held_coeffs = slices * (band_rows + RIM)
+    )(rows, plans, own_rim, sent_rim, ids)
+
+    held_coeffs = slices * (band_rows + EDGE)
     fourier = pl.pallas_call(
         functools.partial(rim_kernel, slices=slices, levs=levs),
         out_shape=jax.ShapeDtypeStruct((bands * levs, 4, held_coeffs), jnp.bfloat16),
-        in_specs=[vmem] * 5,
+        in_specs=[vmem] * 4,
         out_specs=vmem,
         scratch_shapes=[
-            pltpu.VMEM((RIM_AT_ONCE, (RIM + EDGE) * slices, LANES), jnp.float32),
+            pltpu.VMEM((RIM_AT_ONCE, fields, LANES), jnp.float32),
             pltpu.VMEM((fields, windows * LANES), jnp.bfloat16),
+            pltpu.VMEM((2 * LANES, LANES), jnp.int16),
         ],
         compiler_params=params,
-    )(arrived_rim, rows, own_rim, basis, inner_fourier)
-    fourier, analysis, late_ids = lax.optimization_barrier((fourier, analysis, pair_ids))
+    )(arrived_rim, own_rim, basis, inner_fourier)
+    fourier, late_ids = lax.optimization_barrier((fourier, pair_ids))
+    own_id = lax.dynamic_slice_in_dim(late_ids, lax.axis_index("lat"), 1)
+    own_id, analysis = lax.optimization_barrier((own_id, analysis))
 
     values = analysis[0].reshape(bands, band_rows, col_count)
     before = jnp.roll(values[:, band_rows - RIM :], 1, axis=0)
     spread_rows = [values[:, RIM : RIM + inner]] * slices
-    for rim in (values[:, band_rows - RIM :], before, values[:, :RIM]):
+    for rim in (values[:, :RIM], values[:, band_rows - RIM :], before, values[:, :RIM]):
         for row in range(RIM):
             spread_rows += [rim[:, row : row + 1]] * slices
     spread_rows.append(jnp.zeros((bands, LANES - held_coeffs, col_count), jnp.bfloat16))
     spread_analysis = jnp.concatenate(spread_rows, axis=1).reshape(bands * LANES, col_count)
 
-    own_id = lax.dynamic_slice_in_dim(late_ids, lax.axis_index("lat"), 1)
     columns = lax.axis_index("lev") * col_count + jnp.arange(col_count, dtype=jnp.int32)
     first_wave = jnp.where(columns < NMAX + 1 - own_id, 1.0, 0.0)
     first_wave = jnp.broadcast_to(first_wave[None, :], (8, col_count))

time: 23.9 us -> 25.2 us (1.054)
  waiting for transfers between devices: 7.08 us -> 8.08 us
    pallas_call x1, Pallas kernels: 1.72 us -> 2.41 us  [shards(): pl.pallas_call(functools.partial(rim_kernel, slices=slices, levs=levs), o...]
    all_to_all x1, waiting for transfers between devices: 5.12 us -> 5.63 us  [shards(): lax.all_to_all(fourier, ('lat', 'lev'), split_axis=0, concat_axis=0, tile...]
    pallas_call x1, Pallas kernels: 3.88 us -> 3.39 us  [shards(): pl.pallas_call(functools.partial(inner_kernel, slices=slices), out_shape=...]
    ppermute x1, waiting for transfers between devices: 1.96 us -> 2.45 us  [shards(): lax.ppermute(sent_rim, 'lat', [(i, (i + 1) % bands) for i in range(bands)])]
  transfers between devices with their start and end apart: 2 -> 2, of which waited for: 2 -> 2; matrix products, arithmetic and copies ran while one was open for 6% -> 4% of each run, Pallas kernels for 16% -> 13%
where the time goes in v11:
time: 25.2 us; the launch traced here: 25.1 us
  waiting for transfers between devices  8.08 us (32%)
  Pallas kernels  7.02 us (28%)
  starting transfers between devices  6.1 us (24%)
  local copies, waits for them, and re-layouts  2.96 us (12%)
  between operations  0.75 us (3%)
    all_to_all x1, waiting for transfers between devices, shards(): lax.all_to_all(fourier, ('lat', 'lev'), split_axis=0, concat_axis=0, tile...  5.63 us
    pallas_call x1, Pallas kernels, shards(): pl.pallas_call(functools.partial(inner_kernel, slices=slices), out_shape=...  3.39 us
    all_to_all x1, starting transfers between devices, shards(): lax.all_to_all(fourier, ('lat', 'lev'), split_axis=0, concat_axis=0, tile...  3.08 us
    ppermute x1, starting transfers between devices, shards(): lax.ppermute(sent_rim, 'lat', [(i, (i + 1) % bands) for i in range(bands)])  3.02 us
    ppermute x1, waiting for transfers between devices, shards(): lax.ppermute(sent_rim, 'lat', [(i, (i + 1) % bands) for i in range(bands)])  2.45 us
    pallas_call x1, Pallas kernels, shards(): pl.pallas_call(functools.partial(rim_kernel, slices=slices, levs=levs), o...  2.41 us
    reshape x1, local copies, waits for them, and re-layouts, shards(): rows = grid.transpose(1, 0, 2).reshape(band_rows * slices, lon_count)  1.23 us
    concatenate x1, local copies, waits for them, and re-layouts, shards(): jnp.concatenate(spread_rows, axis=1).reshape(bands * LANES, col_count)  0.9 us
  transfers between devices with their start and end apart: 2, of which 2 were waited for; matrix products, arithmetic and copies ran while one was open for 4% of the time, Pallas kernels for 13%

profile of v11, /device:TPU:0, one launch (start us, length us, event | category | flops | bytes accessed | tf_op | source)
XLA Modules:
  0.0 25.1 jit_solution(9174560487105252554)
XLA Ops:
  0.0 0.0 copy-start
  0.0 0.0 copy-start.1
  0.0 0.0 copy-start.2
  0.0 0.0 copy-start.3
  0.0 1.2 %reshape.17.rows.grid = bf16[80,3200]{1,0:T(8,128)(2,1)S(1)} reshape(bf16[20,4,3200]{2,1,0:T(4,128)(2,1)} %bitcast.6) | data formatting | bytes 1024000 | tf_op jit(solution)/shard_map/reshape | solution.py:357
  1.2 0.0 copy-done
  1.3 0.0 copy-done.1
  1.3 0.0 copy-done.2
  1.3 0.0 copy-done.3
  1.3 0.3 %shard_map.73 = (bf16[16,3200]{1,0:T(8,128)(2,1)S(1)}, bf16[16,3200]{1,0:T(8,128)(2,1)S(1)}, bf16[48,3200]{1,0:T(8,128)(2,1)S(1)}) custom-call(s32[1]{0:T(128)} %bitcast.band_start, bf16[80,3200]{1,0:T(8,128)(2,1)S(1)} %reshape.17.rows.grid, s32[20,3200]{1,0:T(8,128)S(1)} %copy-done, s32[20,3200]{1,0:T(8,128)S(1)} %copy-done.1, ...), custom_call_target="tpu_custom_call" | custom-call | tf_op jit(solution)/shard_map/pallas_call | solution.py:359
  1.6 0.0 copy-start.5
  1.6 3.0 %collective-permute-start = (bf16[16,3200]{1,0:T(8,128)(2,1)S(1)}, bf16[16,3200]{1,0:T(8,128)(2,1)S(1)}, u32[]{:S(2)}, u32[]{:S(2)}) collective-permute-start(bf16[16,3200]{1,0:T(8,128)(2,1)S(1)} %get-tuple-element.16.sent), channel_id=1, source_target_pairs={{0,4},{4,8},{8,12},{12,16},{16,20},{20,24},{24,28},{28,0},{1,5},{5... | collective-permute-start | bytes 307208 | tf_op jit(solution)/shard_map/ppermute | solution.py:371
  4.7 0.0 copy-done.5
  4.7 0.1 broadcast_in_dim.26.ids
  4.7 3.4 %shard_map.74 = (f32[32,80]{1,0:T(8,128)S(1)}, bf16[32,3712]{1,0:T(8,128)(2,1)S(1)}) custom-call(bf16[80,3200]{1,0:T(8,128)(2,1)S(1)} %reshape.17.rows.grid, bf16[48,3200]{1,0:T(8,128)(2,1)S(1)} %get-tuple-element.19.plans, bf16[16,3200]{1,0:T(8,128)(2,1)S(1)} %get-tuple-element.17.own, bf16[16,3200]{1,0:T(8,128)(2,1)S(1)} %get-tuple-element.16.sent, ...), custom_call_target="tpu_custom_call" | custom-call | flops 100000000 | bytes 2000000 | tf_op jit(solution)/shard_map/pallas_call | solution.py:375
  8.1 2.5 %collective-permute-done.arrived = bf16[16,3200]{1,0:T(8,128)(2,1)S(1)} collective-permute-done((bf16[16,3200]{1,0:T(8,128)(2,1)S(1)}, bf16[16,3200]{1,0:T(8,128)(2,1)S(1)}, u32[]{:S(2)}, u32[]{:S(2)}) %collective-permute-start) | collective-permute-done | bytes 102432 | tf_op jit(solution)/shard_map/ppermute | solution.py:371
  10.6 0.0 copy-start.4
  10.6 2.4 %shard_map.75 = bf16[32,4,96]{2,1,0:T(4,128)(2,1)} custom-call(bf16[16,3200]{1,0:T(8,128)(2,1)S(1)} %collective-permute-done.arrived, bf16[16,3200]{1,0:T(8,128)(2,1)S(1)} %get-tuple-element.17.own, bf16[32,3712]{1,0:T(8,128)(2,1)S(1)} %get-tuple-element.21.basis, f32[32,80]{1,0:T(8,128)S(1)} %get-tuple-element.22.inner_fourier), custom_call_target="tpu_custom_call" | custom-call | tf_op jit(solution)/shard_map/pallas_call | solution.py:394
  13.0 0.6 %dynamic_slice.3 = s32[1]{0:T(128)} dynamic-slice(s32[8]{0:T(128)S(1)} %copy-done.5, s32[]{:T(128)S(6)} %select_n.11), dynamic_slice_sizes={1} | dynamic-slice | bytes 12 | tf_op jit(solution)/shard_map/dynamic_slice | solution.py:407
  13.6 0.0 copy-done.4
  13.7 0.1 slice_maximum_fusion
  13.8 3.1 %all-to-all-start = ((bf16[32,4,96]{2,1,0:T(4,128)(2,1)}), bf16[32,4,96]{2,1,0:T(4,128)(2,1)S(1)}, u32[]{:S(2)}, u32[]{:S(2)}) async-start(bf16[32,4,96]{2,1,0:T(4,128)(2,1)} %shard_map.75), calls=%async_computation | async-start | bytes 65536 | tf_op jit(solution)/shard_map/all_to_all | solution.py:423
  17.6 0.9 %concatenate.9 = bf16[8,128,320]{2,1,0:T(8,128)(2,1)S(1)} concatenate(bf16[8,16,320]{2,1,0:T(8,128)(2,1)S(1)} %slice.60, bf16[8,16,320]{2,1,0:T(8,128)(2,1)S(1)} %slice.60, bf16[8,16,320]{2,1,0:T(8,128)(2,1)S(1)} %slice.60, bf16[8,16,320]{2,1,0:T(8,128)(2,1)S(1)} %slice.60, bf16[8,1,320]{2,1,0:T(2,128)(2,1)S(1)} %get-tuple-element.35, bf16[8,1,320]{2,1,0:T(2,128)(2,1)S(1)} %get-tuple-element.35, ...), dimensions={1} | concatenate | bytes 1310720 | tf_op jit(solution)/shard_map/concatenate | solution.py:417
  18.5 5.6 %all-to-all-done.coeffs = bf16[32,4,96]{2,1,0:T(4,128)(2,1)S(1)} async-done(((bf16[32,4,96]{2,1,0:T(4,128)(2,1)}), bf16[32,4,96]{2,1,0:T(4,128)(2,1)S(1)}, u32[]{:S(2)}, u32[]{:S(2)}) %all-to-all-start) | async-done | bytes 24608 | tf_op jit(solution)/shard_map/all_to_all | solution.py:423
  24.2 0.9 %shard_map.76 = f32[16,2,320]{2,1,0:T(2,128)} custom-call(f32[8,320]{1,0:T(8,128)S(1)} %broadcast_in_dim.29.first_wave, bf16[32,4,96]{2,1,0:T(4,128)(2,1)S(1)} %all-to-all-done.coeffs, bf16[1024,320]{1,0:T(8,128)(2,1)S(1)} %bitcast.5), custom_call_target="tpu_custom_call" | custom-call | tf_op jit(solution)/shard_map/pallas_call | solution.py:426
  (9 shorter events, 0.2 us)
Async XLA Ops:
  0.0 1.3 %copy-start = (s32[20,3200]{1,0:T(8,128)S(1)}, s32[20,3200]{1,0:T(8,128)}, u32[]{:S(2)}) copy-start(s32[20,3200]{1,0:T(8,128)} %dep_row.1) | copy-start | bytes 768004
  0.0 1.3 %copy-start.1 = (s32[20,3200]{1,0:T(8,128)S(1)}, s32[20,3200]{1,0:T(8,128)}, u32[]{:S(2)}) copy-start(s32[20,3200]{1,0:T(8,128)} %dep_col.1) | copy-start | bytes 768004
  0.0 1.3 %copy-start.2 = (bf16[20,3200]{1,0:T(8,128)(2,1)S(1)}, bf16[20,3200]{1,0:T(8,128)(2,1)}, u32[]{:S(2)}) copy-start(bf16[20,3200]{1,0:T(8,128)(2,1)} %lat_frac.1) | copy-start | bytes 384004
  0.0 1.3 %copy-start.3 = (bf16[20,3200]{1,0:T(8,128)(2,1)S(1)}, bf16[20,3200]{1,0:T(8,128)(2,1)}, u32[]{:S(2)}) copy-start(bf16[20,3200]{1,0:T(8,128)(2,1)} %lon_frac.1) | copy-start | bytes 384004
  1.6 3.0 %copy-start.5 = (s32[8]{0:T(128)S(1)}, s32[8]{0:T(128)}, u32[]{:S(2)}) copy-start(s32[8]{0:T(128)} %param.12) | copy-start | bytes 100
  1.6 8.9 %collective-permute-start = (bf16[16,3200]{1,0:T(8,128)(2,1)S(1)}, bf16[16,3200]{1,0:T(8,128)(2,1)S(1)}, u32[]{:S(2)}, u32[]{:S(2)}) collective-permute-start(bf16[16,3200]{1,0:T(8,128)(2,1)S(1)} %get-tuple-element.16.sent), channel_id=1, source_target_pairs={{0,4},{4,8},{8,12},{12,16},{16,20},{20,24},{24,28},{28,0},{1,5},{5... | collective-permute-start | bytes 307208 | tf_op jit(solution)/shard_map/ppermute | solution.py:371
  10.6 3.0 %copy-start.4 = (bf16[1,160,320]{2,1,0:T(8,128)(2,1)S(1)}, bf16[1,160,320]{2,1,0:T(8,128)(2,1)}, u32[]{:S(2)}) copy-start(bf16[1,160,320]{2,1,0:T(8,128)(2,1)} %param.13) | copy-start | bytes 307204
  13.8 10.3 %all-to-all-start = ((bf16[32,4,96]{2,1,0:T(4,128)(2,1)}), bf16[32,4,96]{2,1,0:T(4,128)(2,1)S(1)}, u32[]{:S(2)}, u32[]{:S(2)}) async-start(bf16[32,4,96]{2,1,0:T(4,128)(2,1)} %shard_map.75), calls=%async_computation | async-start | bytes 65536 | tf_op jit(solution)/shard_map/all_to_all | solution.py:423

commit v12 on v11

--- a/solution.py
+++ b/solution.py
@@ -184,6 +184,28 @@
     return lane_plan(code), corner_weights(lat_weight, lon_weight)
 
 
+def spread_rows(analysis, out, band_rows, slices):
+    inner = band_rows - EDGE
+    rim = RIM * slices
+    place = lax.broadcasted_iota(jnp.int32, (LANES, 1), 0)
+    edge = place - slices * inner
+    edge_row = edge // slices
+    row = jnp.where(edge < 0, RIM + place % inner, edge_row)
+    row = jnp.where(edge >= rim, band_rows - EDGE + edge_row, row)
+    row = jnp.where(edge >= 2 * rim, edge_row - 3 * RIM, row)
+    row = jnp.where(edge >= 4 * rim, -band_rows, row)
+    for band in range(out.shape[0] // LANES):
+        start = max(0, band * band_rows - RIM) // 16 * 16
+        end = min(analysis.shape[0], -(-(band + 1) * band_rows // 16) * 16)
+        column = lax.broadcasted_iota(jnp.int32, (LANES, end - start), 1) + start
+        chosen = jnp.where((column - band * band_rows == row) & (row >= -RIM), 1.0, 0.0)
+        out[band * LANES : (band + 1) * LANES, :] = jnp.dot(
+            chosen.astype(jnp.bfloat16),
+            analysis[start:end, :],
+            preferred_element_type=jnp.float32,
+        ).astype(jnp.bfloat16)
+
+
 def add_up(basis, values):
     return lax.dot_general(
         basis, values, (((1,), (1,)), ((), ())), preferred_element_type=jnp.float32
@@ -191,8 +213,8 @@
 
 
 def inner_kernel(
-    grid, plans, own, sent, ids,
-    fourier_out, basis, windows, departed, rim_departed, steps, *, slices,
+    grid, plans, own, sent, ids, analysis,
+    fourier_out, basis, spread_analysis, windows, departed, rim_departed, steps, *, slices,
 ):
     lon_count = grid.shape[1]
     inner = plans.shape[0] // 3
@@ -200,7 +222,7 @@
     plan_end = held + 3 * inner
     spread = rim_spread(slices)
     fill_steps(steps)
-    for slot in range(INNER_AT_ONCE):
+    for slot in range(windows.shape[0]):
         windows[slot, 0:rim, :] = jnp.zeros((rim, LANES), jnp.float32)
         windows[slot, rim + held :, :] = jnp.zeros((rim, LANES), jnp.float32)
     groups = ids.shape[0] // 4
@@ -209,8 +231,8 @@
 
     def group_of(ts):
         blocks = [cut((grid, plans, own, sent), t, lon_count, steps) for t in ts]
-        for slot, block in enumerate(blocks):
-            windows[slot, rim : rim + held, :] = block[:held]
+        for t, block in zip(ts, blocks):
+            windows[t, rim : rim + held, :] = block[:held]
         results, rim_results = [], []
         for slot, t in enumerate(ts):
             code, lat_weight, lon_weight = [
@@ -221,7 +243,7 @@
             for f in range(slices):
                 sources = [
                     windows[
-                        slot, pl.ds(rim + slices * position + f, inner, stride=slices), :
+                        t, pl.ds(rim + slices * position + f, inner, stride=slices), :
                     ].astype(jnp.bfloat16)
                     for position in range(2 * RIM + 1)
                 ]
@@ -229,8 +251,8 @@
             sources = [
                 jnp.concatenate(
                     [
-                        windows[slot, start + slices * position : start + slices * position + rim, :]
-                        for start in (0, held - rim)
+                        windows[t, start : start + rim, :]
+                        for start in (slices * position, held - rim + slices * position)
                     ],
                     axis=0,
                 ).astype(jnp.bfloat16)
@@ -255,6 +277,7 @@
 
         lax.fori_loop(0, groups, rows_of, 0)
     in_groups(departed.shape[1] // LANES, INNER_AT_ONCE, group_of)
+    spread_rows(analysis, spread_analysis, inner + EDGE, slices)
     fourier_out[...] = jnp.concatenate(
         [add_up(basis[...], departed[...]), add_up(basis[...], rim_departed[...])], axis=1
     )
@@ -283,15 +306,15 @@
 
     def group_of(ts):
         blocks = [cut((arrived, own), t, lon_count, steps) for t in ts]
-        for slot, block in enumerate(blocks):
-            windows[slot, 0:rim, :] = block[:rim]
-            windows[slot, rim:, :] = block[fields : fields + rim]
+        for t, block in zip(ts, blocks):
+            windows[t, 0:rim, :] = block[:rim]
+            windows[t, rim:, :] = block[fields : fields + rim]
         for slot, t in enumerate(ts):
             block = blocks[slot]
             (west_lane, east_lane, row_step), weights = rim_plan(spread, block)
             plan = west_lane, east_lane, row_step.astype(jnp.float32).astype(jnp.int32)
             far = jnp.concatenate([block[fields : fields + rim], block[:rim]], axis=0)
-            near = jnp.concatenate([windows[slot, slices : slices + rim, :]] * 2, axis=0)
+            near = jnp.concatenate([windows[t, slices : slices + rim, :]] * 2, axis=0)
             result = part(far, plan, weights, far_step) + part(near, plan, weights, near_step)
             departed[:, tile_at(t)] = result.astype(jnp.bfloat16)
 
@@ -372,23 +395,24 @@
 
     plans, ids = lax.optimization_barrier((plans, pair_ids))
     ids = jnp.broadcast_to(ids.astype(jnp.float32)[:, None], (pairs, LANES))
-    inner_fourier, basis = pl.pallas_call(
+    inner_fourier, basis, spread_analysis = pl.pallas_call(
         functools.partial(inner_kernel, slices=slices),
         out_shape=(
             jax.ShapeDtypeStruct((4 * pairs, slices * band_rows), jnp.float32),
             jax.ShapeDtypeStruct((4 * pairs, windows * LANES), jnp.bfloat16),
+            jax.ShapeDtypeStruct((bands * LANES, col_count), jnp.bfloat16),
         ),
-        in_specs=[vmem] * 5,
-        out_specs=(vmem,) * 2,
+        in_specs=[vmem] * 6,
+        out_specs=(vmem,) * 3,
         scratch_shapes=[
-            pltpu.VMEM((INNER_AT_ONCE, (band_rows + 2 * RIM) * slices, LANES), jnp.float32),
+            pltpu.VMEM((windows, (band_rows + 2 * RIM) * slices, LANES), jnp.float32),
             pltpu.VMEM((slices * inner, windows * LANES), jnp.bfloat16),
             pltpu.VMEM((fields, windows * LANES), jnp.bfloat16),
             pltpu.VMEM((2 * LANES, LANES), jnp.int16),
         ],
         compiler_params=params,
         cost_estimate=pl.CostEstimate(flops=100_000_000, bytes_accessed=2_000_000, transcendentals=0),
-    )(rows, plans, own_rim, sent_rim, ids)
+    )(rows, plans, own_rim, sent_rim, ids, analysis[0])
 
     held_coeffs = slices * (band_rows + EDGE)
     fourier = pl.pallas_call(
@@ -397,7 +421,7 @@
         in_specs=[vmem] * 4,
         out_specs=vmem,
         scratch_shapes=[
-            pltpu.VMEM((RIM_AT_ONCE, fields, LANES), jnp.float32),
+            pltpu.VMEM((windows, fields, LANES), jnp.float32),
             pltpu.VMEM((fields, windows * LANES), jnp.bfloat16),
             pltpu.VMEM((2 * LANES, LANES), jnp.int16),
         ],
@@ -405,16 +429,6 @@
     )(arrived_rim, own_rim, basis, inner_fourier)
     fourier, late_ids = lax.optimization_barrier((fourier, pair_ids))
     own_id = lax.dynamic_slice_in_dim(late_ids, lax.axis_index("lat"), 1)
-    own_id, analysis = lax.optimization_barrier((own_id, analysis))
-
-    values = analysis[0].reshape(bands, band_rows, col_count)
-    before = jnp.roll(values[:, band_rows - RIM :], 1, axis=0)
-    spread_rows = [values[:, RIM : RIM + inner]] * slices
-    for rim in (values[:, :RIM], values[:, band_rows - RIM :], before, values[:, :RIM]):
-        for row in range(RIM):
-            spread_rows += [rim[:, row : row + 1]] * slices
-    spread_rows.append(jnp.zeros((bands, LANES - held_coeffs, col_count), jnp.bfloat16))
-    spread_analysis = jnp.concatenate(spread_rows, axis=1).reshape(bands * LANES, col_count)
 
     columns = lax.axis_index("lev") * col_count + jnp.arange(col_count, dtype=jnp.int32)
     first_wave = jnp.where(columns < NMAX + 1 - own_id, 1.0, 0.0)

time: 25.2 us -> 24.4 us (0.968)
  local copies, waits for them, and re-layouts: 2.96 us -> 1.96 us
    concatenate x1 -> x0, local copies, waits for them, and re-layouts: 0.9 us -> none  [shards(): jnp.concatenate(spread_rows, axis=1).reshape(bands * LANES, col_count)]
    all_to_all x1, waiting for transfers between devices: 5.63 us -> 5.98 us  [shards(): lax.all_to_all(fourier, ('lat', 'lev'), split_axis=0, concat_axis=0, tile...]
  transfers between devices with their start and end apart: 2 -> 2, of which waited for: 2 -> 2; matrix products, arithmetic and copies ran while one was open for 4% -> 3% of each run, Pallas kernels for 13% -> 15%
where the time goes in v12:
time: 24.4 us; the launch traced here: 24.2 us
  waiting for transfers between devices  8.29 us (34%)
  Pallas kernels  7.17 us (29%)
  starting transfers between devices  6.1 us (25%)
  local copies, waits for them, and re-layouts  1.96 us (8%)
  between operations  0.71 us (3%)
    all_to_all x1, waiting for transfers between devices, shards(): lax.all_to_all(fourier, ('lat', 'lev'), split_axis=0, concat_axis=0, tile...  5.98 us
    pallas_call x1, Pallas kernels, shards(): pl.pallas_call(functools.partial(inner_kernel, slices=slices), out_shape=...  3.53 us
    all_to_all x1, starting transfers between devices, shards(): lax.all_to_all(fourier, ('lat', 'lev'), split_axis=0, concat_axis=0, tile...  3.07 us
    ppermute x1, starting transfers between devices, shards(): lax.ppermute(sent_rim, 'lat', [(i, (i + 1) % bands) for i in range(bands)])  3.03 us
    pallas_call x1, Pallas kernels, shards(): pl.pallas_call(functools.partial(rim_kernel, slices=slices, levs=levs), o...  2.41 us
    ppermute x1, waiting for transfers between devices, shards(): lax.ppermute(sent_rim, 'lat', [(i, (i + 1) % bands) for i in range(bands)])  2.31 us
    reshape x1, local copies, waits for them, and re-layouts, shards(): rows = grid.transpose(1, 0, 2).reshape(band_rows * slices, lon_count)  1.23 us
    pallas_call x1, Pallas kernels, shards(): pl.pallas_call(functools.partial(legendre_kernel, levs=levs, slices=slice...  0.9 us
  transfers between devices with their start and end apart: 2, of which 2 were waited for; matrix products, arithmetic and copies ran while one was open for 3% of the time, Pallas kernels for 15%

profile of v12, /device:TPU:0, one launch (start us, length us, event | category | flops | bytes accessed | tf_op | source)
XLA Modules:
  0.0 24.2 jit_solution(12226617994859200964)
XLA Ops:
  0.0 0.0 copy-start
  0.0 0.0 copy-start.1
  0.0 0.0 copy-start.2
  0.0 0.0 copy-start.3
  0.0 1.2 %reshape.14.rows.grid = bf16[80,3200]{1,0:T(8,128)(2,1)S(1)} reshape(bf16[20,4,3200]{2,1,0:T(4,128)(2,1)} %bitcast.6) | data formatting | bytes 1024000 | tf_op jit(solution)/shard_map/reshape | solution.py:380
  1.2 0.0 copy-done
  1.3 0.0 copy-done.1
  1.3 0.0 copy-done.2
  1.3 0.0 copy-done.3
  1.3 0.0 copy-start.4
  1.3 0.3 %shard_map.73 = (bf16[16,3200]{1,0:T(8,128)(2,1)S(1)}, bf16[16,3200]{1,0:T(8,128)(2,1)S(1)}, bf16[48,3200]{1,0:T(8,128)(2,1)S(1)}) custom-call(s32[1]{0:T(128)} %bitcast.band_start, bf16[80,3200]{1,0:T(8,128)(2,1)S(1)} %reshape.14.rows.grid, s32[20,3200]{1,0:T(8,128)S(1)} %copy-done, s32[20,3200]{1,0:T(8,128)S(1)} %copy-done.1, ...), custom_call_target="tpu_custom_call" | custom-call | tf_op jit(solution)/shard_map/pallas_call | solution.py:382
  1.6 0.0 copy-start.5
  1.6 3.0 %collective-permute-start = (bf16[16,3200]{1,0:T(8,128)(2,1)S(1)}, bf16[16,3200]{1,0:T(8,128)(2,1)S(1)}, u32[]{:S(2)}, u32[]{:S(2)}) collective-permute-start(bf16[16,3200]{1,0:T(8,128)(2,1)S(1)} %get-tuple-element.15.sent), channel_id=1, source_target_pairs={{0,4},{4,8},{8,12},{12,16},{16,20},{20,24},{24,28},{28,0},{1,5},{5... | collective-permute-start | bytes 307208 | tf_op jit(solution)/shard_map/ppermute | solution.py:394
  4.7 0.0 copy-done.5
  4.7 0.1 broadcast_in_dim.23.ids
  4.8 0.0 copy-done.4
  4.8 3.5 %shard_map.74 = (f32[32,80]{1,0:T(8,128)S(1)}, bf16[32,3712]{1,0:T(8,128)(2,1)S(1)}, bf16[1024,320]{1,0:T(8,128)(2,1)S(1)}) custom-call(bf16[80,3200]{1,0:T(8,128)(2,1)S(1)} %reshape.14.rows.grid, bf16[48,3200]{1,0:T(8,128)(2,1)S(1)} %get-tuple-element.18.plans, bf16[16,3200]{1,0:T(8,128)(2,1)S(1)} %get-tuple-element.16.own, ...), custom_call_target="tpu_custom_call" | custom-call | flops 100000000 | bytes 2000000 | tf_op jit(solution)/shard_map/pallas_call | solution.py:398
  8.3 2.3 %collective-permute-done.arrived = bf16[16,3200]{1,0:T(8,128)(2,1)S(1)} collective-permute-done((bf16[16,3200]{1,0:T(8,128)(2,1)S(1)}, bf16[16,3200]{1,0:T(8,128)(2,1)S(1)}, u32[]{:S(2)}, u32[]{:S(2)}) %collective-permute-start) | collective-permute-done | bytes 102432 | tf_op jit(solution)/shard_map/ppermute | solution.py:394
  10.6 2.4 %shard_map.75 = bf16[32,4,96]{2,1,0:T(4,128)(2,1)} custom-call(bf16[16,3200]{1,0:T(8,128)(2,1)S(1)} %collective-permute-done.arrived, bf16[16,3200]{1,0:T(8,128)(2,1)S(1)} %get-tuple-element.16.own, bf16[32,3712]{1,0:T(8,128)(2,1)S(1)} %get-tuple-element.20.basis, f32[32,80]{1,0:T(8,128)S(1)} %get-tuple-element.21.inner_fourier), custom_call_target="tpu_custom_call" | custom-call | tf_op jit(solution)/shard_map/pallas_call | solution.py:418
  13.0 3.1 %all-to-all-start = ((bf16[32,4,96]{2,1,0:T(4,128)(2,1)}), bf16[32,4,96]{2,1,0:T(4,128)(2,1)S(1)}, u32[]{:S(2)}, u32[]{:S(2)}) async-start(bf16[32,4,96]{2,1,0:T(4,128)(2,1)} %shard_map.75), calls=%async_computation | async-start | bytes 65536 | tf_op jit(solution)/shard_map/all_to_all | solution.py:437
  16.1 0.6 %dynamic_slice.3 = s32[1]{0:T(128)} dynamic-slice(s32[8]{0:T(128)S(1)} %copy-done.5, s32[]{:T(128)S(6)} %select_n.11), dynamic_slice_sizes={1} | dynamic-slice | bytes 12 | tf_op jit(solution)/shard_map/dynamic_slice | solution.py:431
  17.3 6.0 %all-to-all-done.coeffs = bf16[32,4,96]{2,1,0:T(4,128)(2,1)S(1)} async-done(((bf16[32,4,96]{2,1,0:T(4,128)(2,1)}), bf16[32,4,96]{2,1,0:T(4,128)(2,1)S(1)}, u32[]{:S(2)}, u32[]{:S(2)}) %all-to-all-start) | async-done | bytes 24608 | tf_op jit(solution)/shard_map/all_to_all | solution.py:437
  23.3 0.9 %shard_map.76 = f32[16,2,320]{2,1,0:T(2,128)} custom-call(f32[8,320]{1,0:T(8,128)S(1)} %broadcast_in_dim.26.first_wave, bf16[32,4,96]{2,1,0:T(4,128)(2,1)S(1)} %all-to-all-done.coeffs, bf16[1024,320]{1,0:T(8,128)(2,1)S(1)} %get-tuple-element.24.spread_analysis), custom_call_target="tpu_custom_call" | custom-call | tf_op jit(solution)/shard_map/pallas_call | solution.py:440
  (3 shorter events, 0.0 us)
Async XLA Ops:
  0.0 1.3 %copy-start = (s32[20,3200]{1,0:T(8,128)S(1)}, s32[20,3200]{1,0:T(8,128)}, u32[]{:S(2)}) copy-start(s32[20,3200]{1,0:T(8,128)} %dep_row.1) | copy-start | bytes 768004
  0.0 1.3 %copy-start.1 = (s32[20,3200]{1,0:T(8,128)S(1)}, s32[20,3200]{1,0:T(8,128)}, u32[]{:S(2)}) copy-start(s32[20,3200]{1,0:T(8,128)} %dep_col.1) | copy-start | bytes 768004
  0.0 1.3 %copy-start.2 = (bf16[20,3200]{1,0:T(8,128)(2,1)S(1)}, bf16[20,3200]{1,0:T(8,128)(2,1)}, u32[]{:S(2)}) copy-start(bf16[20,3200]{1,0:T(8,128)(2,1)} %lat_frac.1) | copy-start | bytes 384004
  0.0 1.3 %copy-start.3 = (bf16[20,3200]{1,0:T(8,128)(2,1)S(1)}, bf16[20,3200]{1,0:T(8,128)(2,1)}, u32[]{:S(2)}) copy-start(bf16[20,3200]{1,0:T(8,128)(2,1)} %lon_frac.1) | copy-start | bytes 384004
  1.3 3.5 %copy-start.4 = (bf16[1,160,320]{2,1,0:T(8,128)(2,1)S(1)}, bf16[1,160,320]{2,1,0:T(8,128)(2,1)}, u32[]{:S(2)}) copy-start(bf16[1,160,320]{2,1,0:T(8,128)(2,1)} %param.13) | copy-start | bytes 307204
  1.6 3.0 %copy-start.5 = (s32[8]{0:T(128)S(1)}, s32[8]{0:T(128)}, u32[]{:S(2)}) copy-start(s32[8]{0:T(128)} %param.12) | copy-start | bytes 100
  1.6 8.9 %collective-permute-start = (bf16[16,3200]{1,0:T(8,128)(2,1)S(1)}, bf16[16,3200]{1,0:T(8,128)(2,1)S(1)}, u32[]{:S(2)}, u32[]{:S(2)}) collective-permute-start(bf16[16,3200]{1,0:T(8,128)(2,1)S(1)} %get-tuple-element.15.sent), channel_id=1, source_target_pairs={{0,4},{4,8},{8,12},{12,16},{16,20},{20,24},{24,28},{28,0},{1,5},{5... | collective-permute-start | bytes 307208 | tf_op jit(solution)/shard_map/ppermute | solution.py:394
  13.0 10.3 %all-to-all-start = ((bf16[32,4,96]{2,1,0:T(4,128)(2,1)}), bf16[32,4,96]{2,1,0:T(4,128)(2,1)S(1)}, u32[]{:S(2)}, u32[]{:S(2)}) async-start(bf16[32,4,96]{2,1,0:T(4,128)(2,1)} %shard_map.75), calls=%async_computation | async-start | bytes 65536 | tf_op jit(solution)/shard_map/all_to_all | solution.py:437

commit v13 on v12

--- a/solution.py
+++ b/solution.py
@@ -55,6 +55,16 @@
     return jnp.dot(columns, chosen, preferred_element_type=jnp.float32)
 
 
+def turned(array, t, lon_count):
+    tiles = lon_count // LANES
+    first, lane_at = divmod((t * SPAN - REACH) % lon_count, LANES)
+    if lane_at == 0:
+        return array[:, tile_at(first)]
+    joined = array[:, tile_at(first)], array[:, tile_at((first + 1) % tiles)]
+    lane = lax.broadcasted_iota(jnp.int32, joined[0].shape, 1).astype(jnp.int16)
+    return pltpu.roll(jnp.where(lane >= jnp.int16(lane_at), *joined), LANES - lane_at, 1)
+
+
 def fill_steps(steps):
     shape = steps.shape
     step = lax.broadcasted_iota(jnp.int32, shape, 0) - lax.broadcasted_iota(jnp.int32, shape, 1)
@@ -67,8 +77,7 @@
     west = lane - REACH + (code & (1 << ROW_BITS) - 1)
     west_lane = (west & (LANES - 1)).astype(jnp.int16)
     east_lane = ((west + 1) & (LANES - 1)).astype(jnp.int16)
-    row_step = (code >> ROW_BITS).astype(jnp.float32).astype(jnp.bfloat16)
-    return west_lane, east_lane, row_step
+    return west_lane, east_lane, code >> ROW_BITS
 
 
 def corner_weights(lat_weight, lon_weight):
@@ -79,6 +88,7 @@
 
 def interpolate(sources, plan, weights):
     west_lane, east_lane, row_step = plan
+    row_step = row_step.astype(jnp.float32).astype(jnp.bfloat16)
     masks = [row_step == float(step) for step in range(2 * RIM - 1)]
 
     def pick(gathered):
@@ -180,8 +190,7 @@
 def rim_plan(spread, packed):
     plan = jnp.dot(spread, packed.astype(jnp.bfloat16), preferred_element_type=jnp.float32)
     fields = spread.shape[0] // 3
-    code, lat_weight, lon_weight = [plan[fields * at : fields * (at + 1)] for at in range(3)]
-    return lane_plan(code), corner_weights(lat_weight, lon_weight)
+    return [plan[fields * at : fields * (at + 1)] for at in range(3)]
 
 
 def spread_rows(analysis, out, band_rows, slices):
@@ -258,7 +267,9 @@
                 ).astype(jnp.bfloat16)
                 for position in range(2 * RIM + 1)
             ]
-            rim_results.append(interpolate(sources, *rim_plan(spread, blocks[slot][plan_end:])))
+            code, lat_weight, lon_weight = rim_plan(spread, blocks[slot][plan_end:])
+            weights = corner_weights(lat_weight, lon_weight)
+            rim_results.append(interpolate(sources, lane_plan(code), weights))
         for t, f, result in results:
             departed[f * inner : (f + 1) * inner, tile_at(t)] = result.astype(jnp.bfloat16)
         for t, result in zip(ts, rim_results):
@@ -284,41 +295,45 @@
 
 
 def rim_kernel(
-    arrived, own, basis, inner_fourier, fourier_out, windows, departed, steps, *, slices, levs
+    arrived, own, basis, inner_fourier, fourier_out, windows, plans, departed, *, slices, levs
 ):
     lon_count = arrived.shape[1]
     rim, fields = RIM * slices, EDGE * slices
     spread = rim_spread(slices)
-    fill_steps(steps)
     out_row = lax.broadcasted_iota(jnp.int32, (fields, LANES), 0) // slices
     far_step = jnp.where(out_row < RIM, 2 * RIM, 0)
     near_step = jnp.where(out_row == RIM - 1, 2 * RIM - 1, jnp.where(out_row == RIM, 1, -2))
 
-    def part(source, plan, weights, step):
-        west_lane, east_lane, row_step = plan
-        source = source.astype(jnp.bfloat16)
-        low, high = row_step == step, row_step == step - 1
-        west = jnp.where(low, weights[0], jnp.where(high, weights[2], 0.0))
-        east = jnp.where(low, weights[1], jnp.where(high, weights[3], 0.0))
-        return west * lane_gather(source, west_lane).astype(
-            jnp.float32
-        ) + east * lane_gather(source, east_lane).astype(jnp.float32)
-
-    def group_of(ts):
-        blocks = [cut((arrived, own), t, lon_count, steps) for t in ts]
-        for t, block in zip(ts, blocks):
-            windows[t, 0:rim, :] = block[:rim]
-            windows[t, rim:, :] = block[fields : fields + rim]
-        for slot, t in enumerate(ts):
-            block = blocks[slot]
-            (west_lane, east_lane, row_step), weights = rim_plan(spread, block)
-            plan = west_lane, east_lane, row_step.astype(jnp.float32).astype(jnp.int32)
-            far = jnp.concatenate([block[fields : fields + rim], block[:rim]], axis=0)
+    def part(source, lanes, row_step, lat_weight, lon_weight, step):
+        west, east = [lane_gather(source, lane).astype(jnp.float32) for lane in lanes]
+        row_weight = jnp.where(
+            row_step == step,
+            1.0 - lat_weight,
+            jnp.where(row_step == step - 1, lat_weight, 0.0),
+        )
+        return row_weight * (west + lon_weight * (east - west))
+
+    def prepare(ts):
+        packed = [[turned(side, t, lon_count) for side in (arrived, own)] for t in ts]
+        for t, sides in zip(ts, packed):
+            for at, plan in enumerate(rim_plan(spread, jnp.concatenate(sides, axis=0))):
+                plans[t, at] = plan
+            for at, side in enumerate(sides):
+                windows[t, rim * at : rim * (at + 1), :] = side.astype(jnp.float32)[:rim]
+
+    def finish(ts):
+        for t in ts:
+            west_lane, east_lane, row_step = lane_plan(plans[t, 0])
+            plan = (west_lane, east_lane), row_step, plans[t, 1], plans[t, 2]
+            far = jnp.concatenate([windows[t, rim:, :], windows[t, 0:rim, :]], axis=0)
             near = jnp.concatenate([windows[t, slices : slices + rim, :]] * 2, axis=0)
-            result = part(far, plan, weights, far_step) + part(near, plan, weights, near_step)
+            result = part(far.astype(jnp.bfloat16), *plan, far_step)
+            result += part(near.astype(jnp.bfloat16), *plan, near_step)
             departed[:, tile_at(t)] = result.astype(jnp.bfloat16)
 
-    in_groups(basis.shape[1] // LANES, RIM_AT_ONCE, group_of)
+    count = basis.shape[1] // LANES
+    in_groups(count, RIM_AT_ONCE, prepare)
+    in_groups(count, RIM_AT_ONCE, finish)
     fourier = jnp.concatenate([inner_fourier[...], add_up(basis[...], departed[...])], axis=1)
     for at in range(fourier_out.shape[0]):
         pair = at // levs
@@ -422,8 +437,8 @@
         out_specs=vmem,
         scratch_shapes=[
             pltpu.VMEM((windows, fields, LANES), jnp.float32),
+            pltpu.VMEM((windows, 3, fields, LANES), jnp.float32),
             pltpu.VMEM((fields, windows * LANES), jnp.bfloat16),
-            pltpu.VMEM((2 * LANES, LANES), jnp.int16),
         ],
         compiler_params=params,
     )(arrived_rim, own_rim, basis, inner_fourier)

time: 24.4 us -> 23.4 us (0.959)
  Pallas kernels: 7.17 us -> 6.19 us
    pallas_call x1, Pallas kernels: 2.41 us -> 1.44 us  [shards(): pl.pallas_call(functools.partial(rim_kernel, slices=slices, levs=levs), o...]
where the time goes in v13:
time: 23.4 us; the launch traced here: 23.3 us
  waiting for transfers between devices  8.29 us (35%)
  Pallas kernels  6.19 us (26%)
  starting transfers between devices  6.1 us (26%)
  local copies, waits for them, and re-layouts  1.96 us (8%)
  between operations  0.71 us (3%)
    all_to_all x1, waiting for transfers between devices, shards(): lax.all_to_all(fourier, ('lat', 'lev'), split_axis=0, concat_axis=0, tile...  5.98 us
    pallas_call x1, Pallas kernels, shards(): pl.pallas_call(functools.partial(inner_kernel, slices=slices), out_shape=...  3.53 us
    all_to_all x1, starting transfers between devices, shards(): lax.all_to_all(fourier, ('lat', 'lev'), split_axis=0, concat_axis=0, tile...  3.07 us
    ppermute x1, starting transfers between devices, shards(): lax.ppermute(sent_rim, 'lat', [(i, (i + 1) % bands) for i in range(bands)])  3.03 us
    ppermute x1, waiting for transfers between devices, shards(): lax.ppermute(sent_rim, 'lat', [(i, (i + 1) % bands) for i in range(bands)])  2.31 us
    pallas_call x1, Pallas kernels, shards(): pl.pallas_call(functools.partial(rim_kernel, slices=slices, levs=levs), o...  1.44 us
    reshape x1, local copies, waits for them, and re-layouts, shards(): rows = grid.transpose(1, 0, 2).reshape(band_rows * slices, lon_count)  1.23 us
    pallas_call x1, Pallas kernels, shards(): pl.pallas_call(functools.partial(legendre_kernel, levs=levs, slices=slice...  0.9 us
  transfers between devices with their start and end apart: 2, of which 2 were waited for; matrix products, arithmetic and copies ran while one was open for 3% of the time, Pallas kernels for 15%

profile of v13, /device:TPU:0, one launch (start us, length us, event | category | flops | bytes accessed | tf_op | source)
XLA Modules:
  0.0 23.3 jit_solution(12491751185141233070)
XLA Ops:
  0.0 0.0 copy-start
  0.0 0.0 copy-start.1
  0.0 0.0 copy-start.2
  0.0 0.0 copy-start.3
  0.0 1.2 %reshape.14.rows.grid = bf16[80,3200]{1,0:T(8,128)(2,1)S(1)} reshape(bf16[20,4,3200]{2,1,0:T(4,128)(2,1)} %bitcast.6) | data formatting | bytes 1024000 | tf_op jit(solution)/shard_map/reshape | solution.py:395
  1.2 0.0 copy-done
  1.3 0.0 copy-done.1
  1.3 0.0 copy-done.2
  1.3 0.0 copy-done.3
  1.3 0.0 copy-start.4
  1.3 0.3 %shard_map.73 = (bf16[16,3200]{1,0:T(8,128)(2,1)S(1)}, bf16[16,3200]{1,0:T(8,128)(2,1)S(1)}, bf16[48,3200]{1,0:T(8,128)(2,1)S(1)}) custom-call(s32[1]{0:T(128)} %bitcast.band_start, bf16[80,3200]{1,0:T(8,128)(2,1)S(1)} %reshape.14.rows.grid, s32[20,3200]{1,0:T(8,128)S(1)} %copy-done, s32[20,3200]{1,0:T(8,128)S(1)} %copy-done.1, ...), custom_call_target="tpu_custom_call" | custom-call | tf_op jit(solution)/shard_map/pallas_call | solution.py:397
  1.6 0.0 copy-start.5
  1.6 3.0 %collective-permute-start = (bf16[16,3200]{1,0:T(8,128)(2,1)S(1)}, bf16[16,3200]{1,0:T(8,128)(2,1)S(1)}, u32[]{:S(2)}, u32[]{:S(2)}) collective-permute-start(bf16[16,3200]{1,0:T(8,128)(2,1)S(1)} %get-tuple-element.15.sent), channel_id=1, source_target_pairs={{0,4},{4,8},{8,12},{12,16},{16,20},{20,24},{24,28},{28,0},{1,5},{5... | collective-permute-start | bytes 307208 | tf_op jit(solution)/shard_map/ppermute | solution.py:409
  4.7 0.0 copy-done.5
  4.7 0.1 broadcast_in_dim.23.ids
  4.8 0.0 copy-done.4
  4.8 3.5 %shard_map.74 = (f32[32,80]{1,0:T(8,128)S(1)}, bf16[32,3712]{1,0:T(8,128)(2,1)S(1)}, bf16[1024,320]{1,0:T(8,128)(2,1)S(1)}) custom-call(bf16[80,3200]{1,0:T(8,128)(2,1)S(1)} %reshape.14.rows.grid, bf16[48,3200]{1,0:T(8,128)(2,1)S(1)} %get-tuple-element.18.plans, bf16[16,3200]{1,0:T(8,128)(2,1)S(1)} %get-tuple-element.16.own, ...), custom_call_target="tpu_custom_call" | custom-call | flops 100000000 | bytes 2000000 | tf_op jit(solution)/shard_map/pallas_call | solution.py:413
  8.3 2.3 %collective-permute-done.arrived = bf16[16,3200]{1,0:T(8,128)(2,1)S(1)} collective-permute-done((bf16[16,3200]{1,0:T(8,128)(2,1)S(1)}, bf16[16,3200]{1,0:T(8,128)(2,1)S(1)}, u32[]{:S(2)}, u32[]{:S(2)}) %collective-permute-start) | collective-permute-done | bytes 102432 | tf_op jit(solution)/shard_map/ppermute | solution.py:409
  10.6 1.4 %shard_map.75 = bf16[32,4,96]{2,1,0:T(4,128)(2,1)} custom-call(bf16[16,3200]{1,0:T(8,128)(2,1)S(1)} %collective-permute-done.arrived, bf16[16,3200]{1,0:T(8,128)(2,1)S(1)} %get-tuple-element.16.own, bf16[32,3712]{1,0:T(8,128)(2,1)S(1)} %get-tuple-element.20.basis, f32[32,80]{1,0:T(8,128)S(1)} %get-tuple-element.21.inner_fourier), custom_call_target="tpu_custom_call" | custom-call | tf_op jit(solution)/shard_map/pallas_call | solution.py:433
  12.0 3.1 %all-to-all-start = ((bf16[32,4,96]{2,1,0:T(4,128)(2,1)}), bf16[32,4,96]{2,1,0:T(4,128)(2,1)S(1)}, u32[]{:S(2)}, u32[]{:S(2)}) async-start(bf16[32,4,96]{2,1,0:T(4,128)(2,1)} %shard_map.75), calls=%async_computation | async-start | bytes 65536 | tf_op jit(solution)/shard_map/all_to_all | solution.py:452
  15.1 0.6 %dynamic_slice.3 = s32[1]{0:T(128)} dynamic-slice(s32[8]{0:T(128)S(1)} %copy-done.5, s32[]{:T(128)S(6)} %select_n.11), dynamic_slice_sizes={1} | dynamic-slice | bytes 12 | tf_op jit(solution)/shard_map/dynamic_slice | solution.py:446
  16.4 6.0 %all-to-all-done.coeffs = bf16[32,4,96]{2,1,0:T(4,128)(2,1)S(1)} async-done(((bf16[32,4,96]{2,1,0:T(4,128)(2,1)}), bf16[32,4,96]{2,1,0:T(4,128)(2,1)S(1)}, u32[]{:S(2)}, u32[]{:S(2)}) %all-to-all-start) | async-done | bytes 24608 | tf_op jit(solution)/shard_map/all_to_all | solution.py:452
  22.4 0.9 %shard_map.76 = f32[16,2,320]{2,1,0:T(2,128)} custom-call(f32[8,320]{1,0:T(8,128)S(1)} %broadcast_in_dim.26.first_wave, bf16[32,4,96]{2,1,0:T(4,128)(2,1)S(1)} %all-to-all-done.coeffs, bf16[1024,320]{1,0:T(8,128)(2,1)S(1)} %get-tuple-element.24.spread_analysis), custom_call_target="tpu_custom_call" | custom-call | tf_op jit(solution)/shard_map/pallas_call | solution.py:455
  (3 shorter events, 0.0 us)
Async XLA Ops:
  0.0 1.3 %copy-start = (s32[20,3200]{1,0:T(8,128)S(1)}, s32[20,3200]{1,0:T(8,128)}, u32[]{:S(2)}) copy-start(s32[20,3200]{1,0:T(8,128)} %dep_row.1) | copy-start | bytes 768004
  0.0 1.3 %copy-start.1 = (s32[20,3200]{1,0:T(8,128)S(1)}, s32[20,3200]{1,0:T(8,128)}, u32[]{:S(2)}) copy-start(s32[20,3200]{1,0:T(8,128)} %dep_col.1) | copy-start | bytes 768004
  0.0 1.3 %copy-start.2 = (bf16[20,3200]{1,0:T(8,128)(2,1)S(1)}, bf16[20,3200]{1,0:T(8,128)(2,1)}, u32[]{:S(2)}) copy-start(bf16[20,3200]{1,0:T(8,128)(2,1)} %lat_frac.1) | copy-start | bytes 384004
  0.0 1.3 %copy-start.3 = (bf16[20,3200]{1,0:T(8,128)(2,1)S(1)}, bf16[20,3200]{1,0:T(8,128)(2,1)}, u32[]{:S(2)}) copy-start(bf16[20,3200]{1,0:T(8,128)(2,1)} %lon_frac.1) | copy-start | bytes 384004
  1.3 3.5 %copy-start.4 = (bf16[1,160,320]{2,1,0:T(8,128)(2,1)S(1)}, bf16[1,160,320]{2,1,0:T(8,128)(2,1)}, u32[]{:S(2)}) copy-start(bf16[1,160,320]{2,1,0:T(8,128)(2,1)} %param.13) | copy-start | bytes 307204
  1.6 3.0 %copy-start.5 = (s32[8]{0:T(128)S(1)}, s32[8]{0:T(128)}, u32[]{:S(2)}) copy-start(s32[8]{0:T(128)} %param.12) | copy-start | bytes 100
  1.6 8.9 %collective-permute-start = (bf16[16,3200]{1,0:T(8,128)(2,1)S(1)}, bf16[16,3200]{1,0:T(8,128)(2,1)S(1)}, u32[]{:S(2)}, u32[]{:S(2)}) collective-permute-start(bf16[16,3200]{1,0:T(8,128)(2,1)S(1)} %get-tuple-element.15.sent), channel_id=1, source_target_pairs={{0,4},{4,8},{8,12},{12,16},{16,20},{20,24},{24,28},{28,0},{1,5},{5... | collective-permute-start | bytes 307208 | tf_op jit(solution)/shard_map/ppermute | solution.py:409
  12.0 10.3 %all-to-all-start = ((bf16[32,4,96]{2,1,0:T(4,128)(2,1)}), bf16[32,4,96]{2,1,0:T(4,128)(2,1)S(1)}, u32[]{:S(2)}, u32[]{:S(2)}) async-start(bf16[32,4,96]{2,1,0:T(4,128)(2,1)} %shard_map.75), calls=%async_computation | async-start | bytes 65536 | tf_op jit(solution)/shard_map/all_to_all | solution.py:452

commit v14 on v13

--- a/solution.py
+++ b/solution.py
@@ -16,7 +16,8 @@
 SPAN = LANES - 2 * REACH - 1
 ROW_BITS = 5
 INNER_AT_ONCE = 2
-RIM_AT_ONCE = 4
+RIM_AT_ONCE = 8
+SUM_AT_ONCE = 4
 
 
 def lane_gather(values, indices):
@@ -90,10 +91,16 @@
     west_lane, east_lane, row_step = plan
     row_step = row_step.astype(jnp.float32).astype(jnp.bfloat16)
     masks = [row_step == float(step) for step in range(2 * RIM - 1)]
+    last = 2 * RIM - 1
 
     def pick(gathered):
-        low, high = gathered[2 * RIM - 1], gathered[2 * RIM]
-        for position in range(2 * RIM - 2, -1, -1):
+        if len(gathered) > 2 * RIM:
+            low, high = gathered[last], gathered[last + 1]
+        else:
+            zero = jnp.zeros_like(gathered[0])
+            low = jnp.where(row_step == float(last), gathered[last], zero)
+            high = jnp.where(row_step == -1.0, gathered[0], zero)
+        for position in range(last - 1, -1, -1):
             low = jnp.where(masks[position], gathered[position], low)
             high = jnp.where(masks[position], gathered[position + 1], high)
         return low.astype(jnp.float32), high.astype(jnp.float32)
@@ -109,9 +116,8 @@
     return departed
 
 
-def in_groups(count, at_once, group):
-    for at in range(0, count, at_once):
-        group(list(range(at, min(at + at_once, count))))
+def groups_of(count, at_once):
+    return [range(at, min(at + at_once, count)) for at in range(0, count, at_once)]
 
 
 def pack_kernel(
@@ -215,37 +221,44 @@
         ).astype(jnp.bfloat16)
 
 
-def add_up(basis, values):
-    return lax.dot_general(
-        basis, values, (((1,), (1,)), ((), ())), preferred_element_type=jnp.float32
-    )
+def add_up(total, basis, values, windows):
+    cols = slice(windows[0] * LANES, (windows[-1] + 1) * LANES)
+    part = lax.dot_general(
+        basis[:, cols], values[:, cols], (((1,), (1,)), ((), ())), preferred_element_type=jnp.float32
+    )
+    return part if total is None else total + part
 
 
 def inner_kernel(
     grid, plans, own, sent, ids, analysis,
-    fourier_out, basis, spread_analysis, windows, departed, rim_departed, steps, *, slices,
+    fourier_out, basis, spread_analysis, windows, held_plans, departed, rim_departed, steps, *, slices,
 ):
     lon_count = grid.shape[1]
     inner = plans.shape[0] // 3
     rim, fields, held = RIM * slices, EDGE * slices, grid.shape[0]
-    plan_end = held + 3 * inner
     spread = rim_spread(slices)
     fill_steps(steps)
-    for slot in range(windows.shape[0]):
-        windows[slot, 0:rim, :] = jnp.zeros((rim, LANES), jnp.float32)
-        windows[slot, rim + held :, :] = jnp.zeros((rim, LANES), jnp.float32)
-    groups = ids.shape[0] // 4
-    few = groups <= 4
-    waves = [waves_of(ids, at) for at in range(groups if few else 0)]
-
-    def group_of(ts):
-        blocks = [cut((grid, plans, own, sent), t, lon_count, steps) for t in ts]
-        for t, block in zip(ts, blocks):
+    rim_base = jnp.where(lax.broadcasted_iota(jnp.int32, (fields, LANES), 0) < rim, 1, 0)
+    quads = ids.shape[0] // 4
+    few = quads <= 4
+    waves = [waves_of(ids, at) for at in range(quads if few else 0)]
+
+    def prepare(ts):
+        for t in ts:
+            block = cut((grid, plans, own, sent), t, lon_count, steps)
             windows[t, rim : rim + held, :] = block[:held]
+            windows[t, 0:rim, :] = jnp.zeros((rim, LANES), jnp.float32)
+            windows[t, rim + held :, :] = jnp.zeros((rim, LANES), jnp.float32)
+            held_plans[t, 0 : 3 * inner, :] = block[held : held + 3 * inner]
+            for at, plan in enumerate(rim_plan(spread, block[held + 3 * inner :])):
+                start = 3 * inner + at * fields
+                held_plans[t, start : start + fields, :] = plan
+
+    def finish(ts):
         results, rim_results = [], []
-        for slot, t in enumerate(ts):
+        for t in ts:
             code, lat_weight, lon_weight = [
-                blocks[slot][held + at * inner : held + (at + 1) * inner] for at in range(3)
+                held_plans[t, at * inner : (at + 1) * inner, :] for at in range(3)
             ]
             plan = lane_plan(code)
             weights = corner_weights(lat_weight, lon_weight)
@@ -261,18 +274,23 @@
                 jnp.concatenate(
                     [
                         windows[t, start : start + rim, :]
-                        for start in (slices * position, held - rim + slices * position)
+                        for start in (slices * (position + 1), held - rim + slices * position)
                     ],
                     axis=0,
                 ).astype(jnp.bfloat16)
-                for position in range(2 * RIM + 1)
+                for position in range(2 * RIM)
             ]
-            code, lat_weight, lon_weight = rim_plan(spread, blocks[slot][plan_end:])
+            code, lat_weight, lon_weight = [
+                held_plans[t, 3 * inner + at * fields : 3 * inner + (at + 1) * fields, :]
+                for at in range(3)
+            ]
+            west_lane, east_lane, row_step = lane_plan(code)
             weights = corner_weights(lat_weight, lon_weight)
-            rim_results.append(interpolate(sources, lane_plan(code), weights))
+            plan = west_lane, east_lane, row_step - rim_base
+            rim_results.append((t, interpolate(sources, plan, weights)))
         for t, f, result in results:
             departed[f * inner : (f + 1) * inner, tile_at(t)] = result.astype(jnp.bfloat16)
-        for t, result in zip(ts, rim_results):
+        for t, result in rim_results:
             rim_departed[:, tile_at(t)] = result.astype(jnp.bfloat16)
         for t in ts if few else ():
             for at, wave in enumerate(waves):
@@ -286,12 +304,24 @@
                 basis[rows, tile_at(t)] = basis_tile(t, waves_of(ids, group), lon_count)
             return carry
 
-        lax.fori_loop(0, groups, rows_of, 0)
-    in_groups(departed.shape[1] // LANES, INNER_AT_ONCE, group_of)
+        lax.fori_loop(0, quads, rows_of, 0)
+    count = departed.shape[1] // LANES
+    groups = groups_of(count, INNER_AT_ONCE)
+    totals = [None, None]
+    prepare(groups[0])
+    for at, ts in enumerate(groups):
+        if at + 1 < len(groups):
+            prepare(groups[at + 1])
+        finish(ts)
+        first = max(0, at // SUM_AT_ONCE * SUM_AT_ONCE)
+        if at % SUM_AT_ONCE == SUM_AT_ONCE - 1 or at + 1 == len(groups):
+            done = range(groups[first][0], ts[-1] + 1)
+            totals = [
+                add_up(total, basis, values, done)
+                for total, values in zip(totals, (departed, rim_departed))
+            ]
     spread_rows(analysis, spread_analysis, inner + EDGE, slices)
-    fourier_out[...] = jnp.concatenate(
-        [add_up(basis[...], departed[...]), add_up(basis[...], rim_departed[...])], axis=1
-    )
+    fourier_out[...] = jnp.concatenate(totals, axis=1)
 
 
 def rim_kernel(
@@ -314,8 +344,8 @@
         return row_weight * (west + lon_weight * (east - west))
 
     def prepare(ts):
-        packed = [[turned(side, t, lon_count) for side in (arrived, own)] for t in ts]
-        for t, sides in zip(ts, packed):
+        for t in ts:
+            sides = [turned(side, t, lon_count) for side in (arrived, own)]
             for at, plan in enumerate(rim_plan(spread, jnp.concatenate(sides, axis=0))):
                 plans[t, at] = plan
             for at, side in enumerate(sides):
@@ -332,9 +362,12 @@
             departed[:, tile_at(t)] = result.astype(jnp.bfloat16)
 
     count = basis.shape[1] // LANES
-    in_groups(count, RIM_AT_ONCE, prepare)
-    in_groups(count, RIM_AT_ONCE, finish)
-    fourier = jnp.concatenate([inner_fourier[...], add_up(basis[...], departed[...])], axis=1)
+    prepare(range(count))
+    total = None
+    for ts in groups_of(count, RIM_AT_ONCE):
+        finish(ts)
+        total = add_up(total, basis, departed, ts)
+    fourier = jnp.concatenate([inner_fourier[...], total], axis=1)
     for at in range(fourier_out.shape[0]):
         pair = at // levs
         fourier_out[at] = fourier[4 * pair : 4 * pair + 4].astype(jnp.bfloat16)
@@ -421,6 +454,7 @@
         out_specs=(vmem,) * 3,
         scratch_shapes=[
             pltpu.VMEM((windows, (band_rows + 2 * RIM) * slices, LANES), jnp.float32),
+            pltpu.VMEM((windows, 3 * (inner + fields), LANES), jnp.float32),
             pltpu.VMEM((slices * inner, windows * LANES), jnp.bfloat16),
             pltpu.VMEM((fields, windows * LANES), jnp.bfloat16),
             pltpu.VMEM((2 * LANES, LANES), jnp.int16),

time: 23.4 us -> 25.1 us (1.073)
  Pallas kernels: 6.19 us -> 8.29 us
  waiting for transfers between devices: 8.29 us -> 6.19 us
  starting transfers between devices: 6.1 us -> 7.75 us
    ppermute x1, waiting for transfers between devices: 2.31 us -> 0.21 us  [shards(): lax.ppermute(sent_rim, 'lat', [(i, (i + 1) % bands) for i in range(bands)])]
    pallas_call x1, Pallas kernels: 3.53 us -> 5.62 us  [shards(): pl.pallas_call(functools.partial(inner_kernel, slices=slices), out_shape=...]
    all_to_all x1, starting transfers between devices: 3.07 us -> 4.72 us  [shards(): lax.all_to_all(fourier, ('lat', 'lev'), split_axis=0, concat_axis=0, tile...]
  transfers between devices with their start and end apart: 2 -> 2, of which waited for: 2 -> 2; matrix products, arithmetic and copies ran while one was open for 3% -> 3% of each run, Pallas kernels for 15% -> 23%
where the time goes in v14:
time: 25.1 us; the launch traced here: 24.9 us
  Pallas kernels  8.29 us (33%)
  starting transfers between devices  7.75 us (31%)
  waiting for transfers between devices  6.19 us (25%)
  local copies, waits for them, and re-layouts  1.96 us (8%)
  between operations  0.71 us (3%)
    all_to_all x1, waiting for transfers between devices, shards(): lax.all_to_all(fourier, ('lat', 'lev'), split_axis=0, concat_axis=0, tile...  5.98 us
    pallas_call x1, Pallas kernels, shards(): pl.pallas_call(functools.partial(inner_kernel, slices=slices), out_shape=...  5.62 us
    all_to_all x1, starting transfers between devices, shards(): lax.all_to_all(fourier, ('lat', 'lev'), split_axis=0, concat_axis=0, tile...  4.72 us
    ppermute x1, starting transfers between devices, shards(): lax.ppermute(sent_rim, 'lat', [(i, (i + 1) % bands) for i in range(bands)])  3.03 us
    pallas_call x1, Pallas kernels, shards(): pl.pallas_call(functools.partial(rim_kernel, slices=slices, levs=levs), o...  1.44 us
    reshape x1, local copies, waits for them, and re-layouts, shards(): rows = grid.transpose(1, 0, 2).reshape(band_rows * slices, lon_count)  1.23 us
    pallas_call x1, Pallas kernels, shards(): pl.pallas_call(functools.partial(legendre_kernel, levs=levs, slices=slice...  0.9 us
    dynamic_slice x1, local copies, waits for them, and re-layouts, shards(): own_id = lax.dynamic_slice_in_dim(late_ids, lax.axis_index('lat'), 1)  0.61 us
  transfers between devices with their start and end apart: 2, of which 2 were waited for; matrix products, arithmetic and copies ran while one was open for 3% of the time, Pallas kernels for 23%

profile of v14, /device:TPU:0, one launch (start us, length us, event | category | flops | bytes accessed | tf_op | source)
XLA Modules:
  0.0 24.9 jit_solution(7801978253938519226)
XLA Ops:
  0.0 0.0 copy-start
  0.0 0.0 copy-start.1
  0.0 0.0 copy-start.2
  0.0 0.0 copy-start.3
  0.0 1.2 %reshape.14.rows.grid = bf16[80,3200]{1,0:T(8,128)(2,1)S(1)} reshape(bf16[20,4,3200]{2,1,0:T(4,128)(2,1)} %bitcast.6) | data formatting | bytes 1024000 | tf_op jit(solution)/shard_map/reshape | solution.py:428
  1.2 0.0 copy-done
  1.3 0.0 copy-done.1
  1.3 0.0 copy-done.2
  1.3 0.0 copy-done.3
  1.3 0.0 copy-start.4
  1.3 0.3 %shard_map.73 = (bf16[16,3200]{1,0:T(8,128)(2,1)S(1)}, bf16[16,3200]{1,0:T(8,128)(2,1)S(1)}, bf16[48,3200]{1,0:T(8,128)(2,1)S(1)}) custom-call(s32[1]{0:T(128)} %bitcast.band_start, bf16[80,3200]{1,0:T(8,128)(2,1)S(1)} %reshape.14.rows.grid, s32[20,3200]{1,0:T(8,128)S(1)} %copy-done, s32[20,3200]{1,0:T(8,128)S(1)} %copy-done.1, ...), custom_call_target="tpu_custom_call" | custom-call | tf_op jit(solution)/shard_map/pallas_call | solution.py:430
  1.6 0.0 copy-start.5
  1.6 3.0 %collective-permute-start = (bf16[16,3200]{1,0:T(8,128)(2,1)S(1)}, bf16[16,3200]{1,0:T(8,128)(2,1)S(1)}, u32[]{:S(2)}, u32[]{:S(2)}) collective-permute-start(bf16[16,3200]{1,0:T(8,128)(2,1)S(1)} %get-tuple-element.15.sent), channel_id=1, source_target_pairs={{0,4},{4,8},{8,12},{12,16},{16,20},{20,24},{24,28},{28,0},{1,5},{5... | collective-permute-start | bytes 307208 | tf_op jit(solution)/shard_map/ppermute | solution.py:442
  4.7 0.0 copy-done.5
  4.7 0.1 broadcast_in_dim.23.ids
  4.8 0.0 copy-done.4
  4.8 5.6 %shard_map.74 = (f32[32,80]{1,0:T(8,128)S(1)}, bf16[32,3712]{1,0:T(8,128)(2,1)S(1)}, bf16[1024,320]{1,0:T(8,128)(2,1)S(1)}) custom-call(bf16[80,3200]{1,0:T(8,128)(2,1)S(1)} %reshape.14.rows.grid, bf16[48,3200]{1,0:T(8,128)(2,1)S(1)} %get-tuple-element.18.plans, bf16[16,3200]{1,0:T(8,128)(2,1)S(1)} %get-tuple-element.16.own, ...), custom_call_target="tpu_custom_call" | custom-call | flops 100000000 | bytes 2000000 | tf_op jit(solution)/shard_map/pallas_call | solution.py:446
  10.4 0.2 collective-permute-done.arrived
  10.6 1.4 %shard_map.75 = bf16[32,4,96]{2,1,0:T(4,128)(2,1)} custom-call(bf16[16,3200]{1,0:T(8,128)(2,1)S(1)} %collective-permute-done.arrived, bf16[16,3200]{1,0:T(8,128)(2,1)S(1)} %get-tuple-element.16.own, bf16[32,3712]{1,0:T(8,128)(2,1)S(1)} %get-tuple-element.20.basis, f32[32,80]{1,0:T(8,128)S(1)} %get-tuple-element.21.inner_fourier), custom_call_target="tpu_custom_call" | custom-call | tf_op jit(solution)/shard_map/pallas_call | solution.py:467
  12.0 4.7 %all-to-all-start = ((bf16[32,4,96]{2,1,0:T(4,128)(2,1)}), bf16[32,4,96]{2,1,0:T(4,128)(2,1)S(1)}, u32[]{:S(2)}, u32[]{:S(2)}) async-start(bf16[32,4,96]{2,1,0:T(4,128)(2,1)} %shard_map.75), calls=%async_computation | async-start | bytes 65536 | tf_op jit(solution)/shard_map/all_to_all | solution.py:486
  16.8 0.6 %dynamic_slice.3 = s32[1]{0:T(128)} dynamic-slice(s32[8]{0:T(128)S(1)} %copy-done.5, s32[]{:T(128)S(6)} %select_n.11), dynamic_slice_sizes={1} | dynamic-slice | bytes 12 | tf_op jit(solution)/shard_map/dynamic_slice | solution.py:480
  18.0 6.0 %all-to-all-done.coeffs = bf16[32,4,96]{2,1,0:T(4,128)(2,1)S(1)} async-done(((bf16[32,4,96]{2,1,0:T(4,128)(2,1)}), bf16[32,4,96]{2,1,0:T(4,128)(2,1)S(1)}, u32[]{:S(2)}, u32[]{:S(2)}) %all-to-all-start) | async-done | bytes 24608 | tf_op jit(solution)/shard_map/all_to_all | solution.py:486
  24.0 0.9 %shard_map.76 = f32[16,2,320]{2,1,0:T(2,128)} custom-call(f32[8,320]{1,0:T(8,128)S(1)} %broadcast_in_dim.26.first_wave, bf16[32,4,96]{2,1,0:T(4,128)(2,1)S(1)} %all-to-all-done.coeffs, bf16[1024,320]{1,0:T(8,128)(2,1)S(1)} %get-tuple-element.24.spread_analysis), custom_call_target="tpu_custom_call" | custom-call | tf_op jit(solution)/shard_map/pallas_call | solution.py:489
  (3 shorter events, 0.0 us)
Async XLA Ops:
  0.0 1.3 %copy-start = (s32[20,3200]{1,0:T(8,128)S(1)}, s32[20,3200]{1,0:T(8,128)}, u32[]{:S(2)}) copy-start(s32[20,3200]{1,0:T(8,128)} %dep_row.1) | copy-start | bytes 768004
  0.0 1.3 %copy-start.1 = (s32[20,3200]{1,0:T(8,128)S(1)}, s32[20,3200]{1,0:T(8,128)}, u32[]{:S(2)}) copy-start(s32[20,3200]{1,0:T(8,128)} %dep_col.1) | copy-start | bytes 768004
  0.0 1.3 %copy-start.2 = (bf16[20,3200]{1,0:T(8,128)(2,1)S(1)}, bf16[20,3200]{1,0:T(8,128)(2,1)}, u32[]{:S(2)}) copy-start(bf16[20,3200]{1,0:T(8,128)(2,1)} %lat_frac.1) | copy-start | bytes 384004
  0.0 1.3 %copy-start.3 = (bf16[20,3200]{1,0:T(8,128)(2,1)S(1)}, bf16[20,3200]{1,0:T(8,128)(2,1)}, u32[]{:S(2)}) copy-start(bf16[20,3200]{1,0:T(8,128)(2,1)} %lon_frac.1) | copy-start | bytes 384004
  1.3 3.5 %copy-start.4 = (bf16[1,160,320]{2,1,0:T(8,128)(2,1)S(1)}, bf16[1,160,320]{2,1,0:T(8,128)(2,1)}, u32[]{:S(2)}) copy-start(bf16[1,160,320]{2,1,0:T(8,128)(2,1)} %param.13) | copy-start | bytes 307204
  1.6 3.0 %copy-start.5 = (s32[8]{0:T(128)S(1)}, s32[8]{0:T(128)}, u32[]{:S(2)}) copy-start(s32[8]{0:T(128)} %param.12) | copy-start | bytes 100
  1.6 8.9 %collective-permute-start = (bf16[16,3200]{1,0:T(8,128)(2,1)S(1)}, bf16[16,3200]{1,0:T(8,128)(2,1)S(1)}, u32[]{:S(2)}, u32[]{:S(2)}) collective-permute-start(bf16[16,3200]{1,0:T(8,128)(2,1)S(1)} %get-tuple-element.15.sent), channel_id=1, source_target_pairs={{0,4},{4,8},{8,12},{12,16},{16,20},{20,24},{24,28},{28,0},{1,5},{5... | collective-permute-start | bytes 307208 | tf_op jit(solution)/shard_map/ppermute | solution.py:442
  12.0 12.0 %all-to-all-start = ((bf16[32,4,96]{2,1,0:T(4,128)(2,1)}), bf16[32,4,96]{2,1,0:T(4,128)(2,1)S(1)}, u32[]{:S(2)}, u32[]{:S(2)}) async-start(bf16[32,4,96]{2,1,0:T(4,128)(2,1)} %shard_map.75), calls=%async_computation | async-start | bytes 65536 | tf_op jit(solution)/shard_map/all_to_all | solution.py:486

commit v15 on v13

--- a/solution.py
+++ b/solution.py
@@ -16,7 +16,7 @@
 SPAN = LANES - 2 * REACH - 1
 ROW_BITS = 5
 INNER_AT_ONCE = 2
-RIM_AT_ONCE = 4
+RIM_AT_ONCE = 8
 
 
 def lane_gather(values, indices):
@@ -90,10 +90,16 @@
     west_lane, east_lane, row_step = plan
     row_step = row_step.astype(jnp.float32).astype(jnp.bfloat16)
     masks = [row_step == float(step) for step in range(2 * RIM - 1)]
+    last = 2 * RIM - 1
 
     def pick(gathered):
-        low, high = gathered[2 * RIM - 1], gathered[2 * RIM]
-        for position in range(2 * RIM - 2, -1, -1):
+        if len(gathered) > 2 * RIM:
+            low, high = gathered[last], gathered[last + 1]
+        else:
+            zero = jnp.zeros_like(gathered[0])
+            low = jnp.where(row_step == float(last), gathered[last], zero)
+            high = jnp.where(row_step == -1.0, gathered[0], zero)
+        for position in range(last - 1, -1, -1):
             low = jnp.where(masks[position], gathered[position], low)
             high = jnp.where(masks[position], gathered[position + 1], high)
         return low.astype(jnp.float32), high.astype(jnp.float32)
@@ -109,9 +115,8 @@
     return departed
 
 
-def in_groups(count, at_once, group):
-    for at in range(0, count, at_once):
-        group(list(range(at, min(at + at_once, count))))
+def groups_of(count, at_once):
+    return [range(at, min(at + at_once, count)) for at in range(0, count, at_once)]
 
 
 def pack_kernel(
@@ -215,10 +220,12 @@
         ).astype(jnp.bfloat16)
 
 
-def add_up(basis, values):
-    return lax.dot_general(
-        basis, values, (((1,), (1,)), ((), ())), preferred_element_type=jnp.float32
-    )
+def add_up(total, basis, values, windows):
+    cols = slice(windows[0] * LANES, (windows[-1] + 1) * LANES)
+    part = lax.dot_general(
+        basis[:, cols], values[:, cols], (((1,), (1,)), ((), ())), preferred_element_type=jnp.float32
+    )
+    return part if total is None else total + part
 
 
 def inner_kernel(
@@ -231,12 +238,13 @@
     plan_end = held + 3 * inner
     spread = rim_spread(slices)
     fill_steps(steps)
+    rim_base = jnp.where(lax.broadcasted_iota(jnp.int32, (fields, LANES), 0) < rim, 1, 0)
     for slot in range(windows.shape[0]):
         windows[slot, 0:rim, :] = jnp.zeros((rim, LANES), jnp.float32)
         windows[slot, rim + held :, :] = jnp.zeros((rim, LANES), jnp.float32)
-    groups = ids.shape[0] // 4
-    few = groups <= 4
-    waves = [waves_of(ids, at) for at in range(groups if few else 0)]
+    quads = ids.shape[0] // 4
+    few = quads <= 4
+    waves = [waves_of(ids, at) for at in range(quads if few else 0)]
 
     def group_of(ts):
         blocks = [cut((grid, plans, own, sent), t, lon_count, steps) for t in ts]
@@ -261,15 +269,17 @@
                 jnp.concatenate(
                     [
                         windows[t, start : start + rim, :]
-                        for start in (slices * position, held - rim + slices * position)
+                        for start in (slices * (position + 1), held - rim + slices * position)
                     ],
                     axis=0,
                 ).astype(jnp.bfloat16)
-                for position in range(2 * RIM + 1)
+                for position in range(2 * RIM)
             ]
             code, lat_weight, lon_weight = rim_plan(spread, blocks[slot][plan_end:])
             weights = corner_weights(lat_weight, lon_weight)
-            rim_results.append(interpolate(sources, lane_plan(code), weights))
+            west_lane, east_lane, row_step = lane_plan(code)
+            plan = west_lane, east_lane, row_step - rim_base
+            rim_results.append(interpolate(sources, plan, weights))
         for t, f, result in results:
             departed[f * inner : (f + 1) * inner, tile_at(t)] = result.astype(jnp.bfloat16)
         for t, result in zip(ts, rim_results):
@@ -286,11 +296,13 @@
                 basis[rows, tile_at(t)] = basis_tile(t, waves_of(ids, group), lon_count)
             return carry
 
-        lax.fori_loop(0, groups, rows_of, 0)
-    in_groups(departed.shape[1] // LANES, INNER_AT_ONCE, group_of)
+        lax.fori_loop(0, quads, rows_of, 0)
+    count = departed.shape[1] // LANES
+    for ts in groups_of(count, INNER_AT_ONCE):
+        group_of(ts)
     spread_rows(analysis, spread_analysis, inner + EDGE, slices)
     fourier_out[...] = jnp.concatenate(
-        [add_up(basis[...], departed[...]), add_up(basis[...], rim_departed[...])], axis=1
+        [add_up(None, basis, values, range(count)) for values in (departed, rim_departed)], axis=1
     )
 
 
@@ -299,42 +311,62 @@
 ):
     lon_count = arrived.shape[1]
     rim, fields = RIM * slices, EDGE * slices
-    spread = rim_spread(slices)
     out_row = lax.broadcasted_iota(jnp.int32, (fields, LANES), 0) // slices
-    far_step = jnp.where(out_row < RIM, 2 * RIM, 0)
-    near_step = jnp.where(out_row == RIM - 1, 2 * RIM - 1, jnp.where(out_row == RIM, 1, -2))
+    far_step = jnp.where(out_row < RIM, 2.0 * RIM, 0.0)
+    near_step = jnp.where(out_row == RIM - 1, 2.0 * RIM - 1.0, jnp.where(out_row == RIM, 1.0, -2.0))
+    lane = lax.broadcasted_iota(jnp.int32, (fields, LANES), 1) - REACH
+    sublane = lax.broadcasted_iota(jnp.int32, (rim, LANES), 0)
 
     def part(source, lanes, row_step, lat_weight, lon_weight, step):
         west, east = [lane_gather(source, lane).astype(jnp.float32) for lane in lanes]
         row_weight = jnp.where(
             row_step == step,
             1.0 - lat_weight,
-            jnp.where(row_step == step - 1, lat_weight, 0.0),
+            jnp.where(row_step == step - 1.0, lat_weight, 0.0),
         )
         return row_weight * (west + lon_weight * (east - west))
 
-    def prepare(ts):
-        packed = [[turned(side, t, lon_count) for side in (arrived, own)] for t in ts]
-        for t, sides in zip(ts, packed):
-            for at, plan in enumerate(rim_plan(spread, jnp.concatenate(sides, axis=0))):
-                plans[t, at] = plan
-            for at, side in enumerate(sides):
-                windows[t, rim * at : rim * (at + 1), :] = side.astype(jnp.float32)[:rim]
-
-    def finish(ts):
+    def prepare(t):
+        for at, side in enumerate((arrived, own)):
+            block = turned(side, t, lon_count).astype(jnp.float32)
+            windows[t, rim * at : rim * (at + 1), :] = block[:rim]
+            plans[t, 4 * RIM * at : 4 * RIM * (at + 1), :] = block[rim:]
+
+    def finish(t):
+        row_step, shift, lat_weight, lon_weight = [
+            jnp.concatenate(
+                [
+                    jnp.where(
+                        sublane < slices,
+                        *[
+                            jnp.broadcast_to(plans[t, row : row + 1, :], (rim, LANES))
+                            for row in (start, start + 1)
+                        ],
+                    )
+                    for start in (RIM * at, RIM * (at + 4))
+                ],
+                axis=0,
+            )
+            for at in range(4)
+        ]
+        west = lane + shift.astype(jnp.int32)
+        lanes = [(column & LANES - 1).astype(jnp.int16) for column in (west, west + 1)]
+        plan = lanes, row_step, lat_weight, lon_weight
+        far = jnp.concatenate([windows[t, rim:, :], windows[t, 0:rim, :]], axis=0)
+        near = jnp.concatenate([windows[t, slices : slices + rim, :]] * 2, axis=0)
+        result = part(far.astype(jnp.bfloat16), *plan, far_step)
+        result += part(near.astype(jnp.bfloat16), *plan, near_step)
+        departed[:, tile_at(t)] = result.astype(jnp.bfloat16)
+
+    count = basis.shape[1] // LANES
+    for t in range(count):
+        prepare(t)
+    total = None
+    for ts in groups_of(count, RIM_AT_ONCE):
         for t in ts:
-            west_lane, east_lane, row_step = lane_plan(plans[t, 0])
-            plan = (west_lane, east_lane), row_step, plans[t, 1], plans[t, 2]
-            far = jnp.concatenate([windows[t, rim:, :], windows[t, 0:rim, :]], axis=0)
-            near = jnp.concatenate([windows[t, slices : slices + rim, :]] * 2, axis=0)
-            result = part(far.astype(jnp.bfloat16), *plan, far_step)
-            result += part(near.astype(jnp.bfloat16), *plan, near_step)
-            departed[:, tile_at(t)] = result.astype(jnp.bfloat16)
-
-    count = basis.shape[1] // LANES
-    in_groups(count, RIM_AT_ONCE, prepare)
-    in_groups(count, RIM_AT_ONCE, finish)
-    fourier = jnp.concatenate([inner_fourier[...], add_up(basis[...], departed[...])], axis=1)
+            finish(t)
+        total = add_up(total, basis, departed, ts)
+    fourier = jnp.concatenate([inner_fourier[...], total], axis=1)
     for at in range(fourier_out.shape[0]):
         pair = at // levs
         fourier_out[at] = fourier[4 * pair : 4 * pair + 4].astype(jnp.bfloat16)
@@ -437,7 +469,7 @@
         out_specs=vmem,
         scratch_shapes=[
             pltpu.VMEM((windows, fields, LANES), jnp.float32),
-            pltpu.VMEM((windows, 3, fields, LANES), jnp.float32),
+            pltpu.VMEM((windows, 8 * RIM, LANES), jnp.float32),
             pltpu.VMEM((fields, windows * LANES), jnp.bfloat16),
         ],
         compiler_params=params,

time: 23.4 us -> 23.3 us (level)
  no operation moved by 1% of the time
where the time goes in v15:
time: 23.3 us; the launch traced here: 23.1 us
  waiting for transfers between devices  8.28 us (36%)
  starting transfers between devices  6.1 us (26%)
  Pallas kernels  6.07 us (26%)
  local copies, waits for them, and re-layouts  1.96 us (8%)
  between operations  0.71 us (3%)
    all_to_all x1, waiting for transfers between devices, shards(): lax.all_to_all(fourier, ('lat', 'lev'), split_axis=0, concat_axis=0, tile...  5.98 us
    pallas_call x1, Pallas kernels, shards(): pl.pallas_call(functools.partial(inner_kernel, slices=slices), out_shape=...  3.54 us
    all_to_all x1, starting transfers between devices, shards(): lax.all_to_all(fourier, ('lat', 'lev'), split_axis=0, concat_axis=0, tile...  3.07 us
    ppermute x1, starting transfers between devices, shards(): lax.ppermute(sent_rim, 'lat', [(i, (i + 1) % bands) for i in range(bands)])  3.03 us
    ppermute x1, waiting for transfers between devices, shards(): lax.ppermute(sent_rim, 'lat', [(i, (i + 1) % bands) for i in range(bands)])  2.3 us
    pallas_call x1, Pallas kernels, shards(): pl.pallas_call(functools.partial(rim_kernel, slices=slices, levs=levs), o...  1.3 us
    reshape x1, local copies, waits for them, and re-layouts, shards(): rows = grid.transpose(1, 0, 2).reshape(band_rows * slices, lon_count)  1.23 us
    pallas_call x1, Pallas kernels, shards(): pl.pallas_call(functools.partial(legendre_kernel, levs=levs, slices=slice...  0.9 us
  transfers between devices with their start and end apart: 2, of which 2 were waited for; matrix products, arithmetic and copies ran while one was open for 3% of the time, Pallas kernels for 15%

profile of v15, /device:TPU:0, one launch (start us, length us, event | category | flops | bytes accessed | tf_op | source)
XLA Modules:
  0.0 23.1 jit_solution(14984796797344226847)
XLA Ops:
  0.0 0.0 copy-start
  0.0 0.0 copy-start.1
  0.0 0.0 copy-start.2
  0.0 0.0 copy-start.3
  0.0 1.2 %reshape.14.rows.grid = bf16[80,3200]{1,0:T(8,128)(2,1)S(1)} reshape(bf16[20,4,3200]{2,1,0:T(4,128)(2,1)} %bitcast.6) | data formatting | bytes 1024000 | tf_op jit(solution)/shard_map/reshape | solution.py:427
  1.2 0.0 copy-done
  1.3 0.0 copy-done.1
  1.3 0.0 copy-done.2
  1.3 0.0 copy-done.3
  1.3 0.0 copy-start.4
  1.3 0.3 %shard_map.73 = (bf16[16,3200]{1,0:T(8,128)(2,1)S(1)}, bf16[16,3200]{1,0:T(8,128)(2,1)S(1)}, bf16[48,3200]{1,0:T(8,128)(2,1)S(1)}) custom-call(s32[1]{0:T(128)} %bitcast.band_start, bf16[80,3200]{1,0:T(8,128)(2,1)S(1)} %reshape.14.rows.grid, s32[20,3200]{1,0:T(8,128)S(1)} %copy-done, s32[20,3200]{1,0:T(8,128)S(1)} %copy-done.1, ...), custom_call_target="tpu_custom_call" | custom-call | tf_op jit(solution)/shard_map/pallas_call | solution.py:429
  1.6 0.0 copy-start.5
  1.6 3.0 %collective-permute-start = (bf16[16,3200]{1,0:T(8,128)(2,1)S(1)}, bf16[16,3200]{1,0:T(8,128)(2,1)S(1)}, u32[]{:S(2)}, u32[]{:S(2)}) collective-permute-start(bf16[16,3200]{1,0:T(8,128)(2,1)S(1)} %get-tuple-element.15.sent), channel_id=1, source_target_pairs={{0,4},{4,8},{8,12},{12,16},{16,20},{20,24},{24,28},{28,0},{1,5},{5... | collective-permute-start | bytes 307208 | tf_op jit(solution)/shard_map/ppermute | solution.py:441
  4.7 0.0 copy-done.5
  4.7 0.1 broadcast_in_dim.23.ids
  4.8 0.0 copy-done.4
  4.8 3.5 %shard_map.74 = (f32[32,80]{1,0:T(8,128)S(1)}, bf16[32,3712]{1,0:T(8,128)(2,1)S(1)}, bf16[1024,320]{1,0:T(8,128)(2,1)S(1)}) custom-call(bf16[80,3200]{1,0:T(8,128)(2,1)S(1)} %reshape.14.rows.grid, bf16[48,3200]{1,0:T(8,128)(2,1)S(1)} %get-tuple-element.18.plans, bf16[16,3200]{1,0:T(8,128)(2,1)S(1)} %get-tuple-element.16.own, ...), custom_call_target="tpu_custom_call" | custom-call | flops 100000000 | bytes 2000000 | tf_op jit(solution)/shard_map/pallas_call | solution.py:445
  8.3 2.3 %collective-permute-done.arrived = bf16[16,3200]{1,0:T(8,128)(2,1)S(1)} collective-permute-done((bf16[16,3200]{1,0:T(8,128)(2,1)S(1)}, bf16[16,3200]{1,0:T(8,128)(2,1)S(1)}, u32[]{:S(2)}, u32[]{:S(2)}) %collective-permute-start) | collective-permute-done | bytes 102432 | tf_op jit(solution)/shard_map/ppermute | solution.py:441
  10.6 1.3 %shard_map.75 = bf16[32,4,96]{2,1,0:T(4,128)(2,1)} custom-call(bf16[16,3200]{1,0:T(8,128)(2,1)S(1)} %collective-permute-done.arrived, bf16[16,3200]{1,0:T(8,128)(2,1)S(1)} %get-tuple-element.16.own, bf16[32,3712]{1,0:T(8,128)(2,1)S(1)} %get-tuple-element.20.basis, f32[32,80]{1,0:T(8,128)S(1)} %get-tuple-element.21.inner_fourier), custom_call_target="tpu_custom_call" | custom-call | tf_op jit(solution)/shard_map/pallas_call | solution.py:465
  11.9 3.1 %all-to-all-start = ((bf16[32,4,96]{2,1,0:T(4,128)(2,1)}), bf16[32,4,96]{2,1,0:T(4,128)(2,1)S(1)}, u32[]{:S(2)}, u32[]{:S(2)}) async-start(bf16[32,4,96]{2,1,0:T(4,128)(2,1)} %shard_map.75), calls=%async_computation | async-start | bytes 65536 | tf_op jit(solution)/shard_map/all_to_all | solution.py:484
  15.0 0.6 %dynamic_slice.3 = s32[1]{0:T(128)} dynamic-slice(s32[8]{0:T(128)S(1)} %copy-done.5, s32[]{:T(128)S(6)} %select_n.11), dynamic_slice_sizes={1} | dynamic-slice | bytes 12 | tf_op jit(solution)/shard_map/dynamic_slice | solution.py:478
  16.2 6.0 %all-to-all-done.coeffs = bf16[32,4,96]{2,1,0:T(4,128)(2,1)S(1)} async-done(((bf16[32,4,96]{2,1,0:T(4,128)(2,1)}), bf16[32,4,96]{2,1,0:T(4,128)(2,1)S(1)}, u32[]{:S(2)}, u32[]{:S(2)}) %all-to-all-start) | async-done | bytes 24608 | tf_op jit(solution)/shard_map/all_to_all | solution.py:484
  22.2 0.9 %shard_map.76 = f32[16,2,320]{2,1,0:T(2,128)} custom-call(f32[8,320]{1,0:T(8,128)S(1)} %broadcast_in_dim.26.first_wave, bf16[32,4,96]{2,1,0:T(4,128)(2,1)S(1)} %all-to-all-done.coeffs, bf16[1024,320]{1,0:T(8,128)(2,1)S(1)} %get-tuple-element.24.spread_analysis), custom_call_target="tpu_custom_call" | custom-call | tf_op jit(solution)/shard_map/pallas_call | solution.py:487
  (3 shorter events, 0.0 us)
Async XLA Ops:
  0.0 1.3 %copy-start = (s32[20,3200]{1,0:T(8,128)S(1)}, s32[20,3200]{1,0:T(8,128)}, u32[]{:S(2)}) copy-start(s32[20,3200]{1,0:T(8,128)} %dep_row.1) | copy-start | bytes 768004
  0.0 1.3 %copy-start.1 = (s32[20,3200]{1,0:T(8,128)S(1)}, s32[20,3200]{1,0:T(8,128)}, u32[]{:S(2)}) copy-start(s32[20,3200]{1,0:T(8,128)} %dep_col.1) | copy-start | bytes 768004
  0.0 1.3 %copy-start.2 = (bf16[20,3200]{1,0:T(8,128)(2,1)S(1)}, bf16[20,3200]{1,0:T(8,128)(2,1)}, u32[]{:S(2)}) copy-start(bf16[20,3200]{1,0:T(8,128)(2,1)} %lat_frac.1) | copy-start | bytes 384004
  0.0 1.3 %copy-start.3 = (bf16[20,3200]{1,0:T(8,128)(2,1)S(1)}, bf16[20,3200]{1,0:T(8,128)(2,1)}, u32[]{:S(2)}) copy-start(bf16[20,3200]{1,0:T(8,128)(2,1)} %lon_frac.1) | copy-start | bytes 384004
  1.3 3.5 %copy-start.4 = (bf16[1,160,320]{2,1,0:T(8,128)(2,1)S(1)}, bf16[1,160,320]{2,1,0:T(8,128)(2,1)}, u32[]{:S(2)}) copy-start(bf16[1,160,320]{2,1,0:T(8,128)(2,1)} %param.13) | copy-start | bytes 307204
  1.6 3.0 %copy-start.5 = (s32[8]{0:T(128)S(1)}, s32[8]{0:T(128)}, u32[]{:S(2)}) copy-start(s32[8]{0:T(128)} %param.12) | copy-start | bytes 100
  1.6 8.9 %collective-permute-start = (bf16[16,3200]{1,0:T(8,128)(2,1)S(1)}, bf16[16,3200]{1,0:T(8,128)(2,1)S(1)}, u32[]{:S(2)}, u32[]{:S(2)}) collective-permute-start(bf16[16,3200]{1,0:T(8,128)(2,1)S(1)} %get-tuple-element.15.sent), channel_id=1, source_target_pairs={{0,4},{4,8},{8,12},{12,16},{16,20},{20,24},{24,28},{28,0},{1,5},{5... | collective-permute-start | bytes 307208 | tf_op jit(solution)/shard_map/ppermute | solution.py:441
  11.9 10.3 %all-to-all-start = ((bf16[32,4,96]{2,1,0:T(4,128)(2,1)}), bf16[32,4,96]{2,1,0:T(4,128)(2,1)S(1)}, u32[]{:S(2)}, u32[]{:S(2)}) async-start(bf16[32,4,96]{2,1,0:T(4,128)(2,1)} %shard_map.75), calls=%async_computation | async-start | bytes 65536 | tf_op jit(solution)/shard_map/all_to_all | solution.py:484

commit v16 on v15

--- a/solution.py
+++ b/solution.py
@@ -120,13 +120,24 @@
 
 
 def pack_kernel(
-    band_start, rows, dep_row, dep_col, lat_frac, lon_frac, own_out, sent_out, plan_out, held
+    place, pair_ids, grid, dep_row, dep_col, lat_frac, lon_frac, _,
+    own_out, sent_out, plan_out, ids_out, first_wave_out, _blank, held, edges, *, levs,
 ):
     band_rows, lon_count = dep_row.shape
     inner = band_rows - 2 * RIM
-    slices = rows.shape[0] // band_rows
+    slices = grid.shape[1]
     rim = RIM * slices
-    first_row = band_start[0]
+    lat_at, lev_at = place[0] // levs, place[0] % levs
+    first_row = lat_at * band_rows
+    pairs, col_count = ids_out.shape[0], first_wave_out.shape[1]
+    square = jnp.broadcast_to(pair_ids[...], (pairs, pairs)).astype(jnp.float32)
+    row = lax.broadcasted_iota(jnp.int32, (pairs, pairs), 0)
+    column = lax.broadcasted_iota(jnp.int32, (pairs, pairs), 1)
+    ids = jnp.sum(jnp.where(row == column, square, 0.0), axis=1, keepdims=True)
+    ids_out[...] = jnp.broadcast_to(ids, ids_out.shape)
+    own_id = jnp.sum(jnp.where(column[:8] == lat_at, square[:8], 0.0), axis=1, keepdims=True)
+    column = lax.broadcasted_iota(jnp.int32, (8, col_count), 1) + lev_at * col_count
+    first_wave_out[...] = jnp.where(column.astype(jnp.float32) < NMAX + 1 - own_id, 1.0, 0.0)
 
     for t in range(lon_count // LANES):
         cols, slot = tile_at(t), t % 5
@@ -140,11 +151,11 @@
         held[slot, 1, 0:band_rows, :] = (shift + REACH).astype(jnp.float32)
         held[slot, 2, 0:band_rows, :] = lat_frac[:, cols].astype(jnp.float32)
         held[slot, 3, 0:band_rows, :] = lon_frac[:, cols].astype(jnp.float32)
-        edges = rows[0 : 2 * rim, cols], rows[rows.shape[0] - 2 * rim :, cols]
-        first_rows, last_rows = [edge.astype(jnp.float32) for edge in edges]
+        for at, row in enumerate((0, 1, band_rows - 2, band_rows - 1)):
+            edges[slot, at * slices : (at + 1) * slices, :] = grid[row, :, cols].astype(jnp.float32)
         for out, grid_rows, start in (
-            (own_out, first_rows[:rim], 0),
-            (sent_out, last_rows[rim:], band_rows - RIM),
+            (own_out, edges[slot, 0:rim, :], 0),
+            (sent_out, edges[slot, rim:, :], band_rows - RIM),
         ):
             out[:, cols] = jnp.concatenate(
                 [grid_rows] + [held[slot, at, start : start + RIM, :] for at in range(4)], axis=0
@@ -229,19 +240,23 @@
 
 
 def inner_kernel(
-    grid, plans, own, sent, ids, analysis,
-    fourier_out, basis, spread_analysis, windows, departed, rim_departed, steps, *, slices,
+    by_row, plans, own, sent, ids, analysis, _,
+    fourier_out, basis, spread_analysis, windows, departed, rim_departed, steps, grid, rows, *, slices,
 ):
     lon_count = grid.shape[1]
+    for t in range(lon_count // LANES):
+        slot = t % rows.shape[0]
+        for row in range(by_row.shape[0]):
+            rows[slot, row * slices : (row + 1) * slices, :] = by_row[row, :, tile_at(t)].astype(
+                jnp.float32
+            )
+        grid[:, tile_at(t)] = rows[slot].astype(jnp.bfloat16)
     inner = plans.shape[0] // 3
     rim, fields, held = RIM * slices, EDGE * slices, grid.shape[0]
     plan_end = held + 3 * inner
     spread = rim_spread(slices)
     fill_steps(steps)
     rim_base = jnp.where(lax.broadcasted_iota(jnp.int32, (fields, LANES), 0) < rim, 1, 0)
-    for slot in range(windows.shape[0]):
-        windows[slot, 0:rim, :] = jnp.zeros((rim, LANES), jnp.float32)
-        windows[slot, rim + held :, :] = jnp.zeros((rim, LANES), jnp.float32)
     quads = ids.shape[0] // 4
     few = quads <= 4
     waves = [waves_of(ids, at) for at in range(quads if few else 0)]
@@ -419,47 +434,56 @@
     windows = -(-lon_count // SPAN)
     held_rows = -(-band_rows // 8) * 8
     fields = slices * EDGE
-    band_start = jnp.reshape(lax.axis_index("lat") * band_rows, (1,)).astype(jnp.int32)
+    place = jnp.reshape(lax.axis_index(("lat", "lev")), (1,)).astype(jnp.int32)
     vmem = pl.BlockSpec(memory_space=pltpu.VMEM)
     smem = pl.BlockSpec(memory_space=pltpu.SMEM)
     params = pltpu.CompilerParams(vmem_limit_bytes=48 * 2**20)
 
-    rows = grid.transpose(1, 0, 2).reshape(band_rows * slices, lon_count)
+    blank = jnp.zeros((windows, (band_rows + 2 * RIM) * slices, LANES), jnp.float32)
+    by_row = grid.transpose(1, 0, 2)
     rim_shape = jax.ShapeDtypeStruct((RIM * (slices + 4), lon_count), jnp.bfloat16)
-    own_rim, sent_rim, plans = pl.pallas_call(
-        pack_kernel,
+    own_rim, sent_rim, plans, ids, first_wave, blank = pl.pallas_call(
+        functools.partial(pack_kernel, levs=levs),
         out_shape=(
             rim_shape,
             rim_shape,
             jax.ShapeDtypeStruct((3 * inner, lon_count), jnp.bfloat16),
+            jax.ShapeDtypeStruct((pairs, LANES), jnp.float32),
+            jax.ShapeDtypeStruct((8, col_count), jnp.float32),
+            jax.ShapeDtypeStruct(blank.shape, jnp.float32),
         ),
-        in_specs=[smem] + [vmem] * 5,
-        out_specs=(vmem,) * 3,
-        scratch_shapes=[pltpu.VMEM((5, 4, held_rows, LANES), jnp.float32)],
+        in_specs=[smem] + [vmem] * 7,
+        out_specs=(vmem,) * 6,
+        input_output_aliases={7: 5},
+        scratch_shapes=[
+            pltpu.VMEM((5, 4, held_rows, LANES), jnp.float32),
+            pltpu.VMEM((5, 2 * RIM * slices, LANES), jnp.float32),
+        ],
         compiler_params=params,
-    )(band_start, rows, dep_row, dep_col, lat_frac, lon_frac)
+    )(place, pair_ids[None, :], by_row, dep_row, dep_col, lat_frac, lon_frac, blank)
     arrived_rim = lax.ppermute(sent_rim, "lat", [(i, (i + 1) % bands) for i in range(bands)])
 
-    plans, ids = lax.optimization_barrier((plans, pair_ids))
-    ids = jnp.broadcast_to(ids.astype(jnp.float32)[:, None], (pairs, LANES))
-    inner_fourier, basis, spread_analysis = pl.pallas_call(
+    inner_fourier, basis, spread_analysis, _ = pl.pallas_call(
         functools.partial(inner_kernel, slices=slices),
         out_shape=(
             jax.ShapeDtypeStruct((4 * pairs, slices * band_rows), jnp.float32),
             jax.ShapeDtypeStruct((4 * pairs, windows * LANES), jnp.bfloat16),
             jax.ShapeDtypeStruct((bands * LANES, col_count), jnp.bfloat16),
+            jax.ShapeDtypeStruct(blank.shape, jnp.float32),
         ),
-        in_specs=[vmem] * 6,
-        out_specs=(vmem,) * 3,
+        in_specs=[vmem] * 7,
+        out_specs=(vmem,) * 4,
+        input_output_aliases={6: 3},
         scratch_shapes=[
-            pltpu.VMEM((windows, (band_rows + 2 * RIM) * slices, LANES), jnp.float32),
             pltpu.VMEM((slices * inner, windows * LANES), jnp.bfloat16),
             pltpu.VMEM((fields, windows * LANES), jnp.bfloat16),
             pltpu.VMEM((2 * LANES, LANES), jnp.int16),
+            pltpu.VMEM((band_rows * slices, lon_count), jnp.bfloat16),
+            pltpu.VMEM((5, band_rows * slices, LANES), jnp.float32),
         ],
         compiler_params=params,
         cost_estimate=pl.CostEstimate(flops=100_000_000, bytes_accessed=2_000_000, transcendentals=0),
-    )(rows, plans, own_rim, sent_rim, ids, analysis[0])
+    )(by_row, plans, own_rim, sent_rim, ids, analysis[0], blank)
 
     held_coeffs = slices * (band_rows + EDGE)
     fourier = pl.pallas_call(
@@ -474,13 +498,6 @@
         ],
         compiler_params=params,
     )(arrived_rim, own_rim, basis, inner_fourier)
-    fourier, late_ids = lax.optimization_barrier((fourier, pair_ids))
-    own_id = lax.dynamic_slice_in_dim(late_ids, lax.axis_index("lat"), 1)
-
-    columns = lax.axis_index("lev") * col_count + jnp.arange(col_count, dtype=jnp.int32)
-    first_wave = jnp.where(columns < NMAX + 1 - own_id, 1.0, 0.0)
-    first_wave = jnp.broadcast_to(first_wave[None, :], (8, col_count))
-
     coeffs = lax.all_to_all(
         fourier, ("lat", "lev"), split_axis=0, concat_axis=0, tiled=True
     )

time: 23.3 us -> 22.5 us (0.966)
  blocking collectives: 0 us -> 10.1 us
  waiting for transfers between devices: 8.28 us -> 2.36 us
  starting transfers between devices: 6.1 us -> 3.02 us
  between operations: 0.71 us -> 0.05 us
  local copies, waits for them, and re-layouts: 1.96 us -> 1.32 us
  Pallas kernels: 6.07 us -> 5.5 us
    all_to_all x0 -> x1, blocking collectives: none -> 10.1 us  [shards(): lax.all_to_all(fourier, ('lat', 'lev'), split_axis=0, concat_axis=0, tile...]
    all_to_all x1 -> x0, waiting for transfers between devices: 5.98 us -> none  [shards(): lax.all_to_all(fourier, ('lat', 'lev'), split_axis=0, concat_axis=0, tile...]
    all_to_all x1 -> x0, starting transfers between devices: 3.07 us -> none  [shards(): lax.all_to_all(fourier, ('lat', 'lev'), split_axis=0, concat_axis=0, tile...]
    reshape x1 -> x0, local copies, waits for them, and re-layouts: 1.23 us -> none  [shards(): rows = grid.transpose(1, 0, 2).reshape(band_rows * slices, lon_count)]
    unnamed x12 -> x14, local copies, waits for them, and re-layouts: 0.04 us -> 1.17 us
    pallas_call x1, Pallas kernels: 1.3 us -> 0.69 us  [shards(): pl.pallas_call(functools.partial(rim_kernel, slices=slices, levs=levs), o...]
    dynamic_slice x1 -> x0, local copies, waits for them, and re-layouts: 0.61 us -> none  [shards(): own_id = lax.dynamic_slice_in_dim(late_ids, lax.axis_index('lat'), 1)]
  transfers between devices with their start and end apart: 2 -> 1, of which waited for: 2 -> 1; matrix products, arithmetic and copies ran while one was open for 3% -> 0% of each run, Pallas kernels for 15% -> 16%
where the time goes in v16:
time: 22.5 us; the launch traced here: 22.4 us
  blocking collectives  10.1 us (45%)
  Pallas kernels  5.5 us (24%)
  starting transfers between devices  3.02 us (13%)
  waiting for transfers between devices  2.36 us (10%)
  local copies, waits for them, and re-layouts  1.32 us (6%)
    all_to_all x1, blocking collectives, shards(): lax.all_to_all(fourier, ('lat', 'lev'), split_axis=0, concat_axis=0, tile...  10.1 us
    pallas_call x1, Pallas kernels, shards(): pl.pallas_call(functools.partial(inner_kernel, slices=slices), out_shape=...  3.56 us
    ppermute x1, starting transfers between devices, shards(): lax.ppermute(sent_rim, 'lat', [(i, (i + 1) % bands) for i in range(bands)])  3.02 us
    ppermute x1, waiting for transfers between devices, shards(): lax.ppermute(sent_rim, 'lat', [(i, (i + 1) % bands) for i in range(bands)])  2.36 us
    unnamed x14, local copies, waits for them, and re-layouts  1.17 us
    pallas_call x1, Pallas kernels, shards(): pl.pallas_call(functools.partial(legendre_kernel, levs=levs, slices=slice...  0.9 us
    pallas_call x1, Pallas kernels, shards(): pl.pallas_call(functools.partial(rim_kernel, slices=slices, levs=levs), o...  0.69 us
  transfers between devices with their start and end apart: 1, of which 1 were waited for; matrix products, arithmetic and copies ran while one was open for 0% of the time, Pallas kernels for 16%

profile of v16, /device:TPU:0, one launch (start us, length us, event | category | flops | bytes accessed | tf_op | source)
XLA Modules:
  0.0 22.4 jit_solution(6167940369292696015)
XLA Ops:
  0.0 0.0 copy-start
  0.0 0.0 copy-start.6
  0.0 0.0 copy-start.3
  0.0 0.0 copy-start.4
  0.0 0.0 copy-start.1
  0.0 0.0 copy-start.2
  0.0 0.2 broadcast_in_dim.10._
  0.2 0.8 %copy-done = bf16[4,20,3200]{2,0,1:T(4,128)(2,1)S(1)} copy-done((bf16[4,20,3200]{2,0,1:T(4,128)(2,1)S(1)}, bf16[4,20,3200]{2,0,1:T(4,128)(2,1)}, u32[]{:S(2)}) %copy-start) | copy-done | bytes 512024
  1.0 0.0 copy-done.6
  1.0 0.0 copy-done.3
  1.1 0.1 copy-done.4
  1.2 0.1 copy-done.1
  1.3 0.1 copy-done.2
  1.3 0.0 copy-start.5
  1.4 0.3 %shard_map.73 = (bf16[16,3200]{1,0:T(8,128)(2,1)S(1)}, bf16[16,3200]{1,0:T(8,128)(2,1)S(1)}, bf16[48,3200]{1,0:T(8,128)(2,1)S(1)}, f32[8,128]{1,0:T(8,128)S(1)},...) custom-call(s32[1]{0:T(128)} %bitcast.place, s32[1,8]{1,0:T(1,128)S(1)} %bitcast.8, ...), custom_call_target="tpu_custom_call", output_to_operand_aliasing={{5}: (7, {})} | custom-call | tf_op jit(solution)/shard_map/pallas_call | solution.py:445
  1.7 3.0 %collective-permute-start = (bf16[16,3200]{1,0:T(8,128)(2,1)S(1)}, bf16[16,3200]{1,0:T(8,128)(2,1)S(1)}, u32[]{:S(2)}, u32[]{:S(2)}) collective-permute-start(bf16[16,3200]{1,0:T(8,128)(2,1)S(1)} %get-tuple-element.15.sent), channel_id=1, source_target_pairs={{0,4},{4,8},{8,12},{12,16},{16,20},{20,24},{24,28},{28,0},{1,5},{5... | collective-permute-start | bytes 307208 | tf_op jit(solution)/shard_map/ppermute | solution.py:464
  4.7 0.0 copy-done.5
  4.7 3.6 %shard_map.74 = (f32[32,80]{1,0:T(8,128)S(1)}, bf16[32,3712]{1,0:T(8,128)(2,1)S(1)}, bf16[1024,320]{1,0:T(8,128)(2,1)S(1)}, f32[29,96,128]{2,1,0:T(8,128)S(1)}) custom-call(bf16[20,4,3200]{2,1,0:T(4,128)(2,1)S(1)} %bitcast.6, bf16[48,3200]{1,0:T(8,128)(2,1)S(1)} %get-tuple-element.17.plans, ...), custom_call_target="tpu_custom_call", output_to_operand_aliasing={{3}: (6, {})} | custom-call | flops 100000000 | bytes 2000000 | tf_op jit(solution)/shard_map/pallas_call | solution.py:466
  8.3 2.4 %collective-permute-done.arrived = bf16[16,3200]{1,0:T(8,128)(2,1)S(1)} collective-permute-done((bf16[16,3200]{1,0:T(8,128)(2,1)S(1)}, bf16[16,3200]{1,0:T(8,128)(2,1)S(1)}, u32[]{:S(2)}, u32[]{:S(2)}) %collective-permute-start) | collective-permute-done | bytes 102432 | tf_op jit(solution)/shard_map/ppermute | solution.py:464
  10.6 0.7 %shard_map.75 = bf16[32,4,96]{2,1,0:T(4,128)(2,1)S(1)} custom-call(bf16[16,3200]{1,0:T(8,128)(2,1)S(1)} %collective-permute-done.arrived, bf16[16,3200]{1,0:T(8,128)(2,1)S(1)} %get-tuple-element.16.own, bf16[32,3712]{1,0:T(8,128)(2,1)S(1)} %get-tuple-element.20.basis, f32[32,80]{1,0:T(8,128)S(1)} %get-tuple-element.21.inner_fourier), custom_call_target="tpu_custom_call" | custom-call | tf_op jit(solution)/shard_map/pallas_call | solution.py:489
  11.3 10.1 %all_to_all.5.coeffs = bf16[32,4,96]{2,1,0:T(4,128)(2,1)S(1)} all-to-all(bf16[32,4,96]{2,1,0:T(4,128)(2,1)S(1)} %shard_map.75), channel_id=1, replica_groups=mesh['lat'=8,'lev'=4] {'lat','lev'}, dimensions={0} | all-to-all | bytes 49152 | tf_op jit(solution)/shard_map/all_to_all | solution.py:501
  21.5 0.9 %shard_map.76 = f32[16,2,320]{2,1,0:T(2,128)} custom-call(f32[8,320]{1,0:T(8,128)S(1)} %get-tuple-element.14.first_wave, bf16[32,4,96]{2,1,0:T(4,128)(2,1)S(1)} %all_to_all.5.coeffs, bf16[1024,320]{1,0:T(8,128)(2,1)S(1)} %get-tuple-element.22.spread_analysis), custom_call_target="tpu_custom_call" | custom-call | tf_op jit(solution)/shard_map/pallas_call | solution.py:504
Async XLA Ops:
  0.0 1.0 %copy-start = (bf16[4,20,3200]{2,0,1:T(4,128)(2,1)S(1)}, bf16[4,20,3200]{2,0,1:T(4,128)(2,1)}, u32[]{:S(2)}) copy-start(bf16[4,20,3200]{2,0,1:T(4,128)(2,1)} %param.7) | copy-start | bytes 1536004
  0.0 1.0 %copy-start.6 = (s32[8]{0:T(128)S(1)}, s32[8]{0:T(128)}, u32[]{:S(2)}) copy-start(s32[8]{0:T(128)} %param.12) | copy-start | bytes 100
  0.0 1.1 %copy-start.3 = (bf16[20,3200]{1,0:T(8,128)(2,1)S(1)}, bf16[20,3200]{1,0:T(8,128)(2,1)}, u32[]{:S(2)}) copy-start(bf16[20,3200]{1,0:T(8,128)(2,1)} %lat_frac.1) | copy-start | bytes 384004
  0.0 1.1 %copy-start.4 = (bf16[20,3200]{1,0:T(8,128)(2,1)S(1)}, bf16[20,3200]{1,0:T(8,128)(2,1)}, u32[]{:S(2)}) copy-start(bf16[20,3200]{1,0:T(8,128)(2,1)} %lon_frac.1) | copy-start | bytes 384004
  0.0 1.2 %copy-start.1 = (s32[20,3200]{1,0:T(8,128)S(1)}, s32[20,3200]{1,0:T(8,128)}, u32[]{:S(2)}) copy-start(s32[20,3200]{1,0:T(8,128)} %dep_row.1) | copy-start | bytes 768004
  0.0 1.3 %copy-start.2 = (s32[20,3200]{1,0:T(8,128)S(1)}, s32[20,3200]{1,0:T(8,128)}, u32[]{:S(2)}) copy-start(s32[20,3200]{1,0:T(8,128)} %dep_col.1) | copy-start | bytes 768004
  1.3 3.4 %copy-start.5 = (bf16[1,160,320]{2,1,0:T(8,128)(2,1)S(1)}, bf16[1,160,320]{2,1,0:T(8,128)(2,1)}, u32[]{:S(2)}) copy-start(bf16[1,160,320]{2,1,0:T(8,128)(2,1)} %param.13) | copy-start | bytes 307204
  1.7 8.9 %collective-permute-start = (bf16[16,3200]{1,0:T(8,128)(2,1)S(1)}, bf16[16,3200]{1,0:T(8,128)(2,1)S(1)}, u32[]{:S(2)}, u32[]{:S(2)}) collective-permute-start(bf16[16,3200]{1,0:T(8,128)(2,1)S(1)} %get-tuple-element.15.sent), channel_id=1, source_target_pairs={{0,4},{4,8},{8,12},{12,16},{16,20},{20,24},{24,28},{28,0},{1,5},{5... | collective-permute-start | bytes 307208 | tf_op jit(solution)/shard_map/ppermute | solution.py:464

commit v17 on v16

--- a/solution.py
+++ b/solution.py
@@ -119,56 +119,48 @@
     return [range(at, min(at + at_once, count)) for at in range(0, count, at_once)]
 
 
+def departures(rows, t, first_row, dep_row, dep_col, lat_frac, lon_frac):
+    lon_count = dep_row.shape[1]
+    cols, shape = tile_at(t), (rows.stop - rows.start, LANES)
+    row = lax.broadcasted_iota(jnp.int32, shape, 0) + rows.start
+    lane = lax.broadcasted_iota(jnp.int32, shape, 1)
+    shift = dep_col[rows, cols] - (lane + t * LANES)
+    shift = jnp.where(shift > lon_count // 2, shift - lon_count, shift)
+    shift = jnp.where(shift < -(lon_count // 2), shift + lon_count, shift)
+    row_step = dep_row[rows, cols] - (first_row + row) + RIM
+    fracs = [frac[:, cols].astype(jnp.float32)[rows] for frac in (lat_frac, lon_frac)]
+    return [row_step.astype(jnp.float32), (shift + REACH).astype(jnp.float32)] + fracs
+
+
 def pack_kernel(
-    place, pair_ids, grid, dep_row, dep_col, lat_frac, lon_frac, _,
-    own_out, sent_out, plan_out, ids_out, first_wave_out, _blank, held, edges, *, levs,
+    place, dep_row, dep_col, lat_frac, lon_frac, last_rows, _,
+    sent_out, place_out, _blank, held, *, levs,
 ):
     band_rows, lon_count = dep_row.shape
-    inner = band_rows - 2 * RIM
-    slices = grid.shape[1]
+    slices = last_rows.shape[1]
     rim = RIM * slices
-    lat_at, lev_at = place[0] // levs, place[0] % levs
-    first_row = lat_at * band_rows
-    pairs, col_count = ids_out.shape[0], first_wave_out.shape[1]
-    square = jnp.broadcast_to(pair_ids[...], (pairs, pairs)).astype(jnp.float32)
-    row = lax.broadcasted_iota(jnp.int32, (pairs, pairs), 0)
-    column = lax.broadcasted_iota(jnp.int32, (pairs, pairs), 1)
-    ids = jnp.sum(jnp.where(row == column, square, 0.0), axis=1, keepdims=True)
-    ids_out[...] = jnp.broadcast_to(ids, ids_out.shape)
-    own_id = jnp.sum(jnp.where(column[:8] == lat_at, square[:8], 0.0), axis=1, keepdims=True)
-    column = lax.broadcasted_iota(jnp.int32, (8, col_count), 1) + lev_at * col_count
-    first_wave_out[...] = jnp.where(column.astype(jnp.float32) < NMAX + 1 - own_id, 1.0, 0.0)
-
+    place_out[...] = jnp.full(place_out.shape, place[0], jnp.int32)
+    first_row = place[0] // levs * band_rows
+    start = band_rows // 8 * 8
+    skip = band_rows - RIM - start
     for t in range(lon_count // LANES):
-        cols, slot = tile_at(t), t % 5
-        row = lax.broadcasted_iota(jnp.int32, (band_rows, LANES), 0)
-        lane = lax.broadcasted_iota(jnp.int32, (band_rows, LANES), 1)
-        shift = dep_col[:, cols] - (lane + t * LANES)
-        shift = jnp.where(shift > lon_count // 2, shift - lon_count, shift)
-        shift = jnp.where(shift < -(lon_count // 2), shift + lon_count, shift)
-        row_step = dep_row[:, cols] - (first_row + row) + RIM
-        held[slot, 0, 0:band_rows, :] = row_step.astype(jnp.float32)
-        held[slot, 1, 0:band_rows, :] = (shift + REACH).astype(jnp.float32)
-        held[slot, 2, 0:band_rows, :] = lat_frac[:, cols].astype(jnp.float32)
-        held[slot, 3, 0:band_rows, :] = lon_frac[:, cols].astype(jnp.float32)
-        for at, row in enumerate((0, 1, band_rows - 2, band_rows - 1)):
-            edges[slot, at * slices : (at + 1) * slices, :] = grid[row, :, cols].astype(jnp.float32)
-        for out, grid_rows, start in (
-            (own_out, edges[slot, 0:rim, :], 0),
-            (sent_out, edges[slot, rim:, :], band_rows - RIM),
-        ):
-            out[:, cols] = jnp.concatenate(
-                [grid_rows] + [held[slot, at, start : start + RIM, :] for at in range(4)], axis=0
-            ).astype(jnp.bfloat16)
-        middle = [held[slot, at, RIM : RIM + inner, :] for at in range(4)]
-        middle = [middle[0] * (1 << ROW_BITS) + middle[1], middle[2], middle[3]]
-        for at in range(3):
-            plan_out[at * inner : (at + 1) * inner, cols] = middle[at].astype(jnp.bfloat16)
+        cols = tile_at(t)
+        for row in range(RIM):
+            held[t, row * slices : (row + 1) * slices, :] = last_rows[row, :, cols].astype(
+                jnp.float32
+            )
+        parts = departures(
+            slice(start, band_rows), t, first_row, dep_row, dep_col, lat_frac, lon_frac
+        )
+        for at, part in enumerate(parts):
+            held[t, rim + RIM * at : rim + RIM * (at + 1), :] = part[skip:]
+        sent_out[:, cols] = held[t].astype(jnp.bfloat16)
 
 
 def waves_of(ids, group):
     pair = jnp.concatenate(
-        [jnp.broadcast_to(ids[pl.ds(4 * group + at, 1), :], (4, LANES)) for at in range(4)], axis=0
+        [jnp.broadcast_to(ids[4 * group + at : 4 * group + at + 1], (4, LANES)) for at in range(4)],
+        axis=0,
     )
     row = lax.broadcasted_iota(jnp.int32, (16, LANES), 0)
     return jnp.where((row & 2) == 0, pair, NMAX + 1 - pair)
@@ -240,19 +232,47 @@
 
 
 def inner_kernel(
-    by_row, plans, own, sent, ids, analysis, _,
-    fourier_out, basis, spread_analysis, windows, departed, rim_departed, steps, grid, rows, *, slices,
+    by_row, dep_row, dep_col, lat_frac, lon_frac, sent, place, pair_ids, analysis, _,
+    fourier_out, basis, spread_analysis, own, first_wave_out, windows,
+    departed, rim_departed, steps, grid, rows, parts, plans, *, slices, levs,
 ):
-    lon_count = grid.shape[1]
+    band_rows, lon_count = dep_row.shape
+    inner = band_rows - 2 * RIM
+    rim, fields, held = RIM * slices, EDGE * slices, band_rows * slices
+
+    place = place[0:1, :]
+    lat_at, lev_at = place // levs, place % levs
+    first_row = lat_at * band_rows
     for t in range(lon_count // LANES):
-        slot = t % rows.shape[0]
-        for row in range(by_row.shape[0]):
-            rows[slot, row * slices : (row + 1) * slices, :] = by_row[row, :, tile_at(t)].astype(
+        cols, slot = tile_at(t), t % rows.shape[0]
+        for row in range(band_rows):
+            rows[slot, row * slices : (row + 1) * slices, :] = by_row[row, :, cols].astype(
                 jnp.float32
             )
-        grid[:, tile_at(t)] = rows[slot].astype(jnp.bfloat16)
-    inner = plans.shape[0] // 3
-    rim, fields, held = RIM * slices, EDGE * slices, grid.shape[0]
+        grid[:, cols] = rows[slot].astype(jnp.bfloat16)
+        data = departures(
+            slice(0, band_rows), t, first_row, dep_row, dep_col, lat_frac, lon_frac
+        )
+        for at, part in enumerate([data[0] * (1 << ROW_BITS) + data[1]] + data[2:]):
+            parts[slot, at, 0:band_rows, :] = part
+            plans[at * inner : (at + 1) * inner, cols] = parts[
+                slot, at, RIM : RIM + inner, :
+            ].astype(jnp.bfloat16)
+        own[:, cols] = jnp.concatenate(
+            [rows[slot, 0:rim, :]] + [part[0:RIM] for part in data], axis=0
+        ).astype(jnp.bfloat16)
+
+    pairs, col_count = pair_ids.shape[1], first_wave_out.shape[1]
+    square = jnp.broadcast_to(pair_ids[...], (pairs, pairs)).astype(jnp.float32)
+    row = lax.broadcasted_iota(jnp.int32, (pairs, pairs), 0)
+    column = lax.broadcasted_iota(jnp.int32, (pairs, pairs), 1)
+    ids = jnp.sum(jnp.where(row == column, square, 0.0), axis=1, keepdims=True)
+    ids = jnp.broadcast_to(ids, (pairs, LANES))
+    own_id = jnp.sum(
+        jnp.where(column[:8] == lat_at[0:1, 0:1], square[:8], 0.0), axis=1, keepdims=True
+    )
+    column = lax.broadcasted_iota(jnp.int32, (8, col_count), 1) + lev_at[0:1, 0:1] * col_count
+    first_wave_out[...] = jnp.where(column.astype(jnp.float32) < NMAX + 1 - own_id, 1.0, 0.0)
     plan_end = held + 3 * inner
     spread = rim_spread(slices)
     fill_steps(steps)
@@ -305,13 +325,10 @@
 
     if not few:
 
-        def rows_of(group, carry):
-            rows = pl.ds(pl.multiple_of(group * 16, 16), 16)
+        for group in range(quads):
+            wave = waves_of(ids, group)
             for t in range(basis.shape[1] // LANES):
-                basis[rows, tile_at(t)] = basis_tile(t, waves_of(ids, group), lon_count)
-            return carry
-
-        lax.fori_loop(0, quads, rows_of, 0)
+                basis[16 * group : 16 * group + 16, tile_at(t)] = basis_tile(t, wave, lon_count)
     count = departed.shape[1] // LANES
     for ts in groups_of(count, INNER_AT_ONCE):
         group_of(ts)
@@ -442,48 +459,51 @@
     blank = jnp.zeros((windows, (band_rows + 2 * RIM) * slices, LANES), jnp.float32)
     by_row = grid.transpose(1, 0, 2)
     rim_shape = jax.ShapeDtypeStruct((RIM * (slices + 4), lon_count), jnp.bfloat16)
-    own_rim, sent_rim, plans, ids, first_wave, blank = pl.pallas_call(
+    sent_rim, wide_place, blank = pl.pallas_call(
         functools.partial(pack_kernel, levs=levs),
         out_shape=(
             rim_shape,
-            rim_shape,
-            jax.ShapeDtypeStruct((3 * inner, lon_count), jnp.bfloat16),
-            jax.ShapeDtypeStruct((pairs, LANES), jnp.float32),
-            jax.ShapeDtypeStruct((8, col_count), jnp.float32),
+            jax.ShapeDtypeStruct((8, LANES), jnp.int32),
             jax.ShapeDtypeStruct(blank.shape, jnp.float32),
         ),
-        in_specs=[smem] + [vmem] * 7,
-        out_specs=(vmem,) * 6,
-        input_output_aliases={7: 5},
+        in_specs=[smem] + [vmem] * 6,
+        out_specs=(vmem,) * 3,
+        input_output_aliases={6: 2},
         scratch_shapes=[
-            pltpu.VMEM((5, 4, held_rows, LANES), jnp.float32),
-            pltpu.VMEM((5, 2 * RIM * slices, LANES), jnp.float32),
+            pltpu.VMEM((lon_count // LANES, RIM * (slices + 4), LANES), jnp.float32)
         ],
         compiler_params=params,
-    )(place, pair_ids[None, :], by_row, dep_row, dep_col, lat_frac, lon_frac, blank)
+    )(place, dep_row, dep_col, lat_frac, lon_frac, by_row[band_rows - RIM :], blank)
     arrived_rim = lax.ppermute(sent_rim, "lat", [(i, (i + 1) % bands) for i in range(bands)])
 
-    inner_fourier, basis, spread_analysis, _ = pl.pallas_call(
-        functools.partial(inner_kernel, slices=slices),
+    inner_fourier, basis, spread_analysis, own_rim, first_wave, _ = pl.pallas_call(
+        functools.partial(inner_kernel, slices=slices, levs=levs),
         out_shape=(
             jax.ShapeDtypeStruct((4 * pairs, slices * band_rows), jnp.float32),
             jax.ShapeDtypeStruct((4 * pairs, windows * LANES), jnp.bfloat16),
             jax.ShapeDtypeStruct((bands * LANES, col_count), jnp.bfloat16),
+            rim_shape,
+            jax.ShapeDtypeStruct((8, col_count), jnp.float32),
             jax.ShapeDtypeStruct(blank.shape, jnp.float32),
         ),
-        in_specs=[vmem] * 7,
-        out_specs=(vmem,) * 4,
-        input_output_aliases={6: 3},
+        in_specs=[vmem] * 10,
+        out_specs=(vmem,) * 6,
+        input_output_aliases={9: 5},
         scratch_shapes=[
             pltpu.VMEM((slices * inner, windows * LANES), jnp.bfloat16),
             pltpu.VMEM((fields, windows * LANES), jnp.bfloat16),
             pltpu.VMEM((2 * LANES, LANES), jnp.int16),
             pltpu.VMEM((band_rows * slices, lon_count), jnp.bfloat16),
             pltpu.VMEM((5, band_rows * slices, LANES), jnp.float32),
+            pltpu.VMEM((5, 3, held_rows, LANES), jnp.float32),
+            pltpu.VMEM((3 * inner, lon_count), jnp.bfloat16),
         ],
         compiler_params=params,
         cost_estimate=pl.CostEstimate(flops=100_000_000, bytes_accessed=2_000_000, transcendentals=0),
-    )(by_row, plans, own_rim, sent_rim, ids, analysis[0], blank)
+    )(
+        by_row, dep_row, dep_col, lat_frac, lon_frac, sent_rim, wide_place, pair_ids[None, :],
+        analysis[0], blank,
+    )
 
     held_coeffs = slices * (band_rows + EDGE)
     fourier = pl.pallas_call(

time: 22.5 us -> 22.2 us (0.987)
  Pallas kernels: 5.5 us -> 5.2 us
    unnamed x14, local copies, waits for them, and re-layouts: 1.17 us -> 0.16 us
    slice x0 -> x1, local copies, waits for them, and re-layouts: none -> 0.9 us  [shards(): by_row[band_rows - RIM:]]
    pallas_call x1, Pallas kernels: 0.35 us -> 0.1 us  [shards(): pl.pallas_call(functools.partial(pack_kernel, levs=levs), out_shape=(rim_...]
where the time goes in v17:
time: 22.2 us; the launch traced here: 22 us
  blocking collectives  10.1 us (45%)
  Pallas kernels  5.2 us (23%)
  starting transfers between devices  3.02 us (14%)
  waiting for transfers between devices  2.39 us (11%)
  local copies, waits for them, and re-layouts  1.22 us (5%)
    all_to_all x1, blocking collectives, shards(): lax.all_to_all(fourier, ('lat', 'lev'), split_axis=0, concat_axis=0, tile...  10.1 us
    pallas_call x1, Pallas kernels, shards(): pl.pallas_call(functools.partial(inner_kernel, slices=slices, levs=levs),...  3.52 us
    ppermute x1, starting transfers between devices, shards(): lax.ppermute(sent_rim, 'lat', [(i, (i + 1) % bands) for i in range(bands)])  3.02 us
    ppermute x1, waiting for transfers between devices, shards(): lax.ppermute(sent_rim, 'lat', [(i, (i + 1) % bands) for i in range(bands)])  2.39 us
    slice x1, local copies, waits for them, and re-layouts, shards(): by_row[band_rows - RIM:]  0.9 us
    pallas_call x1, Pallas kernels, shards(): pl.pallas_call(functools.partial(legendre_kernel, levs=levs, slices=slice...  0.9 us
    pallas_call x1, Pallas kernels, shards(): pl.pallas_call(functools.partial(rim_kernel, slices=slices, levs=levs), o...  0.69 us
  transfers between devices with their start and end apart: 1, of which 1 were waited for; matrix products, arithmetic and copies ran while one was open for 0% of the time, Pallas kernels for 16%

profile of v17, /device:TPU:0, one launch (start us, length us, event | category | flops | bytes accessed | tf_op | source)
XLA Modules:
  0.0 22.0 jit_solution(7919102983174832531)
XLA Ops:
  0.0 0.0 copy-start.3
  0.0 0.0 copy-start.4
  0.0 0.0 copy-start
  0.0 0.0 copy-start.1
  0.0 0.9 %slice.4.last_rows = bf16[2,4,3200]{2,1,0:T(4,128)(2,1)S(1)} slice(bf16[20,4,3200]{2,1,0:T(4,128)(2,1)} %bitcast.5), slice={[18:20], [0:4], [0:3200]} | slice | bytes 102400 | tf_op jit(solution)/shard_map/slice | solution.py:476
  0.9 0.2 broadcast_in_dim.9._
  1.1 0.0 copy-done.3
  1.1 0.0 copy-done.4
  1.1 0.0 copy-done
  1.1 0.1 copy-done.1
  1.2 0.0 copy-start.2
  1.2 0.0 copy-start.5
  1.2 0.0 copy-start.6
  1.2 0.1 shard_map.73
  1.3 3.0 %collective-permute-start = (bf16[16,3200]{1,0:T(8,128)(2,1)S(1)}, bf16[16,3200]{1,0:T(8,128)(2,1)S(1)}, u32[]{:S(2)}, u32[]{:S(2)}) collective-permute-start(bf16[16,3200]{1,0:T(8,128)(2,1)S(1)} %get-tuple-element.13.sent), channel_id=1, source_target_pairs={{0,4},{4,8},{8,12},{12,16},{16,20},{20,24},{24,28},{28,0},{1,5},{5... | collective-permute-start | bytes 307208 | tf_op jit(solution)/shard_map/ppermute | solution.py:477
  4.4 0.0 copy-done.2
  4.4 0.0 copy-done.5
  4.4 0.0 copy-done.6
  4.4 3.5 %shard_map.74 = (f32[32,80]{1,0:T(8,128)S(1)}, bf16[32,3712]{1,0:T(8,128)(2,1)S(1)}, bf16[1024,320]{1,0:T(8,128)(2,1)S(1)}, bf16[16,3200]{1,0:T(8,128)(2,1)S(1)}...) custom-call(bf16[20,4,3200]{2,1,0:T(4,128)(2,1)S(1)} %bitcast.6, ...), custom_call_target="tpu_custom_call", output_to_operand_aliasing={{5}: (9, {})} | custom-call | flops 100000000 | bytes 2000000 | tf_op jit(solution)/shard_map/pallas_call | solution.py:479
  7.9 2.4 %collective-permute-done.arrived = bf16[16,3200]{1,0:T(8,128)(2,1)S(1)} collective-permute-done((bf16[16,3200]{1,0:T(8,128)(2,1)S(1)}, bf16[16,3200]{1,0:T(8,128)(2,1)S(1)}, u32[]{:S(2)}, u32[]{:S(2)}) %collective-permute-start) | collective-permute-done | bytes 102432 | tf_op jit(solution)/shard_map/ppermute | solution.py:477
  10.3 0.7 %shard_map.75 = bf16[32,4,96]{2,1,0:T(4,128)(2,1)S(1)} custom-call(bf16[16,3200]{1,0:T(8,128)(2,1)S(1)} %collective-permute-done.arrived, bf16[16,3200]{1,0:T(8,128)(2,1)S(1)} %get-tuple-element.17.own, bf16[32,3712]{1,0:T(8,128)(2,1)S(1)} %get-tuple-element.18.basis, f32[32,80]{1,0:T(8,128)S(1)} %get-tuple-element.19.inner_fourier), custom_call_target="tpu_custom_call" | custom-call | tf_op jit(solution)/shard_map/pallas_call | solution.py:509
  11.0 10.1 %all_to_all.5.coeffs = bf16[32,4,96]{2,1,0:T(4,128)(2,1)S(1)} all-to-all(bf16[32,4,96]{2,1,0:T(4,128)(2,1)S(1)} %shard_map.75), channel_id=1, replica_groups=mesh['lat'=8,'lev'=4] {'lat','lev'}, dimensions={0} | all-to-all | bytes 49152 | tf_op jit(solution)/shard_map/all_to_all | solution.py:521
  21.1 0.9 %shard_map.76 = f32[16,2,320]{2,1,0:T(2,128)} custom-call(f32[8,320]{1,0:T(8,128)S(1)} %get-tuple-element.16.first_wave, bf16[32,4,96]{2,1,0:T(4,128)(2,1)S(1)} %all_to_all.5.coeffs, bf16[1024,320]{1,0:T(8,128)(2,1)S(1)} %get-tuple-element.20.spread_analysis), custom_call_target="tpu_custom_call" | custom-call | tf_op jit(solution)/shard_map/pallas_call | solution.py:524
Async XLA Ops:
  0.0 1.1 %copy-start.3 = (bf16[20,3200]{1,0:T(8,128)(2,1)S(1)}, bf16[20,3200]{1,0:T(8,128)(2,1)}, u32[]{:S(2)}) copy-start(bf16[20,3200]{1,0:T(8,128)(2,1)} %lat_frac.3) | copy-start | bytes 384004
  0.0 1.1 %copy-start.4 = (bf16[20,3200]{1,0:T(8,128)(2,1)S(1)}, bf16[20,3200]{1,0:T(8,128)(2,1)}, u32[]{:S(2)}) copy-start(bf16[20,3200]{1,0:T(8,128)(2,1)} %lon_frac.3) | copy-start | bytes 384004
  0.0 1.1 %copy-start = (s32[20,3200]{1,0:T(8,128)S(1)}, s32[20,3200]{1,0:T(8,128)}, u32[]{:S(2)}) copy-start(s32[20,3200]{1,0:T(8,128)} %dep_row.3) | copy-start | bytes 768004
  0.0 1.2 %copy-start.1 = (s32[20,3200]{1,0:T(8,128)S(1)}, s32[20,3200]{1,0:T(8,128)}, u32[]{:S(2)}) copy-start(s32[20,3200]{1,0:T(8,128)} %dep_col.3) | copy-start | bytes 768004
  1.2 3.1 %copy-start.2 = (bf16[4,20,3200]{2,0,1:T(4,128)(2,1)S(1)}, bf16[4,20,3200]{2,0,1:T(4,128)(2,1)}, u32[]{:S(2)}) copy-start(bf16[4,20,3200]{2,0,1:T(4,128)(2,1)} %param.7) | copy-start | bytes 1536004
  1.2 3.1 %copy-start.5 = (bf16[1,160,320]{2,1,0:T(8,128)(2,1)S(1)}, bf16[1,160,320]{2,1,0:T(8,128)(2,1)}, u32[]{:S(2)}) copy-start(bf16[1,160,320]{2,1,0:T(8,128)(2,1)} %param.13) | copy-start | bytes 307204
  1.2 3.1 %copy-start.6 = (s32[8]{0:T(128)S(1)}, s32[8]{0:T(128)}, u32[]{:S(2)}) copy-start(s32[8]{0:T(128)} %param.12) | copy-start | bytes 100
  1.3 8.9 %collective-permute-start = (bf16[16,3200]{1,0:T(8,128)(2,1)S(1)}, bf16[16,3200]{1,0:T(8,128)(2,1)S(1)}, u32[]{:S(2)}, u32[]{:S(2)}) collective-permute-start(bf16[16,3200]{1,0:T(8,128)(2,1)S(1)} %get-tuple-element.13.sent), channel_id=1, source_target_pairs={{0,4},{4,8},{8,12},{12,16},{16,20},{20,24},{24,28},{28,0},{1,5},{5... | collective-permute-start | bytes 307208 | tf_op jit(solution)/shard_map/ppermute | solution.py:477

commit v18 on v17

--- a/solution.py
+++ b/solution.py
@@ -404,7 +404,9 @@
         fourier_out[at] = fourier[4 * pair : 4 * pair + 4].astype(jnp.bfloat16)
 
 
-def legendre_kernel(first_wave, coeffs, spread_analysis, out, spread_coeffs, *, levs, slices):
+def legendre_kernel(
+    first_wave, coeffs, spread_analysis, out, spread_coeffs, totals, blocks, *, levs, slices
+):
     members, _, rows = coeffs.shape
     bands = members // levs
     col_count = spread_analysis.shape[1]
@@ -415,13 +417,11 @@
     slice_of = jnp.where(column < rows, slice_of, -1)
 
     def spread(band):
-        block = jnp.concatenate(
-            [coeffs[band * levs + lev].astype(jnp.float32) for lev in range(levs)],
-            axis=0,
-        )
-        block = jnp.concatenate(
-            [block, jnp.zeros((block.shape[0], LANES - rows), jnp.float32)], axis=1
-        )
+        for lev in range(levs):
+            blocks[band, 4 * lev : 4 * lev + 4, 0:rows] = coeffs[band * levs + lev].astype(
+                jnp.float32
+            )
+        block = blocks[band]
         spread_coeffs[:, tile_at(band)] = jnp.concatenate(
             [jnp.where(slice_of == f, block, 0.0) for f in range(slices)], axis=0
         ).astype(jnp.bfloat16)
@@ -435,11 +435,17 @@
             spread_coeffs[:, part], spread_analysis[part, :], preferred_element_type=jnp.float32
         )
         total = product if total is None else total + product
-    first = first_wave[0:2, :] > 0.0
-    for f in range(slices):
-        for lev in range(levs):
-            at = (f * levs + lev) * 4
-            out[lev * slices + f] = jnp.where(first, total[at : at + 2], total[at + 2 : at + 4])
+    for t in range(totals.shape[0]):
+        cols = slice(t * LANES, min((t + 1) * LANES, col_count))
+        width = cols.stop - cols.start
+        totals[t, 0 : total.shape[0], 0:width] = total[:, cols]
+        first = first_wave[0:2, cols] > 0.0
+        for f in range(slices):
+            for lev in range(levs):
+                at = (f * levs + lev) * 4
+                out[lev * slices + f, :, cols] = jnp.where(
+                    first, totals[t, at : at + 2, 0:width], totals[t, at + 2 : at + 4, 0:width]
+                )
 
 
 def shards(grid, dep_row, dep_col, lat_frac, lon_frac, pair_ids, analysis):
@@ -526,7 +532,11 @@
         out_shape=jax.ShapeDtypeStruct((levs * slices, 2, col_count), jnp.float32),
         in_specs=[vmem] * 3,
         out_specs=vmem,
-        scratch_shapes=[pltpu.VMEM((4 * levs * slices, bands * LANES), jnp.bfloat16)],
+        scratch_shapes=[
+            pltpu.VMEM((4 * levs * slices, bands * LANES), jnp.bfloat16),
+            pltpu.VMEM((-(-col_count // LANES), 4 * levs * slices, LANES), jnp.float32),
+            pltpu.VMEM((bands, 4 * levs, LANES), jnp.float32),
+        ],
         compiler_params=params,
     )(first_wave, coeffs, spread_analysis)
     return out[None]

time: 22.2 us -> 22.2 us (level)
  no operation moved by 1% of the time
where the time goes in v18:
time: 22.2 us; the launch traced here: 22 us
  blocking collectives  10.1 us (45%)
  Pallas kernels  5.22 us (24%)
  starting transfers between devices  3.02 us (14%)
  waiting for transfers between devices  2.39 us (11%)
  local copies, waits for them, and re-layouts  1.22 us (5%)
    all_to_all x1, blocking collectives, shards(): lax.all_to_all(fourier, ('lat', 'lev'), split_axis=0, concat_axis=0, tile...  10.1 us
    pallas_call x1, Pallas kernels, shards(): pl.pallas_call(functools.partial(inner_kernel, slices=slices, levs=levs),...  3.52 us
    ppermute x1, starting transfers between devices, shards(): lax.ppermute(sent_rim, 'lat', [(i, (i + 1) % bands) for i in range(bands)])  3.02 us
    ppermute x1, waiting for transfers between devices, shards(): lax.ppermute(sent_rim, 'lat', [(i, (i + 1) % bands) for i in range(bands)])  2.39 us
    pallas_call x1, Pallas kernels, shards(): pl.pallas_call(functools.partial(legendre_kernel, levs=levs, slices=slice...  0.91 us
    slice x1, local copies, waits for them, and re-layouts, shards(): by_row[band_rows - RIM:]  0.9 us
    pallas_call x1, Pallas kernels, shards(): pl.pallas_call(functools.partial(rim_kernel, slices=slices, levs=levs), o...  0.69 us
  transfers between devices with their start and end apart: 1, of which 1 were waited for; matrix products, arithmetic and copies ran while one was open for 0% of the time, Pallas kernels for 16%

profile of v18, /device:TPU:0, one launch (start us, length us, event | category | flops | bytes accessed | tf_op | source)
XLA Modules:
  0.0 22.0 jit_solution(1008959203112005864)
XLA Ops:
  0.0 0.0 copy-start.3
  0.0 0.0 copy-start.4
  0.0 0.0 copy-start
  0.0 0.0 copy-start.1
  0.0 0.9 %slice.4.last_rows = bf16[2,4,3200]{2,1,0:T(4,128)(2,1)S(1)} slice(bf16[20,4,3200]{2,1,0:T(4,128)(2,1)} %bitcast.5), slice={[18:20], [0:4], [0:3200]} | slice | bytes 102400 | tf_op jit(solution)/shard_map/slice | solution.py:482
  0.9 0.2 broadcast_in_dim.9._
  1.1 0.0 copy-done.3
  1.1 0.0 copy-done.4
  1.1 0.0 copy-done
  1.1 0.1 copy-done.1
  1.2 0.0 copy-start.2
  1.2 0.0 copy-start.5
  1.2 0.0 copy-start.6
  1.2 0.1 shard_map.73
  1.3 3.0 %collective-permute-start = (bf16[16,3200]{1,0:T(8,128)(2,1)S(1)}, bf16[16,3200]{1,0:T(8,128)(2,1)S(1)}, u32[]{:S(2)}, u32[]{:S(2)}) collective-permute-start(bf16[16,3200]{1,0:T(8,128)(2,1)S(1)} %get-tuple-element.13.sent), channel_id=1, source_target_pairs={{0,4},{4,8},{8,12},{12,16},{16,20},{20,24},{24,28},{28,0},{1,5},{5... | collective-permute-start | bytes 307208 | tf_op jit(solution)/shard_map/ppermute | solution.py:483
  4.4 0.0 copy-done.2
  4.4 0.0 copy-done.5
  4.4 0.0 copy-done.6
  4.4 3.5 %shard_map.74 = (f32[32,80]{1,0:T(8,128)S(1)}, bf16[32,3712]{1,0:T(8,128)(2,1)S(1)}, bf16[1024,320]{1,0:T(8,128)(2,1)S(1)}, bf16[16,3200]{1,0:T(8,128)(2,1)S(1)}...) custom-call(bf16[20,4,3200]{2,1,0:T(4,128)(2,1)S(1)} %bitcast.6, ...), custom_call_target="tpu_custom_call", output_to_operand_aliasing={{5}: (9, {})} | custom-call | flops 100000000 | bytes 2000000 | tf_op jit(solution)/shard_map/pallas_call | solution.py:485
  7.9 2.4 %collective-permute-done.arrived = bf16[16,3200]{1,0:T(8,128)(2,1)S(1)} collective-permute-done((bf16[16,3200]{1,0:T(8,128)(2,1)S(1)}, bf16[16,3200]{1,0:T(8,128)(2,1)S(1)}, u32[]{:S(2)}, u32[]{:S(2)}) %collective-permute-start) | collective-permute-done | bytes 102432 | tf_op jit(solution)/shard_map/ppermute | solution.py:483
  10.3 0.7 %shard_map.75 = bf16[32,4,96]{2,1,0:T(4,128)(2,1)S(1)} custom-call(bf16[16,3200]{1,0:T(8,128)(2,1)S(1)} %collective-permute-done.arrived, bf16[16,3200]{1,0:T(8,128)(2,1)S(1)} %get-tuple-element.17.own, bf16[32,3712]{1,0:T(8,128)(2,1)S(1)} %get-tuple-element.18.basis, f32[32,80]{1,0:T(8,128)S(1)} %get-tuple-element.19.inner_fourier), custom_call_target="tpu_custom_call" | custom-call | tf_op jit(solution)/shard_map/pallas_call | solution.py:515
  11.0 10.1 %all_to_all.5.coeffs = bf16[32,4,96]{2,1,0:T(4,128)(2,1)S(1)} all-to-all(bf16[32,4,96]{2,1,0:T(4,128)(2,1)S(1)} %shard_map.75), channel_id=1, replica_groups=mesh['lat'=8,'lev'=4] {'lat','lev'}, dimensions={0} | all-to-all | bytes 49152 | tf_op jit(solution)/shard_map/all_to_all | solution.py:527
  21.1 0.9 %shard_map.76 = f32[16,2,320]{2,1,0:T(2,128)} custom-call(f32[8,320]{1,0:T(8,128)S(1)} %get-tuple-element.16.first_wave, bf16[32,4,96]{2,1,0:T(4,128)(2,1)S(1)} %all_to_all.5.coeffs, bf16[1024,320]{1,0:T(8,128)(2,1)S(1)} %get-tuple-element.20.spread_analysis), custom_call_target="tpu_custom_call" | custom-call | tf_op jit(solution)/shard_map/pallas_call | solution.py:530
Async XLA Ops:
  0.0 1.1 %copy-start.3 = (bf16[20,3200]{1,0:T(8,128)(2,1)S(1)}, bf16[20,3200]{1,0:T(8,128)(2,1)}, u32[]{:S(2)}) copy-start(bf16[20,3200]{1,0:T(8,128)(2,1)} %lat_frac.3) | copy-start | bytes 384004
  0.0 1.1 %copy-start.4 = (bf16[20,3200]{1,0:T(8,128)(2,1)S(1)}, bf16[20,3200]{1,0:T(8,128)(2,1)}, u32[]{:S(2)}) copy-start(bf16[20,3200]{1,0:T(8,128)(2,1)} %lon_frac.3) | copy-start | bytes 384004
  0.0 1.1 %copy-start = (s32[20,3200]{1,0:T(8,128)S(1)}, s32[20,3200]{1,0:T(8,128)}, u32[]{:S(2)}) copy-start(s32[20,3200]{1,0:T(8,128)} %dep_row.3) | copy-start | bytes 768004
  0.0 1.2 %copy-start.1 = (s32[20,3200]{1,0:T(8,128)S(1)}, s32[20,3200]{1,0:T(8,128)}, u32[]{:S(2)}) copy-start(s32[20,3200]{1,0:T(8,128)} %dep_col.3) | copy-start | bytes 768004
  1.2 3.1 %copy-start.2 = (bf16[4,20,3200]{2,0,1:T(4,128)(2,1)S(1)}, bf16[4,20,3200]{2,0,1:T(4,128)(2,1)}, u32[]{:S(2)}) copy-start(bf16[4,20,3200]{2,0,1:T(4,128)(2,1)} %param.7) | copy-start | bytes 1536004
  1.2 3.1 %copy-start.5 = (bf16[1,160,320]{2,1,0:T(8,128)(2,1)S(1)}, bf16[1,160,320]{2,1,0:T(8,128)(2,1)}, u32[]{:S(2)}) copy-start(bf16[1,160,320]{2,1,0:T(8,128)(2,1)} %param.13) | copy-start | bytes 307204
  1.2 3.1 %copy-start.6 = (s32[8]{0:T(128)S(1)}, s32[8]{0:T(128)}, u32[]{:S(2)}) copy-start(s32[8]{0:T(128)} %param.12) | copy-start | bytes 100
  1.3 8.9 %collective-permute-start = (bf16[16,3200]{1,0:T(8,128)(2,1)S(1)}, bf16[16,3200]{1,0:T(8,128)(2,1)S(1)}, u32[]{:S(2)}, u32[]{:S(2)}) collective-permute-start(bf16[16,3200]{1,0:T(8,128)(2,1)S(1)} %get-tuple-element.13.sent), channel_id=1, source_target_pairs={{0,4},{4,8},{8,12},{12,16},{16,20},{20,24},{24,28},{28,0},{1,5},{5... | collective-permute-start | bytes 307208 | tf_op jit(solution)/shard_map/ppermute | solution.py:483

commit v19 on v18

--- a/solution.py
+++ b/solution.py
@@ -201,22 +201,28 @@
     return [plan[fields * at : fields * (at + 1)] for at in range(3)]
 
 
-def spread_rows(analysis, out, band_rows, slices):
+def slots_of(band_rows):
+    width = band_rows + EDGE
+    return width, LANES // width
+
+
+def spread_rows(analysis, out, band_rows):
+    width, shared = slots_of(band_rows)
     inner = band_rows - EDGE
-    rim = RIM * slices
     place = lax.broadcasted_iota(jnp.int32, (LANES, 1), 0)
-    edge = place - slices * inner
-    edge_row = edge // slices
-    row = jnp.where(edge < 0, RIM + place % inner, edge_row)
-    row = jnp.where(edge >= rim, band_rows - EDGE + edge_row, row)
-    row = jnp.where(edge >= 2 * rim, edge_row - 3 * RIM, row)
-    row = jnp.where(edge >= 4 * rim, -band_rows, row)
-    for band in range(out.shape[0] // LANES):
-        start = max(0, band * band_rows - RIM) // 16 * 16
-        end = min(analysis.shape[0], -(-(band + 1) * band_rows // 16) * 16)
+    slot, rank = place // width, place % width
+    row = jnp.where(rank < inner, RIM + rank, rank - inner)
+    row = jnp.where(rank >= inner + RIM, band_rows - EDGE + rank - inner, row)
+    row = jnp.where(rank >= inner + EDGE, rank - inner - 3 * RIM, row)
+    row = row + slot * band_rows
+    row = jnp.where(slot < shared, row, -band_rows)
+    for group in range(out.shape[0] // LANES):
+        first = group * shared * band_rows
+        start = max(0, first - RIM) // 16 * 16
+        end = min(analysis.shape[0], -(-(first + shared * band_rows) // 16) * 16)
         column = lax.broadcasted_iota(jnp.int32, (LANES, end - start), 1) + start
-        chosen = jnp.where((column - band * band_rows == row) & (row >= -RIM), 1.0, 0.0)
-        out[band * LANES : (band + 1) * LANES, :] = jnp.dot(
+        chosen = jnp.where((column - first == row) & (row >= -RIM), 1.0, 0.0)
+        out[group * LANES : (group + 1) * LANES, :] = jnp.dot(
             chosen.astype(jnp.bfloat16),
             analysis[start:end, :],
             preferred_element_type=jnp.float32,
@@ -332,7 +338,7 @@
     count = departed.shape[1] // LANES
     for ts in groups_of(count, INNER_AT_ONCE):
         group_of(ts)
-    spread_rows(analysis, spread_analysis, inner + EDGE, slices)
+    spread_rows(analysis, spread_analysis, band_rows)
     fourier_out[...] = jnp.concatenate(
         [add_up(None, basis, values, range(count)) for values in (departed, rim_departed)], axis=1
     )
@@ -410,31 +416,32 @@
     members, _, rows = coeffs.shape
     bands = members // levs
     col_count = spread_analysis.shape[1]
-    inner = rows // slices - 2 * EDGE
-    column = lax.broadcasted_iota(jnp.int32, (1, LANES), 1)
-    rim_at = column - inner * slices
-    slice_of = jnp.where(rim_at < 0, column // inner, rim_at % slices)
-    slice_of = jnp.where(column < rows, slice_of, -1)
-
-    def spread(band):
+    width, shared = slots_of(rows // slices - EDGE)
+    inner = width - 2 * EDGE
+    lane = lax.broadcasted_iota(jnp.int32, (4 * levs, LANES), 1)
+    slot, rank = lane // width, lane % width
+    rim_rank = inner * slices + (rank - inner) * slices
+    held_at = [
+        jnp.where(rank < inner, f * inner + rank, rim_rank + f).astype(jnp.int16)
+        for f in range(slices)
+    ]
+    slot = slot.astype(jnp.int16)
+    for band in range(bands):
         for lev in range(levs):
             blocks[band, 4 * lev : 4 * lev + 4, 0:rows] = coeffs[band * levs + lev].astype(
                 jnp.float32
             )
-        block = blocks[band]
-        spread_coeffs[:, tile_at(band)] = jnp.concatenate(
-            [jnp.where(slice_of == f, block, 0.0) for f in range(slices)], axis=0
-        ).astype(jnp.bfloat16)
-
-    for band in range(bands):
-        spread(band)
-    total = None
-    for at in range(0, bands * LANES, 2 * LANES):
-        part = slice(at, min(at + 2 * LANES, bands * LANES))
-        product = jnp.dot(
-            spread_coeffs[:, part], spread_analysis[part, :], preferred_element_type=jnp.float32
-        )
-        total = product if total is None else total + product
+    for group in range(-(-bands // shared)):
+        here = range(group * shared, min((group + 1) * shared, bands))
+        taken = [blocks[band].astype(jnp.bfloat16) for band in here]
+        for f in range(slices):
+            joined = jnp.zeros(slot.shape, jnp.bfloat16)
+            for at, block in enumerate(taken):
+                joined = jnp.where(slot == jnp.int16(at), lane_gather(block, held_at[f]), joined)
+            spread_coeffs[4 * levs * f : 4 * levs * (f + 1), tile_at(group)] = joined
+    total = jnp.dot(
+        spread_coeffs[...], spread_analysis[...], preferred_element_type=jnp.float32
+    )
     for t in range(totals.shape[0]):
         cols = slice(t * LANES, min((t + 1) * LANES, col_count))
         width = cols.stop - cols.start
@@ -457,6 +464,7 @@
     windows = -(-lon_count // SPAN)
     held_rows = -(-band_rows // 8) * 8
     fields = slices * EDGE
+    spread_count = -(-bands // slots_of(band_rows)[1]) * LANES
     place = jnp.reshape(lax.axis_index(("lat", "lev")), (1,)).astype(jnp.int32)
     vmem = pl.BlockSpec(memory_space=pltpu.VMEM)
     smem = pl.BlockSpec(memory_space=pltpu.SMEM)
@@ -487,7 +495,7 @@
         out_shape=(
             jax.ShapeDtypeStruct((4 * pairs, slices * band_rows), jnp.float32),
             jax.ShapeDtypeStruct((4 * pairs, windows * LANES), jnp.bfloat16),
-            jax.ShapeDtypeStruct((bands * LANES, col_count), jnp.bfloat16),
+            jax.ShapeDtypeStruct((spread_count, col_count), jnp.bfloat16),
             rim_shape,
             jax.ShapeDtypeStruct((8, col_count), jnp.float32),
             jax.ShapeDtypeStruct(blank.shape, jnp.float32),
@@ -533,7 +541,7 @@
         in_specs=[vmem] * 3,
         out_specs=vmem,
         scratch_shapes=[
-            pltpu.VMEM((4 * levs * slices, bands * LANES), jnp.bfloat16),
+            pltpu.VMEM((4 * levs * slices, spread_count), jnp.bfloat16),
             pltpu.VMEM((-(-col_count // LANES), 4 * levs * slices, LANES), jnp.float32),
             pltpu.VMEM((bands, 4 * levs, LANES), jnp.float32),
         ],

time: 22.2 us -> 22.2 us (level)
  no operation moved by 1% of the time
where the time goes in v19:
time: 22.2 us; the launch traced here: 22 us
  blocking collectives  10.1 us (45%)
  Pallas kernels  5.17 us (23%)
  starting transfers between devices  3.02 us (14%)
  waiting for transfers between devices  2.43 us (11%)
  local copies, waits for them, and re-layouts  1.22 us (5%)
    all_to_all x1, blocking collectives, shards(): lax.all_to_all(fourier, ('lat', 'lev'), split_axis=0, concat_axis=0, tile...  10.1 us
    pallas_call x1, Pallas kernels, shards(): pl.pallas_call(functools.partial(inner_kernel, slices=slices, levs=levs),...  3.49 us
    ppermute x1, starting transfers between devices, shards(): lax.ppermute(sent_rim, 'lat', [(i, (i + 1) % bands) for i in range(bands)])  3.02 us
    ppermute x1, waiting for transfers between devices, shards(): lax.ppermute(sent_rim, 'lat', [(i, (i + 1) % bands) for i in range(bands)])  2.43 us
    slice x1, local copies, waits for them, and re-layouts, shards(): by_row[band_rows - RIM:]  0.9 us
    pallas_call x1, Pallas kernels, shards(): pl.pallas_call(functools.partial(legendre_kernel, levs=levs, slices=slice...  0.89 us
    pallas_call x1, Pallas kernels, shards(): pl.pallas_call(functools.partial(rim_kernel, slices=slices, levs=levs), o...  0.69 us
  transfers between devices with their start and end apart: 1, of which 1 were waited for; matrix products, arithmetic and copies ran while one was open for 0% of the time, Pallas kernels for 16%

profile of v19, /device:TPU:0, one launch (start us, length us, event | category | flops | bytes accessed | tf_op | source)
XLA Modules:
  0.0 22.0 jit_solution(15134495251262117327)
XLA Ops:
  0.0 0.0 copy-start.3
  0.0 0.0 copy-start.4
  0.0 0.0 copy-start
  0.0 0.0 copy-start.1
  0.0 0.9 %slice.4.last_rows = bf16[2,4,3200]{2,1,0:T(4,128)(2,1)S(1)} slice(bf16[20,4,3200]{2,1,0:T(4,128)(2,1)} %bitcast.5), slice={[18:20], [0:4], [0:3200]} | slice | bytes 102400 | tf_op jit(solution)/shard_map/slice | solution.py:490
  0.9 0.2 broadcast_in_dim.9._
  1.1 0.0 copy-done.3
  1.1 0.0 copy-done.4
  1.1 0.0 copy-done
  1.1 0.1 copy-done.1
  1.2 0.0 copy-start.2
  1.2 0.0 copy-start.5
  1.2 0.0 copy-start.6
  1.2 0.1 shard_map.73
  1.3 3.0 %collective-permute-start = (bf16[16,3200]{1,0:T(8,128)(2,1)S(1)}, bf16[16,3200]{1,0:T(8,128)(2,1)S(1)}, u32[]{:S(2)}, u32[]{:S(2)}) collective-permute-start(bf16[16,3200]{1,0:T(8,128)(2,1)S(1)} %get-tuple-element.13.sent), channel_id=1, source_target_pairs={{0,4},{4,8},{8,12},{12,16},{16,20},{20,24},{24,28},{28,0},{1,5},{5... | collective-permute-start | bytes 307208 | tf_op jit(solution)/shard_map/ppermute | solution.py:491
  4.4 0.0 copy-done.2
  4.4 0.0 copy-done.5
  4.4 0.0 copy-done.6
  4.4 3.5 %shard_map.74 = (f32[32,80]{1,0:T(8,128)S(1)}, bf16[32,3712]{1,0:T(8,128)(2,1)S(1)}, bf16[256,320]{1,0:T(8,128)(2,1)S(1)}, bf16[16,3200]{1,0:T(8,128)(2,1)S(1)},...) custom-call(bf16[20,4,3200]{2,1,0:T(4,128)(2,1)S(1)} %bitcast.6, ...), custom_call_target="tpu_custom_call", output_to_operand_aliasing={{5}: (9, {})} | custom-call | flops 100000000 | bytes 2000000 | tf_op jit(solution)/shard_map/pallas_call | solution.py:493
  7.9 2.4 %collective-permute-done.arrived = bf16[16,3200]{1,0:T(8,128)(2,1)S(1)} collective-permute-done((bf16[16,3200]{1,0:T(8,128)(2,1)S(1)}, bf16[16,3200]{1,0:T(8,128)(2,1)S(1)}, u32[]{:S(2)}, u32[]{:S(2)}) %collective-permute-start) | collective-permute-done | bytes 102432 | tf_op jit(solution)/shard_map/ppermute | solution.py:491
  10.3 0.7 %shard_map.75 = bf16[32,4,96]{2,1,0:T(4,128)(2,1)S(1)} custom-call(bf16[16,3200]{1,0:T(8,128)(2,1)S(1)} %collective-permute-done.arrived, bf16[16,3200]{1,0:T(8,128)(2,1)S(1)} %get-tuple-element.17.own, bf16[32,3712]{1,0:T(8,128)(2,1)S(1)} %get-tuple-element.18.basis, f32[32,80]{1,0:T(8,128)S(1)} %get-tuple-element.19.inner_fourier), custom_call_target="tpu_custom_call" | custom-call | tf_op jit(solution)/shard_map/pallas_call | solution.py:523
  11.0 10.1 %all_to_all.5.coeffs = bf16[32,4,96]{2,1,0:T(4,128)(2,1)S(1)} all-to-all(bf16[32,4,96]{2,1,0:T(4,128)(2,1)S(1)} %shard_map.75), channel_id=1, replica_groups=mesh['lat'=8,'lev'=4] {'lat','lev'}, dimensions={0} | all-to-all | bytes 49152 | tf_op jit(solution)/shard_map/all_to_all | solution.py:535
  21.1 0.9 %shard_map.76 = f32[16,2,320]{2,1,0:T(2,128)} custom-call(f32[8,320]{1,0:T(8,128)S(1)} %get-tuple-element.16.first_wave, bf16[32,4,96]{2,1,0:T(4,128)(2,1)S(1)} %all_to_all.5.coeffs, bf16[256,320]{1,0:T(8,128)(2,1)S(1)} %get-tuple-element.20.spread_analysis), custom_call_target="tpu_custom_call" | custom-call | tf_op jit(solution)/shard_map/pallas_call | solution.py:538
Async XLA Ops:
  0.0 1.1 %copy-start.3 = (bf16[20,3200]{1,0:T(8,128)(2,1)S(1)}, bf16[20,3200]{1,0:T(8,128)(2,1)}, u32[]{:S(2)}) copy-start(bf16[20,3200]{1,0:T(8,128)(2,1)} %lat_frac.3) | copy-start | bytes 384004
  0.0 1.1 %copy-start.4 = (bf16[20,3200]{1,0:T(8,128)(2,1)S(1)}, bf16[20,3200]{1,0:T(8,128)(2,1)}, u32[]{:S(2)}) copy-start(bf16[20,3200]{1,0:T(8,128)(2,1)} %lon_frac.3) | copy-start | bytes 384004
  0.0 1.1 %copy-start = (s32[20,3200]{1,0:T(8,128)S(1)}, s32[20,3200]{1,0:T(8,128)}, u32[]{:S(2)}) copy-start(s32[20,3200]{1,0:T(8,128)} %dep_row.3) | copy-start | bytes 768004
  0.0 1.2 %copy-start.1 = (s32[20,3200]{1,0:T(8,128)S(1)}, s32[20,3200]{1,0:T(8,128)}, u32[]{:S(2)}) copy-start(s32[20,3200]{1,0:T(8,128)} %dep_col.3) | copy-start | bytes 768004
  1.2 3.1 %copy-start.2 = (bf16[4,20,3200]{2,0,1:T(4,128)(2,1)S(1)}, bf16[4,20,3200]{2,0,1:T(4,128)(2,1)}, u32[]{:S(2)}) copy-start(bf16[4,20,3200]{2,0,1:T(4,128)(2,1)} %param.7) | copy-start | bytes 1536004
  1.2 3.1 %copy-start.5 = (bf16[1,160,320]{2,1,0:T(8,128)(2,1)S(1)}, bf16[1,160,320]{2,1,0:T(8,128)(2,1)}, u32[]{:S(2)}) copy-start(bf16[1,160,320]{2,1,0:T(8,128)(2,1)} %param.13) | copy-start | bytes 307204
  1.2 3.1 %copy-start.6 = (s32[8]{0:T(128)S(1)}, s32[8]{0:T(128)}, u32[]{:S(2)}) copy-start(s32[8]{0:T(128)} %param.12) | copy-start | bytes 100
  1.3 8.9 %collective-permute-start = (bf16[16,3200]{1,0:T(8,128)(2,1)S(1)}, bf16[16,3200]{1,0:T(8,128)(2,1)S(1)}, u32[]{:S(2)}, u32[]{:S(2)}) collective-permute-start(bf16[16,3200]{1,0:T(8,128)(2,1)S(1)} %get-tuple-element.13.sent), channel_id=1, source_target_pairs={{0,4},{4,8},{8,12},{12,16},{16,20},{20,24},{24,28},{28,0},{1,5},{5... | collective-permute-start | bytes 307208 | tf_op jit(solution)/shard_map/ppermute | solution.py:491

commit v20 on v19

--- a/solution.py
+++ b/solution.py
@@ -132,29 +132,31 @@
     return [row_step.astype(jnp.float32), (shift + REACH).astype(jnp.float32)] + fracs
 
 
-def pack_kernel(
-    place, dep_row, dep_col, lat_frac, lon_frac, last_rows, _,
-    sent_out, place_out, _blank, held, *, levs,
+def rows_kernel(by_row, _, sent_out, _blank, held):
+    band_rows, slices, lon_count = by_row.shape
+    for t in range(lon_count // LANES):
+        for row in range(RIM):
+            held[t, row * slices : (row + 1) * slices, :] = by_row[
+                band_rows - RIM + row, :, tile_at(t)
+            ].astype(jnp.float32)
+        sent_out[:, tile_at(t)] = held[t].astype(jnp.bfloat16)
+
+
+def data_kernel(
+    place, dep_row, dep_col, lat_frac, lon_frac, _rows, sent_out, place_out, held, *, levs
 ):
     band_rows, lon_count = dep_row.shape
-    slices = last_rows.shape[1]
-    rim = RIM * slices
     place_out[...] = jnp.full(place_out.shape, place[0], jnp.int32)
     first_row = place[0] // levs * band_rows
     start = band_rows // 8 * 8
     skip = band_rows - RIM - start
     for t in range(lon_count // LANES):
-        cols = tile_at(t)
-        for row in range(RIM):
-            held[t, row * slices : (row + 1) * slices, :] = last_rows[row, :, cols].astype(
-                jnp.float32
-            )
         parts = departures(
             slice(start, band_rows), t, first_row, dep_row, dep_col, lat_frac, lon_frac
         )
         for at, part in enumerate(parts):
-            held[t, rim + RIM * at : rim + RIM * (at + 1), :] = part[skip:]
-        sent_out[:, cols] = held[t].astype(jnp.bfloat16)
+            held[t, RIM * at : RIM * (at + 1), :] = part[skip:]
+        sent_out[:, tile_at(t)] = held[t].astype(jnp.bfloat16)
 
 
 def waves_of(ids, group):
@@ -185,11 +187,11 @@
 
 def rim_spread(slices):
     fields = EDGE * slices
-    shape = (3 * fields, 2 * RIM * (slices + 4))
+    shape = (3 * fields, 8 * RIM)
     wanted = lax.broadcasted_iota(jnp.int32, shape, 0)
     held = lax.broadcasted_iota(jnp.int32, shape, 1)
     kind, rim_row = wanted // fields, wanted % fields // slices
-    base = rim_row // RIM * RIM * (slices + 4) + RIM * slices + rim_row % RIM
+    base = rim_row // RIM * 4 * RIM + rim_row % RIM
     spread = jnp.where((kind == 0) & (held == base), float(1 << ROW_BITS), 0.0)
     spread += jnp.where(held == base + RIM * (kind + 1), 1.0, 0.0)
     return spread.astype(jnp.bfloat16)
@@ -238,9 +240,9 @@
 
 
 def inner_kernel(
-    by_row, dep_row, dep_col, lat_frac, lon_frac, sent, place, pair_ids, analysis, _,
+    by_row, dep_row, dep_col, lat_frac, lon_frac, place, pair_ids, analysis, _,
     fourier_out, basis, spread_analysis, own, first_wave_out, windows,
-    departed, rim_departed, steps, grid, rows, parts, plans, *, slices, levs,
+    departed, rim_departed, steps, grid, rows, parts, plans, edges, *, slices, levs,
 ):
     band_rows, lon_count = dep_row.shape
     inner = band_rows - 2 * RIM
@@ -264,8 +266,12 @@
             plans[at * inner : (at + 1) * inner, cols] = parts[
                 slot, at, RIM : RIM + inner, :
             ].astype(jnp.bfloat16)
-        own[:, cols] = jnp.concatenate(
-            [rows[slot, 0:rim, :]] + [part[0:RIM] for part in data], axis=0
+        own_data = [part[0:RIM] for part in data]
+        own[:, cols] = jnp.concatenate([rows[slot, 0:rim, :]] + own_data, axis=0).astype(
+            jnp.bfloat16
+        )
+        edges[:, cols] = jnp.concatenate(
+            own_data + [part[band_rows - RIM :] for part in data], axis=0
         ).astype(jnp.bfloat16)
 
     pairs, col_count = pair_ids.shape[1], first_wave_out.shape[1]
@@ -288,7 +294,7 @@
     waves = [waves_of(ids, at) for at in range(quads if few else 0)]
 
     def group_of(ts):
-        blocks = [cut((grid, plans, own, sent), t, lon_count, steps) for t in ts]
+        blocks = [cut((grid, plans, edges), t, lon_count, steps) for t in ts]
         for t, block in zip(ts, blocks):
             windows[t, rim : rim + held, :] = block[:held]
         results, rim_results = [], []
@@ -345,7 +351,8 @@
 
 
 def rim_kernel(
-    arrived, own, basis, inner_fourier, fourier_out, windows, plans, departed, *, slices, levs
+    arrived, arrived_data, own, basis, inner_fourier, fourier_out, windows, plans, departed,
+    *, slices, levs,
 ):
     lon_count = arrived.shape[1]
     rim, fields = RIM * slices, EDGE * slices
@@ -365,10 +372,11 @@
         return row_weight * (west + lon_weight * (east - west))
 
     def prepare(t):
-        for at, side in enumerate((arrived, own)):
-            block = turned(side, t, lon_count).astype(jnp.float32)
-            windows[t, rim * at : rim * (at + 1), :] = block[:rim]
-            plans[t, 4 * RIM * at : 4 * RIM * (at + 1), :] = block[rim:]
+        block = turned(own, t, lon_count).astype(jnp.float32)
+        windows[t, 0:rim, :] = turned(arrived, t, lon_count).astype(jnp.float32)
+        windows[t, rim:, :] = block[:rim]
+        plans[t, 0 : 4 * RIM, :] = turned(arrived_data, t, lon_count).astype(jnp.float32)
+        plans[t, 4 * RIM :, :] = block[rim:]
 
     def finish(t):
         row_step, shift, lat_weight, lon_weight = [
@@ -472,23 +480,31 @@
 
     blank = jnp.zeros((windows, (band_rows + 2 * RIM) * slices, LANES), jnp.float32)
     by_row = grid.transpose(1, 0, 2)
-    rim_shape = jax.ShapeDtypeStruct((RIM * (slices + 4), lon_count), jnp.bfloat16)
-    sent_rim, wide_place, blank = pl.pallas_call(
-        functools.partial(pack_kernel, levs=levs),
+    upwards = [(i, (i + 1) % bands) for i in range(bands)]
+    rows_shape = jax.ShapeDtypeStruct((RIM * slices, lon_count), jnp.bfloat16)
+    data_shape = jax.ShapeDtypeStruct((4 * RIM, lon_count), jnp.bfloat16)
+    sent_rows, blank = pl.pallas_call(
+        rows_kernel,
+        out_shape=(rows_shape, jax.ShapeDtypeStruct(blank.shape, jnp.float32)),
+        in_specs=[vmem] * 2,
+        out_specs=(vmem,) * 2,
+        input_output_aliases={1: 1},
+        scratch_shapes=[pltpu.VMEM((lon_count // LANES, RIM * slices, LANES), jnp.float32)],
+        compiler_params=params,
+    )(by_row, blank)
+    arrived_rows = lax.ppermute(sent_rows, "lat", upwards)
+    sent_data, wide_place = pl.pallas_call(
+        functools.partial(data_kernel, levs=levs),
         out_shape=(
-            rim_shape,
+            data_shape,
             jax.ShapeDtypeStruct((8, LANES), jnp.int32),
-            jax.ShapeDtypeStruct(blank.shape, jnp.float32),
         ),
-        in_specs=[smem] + [vmem] * 6,
-        out_specs=(vmem,) * 3,
-        input_output_aliases={6: 2},
-        scratch_shapes=[
-            pltpu.VMEM((lon_count // LANES, RIM * (slices + 4), LANES), jnp.float32)
-        ],
+        in_specs=[smem] + [vmem] * 5,
+        out_specs=(vmem,) * 2,
+        scratch_shapes=[pltpu.VMEM((lon_count // LANES, 4 * RIM, LANES), jnp.float32)],
         compiler_params=params,
-    )(place, dep_row, dep_col, lat_frac, lon_frac, by_row[band_rows - RIM :], blank)
-    arrived_rim = lax.ppermute(sent_rim, "lat", [(i, (i + 1) % bands) for i in range(bands)])
+    )(place, dep_row, dep_col, lat_frac, lon_frac, sent_rows)
+    arrived_data = lax.ppermute(sent_data, "lat", upwards)
 
     inner_fourier, basis, spread_analysis, own_rim, first_wave, _ = pl.pallas_call(
         functools.partial(inner_kernel, slices=slices, levs=levs),
@@ -496,13 +512,13 @@
             jax.ShapeDtypeStruct((4 * pairs, slices * band_rows), jnp.float32),
             jax.ShapeDtypeStruct((4 * pairs, windows * LANES), jnp.bfloat16),
             jax.ShapeDtypeStruct((spread_count, col_count), jnp.bfloat16),
-            rim_shape,
+            jax.ShapeDtypeStruct((RIM * (slices + 4), lon_count), jnp.bfloat16),
             jax.ShapeDtypeStruct((8, col_count), jnp.float32),
             jax.ShapeDtypeStruct(blank.shape, jnp.float32),
         ),
-        in_specs=[vmem] * 10,
+        in_specs=[vmem] * 9,
         out_specs=(vmem,) * 6,
-        input_output_aliases={9: 5},
+        input_output_aliases={8: 5},
         scratch_shapes=[
             pltpu.VMEM((slices * inner, windows * LANES), jnp.bfloat16),
             pltpu.VMEM((fields, windows * LANES), jnp.bfloat16),
@@ -511,11 +527,12 @@
             pltpu.VMEM((5, band_rows * slices, LANES), jnp.float32),
             pltpu.VMEM((5, 3, held_rows, LANES), jnp.float32),
             pltpu.VMEM((3 * inner, lon_count), jnp.bfloat16),
+            pltpu.VMEM((8 * RIM, lon_count), jnp.bfloat16),
         ],
         compiler_params=params,
         cost_estimate=pl.CostEstimate(flops=100_000_000, bytes_accessed=2_000_000, transcendentals=0),
     )(
-        by_row, dep_row, dep_col, lat_frac, lon_frac, sent_rim, wide_place, pair_ids[None, :],
+        by_row, dep_row, dep_col, lat_frac, lon_frac, wide_place, pair_ids[None, :],
         analysis[0], blank,
     )
 
@@ -523,7 +540,7 @@
     fourier = pl.pallas_call(
         functools.partial(rim_kernel, slices=slices, levs=levs),
         out_shape=jax.ShapeDtypeStruct((bands * levs, 4, held_coeffs), jnp.bfloat16),
-        in_specs=[vmem] * 4,
+        in_specs=[vmem] * 5,
         out_specs=vmem,
         scratch_shapes=[
             pltpu.VMEM((windows, fields, LANES), jnp.float32),
@@ -531,7 +548,7 @@
             pltpu.VMEM((fields, windows * LANES), jnp.bfloat16),
         ],
         compiler_params=params,
-    )(arrived_rim, own_rim, basis, inner_fourier)
+    )(arrived_rows, arrived_data, own_rim, basis, inner_fourier)
     coeffs = lax.all_to_all(
         fourier, ("lat", "lev"), split_axis=0, concat_axis=0, tiled=True
     )

time: 22.2 us -> 23.2 us (1.045)
  starting transfers between devices: 3.02 us -> 4.54 us
  waiting for transfers between devices: 2.43 us -> 1.78 us
    ppermute x1 -> x2, starting transfers between devices: 3.02 us -> 4.54 us  [the longest x1 3.02 us: shards(): arrived_data = lax.ppermute(sent_data, 'lat', upwards)]
    unnamed x14, local copies, waits for them, and re-layouts: 0.16 us -> 1.11 us
    slice x1 -> x0, local copies, waits for them, and re-layouts: 0.9 us -> none  [shards(): by_row[band_rows - RIM:]]
    ppermute x1 -> x2, waiting for transfers between devices: 2.43 us -> 1.78 us  [the longest x1 1.4 us: shards(): arrived_rows = lax.ppermute(sent_rows, 'lat', upwards)]
  transfers between devices with their start and end apart: 1 -> 2, of which waited for: 1 -> 2; matrix products, arithmetic and copies ran while one was open for 0% -> 0% of each run, Pallas kernels for 16% -> 15%
where the time goes in v20:
time: 23.2 us; the launch traced here: 23 us
  blocking collectives  10.2 us (44%)
  Pallas kernels  5.24 us (23%)
  starting transfers between devices  4.54 us (20%)
  waiting for transfers between devices  1.78 us (8%)
  local copies, waits for them, and re-layouts  1.26 us (5%)
    all_to_all x1, blocking collectives, shards(): lax.all_to_all(fourier, ('lat', 'lev'), split_axis=0, concat_axis=0, tile...  10.2 us
    pallas_call x1, Pallas kernels, shards(): pl.pallas_call(functools.partial(inner_kernel, slices=slices, levs=levs),...  3.51 us
    ppermute x1, starting transfers between devices, shards(): arrived_data = lax.ppermute(sent_data, 'lat', upwards)  3.02 us
    ppermute x1, starting transfers between devices, shards(): arrived_rows = lax.ppermute(sent_rows, 'lat', upwards)  1.52 us
    ppermute x1, waiting for transfers between devices, shards(): arrived_rows = lax.ppermute(sent_rows, 'lat', upwards)  1.4 us
    unnamed x14, local copies, waits for them, and re-layouts  1.11 us
    pallas_call x1, Pallas kernels, shards(): pl.pallas_call(functools.partial(legendre_kernel, levs=levs, slices=slice...  0.89 us
    pallas_call x1, Pallas kernels, shards(): pl.pallas_call(functools.partial(rim_kernel, slices=slices, levs=levs), o...  0.74 us
  transfers between devices with their start and end apart: 2, of which 2 were waited for; matrix products, arithmetic and copies ran while one was open for 0% of the time, Pallas kernels for 15%

profile of v20, /device:TPU:0, one launch (start us, length us, event | category | flops | bytes accessed | tf_op | source)
XLA Modules:
  0.0 23.0 jit_solution(17051959921513767673)
XLA Ops:
  0.0 0.0 copy-start
  0.0 0.0 copy-start.1
  0.0 0.0 copy-start.2
  0.0 0.0 copy-start.3
  0.0 0.0 copy-start.4
  0.0 0.2 broadcast_in_dim.9._
  0.2 0.9 %copy-done = bf16[4,20,3200]{2,0,1:T(4,128)(2,1)S(1)} copy-done((bf16[4,20,3200]{2,0,1:T(4,128)(2,1)S(1)}, bf16[4,20,3200]{2,0,1:T(4,128)(2,1)}, u32[]{:S(2)}) %copy-start) | copy-done | bytes 512024
  1.0 0.0 copy-start.5
  1.0 0.0 copy-start.6
  1.1 0.1 copy-done.1
  1.1 0.1 copy-done.2
  1.2 0.0 copy-done.3
  1.3 0.0 copy-done.4
  1.3 0.1 shard_map.74
  1.4 3.0 %collective-permute-start.1 = (bf16[8,3200]{1,0:T(8,128)(2,1)S(1)}, bf16[8,3200]{1,0:T(8,128)(2,1)S(1)}, u32[]{:S(2)}, u32[]{:S(2)}) collective-permute-start(bf16[8,3200]{1,0:T(8,128)(2,1)S(1)} %get-tuple-element.18), channel_id=1, source_target_pairs={{0,4},{4,8},{8,12},{12,16},{16,20},{20,24},{24,28},{28,0},{1,5},{5... | collective-permute-start | bytes 153608 | tf_op jit(solution)/shard_map/ppermute | solution.py:507
  4.4 1.5 %collective-permute-start = (bf16[8,3200]{1,0:T(8,128)(2,1)S(1)}, bf16[8,3200]{1,0:T(8,128)(2,1)S(1)}, u32[]{:S(2)}, u32[]{:S(2)}) collective-permute-start(bf16[8,3200]{1,0:T(8,128)(2,1)S(1)} %get-tuple-element.14._rows), channel_id=1, source_target_pairs={{0,4},{4,8},{8,12},{12,16},{16,20},{20,24},{24,28},{28,0},{1,5},{5... | collective-permute-start | bytes 153608 | tf_op jit(solution)/shard_map/ppermute | solution.py:495
  5.9 0.0 copy-done.5
  5.9 0.0 copy-done.6
  5.9 3.5 %shard_map.75 = (f32[32,80]{1,0:T(8,128)S(1)}, bf16[32,3712]{1,0:T(8,128)(2,1)S(1)}, bf16[256,320]{1,0:T(8,128)(2,1)S(1)}, bf16[16,3200]{1,0:T(8,128)(2,1)S(1)},...) custom-call(bf16[20,4,3200]{2,1,0:T(4,128)(2,1)S(1)} %bitcast.6, ...), custom_call_target="tpu_custom_call", output_to_operand_aliasing={{5}: (8, {})} | custom-call | flops 100000000 | bytes 2000000 | tf_op jit(solution)/shard_map/pallas_call | solution.py:509
  9.4 0.4 %collective-permute-done.1.arrived_data = bf16[8,3200]{1,0:T(8,128)(2,1)S(1)} collective-permute-done((bf16[8,3200]{1,0:T(8,128)(2,1)S(1)}, bf16[8,3200]{1,0:T(8,128)(2,1)S(1)}, u32[]{:S(2)}, u32[]{:S(2)}) %collective-permute-start.1) | collective-permute-done | bytes 51232 | tf_op jit(solution)/shard_map/ppermute | solution.py:507
  9.8 1.4 %collective-permute-done.arrived = bf16[8,3200]{1,0:T(8,128)(2,1)S(1)} collective-permute-done((bf16[8,3200]{1,0:T(8,128)(2,1)S(1)}, bf16[8,3200]{1,0:T(8,128)(2,1)S(1)}, u32[]{:S(2)}, u32[]{:S(2)}) %collective-permute-start) | collective-permute-done | bytes 51232 | tf_op jit(solution)/shard_map/ppermute | solution.py:495
  11.2 0.7 %shard_map.76 = bf16[32,4,96]{2,1,0:T(4,128)(2,1)S(1)} custom-call(bf16[8,3200]{1,0:T(8,128)(2,1)S(1)} %collective-permute-done.arrived, bf16[8,3200]{1,0:T(8,128)(2,1)S(1)} %collective-permute-done.1.arrived_data, bf16[16,3200]{1,0:T(8,128)(2,1)S(1)} %get-tuple-element.19.own, bf16[32,3712]{1,0:T(8,128)(2,1)S(1)} %get-tuple-element.20.basis, ...), custom_call_target="tpu_custom_call" | custom-call | tf_op jit(solution)/shard_map/pallas_call | solution.py:540
  12.0 10.2 %all_to_all.5.coeffs = bf16[32,4,96]{2,1,0:T(4,128)(2,1)S(1)} all-to-all(bf16[32,4,96]{2,1,0:T(4,128)(2,1)S(1)} %shard_map.76), channel_id=1, replica_groups=mesh['lat'=8,'lev'=4] {'lat','lev'}, dimensions={0} | all-to-all | bytes 49152 | tf_op jit(solution)/shard_map/all_to_all | solution.py:552
  22.1 0.9 %shard_map.77 = f32[16,2,320]{2,1,0:T(2,128)} custom-call(f32[8,320]{1,0:T(8,128)S(1)} %get-tuple-element.17.first_wave, bf16[32,4,96]{2,1,0:T(4,128)(2,1)S(1)} %all_to_all.5.coeffs, bf16[256,320]{1,0:T(8,128)(2,1)S(1)} %get-tuple-element.22.spread_analysis), custom_call_target="tpu_custom_call" | custom-call | tf_op jit(solution)/shard_map/pallas_call | solution.py:555
  (1 shorter events, 0.0 us)
Async XLA Ops:
  0.0 1.0 %copy-start = (bf16[4,20,3200]{2,0,1:T(4,128)(2,1)S(1)}, bf16[4,20,3200]{2,0,1:T(4,128)(2,1)}, u32[]{:S(2)}) copy-start(bf16[4,20,3200]{2,0,1:T(4,128)(2,1)} %param.7) | copy-start | bytes 1536004
  0.0 1.1 %copy-start.1 = (s32[20,3200]{1,0:T(8,128)S(1)}, s32[20,3200]{1,0:T(8,128)}, u32[]{:S(2)}) copy-start(s32[20,3200]{1,0:T(8,128)} %dep_row.3) | copy-start | bytes 768004
  0.0 1.2 %copy-start.2 = (s32[20,3200]{1,0:T(8,128)S(1)}, s32[20,3200]{1,0:T(8,128)}, u32[]{:S(2)}) copy-start(s32[20,3200]{1,0:T(8,128)} %dep_col.3) | copy-start | bytes 768004
  0.0 1.2 %copy-start.3 = (bf16[20,3200]{1,0:T(8,128)(2,1)S(1)}, bf16[20,3200]{1,0:T(8,128)(2,1)}, u32[]{:S(2)}) copy-start(bf16[20,3200]{1,0:T(8,128)(2,1)} %lat_frac.3) | copy-start | bytes 384004
  0.0 1.3 %copy-start.4 = (bf16[20,3200]{1,0:T(8,128)(2,1)S(1)}, bf16[20,3200]{1,0:T(8,128)(2,1)}, u32[]{:S(2)}) copy-start(bf16[20,3200]{1,0:T(8,128)(2,1)} %lon_frac.3) | copy-start | bytes 384004
  1.0 4.9 %copy-start.5 = (bf16[1,160,320]{2,1,0:T(8,128)(2,1)S(1)}, bf16[1,160,320]{2,1,0:T(8,128)(2,1)}, u32[]{:S(2)}) copy-start(bf16[1,160,320]{2,1,0:T(8,128)(2,1)} %param.13) | copy-start | bytes 307204
  1.0 4.9 %copy-start.6 = (s32[8]{0:T(128)S(1)}, s32[8]{0:T(128)}, u32[]{:S(2)}) copy-start(s32[8]{0:T(128)} %param.12) | copy-start | bytes 100
  1.4 8.4 %collective-permute-start.1 = (bf16[8,3200]{1,0:T(8,128)(2,1)S(1)}, bf16[8,3200]{1,0:T(8,128)(2,1)S(1)}, u32[]{:S(2)}, u32[]{:S(2)}) collective-permute-start(bf16[8,3200]{1,0:T(8,128)(2,1)S(1)} %get-tuple-element.18), channel_id=1, source_target_pairs={{0,4},{4,8},{8,12},{12,16},{16,20},{20,24},{24,28},{28,0},{1,5},{5... | collective-permute-start | bytes 153608 | tf_op jit(solution)/shard_map/ppermute | solution.py:507
  4.4 6.8 %collective-permute-start = (bf16[8,3200]{1,0:T(8,128)(2,1)S(1)}, bf16[8,3200]{1,0:T(8,128)(2,1)S(1)}, u32[]{:S(2)}, u32[]{:S(2)}) collective-permute-start(bf16[8,3200]{1,0:T(8,128)(2,1)S(1)} %get-tuple-element.14._rows), channel_id=1, source_target_pairs={{0,4},{4,8},{8,12},{12,16},{16,20},{20,24},{24,28},{28,0},{1,5},{5... | collective-permute-start | bytes 153608 | tf_op jit(solution)/shard_map/ppermute | solution.py:495

commit v21 on v18

--- a/solution.py
+++ b/solution.py
@@ -15,8 +15,8 @@
 REACH = 8
 SPAN = LANES - 2 * REACH - 1
 ROW_BITS = 5
-INNER_AT_ONCE = 2
-RIM_AT_ONCE = 8
+INNER_AT_ONCE = 4
+RIM_AT_ONCE = 15
 
 
 def lane_gather(values, indices):

time: 22.2 us -> 22.2 us (level)
  transfers between devices with their start and end apart: 1 -> 1, of which waited for: 1 -> 1; matrix products, arithmetic and copies ran while one was open for 0% -> 0% of each run, Pallas kernels for 16% -> 17%
where the time goes in v21:
time: 22.2 us; the launch traced here: 22 us
  blocking collectives  10.1 us (45%)
  Pallas kernels  5.37 us (24%)
  starting transfers between devices  3.02 us (14%)
  waiting for transfers between devices  2.24 us (10%)
  local copies, waits for them, and re-layouts  1.22 us (5%)
    all_to_all x1, blocking collectives, shards(): lax.all_to_all(fourier, ('lat', 'lev'), split_axis=0, concat_axis=0, tile...  10.1 us
    pallas_call x1, Pallas kernels, shards(): pl.pallas_call(functools.partial(inner_kernel, slices=slices, levs=levs),...  3.67 us
    ppermute x1, starting transfers between devices, shards(): lax.ppermute(sent_rim, 'lat', [(i, (i + 1) % bands) for i in range(bands)])  3.02 us
    ppermute x1, waiting for transfers between devices, shards(): lax.ppermute(sent_rim, 'lat', [(i, (i + 1) % bands) for i in range(bands)])  2.24 us
    pallas_call x1, Pallas kernels, shards(): pl.pallas_call(functools.partial(legendre_kernel, levs=levs, slices=slice...  0.91 us
    slice x1, local copies, waits for them, and re-layouts, shards(): by_row[band_rows - RIM:]  0.9 us
    pallas_call x1, Pallas kernels, shards(): pl.pallas_call(functools.partial(rim_kernel, slices=slices, levs=levs), o...  0.69 us
  transfers between devices with their start and end apart: 1, of which 1 were waited for; matrix products, arithmetic and copies ran while one was open for 0% of the time, Pallas kernels for 17%

profile of v21, /device:TPU:0, one launch (start us, length us, event | category | flops | bytes accessed | tf_op | source)
XLA Modules:
  0.0 22.0 jit_solution(9500384548833914384)
XLA Ops:
  0.0 0.0 copy-start.3
  0.0 0.0 copy-start.4
  0.0 0.0 copy-start
  0.0 0.0 copy-start.1
  0.0 0.9 %slice.4.last_rows = bf16[2,4,3200]{2,1,0:T(4,128)(2,1)S(1)} slice(bf16[20,4,3200]{2,1,0:T(4,128)(2,1)} %bitcast.5), slice={[18:20], [0:4], [0:3200]} | slice | bytes 102400 | tf_op jit(solution)/shard_map/slice | solution.py:482
  0.9 0.2 broadcast_in_dim.9._
  1.1 0.0 copy-done.3
  1.1 0.0 copy-done.4
  1.1 0.0 copy-done
  1.1 0.1 copy-done.1
  1.2 0.0 copy-start.2
  1.2 0.0 copy-start.5
  1.2 0.0 copy-start.6
  1.2 0.1 shard_map.73
  1.3 3.0 %collective-permute-start = (bf16[16,3200]{1,0:T(8,128)(2,1)S(1)}, bf16[16,3200]{1,0:T(8,128)(2,1)S(1)}, u32[]{:S(2)}, u32[]{:S(2)}) collective-permute-start(bf16[16,3200]{1,0:T(8,128)(2,1)S(1)} %get-tuple-element.13.sent), channel_id=1, source_target_pairs={{0,4},{4,8},{8,12},{12,16},{16,20},{20,24},{24,28},{28,0},{1,5},{5... | collective-permute-start | bytes 307208 | tf_op jit(solution)/shard_map/ppermute | solution.py:483
  4.4 0.0 copy-done.2
  4.4 0.0 copy-done.5
  4.4 0.0 copy-done.6
  4.4 3.7 %shard_map.74 = (f32[32,80]{1,0:T(8,128)S(1)}, bf16[32,3712]{1,0:T(8,128)(2,1)S(1)}, bf16[1024,320]{1,0:T(8,128)(2,1)S(1)}, bf16[16,3200]{1,0:T(8,128)(2,1)S(1)}...) custom-call(bf16[20,4,3200]{2,1,0:T(4,128)(2,1)S(1)} %bitcast.6, ...), custom_call_target="tpu_custom_call", output_to_operand_aliasing={{5}: (9, {})} | custom-call | flops 100000000 | bytes 2000000 | tf_op jit(solution)/shard_map/pallas_call | solution.py:485
  8.0 2.2 %collective-permute-done.arrived = bf16[16,3200]{1,0:T(8,128)(2,1)S(1)} collective-permute-done((bf16[16,3200]{1,0:T(8,128)(2,1)S(1)}, bf16[16,3200]{1,0:T(8,128)(2,1)S(1)}, u32[]{:S(2)}, u32[]{:S(2)}) %collective-permute-start) | collective-permute-done | bytes 102432 | tf_op jit(solution)/shard_map/ppermute | solution.py:483
  10.3 0.7 %shard_map.75 = bf16[32,4,96]{2,1,0:T(4,128)(2,1)S(1)} custom-call(bf16[16,3200]{1,0:T(8,128)(2,1)S(1)} %collective-permute-done.arrived, bf16[16,3200]{1,0:T(8,128)(2,1)S(1)} %get-tuple-element.17.own, bf16[32,3712]{1,0:T(8,128)(2,1)S(1)} %get-tuple-element.18.basis, f32[32,80]{1,0:T(8,128)S(1)} %get-tuple-element.19.inner_fourier), custom_call_target="tpu_custom_call" | custom-call | tf_op jit(solution)/shard_map/pallas_call | solution.py:515
  11.0 10.1 %all_to_all.5.coeffs = bf16[32,4,96]{2,1,0:T(4,128)(2,1)S(1)} all-to-all(bf16[32,4,96]{2,1,0:T(4,128)(2,1)S(1)} %shard_map.75), channel_id=1, replica_groups=mesh['lat'=8,'lev'=4] {'lat','lev'}, dimensions={0} | all-to-all | bytes 49152 | tf_op jit(solution)/shard_map/all_to_all | solution.py:527
  21.1 0.9 %shard_map.76 = f32[16,2,320]{2,1,0:T(2,128)} custom-call(f32[8,320]{1,0:T(8,128)S(1)} %get-tuple-element.16.first_wave, bf16[32,4,96]{2,1,0:T(4,128)(2,1)S(1)} %all_to_all.5.coeffs, bf16[1024,320]{1,0:T(8,128)(2,1)S(1)} %get-tuple-element.20.spread_analysis), custom_call_target="tpu_custom_call" | custom-call | tf_op jit(solution)/shard_map/pallas_call | solution.py:530
Async XLA Ops:
  0.0 1.1 %copy-start.3 = (bf16[20,3200]{1,0:T(8,128)(2,1)S(1)}, bf16[20,3200]{1,0:T(8,128)(2,1)}, u32[]{:S(2)}) copy-start(bf16[20,3200]{1,0:T(8,128)(2,1)} %lat_frac.3) | copy-start | bytes 384004
  0.0 1.1 %copy-start.4 = (bf16[20,3200]{1,0:T(8,128)(2,1)S(1)}, bf16[20,3200]{1,0:T(8,128)(2,1)}, u32[]{:S(2)}) copy-start(bf16[20,3200]{1,0:T(8,128)(2,1)} %lon_frac.3) | copy-start | bytes 384004
  0.0 1.1 %copy-start = (s32[20,3200]{1,0:T(8,128)S(1)}, s32[20,3200]{1,0:T(8,128)}, u32[]{:S(2)}) copy-start(s32[20,3200]{1,0:T(8,128)} %dep_row.3) | copy-start | bytes 768004
  0.0 1.2 %copy-start.1 = (s32[20,3200]{1,0:T(8,128)S(1)}, s32[20,3200]{1,0:T(8,128)}, u32[]{:S(2)}) copy-start(s32[20,3200]{1,0:T(8,128)} %dep_col.3) | copy-start | bytes 768004
  1.2 3.1 %copy-start.2 = (bf16[4,20,3200]{2,0,1:T(4,128)(2,1)S(1)}, bf16[4,20,3200]{2,0,1:T(4,128)(2,1)}, u32[]{:S(2)}) copy-start(bf16[4,20,3200]{2,0,1:T(4,128)(2,1)} %param.7) | copy-start | bytes 1536004
  1.2 3.1 %copy-start.5 = (bf16[1,160,320]{2,1,0:T(8,128)(2,1)S(1)}, bf16[1,160,320]{2,1,0:T(8,128)(2,1)}, u32[]{:S(2)}) copy-start(bf16[1,160,320]{2,1,0:T(8,128)(2,1)} %param.13) | copy-start | bytes 307204
  1.2 3.1 %copy-start.6 = (s32[8]{0:T(128)S(1)}, s32[8]{0:T(128)}, u32[]{:S(2)}) copy-start(s32[8]{0:T(128)} %param.12) | copy-start | bytes 100
  1.3 8.9 %collective-permute-start = (bf16[16,3200]{1,0:T(8,128)(2,1)S(1)}, bf16[16,3200]{1,0:T(8,128)(2,1)S(1)}, u32[]{:S(2)}, u32[]{:S(2)}) collective-permute-start(bf16[16,3200]{1,0:T(8,128)(2,1)S(1)} %get-tuple-element.13.sent), channel_id=1, source_target_pairs={{0,4},{4,8},{8,12},{12,16},{16,20},{20,24},{24,28},{28,0},{1,5},{5... | collective-permute-start | bytes 307208 | tf_op jit(solution)/shard_map/ppermute | solution.py:483

commit v22 on v19

--- a/solution.py
+++ b/solution.py
@@ -16,7 +16,7 @@
 SPAN = LANES - 2 * REACH - 1
 ROW_BITS = 5
 INNER_AT_ONCE = 2
-RIM_AT_ONCE = 8
+RIM_AT_ONCE = 15
 
 
 def lane_gather(values, indices):

time: 22.2 us -> 22.2 us (level)
  no operation moved by 1% of the time
where the time goes in v22:
time: 22.2 us; the launch traced here: 22 us
  blocking collectives  10.1 us (45%)
  Pallas kernels  5.16 us (23%)
  starting transfers between devices  3.02 us (14%)
  waiting for transfers between devices  2.43 us (11%)
  local copies, waits for them, and re-layouts  1.22 us (5%)
    all_to_all x1, blocking collectives, shards(): lax.all_to_all(fourier, ('lat', 'lev'), split_axis=0, concat_axis=0, tile...  10.1 us
    pallas_call x1, Pallas kernels, shards(): pl.pallas_call(functools.partial(inner_kernel, slices=slices, levs=levs),...  3.49 us
    ppermute x1, starting transfers between devices, shards(): lax.ppermute(sent_rim, 'lat', [(i, (i + 1) % bands) for i in range(bands)])  3.02 us
    ppermute x1, waiting for transfers between devices, shards(): lax.ppermute(sent_rim, 'lat', [(i, (i + 1) % bands) for i in range(bands)])  2.43 us
    slice x1, local copies, waits for them, and re-layouts, shards(): by_row[band_rows - RIM:]  0.9 us
    pallas_call x1, Pallas kernels, shards(): pl.pallas_call(functools.partial(legendre_kernel, levs=levs, slices=slice...  0.89 us
    pallas_call x1, Pallas kernels, shards(): pl.pallas_call(functools.partial(rim_kernel, slices=slices, levs=levs), o...  0.69 us
  transfers between devices with their start and end apart: 1, of which 1 were waited for; matrix products, arithmetic and copies ran while one was open for 0% of the time, Pallas kernels for 16%

profile of v22, /device:TPU:0, one launch (start us, length us, event | category | flops | bytes accessed | tf_op | source)
XLA Modules:
  0.0 22.0 jit_solution(14372520797069734595)
XLA Ops:
  0.0 0.0 copy-start.3
  0.0 0.0 copy-start.4
  0.0 0.0 copy-start
  0.0 0.0 copy-start.1
  0.0 0.9 %slice.4.last_rows = bf16[2,4,3200]{2,1,0:T(4,128)(2,1)S(1)} slice(bf16[20,4,3200]{2,1,0:T(4,128)(2,1)} %bitcast.5), slice={[18:20], [0:4], [0:3200]} | slice | bytes 102400 | tf_op jit(solution)/shard_map/slice | solution.py:490
  0.9 0.2 broadcast_in_dim.9._
  1.1 0.0 copy-done.3
  1.1 0.0 copy-done.4
  1.1 0.0 copy-done
  1.1 0.1 copy-done.1
  1.2 0.0 copy-start.2
  1.2 0.0 copy-start.5
  1.2 0.0 copy-start.6
  1.2 0.1 shard_map.73
  1.3 3.0 %collective-permute-start = (bf16[16,3200]{1,0:T(8,128)(2,1)S(1)}, bf16[16,3200]{1,0:T(8,128)(2,1)S(1)}, u32[]{:S(2)}, u32[]{:S(2)}) collective-permute-start(bf16[16,3200]{1,0:T(8,128)(2,1)S(1)} %get-tuple-element.13.sent), channel_id=1, source_target_pairs={{0,4},{4,8},{8,12},{12,16},{16,20},{20,24},{24,28},{28,0},{1,5},{5... | collective-permute-start | bytes 307208 | tf_op jit(solution)/shard_map/ppermute | solution.py:491
  4.4 0.0 copy-done.2
  4.4 0.0 copy-done.5
  4.4 0.0 copy-done.6
  4.4 3.5 %shard_map.74 = (f32[32,80]{1,0:T(8,128)S(1)}, bf16[32,3712]{1,0:T(8,128)(2,1)S(1)}, bf16[256,320]{1,0:T(8,128)(2,1)S(1)}, bf16[16,3200]{1,0:T(8,128)(2,1)S(1)},...) custom-call(bf16[20,4,3200]{2,1,0:T(4,128)(2,1)S(1)} %bitcast.6, ...), custom_call_target="tpu_custom_call", output_to_operand_aliasing={{5}: (9, {})} | custom-call | flops 100000000 | bytes 2000000 | tf_op jit(solution)/shard_map/pallas_call | solution.py:493
  7.9 2.4 %collective-permute-done.arrived = bf16[16,3200]{1,0:T(8,128)(2,1)S(1)} collective-permute-done((bf16[16,3200]{1,0:T(8,128)(2,1)S(1)}, bf16[16,3200]{1,0:T(8,128)(2,1)S(1)}, u32[]{:S(2)}, u32[]{:S(2)}) %collective-permute-start) | collective-permute-done | bytes 102432 | tf_op jit(solution)/shard_map/ppermute | solution.py:491
  10.3 0.7 %shard_map.75 = bf16[32,4,96]{2,1,0:T(4,128)(2,1)S(1)} custom-call(bf16[16,3200]{1,0:T(8,128)(2,1)S(1)} %collective-permute-done.arrived, bf16[16,3200]{1,0:T(8,128)(2,1)S(1)} %get-tuple-element.17.own, bf16[32,3712]{1,0:T(8,128)(2,1)S(1)} %get-tuple-element.18.basis, f32[32,80]{1,0:T(8,128)S(1)} %get-tuple-element.19.inner_fourier), custom_call_target="tpu_custom_call" | custom-call | tf_op jit(solution)/shard_map/pallas_call | solution.py:523
  11.0 10.1 %all_to_all.5.coeffs = bf16[32,4,96]{2,1,0:T(4,128)(2,1)S(1)} all-to-all(bf16[32,4,96]{2,1,0:T(4,128)(2,1)S(1)} %shard_map.75), channel_id=1, replica_groups=mesh['lat'=8,'lev'=4] {'lat','lev'}, dimensions={0} | all-to-all | bytes 49152 | tf_op jit(solution)/shard_map/all_to_all | solution.py:535
  21.1 0.9 %shard_map.76 = f32[16,2,320]{2,1,0:T(2,128)} custom-call(f32[8,320]{1,0:T(8,128)S(1)} %get-tuple-element.16.first_wave, bf16[32,4,96]{2,1,0:T(4,128)(2,1)S(1)} %all_to_all.5.coeffs, bf16[256,320]{1,0:T(8,128)(2,1)S(1)} %get-tuple-element.20.spread_analysis), custom_call_target="tpu_custom_call" | custom-call | tf_op jit(solution)/shard_map/pallas_call | solution.py:538
Async XLA Ops:
  0.0 1.1 %copy-start.3 = (bf16[20,3200]{1,0:T(8,128)(2,1)S(1)}, bf16[20,3200]{1,0:T(8,128)(2,1)}, u32[]{:S(2)}) copy-start(bf16[20,3200]{1,0:T(8,128)(2,1)} %lat_frac.3) | copy-start | bytes 384004
  0.0 1.1 %copy-start.4 = (bf16[20,3200]{1,0:T(8,128)(2,1)S(1)}, bf16[20,3200]{1,0:T(8,128)(2,1)}, u32[]{:S(2)}) copy-start(bf16[20,3200]{1,0:T(8,128)(2,1)} %lon_frac.3) | copy-start | bytes 384004
  0.0 1.1 %copy-start = (s32[20,3200]{1,0:T(8,128)S(1)}, s32[20,3200]{1,0:T(8,128)}, u32[]{:S(2)}) copy-start(s32[20,3200]{1,0:T(8,128)} %dep_row.3) | copy-start | bytes 768004
  0.0 1.2 %copy-start.1 = (s32[20,3200]{1,0:T(8,128)S(1)}, s32[20,3200]{1,0:T(8,128)}, u32[]{:S(2)}) copy-start(s32[20,3200]{1,0:T(8,128)} %dep_col.3) | copy-start | bytes 768004
  1.2 3.1 %copy-start.2 = (bf16[4,20,3200]{2,0,1:T(4,128)(2,1)S(1)}, bf16[4,20,3200]{2,0,1:T(4,128)(2,1)}, u32[]{:S(2)}) copy-start(bf16[4,20,3200]{2,0,1:T(4,128)(2,1)} %param.7) | copy-start | bytes 1536004
  1.2 3.1 %copy-start.5 = (bf16[1,160,320]{2,1,0:T(8,128)(2,1)S(1)}, bf16[1,160,320]{2,1,0:T(8,128)(2,1)}, u32[]{:S(2)}) copy-start(bf16[1,160,320]{2,1,0:T(8,128)(2,1)} %param.13) | copy-start | bytes 307204
  1.2 3.1 %copy-start.6 = (s32[8]{0:T(128)S(1)}, s32[8]{0:T(128)}, u32[]{:S(2)}) copy-start(s32[8]{0:T(128)} %param.12) | copy-start | bytes 100
  1.3 8.9 %collective-permute-start = (bf16[16,3200]{1,0:T(8,128)(2,1)S(1)}, bf16[16,3200]{1,0:T(8,128)(2,1)S(1)}, u32[]{:S(2)}, u32[]{:S(2)}) collective-permute-start(bf16[16,3200]{1,0:T(8,128)(2,1)S(1)} %get-tuple-element.13.sent), channel_id=1, source_target_pairs={{0,4},{4,8},{8,12},{12,16},{16,20},{20,24},{24,28},{28,0},{1,5},{5... | collective-permute-start | bytes 307208 | tf_op jit(solution)/shard_map/ppermute | solution.py:491
